TPU v7x, 256 devices: a whole 4x4x8 slice. The times are simulated.
256 devices in a mesh: wide: 32 (over y, z), narrow: 8 (over x, core).
Axes of the slice: x: 4, y: 4, z: 8, core: 2. Of those that a mesh axis runs over, the one named last changes fastest.
Arguments:
- entry_factor: bfloat16 [1152, 8, 64, 1024], P('wide', 'narrow'), may hold values from -6 to 6
- entry_panel: int32 [1152, 8], P('wide', 'narrow'), may hold values from 0 to 1
- entry_target: int32 [1152, 8], P('wide', 'narrow'), may hold values from 0 to 7, as said below
- entry_count: int32 [8, 32], P('narrow', 'wide'), may hold values from 1 to 36, 384 in all within a row
- panel_shared: bfloat16 [64, 64, 1024], P('wide', None, 'narrow'), may hold values from -0.1875 to 0.1875
- coupling: float32 [64, 64, 64], P('wide'), may hold values from -0.75 to 0.75
- probes: bfloat16 [64, 64, 1024], P('narrow'), may hold values from -6 to 6
Outputs:
- left_factor: float32 [64, 64, 1024], P('narrow', None, 'wide')
- right_factor: float32 [64, 64, 1024], P('narrow', None, 'wide')
Inputs may be any that keep to these rules, and one draw needn't show every extreme that they name: `entry_panel`: the local panel of an entry of any slot, live or not. `entry_target`: the local target of an entry; every target has at least one live entry. `entry_count`: the live slots of one device; for every owner the counts over the 32 wide indices sum to 384, and some device holds exactly 36.
All inputs are finite; a program needn't handle non-finite values.
Results may differ from a plain program's by a relative error of at most 0.0036.
Values may be sent and summed in bfloat16 or wider, within the bound.
No kernel may reach another device: no remote copies, remote signals or barrier semaphores. Data moves between devices by JAX's collectives and lax.ppermute only.
A program may use at most 64 MiB of HBM per device.

v0:
```python
import math

import jax
import jax.numpy as jnp
from jax import lax
from jax.sharding import PartitionSpec as P


def shards(entry_factor, entry_panel, entry_target, entry_count, panel_shared, coupling, probes):
    highest = lax.Precision.HIGHEST
    factors = entry_factor[:, 0]
    slot_count = factors.shape[0]
    rank_dim = factors.shape[1]
    full_width = factors.shape[2]
    panel_count = panel_shared.shape[0]
    target_count = probes.shape[0]
    live_mask = (jnp.arange(slot_count) < entry_count[0, 0]).astype(jnp.float32)
    pick_panel = (entry_panel == jnp.arange(panel_count)[None, :]).astype(jnp.float32) * live_mask[
        :, None
    ]
    pick_target = (entry_target == jnp.arange(target_count)[None, :]).astype(jnp.float32)
    pair_pick = (pick_panel[:, :, None] * pick_target[:, None, :]).reshape(
        slot_count, panel_count * target_count
    )
    gathered = lax.all_gather(panel_shared, "narrow", axis=2, tiled=True)
    projected = jnp.einsum("drb,tkb->dtrk", gathered, probes, preferred_element_type=jnp.float32)
    coefficients = jnp.einsum("dij,dtjk->dtik", coupling, projected, precision=highest).astype(
        jnp.bfloat16
    )
    coeff_table = coefficients.reshape(panel_count * target_count, rank_dim * rank_dim)
    chosen = jnp.dot(
        pair_pick.astype(jnp.bfloat16), coeff_table, preferred_element_type=jnp.float32
    )
    chosen = chosen.astype(jnp.bfloat16).reshape(slot_count, rank_dim, rank_dim)
    contributions = jnp.einsum("eji,ejb->eib", chosen, factors, preferred_element_type=jnp.float32)
    sketch = jnp.einsum("et,eib->tib", pick_target, contributions, precision=highest)
    wide_count = lax.axis_size("wide")
    share_cols = full_width // wide_count
    sketch_sum = lax.psum(sketch, "wide")
    gram_matrix = jnp.einsum("tib,tjb->tij", sketch_sum, sketch_sum, precision=highest)
    lower_factor = jnp.linalg.cholesky(gram_matrix)
    basis = jax.scipy.linalg.solve_triangular(lower_factor, sketch_sum, lower=True)
    basis_round = basis.astype(jnp.bfloat16)
    own_basis = lax.dynamic_slice_in_dim(basis, lax.axis_index("wide") * share_cols, share_cols, 2)
    selected = jnp.einsum(
        "et,tkb->ekb",
        pick_target.astype(jnp.bfloat16),
        basis_round,
        preferred_element_type=jnp.float32,
    )
    selected = selected.astype(jnp.bfloat16)
    back_terms = jnp.einsum("eib,ekb->eik", factors, selected, preferred_element_type=jnp.float32)
    summed = jnp.einsum("ep,eik->pik", pair_pick, back_terms, precision=highest)
    summed = summed.reshape(panel_count, target_count, rank_dim, rank_dim)
    middle_terms = jnp.einsum("dtik,dij->dtkj", summed, coupling, precision=highest)
    partial_rows = jnp.einsum(
        "dtkj,djb->tkb", middle_terms, gathered.astype(jnp.float32), precision=highest
    )
    coeff_part = lax.psum_scatter(partial_rows, "wide", scatter_dimension=2, tiled=True)
    root_width = math.sqrt(full_width)
    return (own_basis * root_width, coeff_part / root_width)


def solution(mesh):
    placed = (
        P("wide", "narrow", None, None),
        P("wide", "narrow"),
        P("wide", "narrow"),
        P("narrow", "wide"),
        P("wide", None, "narrow"),
        P("wide", None, None),
        P("narrow", None, None),
    )
    return jax.shard_map(
        shards,
        mesh=mesh,
        in_specs=placed,
        out_specs=(P("narrow", None, "wide"), P("narrow", None, "wide")),
        check_vma=False,
    )
```

profile of v0, /device:TPU:6, one launch (start us, length us, event | category | flops | bytes accessed | tf_op | source)
XLA Modules:
  0.0 539.2 jit_solution(12465950192728118837)
XLA Ops:
  7.2 0.0 copy-start
  7.2 0.0 all-reduce.2.cloned.1.call-start
  7.2 0.7 fusion.36
  8.0 11.5 %all_gather.3 = bf16[2,64,1024]{2,1,0:T(8,128)(2,1)S(1)} all-gather(bf16[2,64,128]{2,1,0:T(8,128)(2,1)} %param.11), channel_id=1, replica_groups=mesh['wide'=32,'narrow'=8] {'narrow'}, dimensions={2}, use_global_device_ids=true | all-gather | bytes 294912 | tf_op jit(solution)/shard_map/all_gather | solution.py:25
  19.4 0.0 copy-start.2
  19.4 0.7 copy-done.2
  20.2 0.0 copy-done
  20.2 0.5 convolution_bitcast_fusion.1
  20.6 1.4 fusion.18
  22.1 0.2 copy.23
  22.2 0.3 reshape.98
  23.2 0.7 compare_select_fusion
  23.8 0.3 convolution_convert_fusion
  24.1 0.6 reshape.99
  24.8 0.0 copy-start.3
  24.8 3.8 fusion.4
  28.6 0.0 copy-done.3
  28.6 10.1 %fusion = f32[8,64,1024]{2,0,1:T(8,128)} fusion(f32[36,64,1024]{2,1,0:T(8,128)S(1)} %fusion.4, s32[36]{0:T(128)S(1)} %bitcast.78), kind=kOutput, calls=%fused_computation | convolution fusion | flops 226492704 | bytes 11534480 | tf_op jit(solution)/shard_map/et,eib->tib/dot_general | solution.py:36
  38.6 0.0 all-reduce.2.cloned.1.call-update
  38.7 0.0 reduce-scatter.2.cloned.1.call-start
  38.8 157.3 %all-reduce.2.cloned.1.call-done = f32[8,64,1024]{2,0,1:T(8,128)} async-done(((f32[8,64,1024]{2,0,1:T(8,128)}), f32[8,64,1024]{2,0,1:T(8,128)}) %all-reduce.2.cloned.1.call-update) | async-done | bytes 2097168 | tf_op jit(solution)/shard_map/psum | solution.py:39
  196.0 0.0 copy-start.1
  196.0 6.7 %fusion.9 = f32[8,64,64]{2,1,0:T(8,128)S(1)} fusion(f32[8,64,1024]{2,0,1:T(8,128)} %all-reduce.2.cloned.1.call-done), kind=kOutput, calls=%fused_computation.12 | convolution fusion | flops 402653184 | bytes 2228224 | tf_op jit(solution)/shard_map/tib,tjb->tij/dot_general | solution.py:40
  202.7 0.9 copy.28
  203.6 1.7 fusion.25
  205.3 47.6 %custom-call.8 = f32[8,64,64]{2,1,0:T(8,128)S(1)} custom-call(f32[8,64,64]{2,1,0:T(8,128)} %fusion.25), custom_call_target="Cholesky" | custom-call | tf_op jit(solution)/shard_map/jit(cholesky)/cholesky | solution.py:41
  253.0 0.1 compare_reduce_fusion
  253.1 0.8 select_bitcast_fusion
  253.9 40.0 %custom-call.9 = f32[8,1,64,64]{2,3,1,0:T(8,128)S(1)} custom-call(f32[8,1,64,64]{3,2,1,0:T(8,128)} %select_bitcast_fusion), custom_call_target="InvertDiagBlocksLowerTriangular" | custom-call | tf_op jit(solution)/shard_map/jit(_solve_triangular)/vmap()/triangular_solve | solution.py:42
  294.0 0.0 copy-done.1
  294.0 4.4 fusion.42
  298.4 1.6 convolution_convert_fusion.1
  299.9 5.5 %fusion.11 = f32[36,64,64]{1,2,0:T(8,128)S(1)} fusion(bf16[36,1,64,1024]{3,2,1,0:T(8,128)(2,1)} %param.7, bf16[36,64,1024]{2,0,1:T(8,128)(2,1)S(1)} %convolution_convert_fusion.1), kind=kOutput, calls=%fused_computation.14 | convolution fusion | flops 301989888 | bytes 10027008 | tf_op jit(solution)/shard_map/eib,ekb->eik/dot_general | solution.py:52
  305.4 0.5 copy.33
  305.9 0.8 fusion.16
  306.7 1.8 fusion.21
  308.5 4.3 convolution_bitcast_fusion
  312.8 0.0 reduce-scatter.2.cloned.1.call-update
  312.9 1.1 dynamic-slice_multiply_fusion
  314.0 0.8 copy.35
  314.8 216.0 %reduce-scatter.2.cloned.1.call-done = f32[8,64,32]{1,2,0:T(8,128)} async-done(((f32[8,64,1024]{1,2,0:T(8,128)}), f32[8,64,32]{1,2,0:T(8,128)}) %reduce-scatter.2.cloned.1.call-update) | async-done | bytes 65552 | tf_op jit(solution)/shard_map/reduce_scatter | solution.py:59
  530.8 1.6 broadcast_multiply_fusion
  (4 shorter events, 0.1 us)
Async XLA Ops:
  7.2 13.0 %copy-start = (bf16[8,64,1024]{2,1,0:T(8,128)(2,1)S(1)}, bf16[8,64,1024]{2,1,0:T(8,128)(2,1)}, u32[]{:S(2)}) copy-start(bf16[8,64,1024]{2,1,0:T(8,128)(2,1)} %param.13) | copy-start | bytes 3145732
  7.2 188.8 %all-reduce.2.cloned.1.call-start = ((), (), s32[]{:S(2)}) async-start(), calls=%async_computation.1 | async-start | bytes 4194304 | tf_op jit(solution)/shard_map/psum | solution.py:39
  19.4 0.7 copy-start.2
  24.8 3.8 copy-start.3
  38.7 492.1 %reduce-scatter.2.cloned.1.call-start = ((), (), s32[]{:S(2)}) async-start(), calls=%async_computation.2 | async-start | bytes 4325376 | tf_op jit(solution)/shard_map/reduce_scatter | solution.py:59
  196.0 97.9 %copy-start.1 = (f32[8,64,1024]{2,0,1:T(8,128)S(1)}, f32[8,64,1024]{2,0,1:T(8,128)}, u32[]{:S(2)}) copy-start(f32[8,64,1024]{2,0,1:T(8,128)} %all-reduce.2.cloned.1.call-done) | copy-start | bytes 6291460
Sparse Core Ops, SparseCore 0:
  38.8 157.1 all-reduce.1
  313.0 217.7 reduce-scatter.1
where the time goes:
time: 540 us; the launch traced here: 539 us
  waiting for transfers between devices  373 us (69%)
  other arithmetic  94.4 us (17%)
  matrix products  41.1 us (8%)
  between operations  14.9 us (3%)
  blocking collectives  11.5 us (2%)
    reduce_scatter x1, waiting for transfers between devices, shards(): lax.psum_scatter(partial_rows, 'wide', scatter_dimension=2, tiled=True)  216 us
    psum x1, waiting for transfers between devices, shards(): sketch_sum = lax.psum(sketch, 'wide')  157 us
    another operation x4, other arithmetic, shards(): lower_factor = jnp.linalg.cholesky(gram_matrix)  47.8 us
    another operation x3, other arithmetic, shards(): jax.scipy.linalg.solve_triangular(lower_factor, sketch_sum, lower=True)  40.9 us
    all_gather x1, blocking collectives, shards(): gathered = lax.all_gather(panel_shared, 'narrow', axis=2, tiled=True)  11.5 us
  transfers between devices with their start and end apart: 2, of which 2 were waited for; matrix products, arithmetic and copies ran while one was open for 0% of the time, Pallas kernels for 0%

commit v1 on v0

v1 whole, which is shorter than its diff:
```python
import functools
import math

import jax
import jax.numpy as jnp
from jax import lax
from jax.experimental import pallas as pl
from jax.experimental.pallas import tpu as pltpu
from jax.sharding import Mesh
from jax.sharding import PartitionSpec as P

BF = jnp.bfloat16
F32 = jnp.float32
HIGHEST = lax.Precision.HIGHEST
NT = (((1,), (1,)), ((), ()))
TN = (((0,), (0,)), ((), ()))
SMEM = pltpu.SMEM
VMEM = pltpu.VMEM
LANES = 128
TAIL = 16


def params(mib):
    return pltpu.CompilerParams(vmem_limit_bytes=mib * 1024 * 1024)


def split_bf(x, parts):
    out = []
    for _ in range(parts):
        part = x.astype(BF)
        out.append(part)
        x = x - part.astype(F32)
    return out


def pack_rows(block):
    return jnp.concatenate([block[q * TAIL : (q + 1) * TAIL] for q in range(block.shape[0] // TAIL)], axis=1)


def unpack_rows(ref, lead, row, first, count):
    return jnp.concatenate(
        [ref[lead, row : row + TAIL, q * LANES : (q + 1) * LANES] for q in range(first, first + count)], axis=0
    )


def sum_factors(panel, target, count, factors, out, acc):
    pairs = acc.shape[0]
    panels = pairs // 8
    rank = acc.shape[1]

    def clear(i, _):
        acc[i] = jnp.zeros(acc.shape[1:], F32)
        return 0

    lax.fori_loop(0, pairs, clear, 0)

    def add(e, _):
        pair = target[e] * panels + panel[e]
        acc[pair] += factors[e].astype(F32)
        return 0

    lax.fori_loop(0, count[0], add, 0)
    groups = out.shape[0]
    each = pairs // groups
    for i in range(pairs):
        row = (i % each) * rank
        out[i // each, row : row + rank, :] = acc[i].astype(BF)


def project(columns, *refs):
    pieces, (probes, coupling, _, sent, shared, tails, sem) = refs[:-7], refs[-7:]
    rows = pieces[0].shape[1]
    at = 0
    for piece in pieces:
        for half in range(piece.shape[0]):
            start = pl.multiple_of(columns[at] * LANES, LANES)
            shared[0:rows, pl.ds(start, LANES)] = piece[half]
            at += 1
    rank = coupling.shape[1]
    zero = jnp.zeros((rank, rank), F32)
    first, second = coupling[0], coupling[1]
    diagonal = jnp.concatenate(
        [jnp.concatenate([first, zero], axis=1), jnp.concatenate([zero, second], axis=1)], axis=0
    )
    projected = lax.dot_general(probes[...], shared[0:rows, :], NT, preferred_element_type=F32)
    coefficients = lax.dot_general(
        projected, diagonal, NT, precision=HIGHEST, preferred_element_type=F32
    ).astype(BF)
    groups = tails.shape[0]
    each = coefficients.shape[0] // groups
    for g in range(groups):
        part = coefficients[g * each : (g + 1) * each]
        tails[g, :, 0 : each * 8] = pack_rows(part)
    copy = pltpu.make_async_copy(tails, sent.at[:, sent.shape[1] - TAIL :, :], sem)
    copy.start()
    high, mid, low = split_bf(jnp.concatenate([first, second], axis=1), 3)
    shared[rows : rows + TAIL, :] = jnp.concatenate([pack_rows(high), pack_rows(mid)], axis=1)
    tail = pack_rows(low)
    shared[rows + TAIL : rows + 2 * TAIL, :] = jnp.concatenate([tail, jnp.zeros_like(tail)], axis=1)
    copy.wait()


def first_pass(held, out):
    groups, rows, width = held.shape
    rows = rows - TAIL
    targets = rows // LANES
    rank = out.shape[1] // targets
    cut = out.shape[2]
    for t in range(targets):
        total = jnp.zeros((rank, width), F32)
        for g in range(groups):
            coefficients = unpack_rows(held, g, rows, t * (rank // TAIL), rank // TAIL)
            total = total + jnp.dot(
                coefficients, held[g, t * LANES : (t + 1) * LANES, :], preferred_element_type=F32
            )
        for z in range(out.shape[0]):
            out[z, t * rank : (t + 1) * rank, :] = total[:, z * cut : (z + 1) * cut]


def add_up(parts, out):
    total = parts[0]
    for z in range(1, parts.shape[0]):
        total = total + parts[z]
    for z in range(out.shape[0]):
        out[z] = total


def inverse_factors(grams):
    rank = grams[0].shape[0]
    row_at = lax.broadcasted_iota(jnp.int32, (rank, 2 * rank), 0)
    lane_at = lax.broadcasted_iota(jnp.int32, (rank, 2 * rank), 1)
    eye = (row_at + rank == lane_at).astype(F32)
    tables = [jnp.concatenate([g, jnp.zeros((rank, rank), F32)], axis=1) + eye for g in grams]
    scales = [jnp.ones((rank, 2 * rank), F32) for _ in grams]
    for k in range(rank):
        for i, table in enumerate(tables):
            top = (k // 8) * 8
            pivot_row = table[k : k + 1, :]
            pivot = pivot_row[:, k : k + 1]
            scaled = pivot_row * (1.0 / pivot)
            column = table[top:, k : k + 1]
            below = row_at[top:, :] > k
            lower = table[top:, :] - jnp.where(below, column * scaled, 0.0)
            tables[i] = lower if top == 0 else jnp.concatenate([table[:top], lower], axis=0)
            scales[i] = jnp.where(row_at == k, pivot, scales[i])
    return [(table * lax.rsqrt(scale))[:, rank:] for table, scale in zip(tables, scales, strict=True)]


def orthonormal(place, sketches, rounded, *refs):
    left, (basis, turned) = refs[:-2], refs[-2:]
    groups, rows, cut = sketches.shape
    targets = 2
    rank = rows // targets
    own = left[0].shape[0]
    owners = len(left)
    width = groups * cut
    whole = [
        jnp.concatenate([sketches[z, t * rank : (t + 1) * rank, :] for z in range(groups)], axis=1)
        for t in range(targets)
    ]
    grams = [lax.dot_general(s, s, NT, precision=HIGHEST, preferred_element_type=F32) for s in whole]
    inverses = inverse_factors(grams)
    for t in range(targets):
        found = jnp.dot(inverses[t], whole[t], precision=HIGHEST, preferred_element_type=F32)
        basis[t * rank : (t + 1) * rank, :] = found
        rounded[t * rank : (t + 1) * rank, :] = found.astype(BF)
    for s in range(owners):
        owner = lax.rem(place[0] + s, owners)
        start = owner * (width // owners) + place[1] * own
        aligned = (start // LANES) * LANES
        turned[...] = basis[:, pl.ds(pl.multiple_of(aligned, LANES), LANES)].T
        left[s][...] = turned[pl.ds(pl.multiple_of(start - aligned, 32), own), :]


def second_pass(held, rounded, shared, out):
    groups, rows, width = held.shape
    rows = rows - TAIL
    targets = rows // LANES
    rank = rounded.shape[0] // targets
    total = jnp.zeros((rounded.shape[0], width), F32)
    for g in range(groups):
        summed = jnp.concatenate(
            [
                lax.dot_general(
                    held[g, t * LANES : (t + 1) * LANES, :],
                    rounded[t * rank : (t + 1) * rank, :],
                    NT,
                    preferred_element_type=F32,
                )
                for t in range(targets)
            ],
            axis=1,
        )
        coupling = (
            unpack_rows(shared, g, LANES, 0, 4).astype(F32) + unpack_rows(shared, g, LANES, 4, 4).astype(F32)
        ) + unpack_rows(shared, g, LANES + TAIL, 0, 4).astype(F32)
        middle = jnp.concatenate(
            [
                lax.dot_general(
                    coupling[:, d * rank : (d + 1) * rank],
                    summed[d * rank : (d + 1) * rank, :],
                    TN,
                    precision=HIGHEST,
                    preferred_element_type=F32,
                )
                for d in range(LANES // rank)
            ],
            axis=0,
        ).T
        for part in split_bf(middle, 2):
            total = total + jnp.dot(part, shared[g, 0:LANES, :], preferred_element_type=F32)
    for c in range(width // LANES):
        out[c * LANES : (c + 1) * LANES, :] = total[:, c * LANES : (c + 1) * LANES].T.astype(out.dtype)


def finish(place, parts, *refs):
    left_parts, (left, right) = refs[:-2], refs[-2:]
    owners = len(left_parts)
    groups = parts.shape[0] // owners
    targets = left.shape[0] // owners
    rank = left.shape[2]
    root = math.sqrt(1024)
    for y in range(owners):
        total = parts[y * groups].astype(F32)
        for z in range(1, groups):
            total = total + parts[y * groups + z].astype(F32)
        total = total / root
        for t in range(targets):
            right[y * targets + t] = total[:, t * rank : (t + 1) * rank]
    for s in range(owners):
        owner = lax.rem(place[0] + owners - s, owners)
        rows = left_parts[s][...] * root
        for t in range(targets):
            left[owner * targets + t] = rows[:, t * rank : (t + 1) * rank]


def shards(sizes, entry_factor, entry_panel, entry_target, entry_count, panel_shared, coupling, probes):
    ny, nz, nx, nc = sizes
    y, z = lax.axis_index("y"), lax.axis_index("z")
    x, c = lax.axis_index("x"), lax.axis_index("core")
    place = jnp.stack([y, z]).astype(jnp.int32)
    factors = entry_factor[:, 0]
    slots, rank, width = factors.shape
    panels = panel_shared.shape[0]
    targets = probes.shape[0]
    rows = panels * rank
    mine = targets // ny
    held_rows = mine * panels * rank + TAIL
    in_vmem = pl.BlockSpec(memory_space=VMEM)
    in_smem = pl.BlockSpec(memory_space=SMEM)
    in_any = pl.BlockSpec(memory_space=pl.ANY)

    own = panel_shared.reshape(rows, LANES)
    other = lax.ppermute(own, "core", [(i, (i + 1) % nc) for i in range(nc)])
    pair = jnp.stack([own, other])
    pieces = [pair] + [lax.ppermute(pair, "x", [(i, (i + s) % nx) for i in range(nx)]) for s in range(1, nx)]
    columns = jnp.stack(
        [((x + nx - s) % nx) * nc + k for s in range(nx) for k in (c, (c + 1) % nc)]
    ).astype(jnp.int32)

    sums = pl.pallas_call(
        sum_factors,
        out_shape=jax.ShapeDtypeStruct((ny, held_rows, width), BF),
        in_specs=[in_smem, in_smem, in_smem, in_vmem],
        out_specs=in_vmem,
        scratch_shapes=[VMEM((targets * panels, rank, width), F32)],
        compiler_params=params(24),
        cost_estimate=pl.CostEstimate(flops=10**7, bytes_accessed=7 * 10**6, transcendentals=0),
        name="sum_factors",
    )(entry_panel[:, 0], entry_target[:, 0], entry_count[0], factors)

    packed, shared = pl.pallas_call(
        project,
        out_shape=(
            jax.ShapeDtypeStruct((ny, held_rows, width), BF),
            jax.ShapeDtypeStruct((rows + 2 * TAIL, width), BF),
        ),
        in_specs=[in_smem] + [in_vmem] * (nx + 2) + [in_any],
        out_specs=(in_any, in_vmem),
        scratch_shapes=[VMEM((ny, TAIL, width), BF), pltpu.SemaphoreType.DMA],
        input_output_aliases={nx + 3: 0},
        compiler_params=params(24),
        name="project",
    )(columns, *pieces, probes.reshape(targets * rank, width), coupling, sums)

    held = lax.all_to_all(packed, "y", 0, 0, tiled=True)
    shared, held = lax.optimization_barrier((shared, held))
    all_shared = lax.all_gather(shared, "y", axis=0, tiled=False)

    cut = width // nz
    sketch = pl.pallas_call(
        first_pass,
        out_shape=jax.ShapeDtypeStruct((nz, mine * rank, cut), F32),
        in_specs=[in_vmem],
        out_specs=in_vmem,
        compiler_params=params(24),
        name="first_pass",
    )(held)
    parts = lax.all_to_all(sketch, "z", 0, 0, tiled=True)
    copies = pl.pallas_call(
        add_up,
        out_shape=jax.ShapeDtypeStruct((nz, mine * rank, cut), F32),
        in_specs=[in_vmem],
        out_specs=in_vmem,
        name="add_up",
    )(parts)
    sketches = lax.all_to_all(copies, "z", 0, 0, tiled=True)

    keep = width // (ny * nz)
    rounded, *left = pl.pallas_call(
        orthonormal,
        out_shape=(jax.ShapeDtypeStruct((mine * rank, width), BF),)
        + (jax.ShapeDtypeStruct((keep, mine * rank), F32),) * ny,
        in_specs=[in_smem, in_vmem],
        out_specs=(in_vmem,) * (ny + 1),
        scratch_shapes=[VMEM((mine * rank, width), F32), VMEM((LANES, mine * rank), F32)],
        compiler_params=params(24),
        name="orthonormal",
    )(place, sketches)
    left_parts = [left[0]] + [
        lax.ppermute(left[s], "y", [(i, (i + s) % ny) for i in range(ny)]) for s in range(1, ny)
    ]
    rows_part = pl.pallas_call(
        second_pass,
        out_shape=jax.ShapeDtypeStruct((width, mine * rank), BF),
        in_specs=[in_vmem] * 3,
        out_specs=in_vmem,
        compiler_params=params(24),
        name="second_pass",
    )(held, rounded, all_shared)
    row_parts = lax.all_to_all(rows_part.reshape(ny * nz, keep, mine * rank), ("y", "z"), 0, 0, tiled=True)
    out = jax.ShapeDtypeStruct((targets, keep, rank), F32)
    left_out, right_out = pl.pallas_call(
        finish,
        out_shape=(out, out),
        in_specs=[in_smem] + [in_vmem] * (ny + 1),
        out_specs=(in_vmem, in_vmem),
        name="finish",
    )(place, row_parts, *left_parts)
    return left_out.transpose(0, 2, 1), right_out.transpose(0, 2, 1)


def solution(mesh):
    wide, narrow = mesh.devices.shape
    sizes = (4, wide // 4, narrow // 2, 2)
    axes = ("y", "z", "x", "core")
    finer = Mesh(mesh.devices.reshape(sizes), axes)
    split, owner = ("y", "z"), ("x", "core")
    placed = (
        P(split, owner, None, None),
        P(split, owner),
        P(split, owner),
        P(owner, split),
        P(split, None, owner),
        P(split, None, None),
        P(owner, None, None),
    )
    return jax.shard_map(
        functools.partial(shards, sizes),
        mesh=finer,
        in_specs=placed,
        out_specs=(P(owner, None, split), P(owner, None, split)),
        check_vma=False,
    )
```

time: 540 us -> 137 us (0.25)
  waiting for transfers between devices: 373 us -> 20.3 us
  other arithmetic: 94.4 us -> 0.84 us
  blocking collectives: 11.5 us -> 55.1 us
  matrix products: 41.1 us -> 0 us
  Pallas kernels: 0 us -> 19.4 us
  starting transfers between devices: 0.08 us -> 17.5 us
    reduce_scatter x1 -> x0, waiting for transfers between devices: 216 us -> none  [shards(): lax.psum_scatter(partial_rows, 'wide', scatter_dimension=2, tiled=True)]
    psum x1 -> x0, waiting for transfers between devices: 157 us -> none  [shards(): sketch_sum = lax.psum(sketch, 'wide')]
    another operation x7 -> x2, other arithmetic: 88.7 us -> 0.84 us  [the longest x1 0.76 us: shards(): pair = jnp.stack([own, other])]
    all_to_all x0 -> x2, blocking collectives: none -> 55.1 us  [the longest x1 31.1 us: shards(): held = lax.all_to_all(packed, 'y', 0, 0, tiled=True)]
    dot_general x11 -> x0, matrix products: 36.7 us -> none  [the longest x1 10.1 us: shards(): jnp.einsum('et,eib->tib', pick_target, contributions, precision=highest)]
    pallas_call x0 -> x7, Pallas kernels: none -> 19.4 us  [the longest x1 7.34 us: shards(): pl.pallas_call(orthonormal, out_shape=(jax.ShapeDtypeStruct((mine * rank,...]
    all_to_all x0 -> x2, waiting for transfers between devices: none -> 16.6 us  [the longest x1 14.1 us: shards(): sketches = lax.all_to_all(copies, 'z', 0, 0, tiled=True)]
    all_gather x1 -> x0, blocking collectives: 11.5 us -> none  [shards(): gathered = lax.all_gather(panel_shared, 'narrow', axis=2, tiled=True)]
  transfers between devices with their start and end apart: 2 -> 10, of which waited for: 2 -> 5; matrix products, arithmetic and copies ran while one was open for 0% -> 0% of each run, Pallas kernels for 0% -> 8%
where the time goes in v1:
time: 137 us; the launch traced here: 134 us
  blocking collectives  55.1 us (40%)
  waiting for transfers between devices  20.3 us (15%)
  Pallas kernels  19.4 us (14%)
  starting transfers between devices  17.5 us (13%)
  between operations  14.8 us (11%)
  local copies, waits for them, and re-layouts  6.37 us (5%)
    all_to_all x1, blocking collectives, shards(): held = lax.all_to_all(packed, 'y', 0, 0, tiled=True)  31.1 us
    all_to_all x1, blocking collectives, shards(): parts = lax.all_to_all(sketch, 'z', 0, 0, tiled=True)  24.1 us
    all_to_all x1, waiting for transfers between devices, shards(): sketches = lax.all_to_all(copies, 'z', 0, 0, tiled=True)  14.1 us
    pallas_call x1, Pallas kernels, shards(): pl.pallas_call(orthonormal, out_shape=(jax.ShapeDtypeStruct((mine * rank,...  7.34 us
    unnamed x24, local copies, waits for them, and re-layouts  6.28 us
    ppermute x3, starting transfers between devices, shards(): lax.ppermute(left[s], 'y', [(i, (i + s) % ny) for i in range(ny)])  5.99 us
    ppermute x3, starting transfers between devices, shards(): lax.ppermute(pair, 'x', [(i, (i + s) % nx) for i in range(nx)])  4.04 us
    all_to_all x1, starting transfers between devices, shards(): lax.all_to_all(rows_part.reshape(ny * nz, keep, mine * rank), ('y', 'z'),...  3.87 us
  transfers between devices with their start and end apart: 10, of which 5 were waited for; matrix products, arithmetic and copies ran while one was open for 0% of the time, Pallas kernels for 8%

profile of v1, /device:TPU:6, one launch (start us, length us, event | category | flops | bytes accessed | tf_op | source)
XLA Modules:
  0.0 134.4 jit_solution(12020199404559228882)
XLA Ops:
  7.2 0.0 all-gather.3.cloned.1.call-start
  7.2 0.1 collective-permute-start
  7.3 1.4 %collective-permute-done = bf16[128,128]{1,0:T(8,128)(2,1)S(1)} collective-permute-done((bf16[128,128]{1,0:T(8,128)(2,1)}, bf16[128,128]{1,0:T(8,128)(2,1)S(1)}, u32[]{:S(2)}, u32[]{:S(2)}) %collective-permute-start) | collective-permute-done | bytes 32800 | tf_op jit(solution)/shard_map/ppermute | solution.py:254
  8.7 0.8 pad_maximum_fusion.refs_0_
  9.5 0.8 collective-permute-start.3
  10.3 2.8 %collective-permute-start.2 = (bf16[2,128,128]{2,1,0:T(8,128)(2,1)S(1)}, bf16[2,128,128]{2,1,0:T(8,128)(2,1)S(1)}, u32[]{:S(2)}, u32[]{:S(2)}) collective-permute-start(bf16[2,128,128]{2,1,0:T(8,128)(2,1)S(1)} %pad_maximum_fusion.refs_0_), channel_id=1, source_target_pairs={{0,4},{2,6},{4,0},{6,2},{1,5},{3,7},{5,1},{7,3},{8,12},{10,14},{12... | collective-permute-start | bytes 196616 | tf_op jit(solution)/shard_map/ppermute | solution.py:256
  13.2 0.4 collective-permute-start.1
  14.2 0.1 stack.53.columns
  14.3 0.0 copy-start
  14.3 2.3 %copy-done = bf16[36,1,64,1024]{3,2,1,0:T(8,128)(2,1)S(1)} copy-done((bf16[36,1,64,1024]{3,2,1,0:T(8,128)(2,1)S(1)}, bf16[36,1,64,1024]{3,2,1,0:T(8,128)(2,1)}, u32[]{:S(2)}) %copy-start) | copy-done | bytes 4718616
  16.6 0.7 copy-done.6
  17.3 0.0 copy-start.7
  17.3 0.7 copy-done.7
  17.9 0.0 copy-start.2
  17.9 1.6 %sum_factors.1.refs_6_ = bf16[4,272,1024]{2,1,0:T(8,128)(2,1)S(1)} custom-call(s32[36]{0:T(128)S(1)} %bitcast.26, s32[36]{0:T(128)S(1)} %bitcast.27, s32[1]{0:T(128)} %bitcast.22.count, bf16[36,64,1024]{2,1,0:T(8,128)(2,1)S(1)} %bitcast.23), custom_call_target="tpu_custom_call" | custom-call | flops 10000000 | bytes 7000000 | tf_op jit(solution)/shard_map/sum_factors/pallas_call | solution.py:261
  19.5 0.0 collective-permute-done.3.refs_3_
  19.5 0.0 collective-permute-done.2.refs_2_
  19.6 0.0 collective-permute-done.1.refs_1_
  19.6 0.0 copy-done.2
  19.6 0.0 copy-done.3
  19.6 2.5 %project.1 = (bf16[4,272,1024]{2,1,0:T(8,128)(2,1)S(1)}, bf16[160,1024]{1,0:T(8,128)(2,1)}) custom-call(s32[8]{0:T(128)S(1)} %stack.53.columns, bf16[2,128,128]{2,1,0:T(8,128)(2,1)S(1)} %pad_maximum_fusion.refs_0_, bf16[2,128,128]{2,1,0:T(8,128)(2,1)S(1)} %collective-permute-done.1.refs_1_, ...), custom_call_target="tpu_custom_call", output_to_operand_aliasing={{0}: (7, {})} | custom-call | tf_op jit(solution)/shard_map/project/pallas_call | solution.py:272
  22.1 31.1 %all_to_all.20.held = bf16[4,272,1024]{2,1,0:T(8,128)(2,1)S(1)} all-to-all(bf16[4,272,1024]{2,1,0:T(8,128)(2,1)S(1)} %get-tuple-element.14), channel_id=1, replica_groups=mesh['y'=4,'z'=8,'x'=4,'core'=2] {'y'}, dimensions={0} | all-to-all | bytes 4456448 | tf_op jit(solution)/shard_map/all_to_all | solution.py:286
  53.2 0.0 all-gather.3.cloned.1.call-update
  53.2 0.4 first_pass.1
  53.6 24.1 %all_to_all.21.parts = f32[8,128,128]{2,1,0:T(8,128)} all-to-all(f32[8,128,128]{2,1,0:T(8,128)S(1)} %first_pass.1), channel_id=1, replica_groups=mesh['y'=4,'z'=8,'x'=4,'core'=2] {'z'}, dimensions={0} | all-to-all | bytes 1048576 | tf_op jit(solution)/shard_map/all_to_all | solution.py:299
  77.7 1.9 %add_up.1 = f32[8,128,128]{2,1,0:T(8,128)} custom-call(f32[8,128,128]{2,1,0:T(8,128)} %all_to_all.21.parts), custom_call_target="tpu_custom_call" | custom-call | tf_op jit(solution)/shard_map/add_up/pallas_call | solution.py:300
  79.6 3.5 %all-to-all-start.2 = ((f32[8,128,128]{2,1,0:T(8,128)}), f32[8,128,128]{2,1,0:T(8,128)S(1)}, u32[]{:S(2)}, u32[]{:S(2)}) async-start(f32[8,128,128]{2,1,0:T(8,128)} %add_up.1), calls=%async_computation.2 | async-start | bytes 1048576 | tf_op jit(solution)/shard_map/all_to_all | solution.py:307
  83.1 0.1 pad_add_fusion.place
  83.2 14.1 %all-to-all-done.2.sketches = f32[8,128,128]{2,1,0:T(8,128)S(1)} async-done(((f32[8,128,128]{2,1,0:T(8,128)}), f32[8,128,128]{2,1,0:T(8,128)S(1)}, u32[]{:S(2)}, u32[]{:S(2)}) %all-to-all-start.2) | async-done | bytes 524320 | tf_op jit(solution)/shard_map/all_to_all | solution.py:307
  97.3 7.3 %orthonormal.1 = (bf16[128,1024]{1,0:T(8,128)(2,1)S(1)}, f32[32,128]{1,0:T(8,128)S(1)}, f32[32,128]{1,0:T(8,128)S(1)}, f32[32,128]{1,0:T(8,128)S(1)}, f32[32,128]{1,0:T(8,128)S(1)}) custom-call(s32[2]{0:T(128)S(1)} %pad_add_fusion.place, f32[8,128,128]{2,1,0:T(8,128)S(1)} %all-to-all-done.2.sketches), custom_call_target="tpu_custom_call" | custom-call | tf_op jit(solution)/shard_map/orthonormal/pallas_call | solution.py:310
  104.6 0.0 copy-start.4
  104.6 0.6 copy-done.4
  105.2 1.3 copy-done.1
  106.5 3.9 %second_pass.1 = bf16[1024,128]{1,0:T(8,128)(2,1)} custom-call(bf16[4,272,1024]{2,1,0:T(8,128)(2,1)S(1)} %all_to_all.20.held, bf16[128,1024]{1,0:T(8,128)(2,1)S(1)} %get-tuple-element.16.rounded, bf16[4,160,1024]{2,1,0:T(8,128)(2,1)S(1)} %bitcast.24), custom_call_target="tpu_custom_call" | custom-call | tf_op jit(solution)/shard_map/second_pass/pallas_call | solution.py:323
  110.4 0.0 copy-done.5
  110.4 3.9 %all-to-all-start.3 = ((bf16[32,32,128]{2,1,0:T(8,128)(2,1)}), bf16[32,32,128]{2,1,0:T(8,128)(2,1)S(1)}, u32[]{:S(2)}, u32[]{:S(2)}) async-start(bf16[32,32,128]{2,1,0:T(8,128)(2,1)} %bitcast.19), calls=%async_computation.3 | async-start | bytes 524288 | tf_op jit(solution)/shard_map/all_to_all | solution.py:331
  114.3 1.8 %collective-permute-start.4 = (f32[32,128]{1,0:T(8,128)S(1)}, f32[32,128]{1,0:T(8,128)S(1)}, u32[]{:S(2)}, u32[]{:S(2)}) collective-permute-start(f32[32,128]{1,0:T(8,128)S(1)} %get-tuple-element.19), channel_id=1, source_target_pairs={{0,64},{64,128},{128,192},{192,0},{1,65},{65,129},{129,193},{193,1... | collective-permute-start | bytes 49160 | tf_op jit(solution)/shard_map/ppermute | solution.py:321
  116.1 2.8 %collective-permute-start.5 = (f32[32,128]{1,0:T(8,128)S(1)}, f32[32,128]{1,0:T(8,128)S(1)}, u32[]{:S(2)}, u32[]{:S(2)}) collective-permute-start(f32[32,128]{1,0:T(8,128)S(1)} %get-tuple-element.20), channel_id=1, source_target_pairs={{0,128},{64,192},{128,0},{192,64},{1,129},{65,193},{129,1},{193,65... | collective-permute-start | bytes 49160 | tf_op jit(solution)/shard_map/ppermute | solution.py:321
  118.9 1.4 %collective-permute-start.6 = (f32[32,128]{1,0:T(8,128)S(1)}, f32[32,128]{1,0:T(8,128)S(1)}, u32[]{:S(2)}, u32[]{:S(2)}) collective-permute-start(f32[32,128]{1,0:T(8,128)S(1)} %get-tuple-element.21), channel_id=1, source_target_pairs={{0,192},{64,0},{128,64},{192,128},{1,193},{65,1},{129,65},{193,129... | collective-permute-start | bytes 49160 | tf_op jit(solution)/shard_map/ppermute | solution.py:321
  120.3 0.0 collective-permute-done.4.refs_1_
  120.3 1.2 collective-permute-done.5.refs_2_
  121.5 1.1 collective-permute-done.6.refs_3_
  122.6 2.5 %all-to-all-done.3.parts = bf16[32,32,128]{2,1,0:T(8,128)(2,1)S(1)} async-done(((bf16[32,32,128]{2,1,0:T(8,128)(2,1)}), bf16[32,32,128]{2,1,0:T(8,128)(2,1)S(1)}, u32[]{:S(2)}, u32[]{:S(2)}) %all-to-all-start.3) | async-done | bytes 262176 | tf_op jit(solution)/shard_map/all_to_all | solution.py:331
  125.1 0.0 copy-done.9
  125.1 0.0 copy-done.10
  125.1 0.0 copy-done.11
  125.1 0.7 copy-done.8
  125.8 1.8 %finish.1 = (f32[8,32,64]{2,1,0:T(8,128)}, f32[8,32,64]{2,1,0:T(8,128)}) custom-call(s32[2]{0:T(128)} %copy-done.5, bf16[32,32,128]{2,1,0:T(8,128)(2,1)} %copy-done.8, f32[32,128]{1,0:T(8,128)} %copy-done.4, f32[32,128]{1,0:T(8,128)} %copy-done.9, f32[32,128]{1,0:T(8,128)} %copy-done.10, f32[32,128]{1,0:T(8,128)} %copy-done.11), custom_call_target="tpu_custom_call" | custom-call | tf_op jit(solution)/shard_map/finish/pallas_call | solution.py:333
  (9 shorter events, 0.0 us)
Async XLA Ops:
  7.2 98.1 %all-gather.3.cloned.1.call-start = ((), (), s32[]{:S(2)}) async-start(), calls=%async_computation.4 | async-start | bytes 1638400 | tf_op jit(solution)/shard_map/all_gather | solution.py:288
  7.2 1.5 %collective-permute-start = (bf16[128,128]{1,0:T(8,128)(2,1)}, bf16[128,128]{1,0:T(8,128)(2,1)S(1)}, u32[]{:S(2)}, u32[]{:S(2)}) collective-permute-start(bf16[128,128]{1,0:T(8,128)(2,1)} %bitcast.28), channel_id=1, source_target_pairs={{0,1},{1,0},{2,3},{3,2},{4,5},{5,4},{6,7},{7,6},{8,9},{9,8},{10,11... | collective-permute-start | bytes 98312 | tf_op jit(solution)/shard_map/ppermute | solution.py:254
  9.5 10.1 %collective-permute-start.3 = (bf16[2,128,128]{2,1,0:T(8,128)(2,1)S(1)}, bf16[2,128,128]{2,1,0:T(8,128)(2,1)S(1)}, u32[]{:S(2)}, u32[]{:S(2)}) collective-permute-start(bf16[2,128,128]{2,1,0:T(8,128)(2,1)S(1)} %pad_maximum_fusion.refs_0_), channel_id=1, source_target_pairs={{0,6},{2,0},{4,2},{6,4},{1,7},{3,1},{5,3},{7,5},{8,14},{10,8},{12,... | collective-permute-start | bytes 196616 | tf_op jit(solution)/shard_map/ppermute | solution.py:256
  10.3 9.2 %collective-permute-start.2 = (bf16[2,128,128]{2,1,0:T(8,128)(2,1)S(1)}, bf16[2,128,128]{2,1,0:T(8,128)(2,1)S(1)}, u32[]{:S(2)}, u32[]{:S(2)}) collective-permute-start(bf16[2,128,128]{2,1,0:T(8,128)(2,1)S(1)} %pad_maximum_fusion.refs_0_), channel_id=1, source_target_pairs={{0,4},{2,6},{4,0},{6,2},{1,5},{3,7},{5,1},{7,3},{8,12},{10,14},{12... | collective-permute-start | bytes 196616 | tf_op jit(solution)/shard_map/ppermute | solution.py:256
  13.2 6.4 %collective-permute-start.1 = (bf16[2,128,128]{2,1,0:T(8,128)(2,1)S(1)}, bf16[2,128,128]{2,1,0:T(8,128)(2,1)S(1)}, u32[]{:S(2)}, u32[]{:S(2)}) collective-permute-start(bf16[2,128,128]{2,1,0:T(8,128)(2,1)S(1)} %pad_maximum_fusion.refs_0_), channel_id=1, source_target_pairs={{0,2},{2,4},{4,6},{6,0},{1,3},{3,5},{5,7},{7,1},{8,10},{10,12},{12... | collective-permute-start | bytes 196616 | tf_op jit(solution)/shard_map/ppermute | solution.py:256
  14.3 2.3 %copy-start = (bf16[36,1,64,1024]{3,2,1,0:T(8,128)(2,1)S(1)}, bf16[36,1,64,1024]{3,2,1,0:T(8,128)(2,1)}, u32[]{:S(2)}) copy-start(bf16[36,1,64,1024]{3,2,1,0:T(8,128)(2,1)} %param.7) | copy-start | bytes 14155780
  16.6 0.7 copy-start.6
  17.3 0.7 copy-start.7
  17.9 1.7 %copy-start.2 = (bf16[8,64,1024]{2,1,0:T(8,128)(2,1)S(1)}, bf16[8,64,1024]{2,1,0:T(8,128)(2,1)}, u32[]{:S(2)}) copy-start(bf16[8,64,1024]{2,1,0:T(8,128)(2,1)} %param.13) | copy-start | bytes 3145732
  17.9 1.7 %copy-start.3 = (f32[2,64,64]{2,1,0:T(8,128)S(1)}, f32[2,64,64]{2,1,0:T(8,128)}, u32[]{:S(2)}) copy-start(f32[2,64,64]{2,1,0:T(8,128)} %refs_5_.1) | copy-start | bytes 98308
  79.6 17.7 %all-to-all-start.2 = ((f32[8,128,128]{2,1,0:T(8,128)}), f32[8,128,128]{2,1,0:T(8,128)S(1)}, u32[]{:S(2)}, u32[]{:S(2)}) async-start(f32[8,128,128]{2,1,0:T(8,128)} %add_up.1), calls=%async_computation.2 | async-start | bytes 1048576 | tf_op jit(solution)/shard_map/all_to_all | solution.py:307
  83.2 27.2 %copy-start.5 = (s32[2]{0:T(128)}, s32[2]{0:T(128)S(1)}, u32[]{:S(2)}) copy-start(s32[2]{0:T(128)S(1)} %pad_add_fusion.place) | copy-start | bytes 28
  104.6 0.6 copy-start.4
  105.2 1.3 copy-start.1
  110.4 14.7 %all-to-all-start.3 = ((bf16[32,32,128]{2,1,0:T(8,128)(2,1)}), bf16[32,32,128]{2,1,0:T(8,128)(2,1)S(1)}, u32[]{:S(2)}, u32[]{:S(2)}) async-start(bf16[32,32,128]{2,1,0:T(8,128)(2,1)} %bitcast.19), calls=%async_computation.3 | async-start | bytes 524288 | tf_op jit(solution)/shard_map/all_to_all | solution.py:331
  114.3 6.0 %collective-permute-start.4 = (f32[32,128]{1,0:T(8,128)S(1)}, f32[32,128]{1,0:T(8,128)S(1)}, u32[]{:S(2)}, u32[]{:S(2)}) collective-permute-start(f32[32,128]{1,0:T(8,128)S(1)} %get-tuple-element.19), channel_id=1, source_target_pairs={{0,64},{64,128},{128,192},{192,0},{1,65},{65,129},{129,193},{193,1... | collective-permute-start | bytes 49160 | tf_op jit(solution)/shard_map/ppermute | solution.py:321
  116.1 5.4 %collective-permute-start.5 = (f32[32,128]{1,0:T(8,128)S(1)}, f32[32,128]{1,0:T(8,128)S(1)}, u32[]{:S(2)}, u32[]{:S(2)}) collective-permute-start(f32[32,128]{1,0:T(8,128)S(1)} %get-tuple-element.20), channel_id=1, source_target_pairs={{0,128},{64,192},{128,0},{192,64},{1,129},{65,193},{129,1},{193,65... | collective-permute-start | bytes 49160 | tf_op jit(solution)/shard_map/ppermute | solution.py:321
  118.9 3.7 %collective-permute-start.6 = (f32[32,128]{1,0:T(8,128)S(1)}, f32[32,128]{1,0:T(8,128)S(1)}, u32[]{:S(2)}, u32[]{:S(2)}) collective-permute-start(f32[32,128]{1,0:T(8,128)S(1)} %get-tuple-element.21), channel_id=1, source_target_pairs={{0,192},{64,0},{128,64},{192,128},{1,193},{65,1},{129,65},{193,129... | collective-permute-start | bytes 49160 | tf_op jit(solution)/shard_map/ppermute | solution.py:321
  120.3 4.8 %copy-start.9 = (f32[32,128]{1,0:T(8,128)}, f32[32,128]{1,0:T(8,128)S(1)}, u32[]{:S(2)}) copy-start(f32[32,128]{1,0:T(8,128)S(1)} %collective-permute-done.4.refs_1_) | copy-start | bytes 49156
  121.5 3.6 %copy-start.10 = (f32[32,128]{1,0:T(8,128)}, f32[32,128]{1,0:T(8,128)S(1)}, u32[]{:S(2)}) copy-start(f32[32,128]{1,0:T(8,128)S(1)} %collective-permute-done.5.refs_2_) | copy-start | bytes 49156
  122.6 2.5 %copy-start.11 = (f32[32,128]{1,0:T(8,128)}, f32[32,128]{1,0:T(8,128)S(1)}, u32[]{:S(2)}) copy-start(f32[32,128]{1,0:T(8,128)S(1)} %collective-permute-done.6.refs_3_) | copy-start | bytes 49156
  125.1 0.7 copy-start.8
Sparse Core Ops, SparseCore 0:
  53.3 28.1 all-gather.2

commit v2 on v1

--- a/solution.py
+++ b/solution.py
@@ -43,23 +43,41 @@
     )
 
 
-def sum_factors(panel, target, count, factors, out, acc):
+def sum_factors(panel, target, count, factors, out, loaded, acc, panel_at, target_at, count_at, sems, small):
+    slots, rank, _ = loaded.shape
     pairs = acc.shape[0]
     panels = pairs // 8
-    rank = acc.shape[1]
+    chunk = slots // sems.shape[0]
+    indices = [
+        pltpu.make_async_copy(source, to, small.at[i])
+        for i, (source, to) in enumerate(((panel, panel_at), (target, target_at), (count, count_at)))
+    ]
+    for copy in indices:
+        copy.start()
+    loads = [
+        pltpu.make_async_copy(factors.at[pl.ds(i * chunk, chunk)], loaded.at[pl.ds(i * chunk, chunk)], sems.at[i])
+        for i in range(slots // chunk)
+    ]
+    for copy in loads:
+        copy.start()
 
     def clear(i, _):
         acc[i] = jnp.zeros(acc.shape[1:], F32)
         return 0
 
     lax.fori_loop(0, pairs, clear, 0)
+    for copy in indices:
+        copy.wait()
+    live = count_at[0]
 
     def add(e, _):
-        pair = target[e] * panels + panel[e]
-        acc[pair] += factors[e].astype(F32)
+        pair = target_at[e] * panels + panel_at[e]
+        acc[pair] += loaded[e].astype(F32)
         return 0
 
-    lax.fori_loop(0, count[0], add, 0)
+    for i, copy in enumerate(loads):
+        copy.wait()
+        lax.fori_loop(i * chunk, jnp.minimum(live, (i + 1) * chunk), add, 0)
     groups = out.shape[0]
     each = pairs // groups
     for i in range(pairs):
@@ -68,7 +86,9 @@
 
 
 def project(columns, *refs):
-    pieces, (probes, coupling, _, sent, shared, tails, sem) = refs[:-7], refs[-7:]
+    pieces, refs = refs[:4], refs[4:]
+    probes, coupling, shared, table = refs[0], refs[1], refs[2], refs[-1]
+    sent = refs[3:-1]
     rows = pieces[0].shape[1]
     at = 0
     for piece in pieces:
@@ -83,35 +103,33 @@
         [jnp.concatenate([first, zero], axis=1), jnp.concatenate([zero, second], axis=1)], axis=0
     )
     projected = lax.dot_general(probes[...], shared[0:rows, :], NT, preferred_element_type=F32)
-    coefficients = lax.dot_general(
+    table[...] = lax.dot_general(
         projected, diagonal, NT, precision=HIGHEST, preferred_element_type=F32
     ).astype(BF)
-    groups = tails.shape[0]
-    each = coefficients.shape[0] // groups
-    for g in range(groups):
-        part = coefficients[g * each : (g + 1) * each]
-        tails[g, :, 0 : each * 8] = pack_rows(part)
-    copy = pltpu.make_async_copy(tails, sent.at[:, sent.shape[1] - TAIL :, :], sem)
-    copy.start()
+    each = sent[0].shape[0]
+    for s in range(len(sent)):
+        owner = lax.rem(columns[at] + s, len(sent))
+        sent[s][...] = table[pl.ds(pl.multiple_of(owner * each, each), each), :]
     high, mid, low = split_bf(jnp.concatenate([first, second], axis=1), 3)
     shared[rows : rows + TAIL, :] = jnp.concatenate([pack_rows(high), pack_rows(mid)], axis=1)
     tail = pack_rows(low)
     shared[rows + TAIL : rows + 2 * TAIL, :] = jnp.concatenate([tail, jnp.zeros_like(tail)], axis=1)
-    copy.wait()
-
-
-def first_pass(held, out):
+
+
+def first_pass(place, held, *refs):
+    coefficients, out = refs[:-1], refs[-1]
     groups, rows, width = held.shape
-    rows = rows - TAIL
     targets = rows // LANES
     rank = out.shape[1] // targets
     cut = out.shape[2]
     for t in range(targets):
         total = jnp.zeros((rank, width), F32)
-        for g in range(groups):
-            coefficients = unpack_rows(held, g, rows, t * (rank // TAIL), rank // TAIL)
+        for s in range(groups):
+            source = lax.rem(place[0] + groups - s, groups)
             total = total + jnp.dot(
-                coefficients, held[g, t * LANES : (t + 1) * LANES, :], preferred_element_type=F32
+                coefficients[s][t * rank : (t + 1) * rank, :],
+                held[source, t * LANES : (t + 1) * LANES, :],
+                preferred_element_type=F32,
             )
         for z in range(out.shape[0]):
             out[z, t * rank : (t + 1) * rank, :] = total[:, z * cut : (z + 1) * cut]
@@ -146,16 +164,21 @@
     return [(table * lax.rsqrt(scale))[:, rank:] for table, scale in zip(tables, scales, strict=True)]
 
 
-def orthonormal(place, sketches, rounded, *refs):
-    left, (basis, turned) = refs[:-2], refs[-2:]
-    groups, rows, cut = sketches.shape
-    targets = 2
+def second_pass(place, sketches, held_far, *refs):
+    groups = held_far.shape[0]
+    shared_far, out, left, refs = refs[:groups], refs[groups], refs[groups + 1 : 2 * groups + 1], refs[2 * groups + 1 :]
+    basis, rounded, turned, held, shared, sems = refs
+    loads = [pltpu.make_async_copy(held_far, held, sems.at[groups])]
+    loads += [pltpu.make_async_copy(shared_far[s], shared.at[s], sems.at[s]) for s in range(groups)]
+    for copy in loads:
+        copy.start()
+    cuts, rows, _ = sketches.shape
+    width = basis.shape[1]
+    targets = held.shape[1] // LANES
     rank = rows // targets
     own = left[0].shape[0]
-    owners = len(left)
-    width = groups * cut
     whole = [
-        jnp.concatenate([sketches[z, t * rank : (t + 1) * rank, :] for z in range(groups)], axis=1)
+        jnp.concatenate([sketches[z, t * rank : (t + 1) * rank, :] for z in range(cuts)], axis=1)
         for t in range(targets)
     ]
     grams = [lax.dot_general(s, s, NT, precision=HIGHEST, preferred_element_type=F32) for s in whole]
@@ -164,25 +187,15 @@
         found = jnp.dot(inverses[t], whole[t], precision=HIGHEST, preferred_element_type=F32)
         basis[t * rank : (t + 1) * rank, :] = found
         rounded[t * rank : (t + 1) * rank, :] = found.astype(BF)
-    for s in range(owners):
-        owner = lax.rem(place[0] + s, owners)
-        start = owner * (width // owners) + place[1] * own
-        aligned = (start // LANES) * LANES
-        turned[...] = basis[:, pl.ds(pl.multiple_of(aligned, LANES), LANES)].T
-        left[s][...] = turned[pl.ds(pl.multiple_of(start - aligned, 32), own), :]
-
-
-def second_pass(held, rounded, shared, out):
-    groups, rows, width = held.shape
-    rows = rows - TAIL
-    targets = rows // LANES
-    rank = rounded.shape[0] // targets
-    total = jnp.zeros((rounded.shape[0], width), F32)
-    for g in range(groups):
+    for copy in loads:
+        copy.wait()
+    total = jnp.zeros((rows, width), F32)
+    for s in range(groups):
+        source = lax.rem(place[0] + groups - s, groups)
         summed = jnp.concatenate(
             [
                 lax.dot_general(
-                    held[g, t * LANES : (t + 1) * LANES, :],
+                    held[source, t * LANES : (t + 1) * LANES, :],
                     rounded[t * rank : (t + 1) * rank, :],
                     NT,
                     preferred_element_type=F32,
@@ -192,8 +205,8 @@
             axis=1,
         )
         coupling = (
-            unpack_rows(shared, g, LANES, 0, 4).astype(F32) + unpack_rows(shared, g, LANES, 4, 4).astype(F32)
-        ) + unpack_rows(shared, g, LANES + TAIL, 0, 4).astype(F32)
+            unpack_rows(shared, s, LANES, 0, 4).astype(F32) + unpack_rows(shared, s, LANES, 4, 4).astype(F32)
+        ) + unpack_rows(shared, s, LANES + TAIL, 0, 4).astype(F32)
         middle = jnp.concatenate(
             [
                 lax.dot_general(
@@ -208,9 +221,15 @@
             axis=0,
         ).T
         for part in split_bf(middle, 2):
-            total = total + jnp.dot(part, shared[g, 0:LANES, :], preferred_element_type=F32)
+            total = total + jnp.dot(part, shared[s, 0:LANES, :], preferred_element_type=F32)
     for c in range(width // LANES):
         out[c * LANES : (c + 1) * LANES, :] = total[:, c * LANES : (c + 1) * LANES].T.astype(out.dtype)
+    for s in range(groups):
+        owner = lax.rem(place[0] + s, groups)
+        start = owner * (width // groups) + place[1] * own
+        aligned = (start // LANES) * LANES
+        turned[...] = basis[:, pl.ds(pl.multiple_of(aligned, LANES), LANES)].T
+        left[s][...] = turned[pl.ds(pl.multiple_of(start - aligned, 32), own), :]
 
 
 def finish(place, parts, *refs):
@@ -245,61 +264,68 @@
     targets = probes.shape[0]
     rows = panels * rank
     mine = targets // ny
-    held_rows = mine * panels * rank + TAIL
+    own_rows = mine * rank
+    held_rows = mine * panels * rank
     in_vmem = pl.BlockSpec(memory_space=VMEM)
     in_smem = pl.BlockSpec(memory_space=SMEM)
     in_any = pl.BlockSpec(memory_space=pl.ANY)
 
-    own = panel_shared.reshape(rows, LANES)
-    other = lax.ppermute(own, "core", [(i, (i + 1) % nc) for i in range(nc)])
-    pair = jnp.stack([own, other])
-    pieces = [pair] + [lax.ppermute(pair, "x", [(i, (i + s) % nx) for i in range(nx)]) for s in range(1, nx)]
-    columns = jnp.stack(
-        [((x + nx - s) % nx) * nc + k for s in range(nx) for k in (c, (c + 1) % nc)]
-    ).astype(jnp.int32)
+    def turn(value, axis, size, by):
+        return lax.ppermute(value, axis, [(i, (i + by) % size) for i in range(size)])
 
     sums = pl.pallas_call(
         sum_factors,
         out_shape=jax.ShapeDtypeStruct((ny, held_rows, width), BF),
-        in_specs=[in_smem, in_smem, in_smem, in_vmem],
+        in_specs=[in_any] * 4,
         out_specs=in_vmem,
-        scratch_shapes=[VMEM((targets * panels, rank, width), F32)],
-        compiler_params=params(24),
+        scratch_shapes=[
+            VMEM((slots, rank, width), BF),
+            VMEM((targets * panels, rank, width), F32),
+            SMEM((slots,), jnp.int32),
+            SMEM((slots,), jnp.int32),
+            SMEM((1,), jnp.int32),
+            pltpu.SemaphoreType.DMA((6,)),
+            pltpu.SemaphoreType.DMA((3,)),
+        ],
+        compiler_params=params(56),
         cost_estimate=pl.CostEstimate(flops=10**7, bytes_accessed=7 * 10**6, transcendentals=0),
         name="sum_factors",
     )(entry_panel[:, 0], entry_target[:, 0], entry_count[0], factors)
-
-    packed, shared = pl.pallas_call(
+    held = lax.all_to_all(sums, "y", 0, 0, tiled=True)
+
+    own, _ = lax.optimization_barrier((panel_shared.reshape(rows, LANES), sums))
+    pair = jnp.stack([own, turn(own, "core", nc, 1)])
+    pieces = [pair] + [turn(pair, "x", nx, s) for s in range(1, nx)]
+    columns = jnp.stack(
+        [((x + nx - s) % nx) * nc + k for s in range(nx) for k in (c, (c + 1) % nc)] + [y]
+    ).astype(jnp.int32)
+    shared, *sent = pl.pallas_call(
         project,
-        out_shape=(
-            jax.ShapeDtypeStruct((ny, held_rows, width), BF),
-            jax.ShapeDtypeStruct((rows + 2 * TAIL, width), BF),
-        ),
-        in_specs=[in_smem] + [in_vmem] * (nx + 2) + [in_any],
-        out_specs=(in_any, in_vmem),
-        scratch_shapes=[VMEM((ny, TAIL, width), BF), pltpu.SemaphoreType.DMA],
-        input_output_aliases={nx + 3: 0},
+        out_shape=(jax.ShapeDtypeStruct((rows + 2 * TAIL, width), BF),)
+        + (jax.ShapeDtypeStruct((own_rows, rows), BF),) * ny,
+        in_specs=[in_smem] + [in_vmem] * (nx + 2),
+        out_specs=(in_vmem,) * (ny + 1),
+        scratch_shapes=[VMEM((targets * rank, rows), BF)],
         compiler_params=params(24),
         name="project",
-    )(columns, *pieces, probes.reshape(targets * rank, width), coupling, sums)
-
-    held = lax.all_to_all(packed, "y", 0, 0, tiled=True)
-    shared, held = lax.optimization_barrier((shared, held))
-    all_shared = lax.all_gather(shared, "y", axis=0, tiled=False)
+    )(columns, *pieces, probes.reshape(targets * rank, width), coupling)
+    coefficients = [sent[0]] + [turn(sent[s], "y", ny, s) for s in range(1, ny)]
 
     cut = width // nz
     sketch = pl.pallas_call(
         first_pass,
-        out_shape=jax.ShapeDtypeStruct((nz, mine * rank, cut), F32),
-        in_specs=[in_vmem],
+        out_shape=jax.ShapeDtypeStruct((nz, own_rows, cut), F32),
+        in_specs=[in_smem] + [in_vmem] * (ny + 1),
         out_specs=in_vmem,
         compiler_params=params(24),
         name="first_pass",
-    )(held)
+    )(place, held, *coefficients)
+    shared, sketch = lax.optimization_barrier((shared, sketch))
+    all_shared = [shared] + [turn(shared, "y", ny, s) for s in range(1, ny)]
     parts = lax.all_to_all(sketch, "z", 0, 0, tiled=True)
     copies = pl.pallas_call(
         add_up,
-        out_shape=jax.ShapeDtypeStruct((nz, mine * rank, cut), F32),
+        out_shape=jax.ShapeDtypeStruct((nz, own_rows, cut), F32),
         in_specs=[in_vmem],
         out_specs=in_vmem,
         name="add_up",
@@ -307,28 +333,25 @@
     sketches = lax.all_to_all(copies, "z", 0, 0, tiled=True)
 
     keep = width // (ny * nz)
-    rounded, *left = pl.pallas_call(
-        orthonormal,
-        out_shape=(jax.ShapeDtypeStruct((mine * rank, width), BF),)
-        + (jax.ShapeDtypeStruct((keep, mine * rank), F32),) * ny,
-        in_specs=[in_smem, in_vmem],
+    rows_part, *left = pl.pallas_call(
+        second_pass,
+        out_shape=(jax.ShapeDtypeStruct((width, own_rows), BF),)
+        + (jax.ShapeDtypeStruct((keep, own_rows), F32),) * ny,
+        in_specs=[in_smem, in_vmem] + [in_any] * (ny + 1),
         out_specs=(in_vmem,) * (ny + 1),
-        scratch_shapes=[VMEM((mine * rank, width), F32), VMEM((LANES, mine * rank), F32)],
-        compiler_params=params(24),
-        name="orthonormal",
-    )(place, sketches)
-    left_parts = [left[0]] + [
-        lax.ppermute(left[s], "y", [(i, (i + s) % ny) for i in range(ny)]) for s in range(1, ny)
-    ]
-    rows_part = pl.pallas_call(
-        second_pass,
-        out_shape=jax.ShapeDtypeStruct((width, mine * rank), BF),
-        in_specs=[in_vmem] * 3,
-        out_specs=in_vmem,
-        compiler_params=params(24),
+        scratch_shapes=[
+            VMEM((own_rows, width), F32),
+            VMEM((own_rows, width), BF),
+            VMEM((LANES, own_rows), F32),
+            VMEM((ny, held_rows, width), BF),
+            VMEM((ny, rows + 2 * TAIL, width), BF),
+            pltpu.SemaphoreType.DMA((ny + 1,)),
+        ],
+        compiler_params=params(40),
         name="second_pass",
-    )(held, rounded, all_shared)
-    row_parts = lax.all_to_all(rows_part.reshape(ny * nz, keep, mine * rank), ("y", "z"), 0, 0, tiled=True)
+    )(place, sketches, held, *all_shared)
+    left_parts = [left[0]] + [turn(left[s], "y", ny, s) for s in range(1, ny)]
+    row_parts = lax.all_to_all(rows_part.reshape(ny * nz, keep, own_rows), ("y", "z"), 0, 0, tiled=True)
     out = jax.ShapeDtypeStruct((targets, keep, rank), F32)
     left_out, right_out = pl.pallas_call(
         finish,

time: 137 us -> 129 us (0.942); the launches traced: 134 us -> 128 us
  blocking collectives: 55.1 us -> 25.7 us
  starting transfers between devices: 17.5 us -> 35.5 us
  between operations: 14.8 us -> 1.41 us
  waiting for transfers between devices: 20.3 us -> 30.4 us
  local copies, waits for them, and re-layouts: 6.37 us -> 13.2 us
  Pallas kernels: 19.4 us -> 22 us
    all_to_all x1 -> x0, blocking collectives: 31.1 us -> none  [shards(): held = lax.all_to_all(packed, 'y', 0, 0, tiled=True)]
    ppermute x7 -> x13, waiting for transfers between devices: 3.74 us -> 26.4 us  [turn(): lax.ppermute(value, axis, [(i, (i + by) % size) for i in range(size)])]
    all_to_all x1, waiting for transfers between devices: 14.1 us -> 0.01 us  [shards(): sketches = lax.all_to_all(copies, 'z', 0, 0, tiled=True)]
    ppermute x7 -> x13, starting transfers between devices: 10.1 us -> 19.3 us  [turn(): lax.ppermute(value, axis, [(i, (i + by) % size) for i in range(size)])]
    all_to_all x1 -> x2, starting transfers between devices: 3.87 us -> 12.6 us  [the longest x1 8.04 us: shards(): lax.all_to_all(rows_part.reshape(ny * nz, keep, own_rows), ('y', 'z'), 0,...]
    unnamed x24 -> x48, local copies, waits for them, and re-layouts: 6.28 us -> 13.1 us
    pallas_call x1, Pallas kernels: 1.61 us -> 3.95 us  [shards(): pl.pallas_call(sum_factors, out_shape=jax.ShapeDtypeStruct((ny, held_rows...]
    all_to_all x1, blocking collectives: 24.1 us -> 25.7 us  [shards(): parts = lax.all_to_all(sketch, 'z', 0, 0, tiled=True)]
  transfers between devices with their start and end apart: 10 -> 16, of which waited for: 5 -> 9; matrix products, arithmetic and copies ran while one was open for 0% -> 0% of each run, Pallas kernels for 8% -> 1%
where the time goes in v2:
time: 129 us; the launch traced here: 128 us
  starting transfers between devices  35.5 us (28%)
  waiting for transfers between devices  30.4 us (24%)
  blocking collectives  25.7 us (20%)
  Pallas kernels  22 us (17%)
  local copies, waits for them, and re-layouts  13.2 us (10%)
  between operations  1.41 us (1%)
    ppermute x13, waiting for transfers between devices, turn(): lax.ppermute(value, axis, [(i, (i + by) % size) for i in range(size)])  26.4 us
    all_to_all x1, blocking collectives, shards(): parts = lax.all_to_all(sketch, 'z', 0, 0, tiled=True)  25.7 us
    ppermute x13, starting transfers between devices, turn(): lax.ppermute(value, axis, [(i, (i + by) % size) for i in range(size)])  19.3 us
    unnamed x48, local copies, waits for them, and re-layouts  13.1 us
    pallas_call x1, Pallas kernels, shards(): pl.pallas_call(second_pass, out_shape=(jax.ShapeDtypeStruct((width, own_r...  11.7 us
    all_to_all x1, starting transfers between devices, shards(): lax.all_to_all(rows_part.reshape(ny * nz, keep, own_rows), ('y', 'z'), 0,...  8.04 us
    all_to_all x1, starting transfers between devices, shards(): held = lax.all_to_all(sums, 'y', 0, 0, tiled=True)  4.61 us
    pallas_call x1, Pallas kernels, shards(): pl.pallas_call(sum_factors, out_shape=jax.ShapeDtypeStruct((ny, held_rows...  3.95 us
  transfers between devices with their start and end apart: 16, of which 9 were waited for; matrix products, arithmetic and copies ran while one was open for 0% of the time, Pallas kernels for 1%

profile of v2, /device:TPU:6, one launch (start us, length us, event | category | flops | bytes accessed | tf_op | source)
XLA Modules:
  0.0 128.2 jit_solution(6358514549945847807)
XLA Ops:
  1.3 4.0 %sum_factors.1 = bf16[4,256,1024]{2,1,0:T(8,128)(2,1)} custom-call(s32[36]{0:T(128)} %bitcast.27, s32[36]{0:T(128)} %bitcast.28, s32[1]{0:T(128)} %bitcast.21.count, bf16[36,64,1024]{2,1,0:T(8,128)(2,1)} %bitcast.23), custom_call_target="tpu_custom_call" | custom-call | flops 10000000 | bytes 7000000 | tf_op jit(solution)/shard_map/sum_factors/pallas_call | solution.py:276
  5.3 4.6 %all-to-all-start = ((bf16[4,256,1024]{2,1,0:T(8,128)(2,1)}), bf16[4,256,1024]{2,1,0:T(8,128)(2,1)S(1)}, u32[]{:S(2)}, u32[]{:S(2)}) async-start(bf16[4,256,1024]{2,1,0:T(8,128)(2,1)} %sum_factors.1), calls=%async_computation | async-start | bytes 4194304 | tf_op jit(solution)/shard_map/all_to_all | solution.py:294
  9.9 1.2 collective-permute-done
  11.1 0.9 collective-permute-start.3
  12.0 2.1 %collective-permute-start.2 = (bf16[2,128,128]{2,1,0:T(8,128)(2,1)S(1)}, bf16[2,128,128]{2,1,0:T(8,128)(2,1)S(1)}, u32[]{:S(2)}, u32[]{:S(2)}) collective-permute-start(bf16[2,128,128]{2,1,0:T(8,128)(2,1)S(1)} %pad_maximum_fusion.refs_0_), channel_id=1, source_target_pairs={{0,4},{2,6},{4,0},{6,2},{1,5},{3,7},{5,1},{7,3},{8,12},{10,14},{12... | collective-permute-start | bytes 196616 | tf_op jit(solution)/shard_map/ppermute | solution.py:274
  14.1 1.1 collective-permute-start.1
  15.3 2.8 %collective-permute-done.3.refs_3_ = bf16[2,128,128]{2,1,0:T(8,128)(2,1)S(1)} collective-permute-done((bf16[2,128,128]{2,1,0:T(8,128)(2,1)S(1)}, bf16[2,128,128]{2,1,0:T(8,128)(2,1)S(1)}, u32[]{:S(2)}, u32[]{:S(2)}) %collective-permute-start.3) | collective-permute-done | bytes 65568 | tf_op jit(solution)/shard_map/ppermute | solution.py:274
  18.0 0.6 copy-done.6
  18.7 0.6 copy-done.8
  19.3 0.6 copy-done.10
  19.9 0.8 copy-done.5
  20.8 0.8 copy-done.7
  21.6 0.8 copy-done.9
  22.5 0.8 copy-done.11
  23.3 1.7 %project.1 = (bf16[160,1024]{1,0:T(8,128)(2,1)S(1)}, bf16[128,128]{1,0:T(8,128)(2,1)S(1)}, bf16[128,128]{1,0:T(8,128)(2,1)S(1)}, bf16[128,128]{1,0:T(8,128)(2,1)S(1)}, bf16[128,128]{1,0:T(8,128)(2,1)S(1)}) custom-call(s32[9]{0:T(128)S(1)} %stack.57.columns, bf16[2,128,128]{2,1,0:T(8,128)(2,1)S(1)} %pad_maximum_fusion.refs_0_, ...), custom_call_target="tpu_custom_call" | custom-call | tf_op jit(solution)/shard_map/project/pallas_call | solution.py:302
  25.0 0.6 copy-done.12
  25.6 2.0 %collective-permute-start.4 = (bf16[128,128]{1,0:T(8,128)(2,1)S(1)}, bf16[128,128]{1,0:T(8,128)(2,1)S(1)}, u32[]{:S(2)}, u32[]{:S(2)}) collective-permute-start(bf16[128,128]{1,0:T(8,128)(2,1)S(1)} %get-tuple-element.20), channel_id=1, source_target_pairs={{0,64},{64,128},{128,192},{192,0},{1,65},{65,129},{129,193},{193,1... | collective-permute-start | bytes 98312 | tf_op jit(solution)/shard_map/ppermute | solution.py:274
  27.6 2.7 %collective-permute-start.5 = (bf16[128,128]{1,0:T(8,128)(2,1)S(1)}, bf16[128,128]{1,0:T(8,128)(2,1)S(1)}, u32[]{:S(2)}, u32[]{:S(2)}) collective-permute-start(bf16[128,128]{1,0:T(8,128)(2,1)S(1)} %get-tuple-element.21), channel_id=1, source_target_pairs={{0,128},{64,192},{128,0},{192,64},{1,129},{65,193},{129,1},{193,65... | collective-permute-start | bytes 98312 | tf_op jit(solution)/shard_map/ppermute | solution.py:274
  30.3 1.5 %collective-permute-start.6 = (bf16[128,128]{1,0:T(8,128)(2,1)S(1)}, bf16[128,128]{1,0:T(8,128)(2,1)S(1)}, u32[]{:S(2)}, u32[]{:S(2)}) collective-permute-start(bf16[128,128]{1,0:T(8,128)(2,1)S(1)} %get-tuple-element.22), channel_id=1, source_target_pairs={{0,192},{64,0},{128,64},{192,128},{1,193},{65,1},{129,65},{193,129... | collective-permute-start | bytes 98312 | tf_op jit(solution)/shard_map/ppermute | solution.py:274
  31.9 5.4 %collective-permute-done.4.refs_1_ = bf16[128,128]{1,0:T(8,128)(2,1)S(1)} collective-permute-done((bf16[128,128]{1,0:T(8,128)(2,1)S(1)}, bf16[128,128]{1,0:T(8,128)(2,1)S(1)}, u32[]{:S(2)}, u32[]{:S(2)}) %collective-permute-start.4) | collective-permute-done | bytes 32800 | tf_op jit(solution)/shard_map/ppermute | solution.py:274
  37.3 0.4 collective-permute-done.5.refs_2_
  37.7 0.8 copy-done.13
  38.4 1.0 first_pass.1
  39.4 25.7 %all_to_all.20.parts = f32[8,128,128]{2,1,0:T(8,128)} all-to-all(f32[8,128,128]{2,1,0:T(8,128)S(1)} %first_pass.1), channel_id=1, replica_groups=mesh['y'=4,'z'=8,'x'=4,'core'=2] {'z'}, dimensions={0} | all-to-all | bytes 1048576 | tf_op jit(solution)/shard_map/all_to_all | solution.py:325
  65.1 1.9 %add_up.1 = f32[8,128,128]{2,1,0:T(8,128)} custom-call(f32[8,128,128]{2,1,0:T(8,128)} %all_to_all.20.parts), custom_call_target="tpu_custom_call" | custom-call | tf_op jit(solution)/shard_map/add_up/pallas_call | solution.py:326
  66.9 3.5 %all-to-all-start.2 = ((f32[8,128,128]{2,1,0:T(8,128)}), f32[8,128,128]{2,1,0:T(8,128)S(1)}, u32[]{:S(2)}, u32[]{:S(2)}) async-start(f32[8,128,128]{2,1,0:T(8,128)} %add_up.1), calls=%async_computation.2 | async-start | bytes 1048576 | tf_op jit(solution)/shard_map/all_to_all | solution.py:333
  70.4 1.6 %collective-permute-start.9 = (bf16[160,1024]{1,0:T(8,128)(2,1)S(1)}, bf16[160,1024]{1,0:T(8,128)(2,1)S(1)}, u32[]{:S(2)}, u32[]{:S(2)}) collective-permute-start(bf16[160,1024]{1,0:T(8,128)(2,1)S(1)} %get-tuple-element.24.refs_0_), channel_id=1, source_target_pairs={{0,192},{64,0},{128,64},{192,128},{1,193},{65,1},{129,65},{193,129... | collective-permute-start | bytes 983048 | tf_op jit(solution)/shard_map/ppermute | solution.py:274
  72.0 1.5 %collective-permute-start.8 = (bf16[160,1024]{1,0:T(8,128)(2,1)S(1)}, bf16[160,1024]{1,0:T(8,128)(2,1)S(1)}, u32[]{:S(2)}, u32[]{:S(2)}) collective-permute-start(bf16[160,1024]{1,0:T(8,128)(2,1)S(1)} %get-tuple-element.24.refs_0_), channel_id=1, source_target_pairs={{0,128},{64,192},{128,0},{192,64},{1,129},{65,193},{129,1},{193,65... | collective-permute-start | bytes 983048 | tf_op jit(solution)/shard_map/ppermute | solution.py:274
  73.5 11.1 %collective-permute-done.9.refs_3_ = bf16[160,1024]{1,0:T(8,128)(2,1)S(1)} collective-permute-done((bf16[160,1024]{1,0:T(8,128)(2,1)S(1)}, bf16[160,1024]{1,0:T(8,128)(2,1)S(1)}, u32[]{:S(2)}, u32[]{:S(2)}) %collective-permute-start.9) | collective-permute-done | bytes 327712 | tf_op jit(solution)/shard_map/ppermute | solution.py:274
  84.6 0.7 copy-done.1
  85.3 3.0 %collective-permute-done.7.refs_1_ = bf16[160,1024]{1,0:T(8,128)(2,1)S(1)} collective-permute-done((bf16[160,1024]{1,0:T(8,128)(2,1)S(1)}, bf16[160,1024]{1,0:T(8,128)(2,1)S(1)}, u32[]{:S(2)}, u32[]{:S(2)}) %collective-permute-start.7) | collective-permute-done | bytes 327712 | tf_op jit(solution)/shard_map/ppermute | solution.py:274
  88.3 0.7 copy-done.3
  89.0 1.0 copy-done.2
  90.0 1.0 copy-done.4
  91.0 11.7 %second_pass.1 = (bf16[1024,128]{1,0:T(8,128)(2,1)}, f32[32,128]{1,0:T(8,128)S(1)}, f32[32,128]{1,0:T(8,128)S(1)}, f32[32,128]{1,0:T(8,128)S(1)}, f32[32,128]{1,0:T(8,128)S(1)}) custom-call(s32[2]{0:T(128)S(1)} %pad_add_fusion.place, f32[8,128,128]{2,1,0:T(8,128)S(1)} %all-to-all-done.2.sketches, bf16[4,256,1024]{2,1,0:T(8,128)(2,1)S(1)} %all-to-all-done.held.held_far, ...), custom_call_target="tpu_custom_call" | custom-call | tf_op jit(solution)/shard_map/second_pass/pallas_call | solution.py:336
  102.6 0.6 copy-done.14
  103.2 0.6 copy-done.16
  103.8 0.6 copy-done.17
  104.4 0.6 copy-done.18
  105.0 8.0 %all-to-all-start.3 = ((bf16[32,32,128]{2,1,0:T(8,128)(2,1)}), bf16[32,32,128]{2,1,0:T(8,128)(2,1)S(1)}, u32[]{:S(2)}, u32[]{:S(2)}) async-start(bf16[32,32,128]{2,1,0:T(8,128)(2,1)} %bitcast.18), calls=%async_computation.3 | async-start | bytes 524288 | tf_op jit(solution)/shard_map/all_to_all | solution.py:354
  113.1 1.9 %collective-permute-start.10 = (f32[32,128]{1,0:T(8,128)}, f32[32,128]{1,0:T(8,128)S(1)}, u32[]{:S(2)}, u32[]{:S(2)}) collective-permute-start(f32[32,128]{1,0:T(8,128)} %copy-done.18), channel_id=1, source_target_pairs={{0,64},{64,128},{128,192},{192,0},{1,65},{65,129},{129,193},{193,1... | collective-permute-start | bytes 49160 | tf_op jit(solution)/shard_map/ppermute | solution.py:274
  115.0 2.7 %collective-permute-start.11 = (f32[32,128]{1,0:T(8,128)}, f32[32,128]{1,0:T(8,128)S(1)}, u32[]{:S(2)}, u32[]{:S(2)}) collective-permute-start(f32[32,128]{1,0:T(8,128)} %copy-done.17), channel_id=1, source_target_pairs={{0,128},{64,192},{128,0},{192,64},{1,129},{65,193},{129,1},{193,65... | collective-permute-start | bytes 49160 | tf_op jit(solution)/shard_map/ppermute | solution.py:274
  117.7 1.4 %collective-permute-start.12 = (f32[32,128]{1,0:T(8,128)}, f32[32,128]{1,0:T(8,128)S(1)}, u32[]{:S(2)}, u32[]{:S(2)}) collective-permute-start(f32[32,128]{1,0:T(8,128)} %copy-done.16), channel_id=1, source_target_pairs={{0,192},{64,0},{128,64},{192,128},{1,193},{65,1},{129,65},{193,129... | collective-permute-start | bytes 49160 | tf_op jit(solution)/shard_map/ppermute | solution.py:274
  119.1 1.4 %collective-permute-done.11.refs_2_ = f32[32,128]{1,0:T(8,128)S(1)} collective-permute-done((f32[32,128]{1,0:T(8,128)}, f32[32,128]{1,0:T(8,128)S(1)}, u32[]{:S(2)}, u32[]{:S(2)}) %collective-permute-start.11) | collective-permute-done | bytes 16416 | tf_op jit(solution)/shard_map/ppermute | solution.py:274
  120.6 1.2 collective-permute-done.12.refs_3_
  121.7 3.9 %all-to-all-done.3.parts = bf16[32,32,128]{2,1,0:T(8,128)(2,1)S(1)} async-done(((bf16[32,32,128]{2,1,0:T(8,128)(2,1)}), bf16[32,32,128]{2,1,0:T(8,128)(2,1)S(1)}, u32[]{:S(2)}, u32[]{:S(2)}) %all-to-all-start.3) | async-done | bytes 262176 | tf_op jit(solution)/shard_map/all_to_all | solution.py:354
  125.7 0.7 copy-done.19
  126.4 1.8 %finish.1 = (f32[8,32,64]{2,1,0:T(8,128)}, f32[8,32,64]{2,1,0:T(8,128)}) custom-call(s32[2]{0:T(128)} %copy-done.15, bf16[32,32,128]{2,1,0:T(8,128)(2,1)} %copy-done.19, f32[32,128]{1,0:T(8,128)} %copy-done.14, f32[32,128]{1,0:T(8,128)} %copy-done.21, f32[32,128]{1,0:T(8,128)} %copy-done.22, f32[32,128]{1,0:T(8,128)} %copy-done.23), custom_call_target="tpu_custom_call" | custom-call | tf_op jit(solution)/shard_map/finish/pallas_call | solution.py:356
  (42 shorter events, 0.3 us)
Async XLA Ops:
  5.2 4.6 %copy-start.20 = (bf16[2,64,128]{2,1,0:T(8,128)(2,1)S(1)}, bf16[2,64,128]{2,1,0:T(8,128)(2,1)}, u32[]{:S(2)}) copy-start(bf16[2,64,128]{2,1,0:T(8,128)(2,1)} %param.11) | copy-start | bytes 98308
  5.3 14.7 %copy-start = (bf16[8,64,1024]{2,1,0:T(8,128)(2,1)S(1)}, bf16[8,64,1024]{2,1,0:T(8,128)(2,1)}, u32[]{:S(2)}) copy-start(bf16[8,64,1024]{2,1,0:T(8,128)(2,1)} %param.13) | copy-start | bytes 3145732
  5.3 32.4 %all-to-all-start = ((bf16[4,256,1024]{2,1,0:T(8,128)(2,1)}), bf16[4,256,1024]{2,1,0:T(8,128)(2,1)S(1)}, u32[]{:S(2)}, u32[]{:S(2)}) async-start(bf16[4,256,1024]{2,1,0:T(8,128)(2,1)} %sum_factors.1), calls=%async_computation | async-start | bytes 4194304 | tf_op jit(solution)/shard_map/all_to_all | solution.py:294
  9.9 1.2 collective-permute-start
  11.1 7.0 %collective-permute-start.3 = (bf16[2,128,128]{2,1,0:T(8,128)(2,1)S(1)}, bf16[2,128,128]{2,1,0:T(8,128)(2,1)S(1)}, u32[]{:S(2)}, u32[]{:S(2)}) collective-permute-start(bf16[2,128,128]{2,1,0:T(8,128)(2,1)S(1)} %pad_maximum_fusion.refs_0_), channel_id=1, source_target_pairs={{0,6},{2,0},{4,2},{6,4},{1,7},{3,1},{5,3},{7,5},{8,14},{10,8},{12,... | collective-permute-start | bytes 196616 | tf_op jit(solution)/shard_map/ppermute | solution.py:274
  12.0 6.7 %collective-permute-start.2 = (bf16[2,128,128]{2,1,0:T(8,128)(2,1)S(1)}, bf16[2,128,128]{2,1,0:T(8,128)(2,1)S(1)}, u32[]{:S(2)}, u32[]{:S(2)}) collective-permute-start(bf16[2,128,128]{2,1,0:T(8,128)(2,1)S(1)} %pad_maximum_fusion.refs_0_), channel_id=1, source_target_pairs={{0,4},{2,6},{4,0},{6,2},{1,5},{3,7},{5,1},{7,3},{8,12},{10,14},{12... | collective-permute-start | bytes 196616 | tf_op jit(solution)/shard_map/ppermute | solution.py:274
  14.1 5.2 %collective-permute-start.1 = (bf16[2,128,128]{2,1,0:T(8,128)(2,1)S(1)}, bf16[2,128,128]{2,1,0:T(8,128)(2,1)S(1)}, u32[]{:S(2)}, u32[]{:S(2)}) collective-permute-start(bf16[2,128,128]{2,1,0:T(8,128)(2,1)S(1)} %pad_maximum_fusion.refs_0_), channel_id=1, source_target_pairs={{0,2},{2,4},{4,6},{6,0},{1,3},{3,5},{5,7},{7,1},{8,10},{10,12},{12... | collective-permute-start | bytes 196616 | tf_op jit(solution)/shard_map/ppermute | solution.py:274
  18.0 0.6 copy-start.6
  18.7 0.6 copy-start.8
  19.3 0.6 copy-start.10
  19.9 0.8 copy-start.5
  20.8 0.8 copy-start.7
  21.6 0.8 copy-start.9
  22.5 0.8 copy-start.11
  25.0 0.6 copy-start.12
  25.6 11.6 %collective-permute-start.4 = (bf16[128,128]{1,0:T(8,128)(2,1)S(1)}, bf16[128,128]{1,0:T(8,128)(2,1)S(1)}, u32[]{:S(2)}, u32[]{:S(2)}) collective-permute-start(bf16[128,128]{1,0:T(8,128)(2,1)S(1)} %get-tuple-element.20), channel_id=1, source_target_pairs={{0,64},{64,128},{128,192},{192,0},{1,65},{65,129},{129,193},{193,1... | collective-permute-start | bytes 98312 | tf_op jit(solution)/shard_map/ppermute | solution.py:274
  27.6 10.0 %collective-permute-start.5 = (bf16[128,128]{1,0:T(8,128)(2,1)S(1)}, bf16[128,128]{1,0:T(8,128)(2,1)S(1)}, u32[]{:S(2)}, u32[]{:S(2)}) collective-permute-start(bf16[128,128]{1,0:T(8,128)(2,1)S(1)} %get-tuple-element.21), channel_id=1, source_target_pairs={{0,128},{64,192},{128,0},{192,64},{1,129},{65,193},{129,1},{193,65... | collective-permute-start | bytes 98312 | tf_op jit(solution)/shard_map/ppermute | solution.py:274
  30.3 7.3 %collective-permute-start.6 = (bf16[128,128]{1,0:T(8,128)(2,1)S(1)}, bf16[128,128]{1,0:T(8,128)(2,1)S(1)}, u32[]{:S(2)}, u32[]{:S(2)}) collective-permute-start(bf16[128,128]{1,0:T(8,128)(2,1)S(1)} %get-tuple-element.22), channel_id=1, source_target_pairs={{0,192},{64,0},{128,64},{192,128},{1,193},{65,1},{129,65},{193,129... | collective-permute-start | bytes 98312 | tf_op jit(solution)/shard_map/ppermute | solution.py:274
  31.9 57.2 %copy-start.15 = (s32[2]{0:T(128)}, s32[2]{0:T(128)S(1)}, u32[]{:S(2)}) copy-start(s32[2]{0:T(128)S(1)} %pad_add_fusion.place) | copy-start | bytes 28
  37.7 0.8 copy-start.13
  66.9 22.1 %all-to-all-start.2 = ((f32[8,128,128]{2,1,0:T(8,128)}), f32[8,128,128]{2,1,0:T(8,128)S(1)}, u32[]{:S(2)}, u32[]{:S(2)}) async-start(f32[8,128,128]{2,1,0:T(8,128)} %add_up.1), calls=%async_computation.2 | async-start | bytes 1048576 | tf_op jit(solution)/shard_map/all_to_all | solution.py:333
  70.4 14.2 %collective-permute-start.9 = (bf16[160,1024]{1,0:T(8,128)(2,1)S(1)}, bf16[160,1024]{1,0:T(8,128)(2,1)S(1)}, u32[]{:S(2)}, u32[]{:S(2)}) collective-permute-start(bf16[160,1024]{1,0:T(8,128)(2,1)S(1)} %get-tuple-element.24.refs_0_), channel_id=1, source_target_pairs={{0,192},{64,0},{128,64},{192,128},{1,193},{65,1},{129,65},{193,129... | collective-permute-start | bytes 983048 | tf_op jit(solution)/shard_map/ppermute | solution.py:274
  72.0 12.6 %collective-permute-start.8 = (bf16[160,1024]{1,0:T(8,128)(2,1)S(1)}, bf16[160,1024]{1,0:T(8,128)(2,1)S(1)}, u32[]{:S(2)}, u32[]{:S(2)}) collective-permute-start(bf16[160,1024]{1,0:T(8,128)(2,1)S(1)} %get-tuple-element.24.refs_0_), channel_id=1, source_target_pairs={{0,128},{64,192},{128,0},{192,64},{1,129},{65,193},{129,1},{193,65... | collective-permute-start | bytes 983048 | tf_op jit(solution)/shard_map/ppermute | solution.py:274
  73.5 14.8 %collective-permute-start.7 = (bf16[160,1024]{1,0:T(8,128)(2,1)S(1)}, bf16[160,1024]{1,0:T(8,128)(2,1)S(1)}, u32[]{:S(2)}, u32[]{:S(2)}) collective-permute-start(bf16[160,1024]{1,0:T(8,128)(2,1)S(1)} %get-tuple-element.24.refs_0_), channel_id=1, source_target_pairs={{0,64},{64,128},{128,192},{192,0},{1,65},{65,129},{129,193},{193,1... | collective-permute-start | bytes 983048 | tf_op jit(solution)/shard_map/ppermute | solution.py:274
  84.6 0.7 copy-start.1
  88.3 0.7 copy-start.3
  89.0 1.0 copy-start.2
  90.0 1.0 copy-start.4
  102.6 0.6 copy-start.14
  103.2 0.6 copy-start.16
  103.8 0.6 copy-start.17
  104.4 0.6 copy-start.18
  105.0 20.6 %all-to-all-start.3 = ((bf16[32,32,128]{2,1,0:T(8,128)(2,1)}), bf16[32,32,128]{2,1,0:T(8,128)(2,1)S(1)}, u32[]{:S(2)}, u32[]{:S(2)}) async-start(bf16[32,32,128]{2,1,0:T(8,128)(2,1)} %bitcast.18), calls=%async_computation.3 | async-start | bytes 524288 | tf_op jit(solution)/shard_map/all_to_all | solution.py:354
  113.1 6.0 %collective-permute-start.10 = (f32[32,128]{1,0:T(8,128)}, f32[32,128]{1,0:T(8,128)S(1)}, u32[]{:S(2)}, u32[]{:S(2)}) collective-permute-start(f32[32,128]{1,0:T(8,128)} %copy-done.18), channel_id=1, source_target_pairs={{0,64},{64,128},{128,192},{192,0},{1,65},{65,129},{129,193},{193,1... | collective-permute-start | bytes 49160 | tf_op jit(solution)/shard_map/ppermute | solution.py:274
  115.0 5.6 %collective-permute-start.11 = (f32[32,128]{1,0:T(8,128)}, f32[32,128]{1,0:T(8,128)S(1)}, u32[]{:S(2)}, u32[]{:S(2)}) collective-permute-start(f32[32,128]{1,0:T(8,128)} %copy-done.17), channel_id=1, source_target_pairs={{0,128},{64,192},{128,0},{192,64},{1,129},{65,193},{129,1},{193,65... | collective-permute-start | bytes 49160 | tf_op jit(solution)/shard_map/ppermute | solution.py:274
  117.7 4.0 %collective-permute-start.12 = (f32[32,128]{1,0:T(8,128)}, f32[32,128]{1,0:T(8,128)S(1)}, u32[]{:S(2)}, u32[]{:S(2)}) collective-permute-start(f32[32,128]{1,0:T(8,128)} %copy-done.16), channel_id=1, source_target_pairs={{0,192},{64,0},{128,64},{192,128},{1,193},{65,1},{129,65},{193,129... | collective-permute-start | bytes 49160 | tf_op jit(solution)/shard_map/ppermute | solution.py:274
  119.1 6.5 %copy-start.21 = (f32[32,128]{1,0:T(8,128)}, f32[32,128]{1,0:T(8,128)S(1)}, u32[]{:S(2)}) copy-start(f32[32,128]{1,0:T(8,128)S(1)} %collective-permute-done.10.refs_1_) | copy-start | bytes 49156
  120.6 5.1 %copy-start.22 = (f32[32,128]{1,0:T(8,128)}, f32[32,128]{1,0:T(8,128)S(1)}, u32[]{:S(2)}) copy-start(f32[32,128]{1,0:T(8,128)S(1)} %collective-permute-done.11.refs_2_) | copy-start | bytes 49156
  121.7 3.9 %copy-start.23 = (f32[32,128]{1,0:T(8,128)}, f32[32,128]{1,0:T(8,128)S(1)}, u32[]{:S(2)}) copy-start(f32[32,128]{1,0:T(8,128)S(1)} %collective-permute-done.12.refs_3_) | copy-start | bytes 49156
  125.6 0.7 copy-start.19

commit v3 on v2

--- a/solution.py
+++ b/solution.py
@@ -18,6 +18,7 @@
 VMEM = pltpu.VMEM
 LANES = 128
 TAIL = 16
+BLOCK = 4
 
 
 def params(mib):
@@ -136,11 +137,11 @@
 
 
 def add_up(parts, out):
-    total = parts[0]
+    total = parts[0].astype(F32)
     for z in range(1, parts.shape[0]):
-        total = total + parts[z]
+        total = total + parts[z].astype(F32)
     for z in range(out.shape[0]):
-        out[z] = total
+        out[z] = total.astype(out.dtype)
 
 
 def inverse_factors(grams):
@@ -149,19 +150,28 @@
     lane_at = lax.broadcasted_iota(jnp.int32, (rank, 2 * rank), 1)
     eye = (row_at + rank == lane_at).astype(F32)
     tables = [jnp.concatenate([g, jnp.zeros((rank, rank), F32)], axis=1) + eye for g in grams]
-    scales = [jnp.ones((rank, 2 * rank), F32) for _ in grams]
-    for k in range(rank):
+    for first in range(0, rank, BLOCK):
+        top = (first // 8) * 8
+        at = first - top
         for i, table in enumerate(tables):
-            top = (k // 8) * 8
-            pivot_row = table[k : k + 1, :]
-            pivot = pivot_row[:, k : k + 1]
-            scaled = pivot_row * (1.0 / pivot)
-            column = table[top:, k : k + 1]
-            below = row_at[top:, :] > k
-            lower = table[top:, :] - jnp.where(below, column * scaled, 0.0)
+            lower = table[top:, :]
+            columns = [
+                jnp.broadcast_to(lower[:, first + j : first + j + 1], lower.shape) for j in range(BLOCK)
+            ]
+            pivots = [lower[at + j : at + j + 1, :] for j in range(BLOCK)]
+            for j in range(BLOCK):
+                own = columns[j][at + j : at + j + 1, :]
+                share = jnp.where(row_at[top:, :] > first + j, columns[j] * (1.0 / own), 0.0)
+                for k in range(j + 1, BLOCK):
+                    columns[k] = columns[k] - share * columns[j][at + k : at + k + 1, :]
+                    pivots[k] = pivots[k] - share[at + k : at + k + 1, :] * pivots[j]
+                lower = lower - share * pivots[j]
             tables[i] = lower if top == 0 else jnp.concatenate([table[:top], lower], axis=0)
-            scales[i] = jnp.where(row_at == k, pivot, scales[i])
-    return [(table * lax.rsqrt(scale))[:, rank:] for table, scale in zip(tables, scales, strict=True)]
+    diagonal = row_at == lane_at
+    return [
+        (table * lax.rsqrt(jnp.sum(jnp.where(diagonal, table, 0.0), axis=1, keepdims=True)))[:, rank:]
+        for table in tables
+    ]
 
 
 def second_pass(place, sketches, held_far, *refs):
@@ -181,10 +191,13 @@
         jnp.concatenate([sketches[z, t * rank : (t + 1) * rank, :] for z in range(cuts)], axis=1)
         for t in range(targets)
     ]
-    grams = [lax.dot_general(s, s, NT, precision=HIGHEST, preferred_element_type=F32) for s in whole]
+    grams = [lax.dot_general(s, s, NT, preferred_element_type=F32) for s in whole]
     inverses = inverse_factors(grams)
     for t in range(targets):
-        found = jnp.dot(inverses[t], whole[t], precision=HIGHEST, preferred_element_type=F32)
+        found = jnp.dot(
+            jnp.concatenate(split_bf(inverses[t], 3), axis=0), whole[t], preferred_element_type=F32
+        )
+        found = (found[0:rank] + found[rank : 2 * rank]) + found[2 * rank : 3 * rank]
         basis[t * rank : (t + 1) * rank, :] = found
         rounded[t * rank : (t + 1) * rank, :] = found.astype(BF)
     for copy in loads:
@@ -306,7 +319,7 @@
         in_specs=[in_smem] + [in_vmem] * (nx + 2),
         out_specs=(in_vmem,) * (ny + 1),
         scratch_shapes=[VMEM((targets * rank, rows), BF)],
-        compiler_params=params(24),
+        compiler_params=params(60),
         name="project",
     )(columns, *pieces, probes.reshape(targets * rank, width), coupling)
     coefficients = [sent[0]] + [turn(sent[s], "y", ny, s) for s in range(1, ny)]
@@ -317,17 +330,20 @@
         out_shape=jax.ShapeDtypeStruct((nz, own_rows, cut), F32),
         in_specs=[in_smem] + [in_vmem] * (ny + 1),
         out_specs=in_vmem,
-        compiler_params=params(24),
+        compiler_params=params(20),
         name="first_pass",
     )(place, held, *coefficients)
     shared, sketch = lax.optimization_barrier((shared, sketch))
-    all_shared = [shared] + [turn(shared, "y", ny, s) for s in range(1, ny)]
+    near = [turn(shared, "y", ny, s) for s in (1, ny - 1)]
     parts = lax.all_to_all(sketch, "z", 0, 0, tiled=True)
+    parts, shared, *near = lax.optimization_barrier((parts, shared, *near))
+    all_shared = [shared, near[0]] + [turn(shared, "y", ny, s) for s in range(2, ny - 1)] + [near[1]]
     copies = pl.pallas_call(
         add_up,
-        out_shape=jax.ShapeDtypeStruct((nz, own_rows, cut), F32),
+        out_shape=jax.ShapeDtypeStruct((nz, own_rows, cut), BF),
         in_specs=[in_vmem],
         out_specs=in_vmem,
+        compiler_params=params(8),
         name="add_up",
     )(parts)
     sketches = lax.all_to_all(copies, "z", 0, 0, tiled=True)
@@ -347,7 +363,7 @@
             VMEM((ny, rows + 2 * TAIL, width), BF),
             pltpu.SemaphoreType.DMA((ny + 1,)),
         ],
-        compiler_params=params(40),
+        compiler_params=params(52),
         name="second_pass",
     )(place, sketches, held, *all_shared)
     left_parts = [left[0]] + [turn(left[s], "y", ny, s) for s in range(1, ny)]
@@ -358,6 +374,7 @@
         out_shape=(out, out),
         in_specs=[in_smem] + [in_vmem] * (ny + 1),
         out_specs=(in_vmem, in_vmem),
+        compiler_params=params(8),
         name="finish",
     )(place, row_parts, *left_parts)
     return left_out.transpose(0, 2, 1), right_out.transpose(0, 2, 1)

time: 129 us -> 112 us (0.87)
  blocking collectives: 25.7 us -> 0 us
  starting transfers between devices: 35.5 us -> 46.8 us
  waiting for transfers between devices: 30.4 us -> 40 us
  local copies, waits for them, and re-layouts: 13.2 us -> 3.7 us
  Pallas kernels: 22 us -> 19.7 us
    all_to_all x1 -> x0, blocking collectives: 25.7 us -> none  [shards(): parts = lax.all_to_all(sketch, 'z', 0, 0, tiled=True)]
    unnamed x48 -> x20, local copies, waits for them, and re-layouts: 13.1 us -> 3.11 us
    all_to_all x0 -> x1, starting transfers between devices: none -> 8.47 us  [shards(): parts = lax.all_to_all(sketch, 'z', 0, 0, tiled=True)]
    ppermute x13, waiting for transfers between devices: 26.4 us -> 31.6 us  [turn(): lax.ppermute(value, axis, [(i, (i + by) % size) for i in range(size)])]
    all_to_all x0 -> x1, waiting for transfers between devices: none -> 4.08 us  [shards(): parts = lax.all_to_all(sketch, 'z', 0, 0, tiled=True)]
    pallas_call x1, Pallas kernels: 11.7 us -> 8.62 us  [shards(): pl.pallas_call(second_pass, out_shape=(jax.ShapeDtypeStruct((width, own_r...]
    all_to_all x1, starting transfers between devices: 8.04 us -> 9.91 us  [shards(): lax.all_to_all(rows_part.reshape(ny * nz, keep, own_rows), ('y', 'z'), 0,...]
    pallas_call x1, Pallas kernels: 1.7 us -> 3.22 us  [shards(): pl.pallas_call(project, out_shape=(jax.ShapeDtypeStruct((rows + 2 * TAIL,...]
  transfers between devices with their start and end apart: 16 -> 17, of which waited for: 9 -> 13; matrix products, arithmetic and copies ran while one was open for 0% -> 1% of each run, Pallas kernels for 1% -> 3%
where the time goes in v3:
time: 112 us
  starting transfers between devices  46.8 us (42%)
  waiting for transfers between devices  40 us (36%)
  Pallas kernels  19.7 us (18%)
  local copies, waits for them, and re-layouts  3.7 us (3%)
  between operations  1.37 us (1%)
    ppermute x13, waiting for transfers between devices, turn(): lax.ppermute(value, axis, [(i, (i + by) % size) for i in range(size)])  31.6 us
    ppermute x13, starting transfers between devices, turn(): lax.ppermute(value, axis, [(i, (i + by) % size) for i in range(size)])  20.6 us
    all_to_all x1, starting transfers between devices, shards(): lax.all_to_all(rows_part.reshape(ny * nz, keep, own_rows), ('y', 'z'), 0,...  9.91 us
    pallas_call x1, Pallas kernels, shards(): pl.pallas_call(second_pass, out_shape=(jax.ShapeDtypeStruct((width, own_r...  8.62 us
    all_to_all x1, starting transfers between devices, shards(): parts = lax.all_to_all(sketch, 'z', 0, 0, tiled=True)  8.47 us
    all_to_all x1, starting transfers between devices, shards(): held = lax.all_to_all(sums, 'y', 0, 0, tiled=True)  4.48 us
    all_to_all x1, waiting for transfers between devices, shards(): parts = lax.all_to_all(sketch, 'z', 0, 0, tiled=True)  4.08 us
    pallas_call x1, Pallas kernels, shards(): pl.pallas_call(sum_factors, out_shape=jax.ShapeDtypeStruct((ny, held_rows...  3.96 us
  transfers between devices with their start and end apart: 17, of which 13 were waited for; matrix products, arithmetic and copies ran while one was open for 1% of the time, Pallas kernels for 3%

profile of v3, /device:TPU:6, one launch (start us, length us, event | category | flops | bytes accessed | tf_op | source)
XLA Modules:
  0.0 111.7 jit_solution(9587210805294622499)
XLA Ops:
  1.3 4.0 %sum_factors.1 = bf16[4,256,1024]{2,1,0:T(8,128)(2,1)} custom-call(s32[36]{0:T(128)} %bitcast.27, s32[36]{0:T(128)} %bitcast.28, s32[1]{0:T(128)} %bitcast.21.count, bf16[36,64,1024]{2,1,0:T(8,128)(2,1)} %bitcast.22), custom_call_target="tpu_custom_call" | custom-call | flops 10000000 | bytes 7000000 | tf_op jit(solution)/shard_map/sum_factors/pallas_call | solution.py:289
  5.2 0.0 copy-start.9
  5.3 4.5 %all-to-all-start = ((bf16[4,256,1024]{2,1,0:T(8,128)(2,1)}), bf16[4,256,1024]{2,1,0:T(8,128)(2,1)S(1)}, u32[]{:S(2)}, u32[]{:S(2)}) async-start(bf16[4,256,1024]{2,1,0:T(8,128)(2,1)} %sum_factors.1), calls=%async_computation | async-start | bytes 4194304 | tf_op jit(solution)/shard_map/all_to_all | solution.py:307
  9.7 0.0 collective-permute-start
  9.7 1.2 %collective-permute-done = bf16[128,128]{1,0:T(8,128)(2,1)S(1)} collective-permute-done((bf16[128,128]{1,0:T(8,128)(2,1)S(1)}, bf16[128,128]{1,0:T(8,128)(2,1)S(1)}, u32[]{:S(2)}, u32[]{:S(2)}) %collective-permute-start) | collective-permute-done | bytes 32800 | tf_op jit(solution)/shard_map/ppermute | solution.py:287
  11.0 0.0 copy-start.5
  11.0 0.9 collective-permute-start.3
  11.9 2.1 %collective-permute-start.2 = (bf16[2,128,128]{2,1,0:T(8,128)(2,1)S(1)}, bf16[2,128,128]{2,1,0:T(8,128)(2,1)S(1)}, u32[]{:S(2)}, u32[]{:S(2)}) collective-permute-start(bf16[2,128,128]{2,1,0:T(8,128)(2,1)S(1)} %pad_maximum_fusion.refs_0_), channel_id=1, source_target_pairs={{0,4},{2,6},{4,0},{6,2},{1,5},{3,7},{5,1},{7,3},{8,12},{10,14},{12... | collective-permute-start | bytes 196616 | tf_op jit(solution)/shard_map/ppermute | solution.py:287
  14.0 1.1 collective-permute-start.1
  15.1 0.6 stack.57.columns
  15.7 2.2 %collective-permute-done.3.refs_3_ = bf16[2,128,128]{2,1,0:T(8,128)(2,1)S(1)} collective-permute-done((bf16[2,128,128]{2,1,0:T(8,128)(2,1)S(1)}, bf16[2,128,128]{2,1,0:T(8,128)(2,1)S(1)}, u32[]{:S(2)}, u32[]{:S(2)}) %collective-permute-start.3) | collective-permute-done | bytes 65568 | tf_op jit(solution)/shard_map/ppermute | solution.py:287
  17.9 0.0 collective-permute-done.2.refs_2_
  17.9 0.5 collective-permute-done.1.refs_1_
  18.4 0.1 copy-done.6
  18.5 0.0 copy-done.7
  18.6 0.4 copy-done.8
  19.0 3.2 %project.1 = (bf16[160,1024]{1,0:T(8,128)(2,1)}, bf16[128,128]{1,0:T(8,128)(2,1)}, bf16[128,128]{1,0:T(8,128)(2,1)}, bf16[128,128]{1,0:T(8,128)(2,1)}, bf16[128,128]{1,0:T(8,128)(2,1)}) custom-call(s32[9]{0:T(128)} %stack.57.columns, bf16[2,128,128]{2,1,0:T(8,128)(2,1)} %copy-done.5, bf16[2,128,128]{2,1,0:T(8,128)(2,1)} %copy-done.8, ...), custom_call_target="tpu_custom_call" | custom-call | tf_op jit(solution)/shard_map/project/pallas_call | solution.py:315
  22.2 2.0 %collective-permute-start.4 = (bf16[128,128]{1,0:T(8,128)(2,1)}, bf16[128,128]{1,0:T(8,128)(2,1)S(1)}, u32[]{:S(2)}, u32[]{:S(2)}) collective-permute-start(bf16[128,128]{1,0:T(8,128)(2,1)} %get-tuple-element.24), channel_id=1, source_target_pairs={{0,64},{64,128},{128,192},{192,0},{1,65},{65,129},{129,193},{193,1... | collective-permute-start | bytes 98312 | tf_op jit(solution)/shard_map/ppermute | solution.py:287
  24.3 2.7 %collective-permute-start.5 = (bf16[128,128]{1,0:T(8,128)(2,1)}, bf16[128,128]{1,0:T(8,128)(2,1)S(1)}, u32[]{:S(2)}, u32[]{:S(2)}) collective-permute-start(bf16[128,128]{1,0:T(8,128)(2,1)} %get-tuple-element.25), channel_id=1, source_target_pairs={{0,128},{64,192},{128,0},{192,64},{1,129},{65,193},{129,1},{193,65... | collective-permute-start | bytes 98312 | tf_op jit(solution)/shard_map/ppermute | solution.py:287
  26.9 1.5 %collective-permute-start.6 = (bf16[128,128]{1,0:T(8,128)(2,1)}, bf16[128,128]{1,0:T(8,128)(2,1)S(1)}, u32[]{:S(2)}, u32[]{:S(2)}) collective-permute-start(bf16[128,128]{1,0:T(8,128)(2,1)} %get-tuple-element.26), channel_id=1, source_target_pairs={{0,192},{64,0},{128,64},{192,128},{1,193},{65,1},{129,65},{193,129... | collective-permute-start | bytes 98312 | tf_op jit(solution)/shard_map/ppermute | solution.py:287
  28.4 0.1 pad_add_fusion.place
  28.5 7.0 %collective-permute-done.4.refs_1_ = bf16[128,128]{1,0:T(8,128)(2,1)S(1)} collective-permute-done((bf16[128,128]{1,0:T(8,128)(2,1)}, bf16[128,128]{1,0:T(8,128)(2,1)S(1)}, u32[]{:S(2)}, u32[]{:S(2)}) %collective-permute-start.4) | collective-permute-done | bytes 32800 | tf_op jit(solution)/shard_map/ppermute | solution.py:287
  35.4 2.1 %collective-permute-done.5.refs_2_ = bf16[128,128]{1,0:T(8,128)(2,1)S(1)} collective-permute-done((bf16[128,128]{1,0:T(8,128)(2,1)}, bf16[128,128]{1,0:T(8,128)(2,1)S(1)}, u32[]{:S(2)}, u32[]{:S(2)}) %collective-permute-start.5) | collective-permute-done | bytes 32800 | tf_op jit(solution)/shard_map/ppermute | solution.py:287
  37.5 0.0 collective-permute-done.6.refs_3_
  37.5 0.7 copy-done.4
  38.3 1.8 %first_pass.1 = f32[8,128,128]{2,1,0:T(8,128)} custom-call(s32[2]{0:T(128)S(1)} %pad_add_fusion.place, bf16[4,256,1024]{2,1,0:T(8,128)(2,1)S(1)} %all-to-all-done.held.held_far, bf16[128,128]{1,0:T(8,128)(2,1)S(1)} %copy-done.4, bf16[128,128]{1,0:T(8,128)(2,1)S(1)} %collective-permute-done.4.refs_1_, bf16[128,128]{1,0:T(8,128)(2,1)S(1)} %collective-permute-done.5.refs_2_, ...), custom_call_target="tpu_custom_call" | custom-call | tf_op jit(solution)/shard_map/first_pass/pallas_call | solution.py:328
  40.1 8.5 %all-to-all-start.1 = ((f32[8,128,128]{2,1,0:T(8,128)}), f32[8,128,128]{2,1,0:T(8,128)S(1)}, u32[]{:S(2)}, u32[]{:S(2)}) async-start(f32[8,128,128]{2,1,0:T(8,128)} %first_pass.1), calls=%async_computation.1 | async-start | bytes 1048576 | tf_op jit(solution)/shard_map/all_to_all | solution.py:338
  48.5 1.2 %collective-permute-start.8 = (bf16[160,1024]{1,0:T(8,128)(2,1)S(1)}, bf16[160,1024]{1,0:T(8,128)(2,1)S(1)}, u32[]{:S(2)}, u32[]{:S(2)}) collective-permute-start(bf16[160,1024]{1,0:T(8,128)(2,1)S(1)} %copy-done.1), channel_id=1, source_target_pairs={{0,192},{64,0},{128,64},{192,128},{1,193},{65,1},{129,65},{193,129... | collective-permute-start | bytes 983048 | tf_op jit(solution)/shard_map/ppermute | solution.py:287
  49.7 0.9 collective-permute-start.7
  50.6 6.1 %collective-permute-done.8.refs_3_ = bf16[160,1024]{1,0:T(8,128)(2,1)S(1)} collective-permute-done((bf16[160,1024]{1,0:T(8,128)(2,1)S(1)}, bf16[160,1024]{1,0:T(8,128)(2,1)S(1)}, u32[]{:S(2)}, u32[]{:S(2)}) %collective-permute-start.8) | collective-permute-done | bytes 327712 | tf_op jit(solution)/shard_map/ppermute | solution.py:287
  56.7 3.3 %collective-permute-done.7.refs_1_ = bf16[160,1024]{1,0:T(8,128)(2,1)S(1)} collective-permute-done((bf16[160,1024]{1,0:T(8,128)(2,1)S(1)}, bf16[160,1024]{1,0:T(8,128)(2,1)S(1)}, u32[]{:S(2)}, u32[]{:S(2)}) %collective-permute-start.7) | collective-permute-done | bytes 327712 | tf_op jit(solution)/shard_map/ppermute | solution.py:287
  60.0 0.7 copy-done.2
  60.8 4.1 %all-to-all-done.1.parts = f32[8,128,128]{2,1,0:T(8,128)S(1)} async-done(((f32[8,128,128]{2,1,0:T(8,128)}), f32[8,128,128]{2,1,0:T(8,128)S(1)}, u32[]{:S(2)}, u32[]{:S(2)}) %all-to-all-start.1) | async-done | bytes 524320 | tf_op jit(solution)/shard_map/all_to_all | solution.py:338
  64.8 0.7 add_up.1
  65.6 3.4 %all-to-all-start.2 = ((bf16[8,128,128]{2,1,0:T(8,128)(2,1)}), bf16[8,128,128]{2,1,0:T(8,128)(2,1)S(1)}, u32[]{:S(2)}, u32[]{:S(2)}) async-start(bf16[8,128,128]{2,1,0:T(8,128)(2,1)} %add_up.1), calls=%async_computation.2 | async-start | bytes 524288 | tf_op jit(solution)/shard_map/all_to_all | solution.py:349
  69.0 2.2 %collective-permute-start.9 = (bf16[160,1024]{1,0:T(8,128)(2,1)S(1)}, bf16[160,1024]{1,0:T(8,128)(2,1)S(1)}, u32[]{:S(2)}, u32[]{:S(2)}) collective-permute-start(bf16[160,1024]{1,0:T(8,128)(2,1)S(1)} %copy-done.1), channel_id=1, source_target_pairs={{0,128},{64,192},{128,0},{192,64},{1,129},{65,193},{129,1},{193,65... | collective-permute-start | bytes 983048 | tf_op jit(solution)/shard_map/ppermute | solution.py:287
  71.2 6.9 %collective-permute-done.9.refs_2_ = bf16[160,1024]{1,0:T(8,128)(2,1)S(1)} collective-permute-done((bf16[160,1024]{1,0:T(8,128)(2,1)S(1)}, bf16[160,1024]{1,0:T(8,128)(2,1)S(1)}, u32[]{:S(2)}, u32[]{:S(2)}) %collective-permute-start.9) | collective-permute-done | bytes 327712 | tf_op jit(solution)/shard_map/ppermute | solution.py:287
  78.0 1.4 %all-to-all-done.2.sketches = bf16[8,128,128]{2,1,0:T(8,128)(2,1)S(1)} async-done(((bf16[8,128,128]{2,1,0:T(8,128)(2,1)}), bf16[8,128,128]{2,1,0:T(8,128)(2,1)S(1)}, u32[]{:S(2)}, u32[]{:S(2)}) %all-to-all-start.2) | async-done | bytes 262176 | tf_op jit(solution)/shard_map/all_to_all | solution.py:349
  79.4 1.0 copy-done.3
  80.4 8.6 %second_pass.1 = (bf16[1024,128]{1,0:T(8,128)(2,1)}, f32[32,128]{1,0:T(8,128)S(1)}, f32[32,128]{1,0:T(8,128)S(1)}, f32[32,128]{1,0:T(8,128)S(1)}, f32[32,128]{1,0:T(8,128)S(1)}) custom-call(s32[2]{0:T(128)S(1)} %pad_add_fusion.place, bf16[8,128,128]{2,1,0:T(8,128)(2,1)S(1)} %all-to-all-done.2.sketches, bf16[4,256,1024]{2,1,0:T(8,128)(2,1)} %copy-done, ...), custom_call_target="tpu_custom_call" | custom-call | tf_op jit(solution)/shard_map/second_pass/pallas_call | solution.py:352
  89.0 9.9 %all-to-all-start.3 = ((bf16[32,32,128]{2,1,0:T(8,128)(2,1)}), bf16[32,32,128]{2,1,0:T(8,128)(2,1)S(1)}, u32[]{:S(2)}, u32[]{:S(2)}) async-start(bf16[32,32,128]{2,1,0:T(8,128)(2,1)} %bitcast.18), calls=%async_computation.3 | async-start | bytes 524288 | tf_op jit(solution)/shard_map/all_to_all | solution.py:370
  98.9 1.9 %collective-permute-start.10 = (f32[32,128]{1,0:T(8,128)S(1)}, f32[32,128]{1,0:T(8,128)S(1)}, u32[]{:S(2)}, u32[]{:S(2)}) collective-permute-start(f32[32,128]{1,0:T(8,128)S(1)} %get-tuple-element.35), channel_id=1, source_target_pairs={{0,64},{64,128},{128,192},{192,0},{1,65},{65,129},{129,193},{193,1... | collective-permute-start | bytes 49160 | tf_op jit(solution)/shard_map/ppermute | solution.py:287
  100.8 2.7 %collective-permute-start.11 = (f32[32,128]{1,0:T(8,128)S(1)}, f32[32,128]{1,0:T(8,128)S(1)}, u32[]{:S(2)}, u32[]{:S(2)}) collective-permute-start(f32[32,128]{1,0:T(8,128)S(1)} %get-tuple-element.36), channel_id=1, source_target_pairs={{0,128},{64,192},{128,0},{192,64},{1,129},{65,193},{129,1},{193,65... | collective-permute-start | bytes 49160 | tf_op jit(solution)/shard_map/ppermute | solution.py:287
  103.5 1.4 %collective-permute-start.12 = (f32[32,128]{1,0:T(8,128)S(1)}, f32[32,128]{1,0:T(8,128)S(1)}, u32[]{:S(2)}, u32[]{:S(2)}) collective-permute-start(f32[32,128]{1,0:T(8,128)S(1)} %get-tuple-element.37), channel_id=1, source_target_pairs={{0,192},{64,0},{128,64},{192,128},{1,193},{65,1},{129,65},{193,129... | collective-permute-start | bytes 49160 | tf_op jit(solution)/shard_map/ppermute | solution.py:287
  104.9 1.4 %collective-permute-done.11.refs_2_ = f32[32,128]{1,0:T(8,128)S(1)} collective-permute-done((f32[32,128]{1,0:T(8,128)S(1)}, f32[32,128]{1,0:T(8,128)S(1)}, u32[]{:S(2)}, u32[]{:S(2)}) %collective-permute-start.11) | collective-permute-done | bytes 16416 | tf_op jit(solution)/shard_map/ppermute | solution.py:287
  106.4 1.0 collective-permute-done.12.refs_3_
  107.4 2.9 %all-to-all-done.3.parts = bf16[32,32,128]{2,1,0:T(8,128)(2,1)S(1)} async-done(((bf16[32,32,128]{2,1,0:T(8,128)(2,1)}), bf16[32,32,128]{2,1,0:T(8,128)(2,1)S(1)}, u32[]{:S(2)}, u32[]{:S(2)}) %all-to-all-start.3) | async-done | bytes 262176 | tf_op jit(solution)/shard_map/all_to_all | solution.py:370
  110.3 1.3 %finish.1 = (f32[8,32,64]{2,1,0:T(8,128)}, f32[8,32,64]{2,1,0:T(8,128)}) custom-call(s32[2]{0:T(128)S(1)} %pad_add_fusion.place, bf16[32,32,128]{2,1,0:T(8,128)(2,1)S(1)} %all-to-all-done.3.parts, f32[32,128]{1,0:T(8,128)S(1)} %get-tuple-element.34.refs_0_, f32[32,128]{1,0:T(8,128)S(1)} %collective-permute-done.10.refs_1_, ...), custom_call_target="tpu_custom_call" | custom-call | tf_op jit(solution)/shard_map/finish/pallas_call | solution.py:372
  (15 shorter events, 0.0 us)
Async XLA Ops:
  5.2 4.5 %copy-start.9 = (bf16[2,64,128]{2,1,0:T(8,128)(2,1)S(1)}, bf16[2,64,128]{2,1,0:T(8,128)(2,1)}, u32[]{:S(2)}) copy-start(bf16[2,64,128]{2,1,0:T(8,128)(2,1)} %param.11) | copy-start | bytes 98308
  5.3 32.3 %all-to-all-start = ((bf16[4,256,1024]{2,1,0:T(8,128)(2,1)}), bf16[4,256,1024]{2,1,0:T(8,128)(2,1)S(1)}, u32[]{:S(2)}, u32[]{:S(2)}) async-start(bf16[4,256,1024]{2,1,0:T(8,128)(2,1)} %sum_factors.1), calls=%async_computation | async-start | bytes 4194304 | tf_op jit(solution)/shard_map/all_to_all | solution.py:307
  9.7 1.2 %collective-permute-start = (bf16[128,128]{1,0:T(8,128)(2,1)S(1)}, bf16[128,128]{1,0:T(8,128)(2,1)S(1)}, u32[]{:S(2)}, u32[]{:S(2)}) collective-permute-start(bf16[128,128]{1,0:T(8,128)(2,1)S(1)} %bitcast.24), channel_id=1, source_target_pairs={{0,1},{1,0},{2,3},{3,2},{4,5},{5,4},{6,7},{7,6},{8,9},{9,8},{10,11... | collective-permute-start | bytes 98312 | tf_op jit(solution)/shard_map/ppermute | solution.py:287
  11.0 7.4 %copy-start.5 = (bf16[2,128,128]{2,1,0:T(8,128)(2,1)}, bf16[2,128,128]{2,1,0:T(8,128)(2,1)S(1)}, u32[]{:S(2)}) copy-start(bf16[2,128,128]{2,1,0:T(8,128)(2,1)S(1)} %pad_maximum_fusion.refs_0_) | copy-start | bytes 196612
  11.0 7.0 %collective-permute-start.3 = (bf16[2,128,128]{2,1,0:T(8,128)(2,1)S(1)}, bf16[2,128,128]{2,1,0:T(8,128)(2,1)S(1)}, u32[]{:S(2)}, u32[]{:S(2)}) collective-permute-start(bf16[2,128,128]{2,1,0:T(8,128)(2,1)S(1)} %pad_maximum_fusion.refs_0_), channel_id=1, source_target_pairs={{0,6},{2,0},{4,2},{6,4},{1,7},{3,1},{5,3},{7,5},{8,14},{10,8},{12,... | collective-permute-start | bytes 196616 | tf_op jit(solution)/shard_map/ppermute | solution.py:287
  11.9 6.1 %collective-permute-start.2 = (bf16[2,128,128]{2,1,0:T(8,128)(2,1)S(1)}, bf16[2,128,128]{2,1,0:T(8,128)(2,1)S(1)}, u32[]{:S(2)}, u32[]{:S(2)}) collective-permute-start(bf16[2,128,128]{2,1,0:T(8,128)(2,1)S(1)} %pad_maximum_fusion.refs_0_), channel_id=1, source_target_pairs={{0,4},{2,6},{4,0},{6,2},{1,5},{3,7},{5,1},{7,3},{8,12},{10,14},{12... | collective-permute-start | bytes 196616 | tf_op jit(solution)/shard_map/ppermute | solution.py:287
  14.0 4.4 %collective-permute-start.1 = (bf16[2,128,128]{2,1,0:T(8,128)(2,1)S(1)}, bf16[2,128,128]{2,1,0:T(8,128)(2,1)S(1)}, u32[]{:S(2)}, u32[]{:S(2)}) collective-permute-start(bf16[2,128,128]{2,1,0:T(8,128)(2,1)S(1)} %pad_maximum_fusion.refs_0_), channel_id=1, source_target_pairs={{0,2},{2,4},{4,6},{6,0},{1,3},{3,5},{5,7},{7,1},{8,10},{10,12},{12... | collective-permute-start | bytes 196616 | tf_op jit(solution)/shard_map/ppermute | solution.py:287
  17.9 0.6 copy-start.6
  17.9 0.6 copy-start.7
  18.4 0.6 copy-start.8
  22.2 26.3 %copy-start.1 = (bf16[160,1024]{1,0:T(8,128)(2,1)S(1)}, bf16[160,1024]{1,0:T(8,128)(2,1)}, u32[]{:S(2)}) copy-start(bf16[160,1024]{1,0:T(8,128)(2,1)} %get-tuple-element.30.refs_0_) | copy-start | bytes 983044
  22.2 13.2 %collective-permute-start.4 = (bf16[128,128]{1,0:T(8,128)(2,1)}, bf16[128,128]{1,0:T(8,128)(2,1)S(1)}, u32[]{:S(2)}, u32[]{:S(2)}) collective-permute-start(bf16[128,128]{1,0:T(8,128)(2,1)} %get-tuple-element.24), channel_id=1, source_target_pairs={{0,64},{64,128},{128,192},{192,0},{1,65},{65,129},{129,193},{193,1... | collective-permute-start | bytes 98312 | tf_op jit(solution)/shard_map/ppermute | solution.py:287
  24.3 13.2 %collective-permute-start.5 = (bf16[128,128]{1,0:T(8,128)(2,1)}, bf16[128,128]{1,0:T(8,128)(2,1)S(1)}, u32[]{:S(2)}, u32[]{:S(2)}) collective-permute-start(bf16[128,128]{1,0:T(8,128)(2,1)} %get-tuple-element.25), channel_id=1, source_target_pairs={{0,128},{64,192},{128,0},{192,64},{1,129},{65,193},{129,1},{193,65... | collective-permute-start | bytes 98312 | tf_op jit(solution)/shard_map/ppermute | solution.py:287
  26.9 10.6 %collective-permute-start.6 = (bf16[128,128]{1,0:T(8,128)(2,1)}, bf16[128,128]{1,0:T(8,128)(2,1)S(1)}, u32[]{:S(2)}, u32[]{:S(2)}) collective-permute-start(bf16[128,128]{1,0:T(8,128)(2,1)} %get-tuple-element.26), channel_id=1, source_target_pairs={{0,192},{64,0},{128,64},{192,128},{1,193},{65,1},{129,65},{193,129... | collective-permute-start | bytes 98312 | tf_op jit(solution)/shard_map/ppermute | solution.py:287
  37.5 28.1 %copy-start = (bf16[4,256,1024]{2,1,0:T(8,128)(2,1)}, bf16[4,256,1024]{2,1,0:T(8,128)(2,1)S(1)}, u32[]{:S(2)}) copy-start(bf16[4,256,1024]{2,1,0:T(8,128)(2,1)S(1)} %all-to-all-done.held.held_far) | copy-start | bytes 6291460
  37.5 0.8 copy-start.4
  40.1 24.8 %all-to-all-start.1 = ((f32[8,128,128]{2,1,0:T(8,128)}), f32[8,128,128]{2,1,0:T(8,128)S(1)}, u32[]{:S(2)}, u32[]{:S(2)}) async-start(f32[8,128,128]{2,1,0:T(8,128)} %first_pass.1), calls=%async_computation.1 | async-start | bytes 1048576 | tf_op jit(solution)/shard_map/all_to_all | solution.py:338
  48.5 8.2 %collective-permute-start.8 = (bf16[160,1024]{1,0:T(8,128)(2,1)S(1)}, bf16[160,1024]{1,0:T(8,128)(2,1)S(1)}, u32[]{:S(2)}, u32[]{:S(2)}) collective-permute-start(bf16[160,1024]{1,0:T(8,128)(2,1)S(1)} %copy-done.1), channel_id=1, source_target_pairs={{0,192},{64,0},{128,64},{192,128},{1,193},{65,1},{129,65},{193,129... | collective-permute-start | bytes 983048 | tf_op jit(solution)/shard_map/ppermute | solution.py:287
  49.7 10.3 %collective-permute-start.7 = (bf16[160,1024]{1,0:T(8,128)(2,1)S(1)}, bf16[160,1024]{1,0:T(8,128)(2,1)S(1)}, u32[]{:S(2)}, u32[]{:S(2)}) collective-permute-start(bf16[160,1024]{1,0:T(8,128)(2,1)S(1)} %copy-done.1), channel_id=1, source_target_pairs={{0,64},{64,128},{128,192},{192,0},{1,65},{65,129},{129,193},{193,1... | collective-permute-start | bytes 983048 | tf_op jit(solution)/shard_map/ppermute | solution.py:287
  60.0 0.7 copy-start.2
  65.6 13.8 %all-to-all-start.2 = ((bf16[8,128,128]{2,1,0:T(8,128)(2,1)}), bf16[8,128,128]{2,1,0:T(8,128)(2,1)S(1)}, u32[]{:S(2)}, u32[]{:S(2)}) async-start(bf16[8,128,128]{2,1,0:T(8,128)(2,1)} %add_up.1), calls=%async_computation.2 | async-start | bytes 524288 | tf_op jit(solution)/shard_map/all_to_all | solution.py:349
  69.0 9.0 %collective-permute-start.9 = (bf16[160,1024]{1,0:T(8,128)(2,1)S(1)}, bf16[160,1024]{1,0:T(8,128)(2,1)S(1)}, u32[]{:S(2)}, u32[]{:S(2)}) collective-permute-start(bf16[160,1024]{1,0:T(8,128)(2,1)S(1)} %copy-done.1), channel_id=1, source_target_pairs={{0,128},{64,192},{128,0},{192,64},{1,129},{65,193},{129,1},{193,65... | collective-permute-start | bytes 983048 | tf_op jit(solution)/shard_map/ppermute | solution.py:287
  79.4 1.0 copy-start.3
  89.0 21.3 %all-to-all-start.3 = ((bf16[32,32,128]{2,1,0:T(8,128)(2,1)}), bf16[32,32,128]{2,1,0:T(8,128)(2,1)S(1)}, u32[]{:S(2)}, u32[]{:S(2)}) async-start(bf16[32,32,128]{2,1,0:T(8,128)(2,1)} %bitcast.18), calls=%async_computation.3 | async-start | bytes 524288 | tf_op jit(solution)/shard_map/all_to_all | solution.py:370
  98.9 6.0 %collective-permute-start.10 = (f32[32,128]{1,0:T(8,128)S(1)}, f32[32,128]{1,0:T(8,128)S(1)}, u32[]{:S(2)}, u32[]{:S(2)}) collective-permute-start(f32[32,128]{1,0:T(8,128)S(1)} %get-tuple-element.35), channel_id=1, source_target_pairs={{0,64},{64,128},{128,192},{192,0},{1,65},{65,129},{129,193},{193,1... | collective-permute-start | bytes 49160 | tf_op jit(solution)/shard_map/ppermute | solution.py:287
  100.8 5.6 %collective-permute-start.11 = (f32[32,128]{1,0:T(8,128)S(1)}, f32[32,128]{1,0:T(8,128)S(1)}, u32[]{:S(2)}, u32[]{:S(2)}) collective-permute-start(f32[32,128]{1,0:T(8,128)S(1)} %get-tuple-element.36), channel_id=1, source_target_pairs={{0,128},{64,192},{128,0},{192,64},{1,129},{65,193},{129,1},{193,65... | collective-permute-start | bytes 49160 | tf_op jit(solution)/shard_map/ppermute | solution.py:287
  103.5 3.9 %collective-permute-start.12 = (f32[32,128]{1,0:T(8,128)S(1)}, f32[32,128]{1,0:T(8,128)S(1)}, u32[]{:S(2)}, u32[]{:S(2)}) collective-permute-start(f32[32,128]{1,0:T(8,128)S(1)} %get-tuple-element.37), channel_id=1, source_target_pairs={{0,192},{64,0},{128,64},{192,128},{1,193},{65,1},{129,65},{193,129... | collective-permute-start | bytes 49160 | tf_op jit(solution)/shard_map/ppermute | solution.py:287

commit v4 on v3

--- a/solution.py
+++ b/solution.py
@@ -133,7 +133,7 @@
                 preferred_element_type=F32,
             )
         for z in range(out.shape[0]):
-            out[z, t * rank : (t + 1) * rank, :] = total[:, z * cut : (z + 1) * cut]
+            out[z, t * rank : (t + 1) * rank, :] = total[:, z * cut : (z + 1) * cut].astype(BF)
 
 
 def add_up(parts, out):
@@ -176,10 +176,21 @@
 
 def second_pass(place, sketches, held_far, *refs):
     groups = held_far.shape[0]
-    shared_far, out, left, refs = refs[:groups], refs[groups], refs[groups + 1 : 2 * groups + 1], refs[2 * groups + 1 :]
+    shared_far, out, left, refs = refs[:5], refs[5], refs[6 : 6 + groups], refs[6 + groups :]
     basis, rounded, turned, held, shared, sems = refs
-    loads = [pltpu.make_async_copy(held_far, held, sems.at[groups])]
-    loads += [pltpu.make_async_copy(shared_far[s], shared.at[s], sems.at[s]) for s in range(groups)]
+    half = shared.shape[1] // 2
+    targets_of = (
+        shared.at[0],
+        shared.at[1],
+        shared.at[2, 0:half, :],
+        shared.at[2, half : 2 * half, :],
+        shared.at[3],
+    )
+    loads = [pltpu.make_async_copy(held_far, held, sems.at[5])]
+    loads += [
+        pltpu.make_async_copy(source, to, sems.at[i])
+        for i, (source, to) in enumerate(zip(shared_far, targets_of, strict=True))
+    ]
     for copy in loads:
         copy.start()
     cuts, rows, _ = sketches.shape
@@ -327,7 +338,7 @@
     cut = width // nz
     sketch = pl.pallas_call(
         first_pass,
-        out_shape=jax.ShapeDtypeStruct((nz, own_rows, cut), F32),
+        out_shape=jax.ShapeDtypeStruct((nz, own_rows, cut), BF),
         in_specs=[in_smem] + [in_vmem] * (ny + 1),
         out_specs=in_vmem,
         compiler_params=params(20),
@@ -337,7 +348,9 @@
     near = [turn(shared, "y", ny, s) for s in (1, ny - 1)]
     parts = lax.all_to_all(sketch, "z", 0, 0, tiled=True)
     parts, shared, *near = lax.optimization_barrier((parts, shared, *near))
-    all_shared = [shared, near[0]] + [turn(shared, "y", ny, s) for s in range(2, ny - 1)] + [near[1]]
+    middle_row = shared.shape[0] // 2
+    far = [turn(near[0][:middle_row], "y", ny, 1), turn(near[1][middle_row:], "y", ny, ny - 1)]
+    all_shared = [shared, near[0], *far, near[1]]
     copies = pl.pallas_call(
         add_up,
         out_shape=jax.ShapeDtypeStruct((nz, own_rows, cut), BF),
@@ -353,7 +366,7 @@
         second_pass,
         out_shape=(jax.ShapeDtypeStruct((width, own_rows), BF),)
         + (jax.ShapeDtypeStruct((keep, own_rows), F32),) * ny,
-        in_specs=[in_smem, in_vmem] + [in_any] * (ny + 1),
+        in_specs=[in_smem, in_vmem] + [in_any] * 6,
         out_specs=(in_vmem,) * (ny + 1),
         scratch_shapes=[
             VMEM((own_rows, width), F32),
@@ -361,7 +374,7 @@
             VMEM((LANES, own_rows), F32),
             VMEM((ny, held_rows, width), BF),
             VMEM((ny, rows + 2 * TAIL, width), BF),
-            pltpu.SemaphoreType.DMA((ny + 1,)),
+            pltpu.SemaphoreType.DMA((6,)),
         ],
         compiler_params=params(52),
         name="second_pass",

time: 112 us -> 104 us (0.929)
  waiting for transfers between devices: 40 us -> 35.6 us
  starting transfers between devices: 46.8 us -> 44.3 us
  local copies, waits for them, and re-layouts: 3.7 us -> 2.03 us
    all_to_all x1, starting transfers between devices: 9.91 us -> 4.08 us  [shards(): lax.all_to_all(rows_part.reshape(ny * nz, keep, own_rows), ('y', 'z'), 0,...]
    all_to_all x1, waiting for transfers between devices: 4.08 us -> 0.01 us  [shards(): parts = lax.all_to_all(sketch, 'z', 0, 0, tiled=True)]
    all_to_all x1, starting transfers between devices: 3.41 us -> 6.85 us  [shards(): sketches = lax.all_to_all(copies, 'z', 0, 0, tiled=True)]
    ppermute x13 -> x14, waiting for transfers between devices: 31.6 us -> 29.4 us  [turn(): lax.ppermute(value, axis, [(i, (i + by) % size) for i in range(size)])]
    all_to_all x1, waiting for transfers between devices: 1.37 us -> 3.55 us  [shards(): sketches = lax.all_to_all(copies, 'z', 0, 0, tiled=True)]
    unnamed x20 -> x16, local copies, waits for them, and re-layouts: 3.11 us -> 1.4 us
    ppermute x13 -> x14, starting transfers between devices: 20.6 us -> 20.5 us  [turn(): lax.ppermute(value, axis, [(i, (i + by) % size) for i in range(size)])]
  transfers between devices with their start and end apart: 17 -> 18, of which waited for: 13 -> 13; matrix products, arithmetic and copies ran while one was open for 1% -> 1% of each run, Pallas kernels for 3% -> 3%
where the time goes in v4:
time: 104 us; the launch traced here: 103 us
  starting transfers between devices  44.3 us (43%)
  waiting for transfers between devices  35.6 us (34%)
  Pallas kernels  19.9 us (19%)
  local copies, waits for them, and re-layouts  2.03 us (2%)
  between operations  1.38 us (1%)
    ppermute x14, waiting for transfers between devices, turn(): lax.ppermute(value, axis, [(i, (i + by) % size) for i in range(size)])  29.4 us
    ppermute x14, starting transfers between devices, turn(): lax.ppermute(value, axis, [(i, (i + by) % size) for i in range(size)])  20.5 us
    pallas_call x1, Pallas kernels, shards(): pl.pallas_call(second_pass, out_shape=(jax.ShapeDtypeStruct((width, own_r...  8.94 us
    all_to_all x1, starting transfers between devices, shards(): parts = lax.all_to_all(sketch, 'z', 0, 0, tiled=True)  8.46 us
    all_to_all x1, starting transfers between devices, shards(): sketches = lax.all_to_all(copies, 'z', 0, 0, tiled=True)  6.85 us
    all_to_all x1, starting transfers between devices, shards(): held = lax.all_to_all(sums, 'y', 0, 0, tiled=True)  4.48 us
    all_to_all x1, starting transfers between devices, shards(): lax.all_to_all(rows_part.reshape(ny * nz, keep, own_rows), ('y', 'z'), 0,...  4.08 us
    pallas_call x1, Pallas kernels, shards(): pl.pallas_call(sum_factors, out_shape=jax.ShapeDtypeStruct((ny, held_rows...  3.96 us
  transfers between devices with their start and end apart: 18, of which 13 were waited for; matrix products, arithmetic and copies ran while one was open for 1% of the time, Pallas kernels for 3%

profile of v4, /device:TPU:6, one launch (start us, length us, event | category | flops | bytes accessed | tf_op | source)
XLA Modules:
  0.0 103.4 jit_solution(2527301188072333977)
XLA Ops:
  1.3 4.0 %sum_factors.1 = bf16[4,256,1024]{2,1,0:T(8,128)(2,1)} custom-call(s32[36]{0:T(128)} %bitcast.27, s32[36]{0:T(128)} %bitcast.28, s32[1]{0:T(128)} %bitcast.21.count, bf16[36,64,1024]{2,1,0:T(8,128)(2,1)} %bitcast.22), custom_call_target="tpu_custom_call" | custom-call | flops 10000000 | bytes 7000000 | tf_op jit(solution)/shard_map/sum_factors/pallas_call | solution.py:300
  5.2 0.0 copy-start.7
  5.3 4.5 %all-to-all-start = ((bf16[4,256,1024]{2,1,0:T(8,128)(2,1)}), bf16[4,256,1024]{2,1,0:T(8,128)(2,1)S(1)}, u32[]{:S(2)}, u32[]{:S(2)}) async-start(bf16[4,256,1024]{2,1,0:T(8,128)(2,1)} %sum_factors.1), calls=%async_computation | async-start | bytes 4194304 | tf_op jit(solution)/shard_map/all_to_all | solution.py:318
  9.7 0.0 collective-permute-start
  9.7 1.2 %collective-permute-done = bf16[128,128]{1,0:T(8,128)(2,1)S(1)} collective-permute-done((bf16[128,128]{1,0:T(8,128)(2,1)S(1)}, bf16[128,128]{1,0:T(8,128)(2,1)S(1)}, u32[]{:S(2)}, u32[]{:S(2)}) %collective-permute-start) | collective-permute-done | bytes 32800 | tf_op jit(solution)/shard_map/ppermute | solution.py:298
  11.0 0.0 copy-start.3
  11.0 0.9 collective-permute-start.3
  11.9 2.2 %collective-permute-start.2 = (bf16[2,128,128]{2,1,0:T(8,128)(2,1)S(1)}, bf16[2,128,128]{2,1,0:T(8,128)(2,1)S(1)}, u32[]{:S(2)}, u32[]{:S(2)}) collective-permute-start(bf16[2,128,128]{2,1,0:T(8,128)(2,1)S(1)} %pad_maximum_fusion.refs_0_), channel_id=1, source_target_pairs={{0,4},{2,6},{4,0},{6,2},{1,5},{3,7},{5,1},{7,3},{8,12},{10,14},{12... | collective-permute-start | bytes 196616 | tf_op jit(solution)/shard_map/ppermute | solution.py:298
  14.1 1.0 collective-permute-start.1
  15.1 0.6 stack.57.columns
  15.7 2.2 %collective-permute-done.3.refs_3_ = bf16[2,128,128]{2,1,0:T(8,128)(2,1)S(1)} collective-permute-done((bf16[2,128,128]{2,1,0:T(8,128)(2,1)S(1)}, bf16[2,128,128]{2,1,0:T(8,128)(2,1)S(1)}, u32[]{:S(2)}, u32[]{:S(2)}) %collective-permute-start.3) | collective-permute-done | bytes 65568 | tf_op jit(solution)/shard_map/ppermute | solution.py:298
  17.9 0.0 collective-permute-done.2.refs_2_
  17.9 0.5 collective-permute-done.1.refs_1_
  18.4 0.1 copy-done.4
  18.6 0.0 copy-done.5
  18.6 0.5 copy-done.6
  19.0 3.2 %project.1 = (bf16[160,1024]{1,0:T(8,128)(2,1)}, bf16[128,128]{1,0:T(8,128)(2,1)}, bf16[128,128]{1,0:T(8,128)(2,1)}, bf16[128,128]{1,0:T(8,128)(2,1)}, bf16[128,128]{1,0:T(8,128)(2,1)}) custom-call(s32[9]{0:T(128)} %stack.57.columns, bf16[2,128,128]{2,1,0:T(8,128)(2,1)} %copy-done.3, bf16[2,128,128]{2,1,0:T(8,128)(2,1)} %copy-done.6, ...), custom_call_target="tpu_custom_call" | custom-call | tf_op jit(solution)/shard_map/project/pallas_call | solution.py:326
  22.3 2.0 %collective-permute-start.4 = (bf16[128,128]{1,0:T(8,128)(2,1)}, bf16[128,128]{1,0:T(8,128)(2,1)S(1)}, u32[]{:S(2)}, u32[]{:S(2)}) collective-permute-start(bf16[128,128]{1,0:T(8,128)(2,1)} %get-tuple-element.24), channel_id=1, source_target_pairs={{0,64},{64,128},{128,192},{192,0},{1,65},{65,129},{129,193},{193,1... | collective-permute-start | bytes 98312 | tf_op jit(solution)/shard_map/ppermute | solution.py:298
  24.3 2.7 %collective-permute-start.5 = (bf16[128,128]{1,0:T(8,128)(2,1)}, bf16[128,128]{1,0:T(8,128)(2,1)S(1)}, u32[]{:S(2)}, u32[]{:S(2)}) collective-permute-start(bf16[128,128]{1,0:T(8,128)(2,1)} %get-tuple-element.25), channel_id=1, source_target_pairs={{0,128},{64,192},{128,0},{192,64},{1,129},{65,193},{129,1},{193,65... | collective-permute-start | bytes 98312 | tf_op jit(solution)/shard_map/ppermute | solution.py:298
  26.9 1.5 %collective-permute-start.6 = (bf16[128,128]{1,0:T(8,128)(2,1)}, bf16[128,128]{1,0:T(8,128)(2,1)S(1)}, u32[]{:S(2)}, u32[]{:S(2)}) collective-permute-start(bf16[128,128]{1,0:T(8,128)(2,1)} %get-tuple-element.26), channel_id=1, source_target_pairs={{0,192},{64,0},{128,64},{192,128},{1,193},{65,1},{129,65},{193,129... | collective-permute-start | bytes 98312 | tf_op jit(solution)/shard_map/ppermute | solution.py:298
  28.4 0.1 pad_add_fusion.place
  28.5 7.0 %collective-permute-done.4.refs_1_ = bf16[128,128]{1,0:T(8,128)(2,1)S(1)} collective-permute-done((bf16[128,128]{1,0:T(8,128)(2,1)}, bf16[128,128]{1,0:T(8,128)(2,1)S(1)}, u32[]{:S(2)}, u32[]{:S(2)}) %collective-permute-start.4) | collective-permute-done | bytes 32800 | tf_op jit(solution)/shard_map/ppermute | solution.py:298
  35.5 2.1 %collective-permute-done.5.refs_2_ = bf16[128,128]{1,0:T(8,128)(2,1)S(1)} collective-permute-done((bf16[128,128]{1,0:T(8,128)(2,1)}, bf16[128,128]{1,0:T(8,128)(2,1)S(1)}, u32[]{:S(2)}, u32[]{:S(2)}) %collective-permute-start.5) | collective-permute-done | bytes 32800 | tf_op jit(solution)/shard_map/ppermute | solution.py:298
  37.5 0.0 collective-permute-done.6.refs_3_
  37.5 0.0 all-to-all-done.held.held_far
  37.5 0.7 copy-done.2
  38.3 1.7 %first_pass.1 = bf16[8,128,128]{2,1,0:T(8,128)(2,1)} custom-call(s32[2]{0:T(128)S(1)} %pad_add_fusion.place, bf16[4,256,1024]{2,1,0:T(8,128)(2,1)S(1)} %all-to-all-done.held.held_far, bf16[128,128]{1,0:T(8,128)(2,1)S(1)} %copy-done.2, bf16[128,128]{1,0:T(8,128)(2,1)S(1)} %collective-permute-done.4.refs_1_, ...), custom_call_target="tpu_custom_call" | custom-call | tf_op jit(solution)/shard_map/first_pass/pallas_call | solution.py:339
  40.0 8.5 %all-to-all-start.1 = ((bf16[8,128,128]{2,1,0:T(8,128)(2,1)}), bf16[8,128,128]{2,1,0:T(8,128)(2,1)S(1)}, u32[]{:S(2)}, u32[]{:S(2)}) async-start(bf16[8,128,128]{2,1,0:T(8,128)(2,1)} %first_pass.1), calls=%async_computation.1 | async-start | bytes 524288 | tf_op jit(solution)/shard_map/all_to_all | solution.py:349
  48.5 1.2 %collective-permute-start.8 = (bf16[160,1024]{1,0:T(8,128)(2,1)S(1)}, bf16[160,1024]{1,0:T(8,128)(2,1)S(1)}, u32[]{:S(2)}, u32[]{:S(2)}) collective-permute-start(bf16[160,1024]{1,0:T(8,128)(2,1)S(1)} %copy-done.1), channel_id=1, source_target_pairs={{0,192},{64,0},{128,64},{192,128},{1,193},{65,1},{129,65},{193,129... | collective-permute-start | bytes 983048 | tf_op jit(solution)/shard_map/ppermute | solution.py:298
  49.7 0.9 collective-permute-start.7
  50.6 6.1 %collective-permute-done.8.refs_4_ = bf16[160,1024]{1,0:T(8,128)(2,1)S(1)} collective-permute-done((bf16[160,1024]{1,0:T(8,128)(2,1)S(1)}, bf16[160,1024]{1,0:T(8,128)(2,1)S(1)}, u32[]{:S(2)}, u32[]{:S(2)}) %collective-permute-start.8) | collective-permute-done | bytes 327712 | tf_op jit(solution)/shard_map/ppermute | solution.py:298
  56.7 3.3 %collective-permute-done.7.refs_1_ = bf16[160,1024]{1,0:T(8,128)(2,1)S(1)} collective-permute-done((bf16[160,1024]{1,0:T(8,128)(2,1)S(1)}, bf16[160,1024]{1,0:T(8,128)(2,1)S(1)}, u32[]{:S(2)}, u32[]{:S(2)}) %collective-permute-start.7) | collective-permute-done | bytes 327712 | tf_op jit(solution)/shard_map/ppermute | solution.py:298
  59.9 0.8 add_up.1
  60.7 6.8 %all-to-all-start.2 = ((bf16[8,128,128]{2,1,0:T(8,128)(2,1)}), bf16[8,128,128]{2,1,0:T(8,128)(2,1)S(1)}, u32[]{:S(2)}, u32[]{:S(2)}) async-start(bf16[8,128,128]{2,1,0:T(8,128)(2,1)} %add_up.1), calls=%async_computation.2 | async-start | bytes 524288 | tf_op jit(solution)/shard_map/all_to_all | solution.py:362
  67.6 0.4 collective-permute-start.10
  68.0 1.7 %collective-permute-start.9 = (bf16[80,1024]{1,0:T(8,128)(2,1)S(1)}, bf16[80,1024]{1,0:T(8,128)(2,1)S(1)}, u32[]{:S(2)}, u32[]{:S(2)}) collective-permute-start(bf16[80,1024]{1,0:T(8,128)(2,1)S(1)} %slice.6), channel_id=1, source_target_pairs={{0,64},{64,128},{128,192},{192,0},{1,65},{65,129},{129,193},{193,1... | collective-permute-start | bytes 491528 | tf_op jit(solution)/shard_map/ppermute | solution.py:298
  69.7 3.3 %collective-permute-done.10.refs_3_ = bf16[80,1024]{1,0:T(8,128)(2,1)S(1)} collective-permute-done((bf16[80,1024]{1,0:T(8,128)(2,1)S(1)}, bf16[80,1024]{1,0:T(8,128)(2,1)S(1)}, u32[]{:S(2)}, u32[]{:S(2)}) %collective-permute-start.10) | collective-permute-done | bytes 163872 | tf_op jit(solution)/shard_map/ppermute | solution.py:298
  73.0 1.5 %collective-permute-done.9.refs_2_ = bf16[80,1024]{1,0:T(8,128)(2,1)S(1)} collective-permute-done((bf16[80,1024]{1,0:T(8,128)(2,1)S(1)}, bf16[80,1024]{1,0:T(8,128)(2,1)S(1)}, u32[]{:S(2)}, u32[]{:S(2)}) %collective-permute-start.9) | collective-permute-done | bytes 163872 | tf_op jit(solution)/shard_map/ppermute | solution.py:298
  74.5 3.5 %all-to-all-done.2.sketches = bf16[8,128,128]{2,1,0:T(8,128)(2,1)S(1)} async-done(((bf16[8,128,128]{2,1,0:T(8,128)(2,1)}), bf16[8,128,128]{2,1,0:T(8,128)(2,1)S(1)}, u32[]{:S(2)}, u32[]{:S(2)}) %all-to-all-start.2) | async-done | bytes 262176 | tf_op jit(solution)/shard_map/all_to_all | solution.py:362
  78.0 8.9 %second_pass.1 = (bf16[1024,128]{1,0:T(8,128)(2,1)}, f32[32,128]{1,0:T(8,128)S(1)}, f32[32,128]{1,0:T(8,128)S(1)}, f32[32,128]{1,0:T(8,128)S(1)}, f32[32,128]{1,0:T(8,128)S(1)}) custom-call(s32[2]{0:T(128)S(1)} %pad_add_fusion.place, bf16[8,128,128]{2,1,0:T(8,128)(2,1)S(1)} %all-to-all-done.2.sketches, bf16[4,256,1024]{2,1,0:T(8,128)(2,1)} %copy-done, ...), custom_call_target="tpu_custom_call" | custom-call | tf_op jit(solution)/shard_map/second_pass/pallas_call | solution.py:365
  87.0 4.1 %all-to-all-start.3 = ((bf16[32,32,128]{2,1,0:T(8,128)(2,1)}), bf16[32,32,128]{2,1,0:T(8,128)(2,1)S(1)}, u32[]{:S(2)}, u32[]{:S(2)}) async-start(bf16[32,32,128]{2,1,0:T(8,128)(2,1)} %bitcast.18), calls=%async_computation.3 | async-start | bytes 524288 | tf_op jit(solution)/shard_map/all_to_all | solution.py:383
  91.1 1.9 %collective-permute-start.11 = (f32[32,128]{1,0:T(8,128)S(1)}, f32[32,128]{1,0:T(8,128)S(1)}, u32[]{:S(2)}, u32[]{:S(2)}) collective-permute-start(f32[32,128]{1,0:T(8,128)S(1)} %get-tuple-element.35), channel_id=1, source_target_pairs={{0,64},{64,128},{128,192},{192,0},{1,65},{65,129},{129,193},{193,1... | collective-permute-start | bytes 49160 | tf_op jit(solution)/shard_map/ppermute | solution.py:298
  92.9 2.7 %collective-permute-start.12 = (f32[32,128]{1,0:T(8,128)S(1)}, f32[32,128]{1,0:T(8,128)S(1)}, u32[]{:S(2)}, u32[]{:S(2)}) collective-permute-start(f32[32,128]{1,0:T(8,128)S(1)} %get-tuple-element.36), channel_id=1, source_target_pairs={{0,128},{64,192},{128,0},{192,64},{1,129},{65,193},{129,1},{193,65... | collective-permute-start | bytes 49160 | tf_op jit(solution)/shard_map/ppermute | solution.py:298
  95.7 1.4 %collective-permute-start.13 = (f32[32,128]{1,0:T(8,128)S(1)}, f32[32,128]{1,0:T(8,128)S(1)}, u32[]{:S(2)}, u32[]{:S(2)}) collective-permute-start(f32[32,128]{1,0:T(8,128)S(1)} %get-tuple-element.37), channel_id=1, source_target_pairs={{0,192},{64,0},{128,64},{192,128},{1,193},{65,1},{129,65},{193,129... | collective-permute-start | bytes 49160 | tf_op jit(solution)/shard_map/ppermute | solution.py:298
  97.1 1.4 %collective-permute-done.12.refs_2_ = f32[32,128]{1,0:T(8,128)S(1)} collective-permute-done((f32[32,128]{1,0:T(8,128)S(1)}, f32[32,128]{1,0:T(8,128)S(1)}, u32[]{:S(2)}, u32[]{:S(2)}) %collective-permute-start.12) | collective-permute-done | bytes 16416 | tf_op jit(solution)/shard_map/ppermute | solution.py:298
  98.4 1.0 collective-permute-done.13.refs_3_
  99.4 2.6 %all-to-all-done.3.parts = bf16[32,32,128]{2,1,0:T(8,128)(2,1)S(1)} async-done(((bf16[32,32,128]{2,1,0:T(8,128)(2,1)}), bf16[32,32,128]{2,1,0:T(8,128)(2,1)S(1)}, u32[]{:S(2)}, u32[]{:S(2)}) %all-to-all-start.3) | async-done | bytes 262176 | tf_op jit(solution)/shard_map/all_to_all | solution.py:383
  102.0 1.3 %finish.1 = (f32[8,32,64]{2,1,0:T(8,128)}, f32[8,32,64]{2,1,0:T(8,128)}) custom-call(s32[2]{0:T(128)S(1)} %pad_add_fusion.place, bf16[32,32,128]{2,1,0:T(8,128)(2,1)S(1)} %all-to-all-done.3.parts, f32[32,128]{1,0:T(8,128)S(1)} %get-tuple-element.34.refs_0_, f32[32,128]{1,0:T(8,128)S(1)} %collective-permute-done.11.refs_1_, ...), custom_call_target="tpu_custom_call" | custom-call | tf_op jit(solution)/shard_map/finish/pallas_call | solution.py:385
  (15 shorter events, 0.1 us)
Async XLA Ops:
  5.2 4.5 %copy-start.7 = (bf16[2,64,128]{2,1,0:T(8,128)(2,1)S(1)}, bf16[2,64,128]{2,1,0:T(8,128)(2,1)}, u32[]{:S(2)}) copy-start(bf16[2,64,128]{2,1,0:T(8,128)(2,1)} %param.11) | copy-start | bytes 98308
  5.3 32.3 %all-to-all-start = ((bf16[4,256,1024]{2,1,0:T(8,128)(2,1)}), bf16[4,256,1024]{2,1,0:T(8,128)(2,1)S(1)}, u32[]{:S(2)}, u32[]{:S(2)}) async-start(bf16[4,256,1024]{2,1,0:T(8,128)(2,1)} %sum_factors.1), calls=%async_computation | async-start | bytes 4194304 | tf_op jit(solution)/shard_map/all_to_all | solution.py:318
  9.7 1.2 %collective-permute-start = (bf16[128,128]{1,0:T(8,128)(2,1)S(1)}, bf16[128,128]{1,0:T(8,128)(2,1)S(1)}, u32[]{:S(2)}, u32[]{:S(2)}) collective-permute-start(bf16[128,128]{1,0:T(8,128)(2,1)S(1)} %bitcast.24), channel_id=1, source_target_pairs={{0,1},{1,0},{2,3},{3,2},{4,5},{5,4},{6,7},{7,6},{8,9},{9,8},{10,11... | collective-permute-start | bytes 98312 | tf_op jit(solution)/shard_map/ppermute | solution.py:298
  11.0 7.5 %copy-start.3 = (bf16[2,128,128]{2,1,0:T(8,128)(2,1)}, bf16[2,128,128]{2,1,0:T(8,128)(2,1)S(1)}, u32[]{:S(2)}) copy-start(bf16[2,128,128]{2,1,0:T(8,128)(2,1)S(1)} %pad_maximum_fusion.refs_0_) | copy-start | bytes 196612
  11.0 7.0 %collective-permute-start.3 = (bf16[2,128,128]{2,1,0:T(8,128)(2,1)S(1)}, bf16[2,128,128]{2,1,0:T(8,128)(2,1)S(1)}, u32[]{:S(2)}, u32[]{:S(2)}) collective-permute-start(bf16[2,128,128]{2,1,0:T(8,128)(2,1)S(1)} %pad_maximum_fusion.refs_0_), channel_id=1, source_target_pairs={{0,6},{2,0},{4,2},{6,4},{1,7},{3,1},{5,3},{7,5},{8,14},{10,8},{12,... | collective-permute-start | bytes 196616 | tf_op jit(solution)/shard_map/ppermute | solution.py:298
  11.9 6.1 %collective-permute-start.2 = (bf16[2,128,128]{2,1,0:T(8,128)(2,1)S(1)}, bf16[2,128,128]{2,1,0:T(8,128)(2,1)S(1)}, u32[]{:S(2)}, u32[]{:S(2)}) collective-permute-start(bf16[2,128,128]{2,1,0:T(8,128)(2,1)S(1)} %pad_maximum_fusion.refs_0_), channel_id=1, source_target_pairs={{0,4},{2,6},{4,0},{6,2},{1,5},{3,7},{5,1},{7,3},{8,12},{10,14},{12... | collective-permute-start | bytes 196616 | tf_op jit(solution)/shard_map/ppermute | solution.py:298
  14.1 4.3 %collective-permute-start.1 = (bf16[2,128,128]{2,1,0:T(8,128)(2,1)S(1)}, bf16[2,128,128]{2,1,0:T(8,128)(2,1)S(1)}, u32[]{:S(2)}, u32[]{:S(2)}) collective-permute-start(bf16[2,128,128]{2,1,0:T(8,128)(2,1)S(1)} %pad_maximum_fusion.refs_0_), channel_id=1, source_target_pairs={{0,2},{2,4},{4,6},{6,0},{1,3},{3,5},{5,7},{7,1},{8,10},{10,12},{12... | collective-permute-start | bytes 196616 | tf_op jit(solution)/shard_map/ppermute | solution.py:298
  17.9 0.6 copy-start.4
  17.9 0.6 copy-start.5
  18.4 0.6 copy-start.6
  22.3 26.2 %copy-start.1 = (bf16[160,1024]{1,0:T(8,128)(2,1)S(1)}, bf16[160,1024]{1,0:T(8,128)(2,1)}, u32[]{:S(2)}) copy-start(bf16[160,1024]{1,0:T(8,128)(2,1)} %get-tuple-element.30.refs_0_) | copy-start | bytes 983044
  22.3 13.2 %collective-permute-start.4 = (bf16[128,128]{1,0:T(8,128)(2,1)}, bf16[128,128]{1,0:T(8,128)(2,1)S(1)}, u32[]{:S(2)}, u32[]{:S(2)}) collective-permute-start(bf16[128,128]{1,0:T(8,128)(2,1)} %get-tuple-element.24), channel_id=1, source_target_pairs={{0,64},{64,128},{128,192},{192,0},{1,65},{65,129},{129,193},{193,1... | collective-permute-start | bytes 98312 | tf_op jit(solution)/shard_map/ppermute | solution.py:298
  24.3 13.2 %collective-permute-start.5 = (bf16[128,128]{1,0:T(8,128)(2,1)}, bf16[128,128]{1,0:T(8,128)(2,1)S(1)}, u32[]{:S(2)}, u32[]{:S(2)}) collective-permute-start(bf16[128,128]{1,0:T(8,128)(2,1)} %get-tuple-element.25), channel_id=1, source_target_pairs={{0,128},{64,192},{128,0},{192,64},{1,129},{65,193},{129,1},{193,65... | collective-permute-start | bytes 98312 | tf_op jit(solution)/shard_map/ppermute | solution.py:298
  26.9 10.6 %collective-permute-start.6 = (bf16[128,128]{1,0:T(8,128)(2,1)}, bf16[128,128]{1,0:T(8,128)(2,1)S(1)}, u32[]{:S(2)}, u32[]{:S(2)}) collective-permute-start(bf16[128,128]{1,0:T(8,128)(2,1)} %get-tuple-element.26), channel_id=1, source_target_pairs={{0,192},{64,0},{128,64},{192,128},{1,193},{65,1},{129,65},{193,129... | collective-permute-start | bytes 98312 | tf_op jit(solution)/shard_map/ppermute | solution.py:298
  37.5 30.0 %copy-start = (bf16[4,256,1024]{2,1,0:T(8,128)(2,1)}, bf16[4,256,1024]{2,1,0:T(8,128)(2,1)S(1)}, u32[]{:S(2)}) copy-start(bf16[4,256,1024]{2,1,0:T(8,128)(2,1)S(1)} %all-to-all-done.held.held_far) | copy-start | bytes 6291460
  37.5 0.8 copy-start.2
  40.0 19.9 %all-to-all-start.1 = ((bf16[8,128,128]{2,1,0:T(8,128)(2,1)}), bf16[8,128,128]{2,1,0:T(8,128)(2,1)S(1)}, u32[]{:S(2)}, u32[]{:S(2)}) async-start(bf16[8,128,128]{2,1,0:T(8,128)(2,1)} %first_pass.1), calls=%async_computation.1 | async-start | bytes 524288 | tf_op jit(solution)/shard_map/all_to_all | solution.py:349
  48.5 8.2 %collective-permute-start.8 = (bf16[160,1024]{1,0:T(8,128)(2,1)S(1)}, bf16[160,1024]{1,0:T(8,128)(2,1)S(1)}, u32[]{:S(2)}, u32[]{:S(2)}) collective-permute-start(bf16[160,1024]{1,0:T(8,128)(2,1)S(1)} %copy-done.1), channel_id=1, source_target_pairs={{0,192},{64,0},{128,64},{192,128},{1,193},{65,1},{129,65},{193,129... | collective-permute-start | bytes 983048 | tf_op jit(solution)/shard_map/ppermute | solution.py:298
  49.7 10.3 %collective-permute-start.7 = (bf16[160,1024]{1,0:T(8,128)(2,1)S(1)}, bf16[160,1024]{1,0:T(8,128)(2,1)S(1)}, u32[]{:S(2)}, u32[]{:S(2)}) collective-permute-start(bf16[160,1024]{1,0:T(8,128)(2,1)S(1)} %copy-done.1), channel_id=1, source_target_pairs={{0,64},{64,128},{128,192},{192,0},{1,65},{65,129},{129,193},{193,1... | collective-permute-start | bytes 983048 | tf_op jit(solution)/shard_map/ppermute | solution.py:298
  60.7 17.3 %all-to-all-start.2 = ((bf16[8,128,128]{2,1,0:T(8,128)(2,1)}), bf16[8,128,128]{2,1,0:T(8,128)(2,1)S(1)}, u32[]{:S(2)}, u32[]{:S(2)}) async-start(bf16[8,128,128]{2,1,0:T(8,128)(2,1)} %add_up.1), calls=%async_computation.2 | async-start | bytes 524288 | tf_op jit(solution)/shard_map/all_to_all | solution.py:362
  67.6 5.4 %collective-permute-start.10 = (bf16[80,1024]{1,0:T(8,128)(2,1)S(1)}, bf16[80,1024]{1,0:T(8,128)(2,1)S(1)}, u32[]{:S(2)}, u32[]{:S(2)}) collective-permute-start(bf16[80,1024]{1,0:T(8,128)(2,1)S(1)} %slice.7), channel_id=1, source_target_pairs={{0,192},{64,0},{128,64},{192,128},{1,193},{65,1},{129,65},{193,129... | collective-permute-start | bytes 491528 | tf_op jit(solution)/shard_map/ppermute | solution.py:298
  68.0 6.5 %collective-permute-start.9 = (bf16[80,1024]{1,0:T(8,128)(2,1)S(1)}, bf16[80,1024]{1,0:T(8,128)(2,1)S(1)}, u32[]{:S(2)}, u32[]{:S(2)}) collective-permute-start(bf16[80,1024]{1,0:T(8,128)(2,1)S(1)} %slice.6), channel_id=1, source_target_pairs={{0,64},{64,128},{128,192},{192,0},{1,65},{65,129},{129,193},{193,1... | collective-permute-start | bytes 491528 | tf_op jit(solution)/shard_map/ppermute | solution.py:298
  87.0 15.0 %all-to-all-start.3 = ((bf16[32,32,128]{2,1,0:T(8,128)(2,1)}), bf16[32,32,128]{2,1,0:T(8,128)(2,1)S(1)}, u32[]{:S(2)}, u32[]{:S(2)}) async-start(bf16[32,32,128]{2,1,0:T(8,128)(2,1)} %bitcast.18), calls=%async_computation.3 | async-start | bytes 524288 | tf_op jit(solution)/shard_map/all_to_all | solution.py:383
  91.1 6.0 %collective-permute-start.11 = (f32[32,128]{1,0:T(8,128)S(1)}, f32[32,128]{1,0:T(8,128)S(1)}, u32[]{:S(2)}, u32[]{:S(2)}) collective-permute-start(f32[32,128]{1,0:T(8,128)S(1)} %get-tuple-element.35), channel_id=1, source_target_pairs={{0,64},{64,128},{128,192},{192,0},{1,65},{65,129},{129,193},{193,1... | collective-permute-start | bytes 49160 | tf_op jit(solution)/shard_map/ppermute | solution.py:298
  92.9 5.5 %collective-permute-start.12 = (f32[32,128]{1,0:T(8,128)S(1)}, f32[32,128]{1,0:T(8,128)S(1)}, u32[]{:S(2)}, u32[]{:S(2)}) collective-permute-start(f32[32,128]{1,0:T(8,128)S(1)} %get-tuple-element.36), channel_id=1, source_target_pairs={{0,128},{64,192},{128,0},{192,64},{1,129},{65,193},{129,1},{193,65... | collective-permute-start | bytes 49160 | tf_op jit(solution)/shard_map/ppermute | solution.py:298
  95.7 3.8 %collective-permute-start.13 = (f32[32,128]{1,0:T(8,128)S(1)}, f32[32,128]{1,0:T(8,128)S(1)}, u32[]{:S(2)}, u32[]{:S(2)}) collective-permute-start(f32[32,128]{1,0:T(8,128)S(1)} %get-tuple-element.37), channel_id=1, source_target_pairs={{0,192},{64,0},{128,64},{192,128},{1,193},{65,1},{129,65},{193,129... | collective-permute-start | bytes 49160 | tf_op jit(solution)/shard_map/ppermute | solution.py:298

commit v5 on v4

--- a/solution.py
+++ b/solution.py
@@ -18,7 +18,7 @@
 VMEM = pltpu.VMEM
 LANES = 128
 TAIL = 16
-BLOCK = 4
+BLOCK = 8
 
 
 def params(mib):
@@ -44,11 +44,11 @@
     )
 
 
-def sum_factors(panel, target, count, factors, out, loaded, acc, panel_at, target_at, count_at, sems, small):
+def sum_factors(panel, target, count, factors, out, loaded, acc, kept, panel_at, target_at, count_at, sems, small):
     slots, rank, _ = loaded.shape
     pairs = acc.shape[0]
     panels = pairs // 8
-    chunk = slots // sems.shape[0]
+    chunk = slots // 6
     indices = [
         pltpu.make_async_copy(source, to, small.at[i])
         for i, (source, to) in enumerate(((panel, panel_at), (target, target_at), (count, count_at)))
@@ -81,9 +81,13 @@
         lax.fori_loop(i * chunk, jnp.minimum(live, (i + 1) * chunk), add, 0)
     groups = out.shape[0]
     each = pairs // groups
-    for i in range(pairs):
-        row = (i % each) * rank
-        out[i // each, row : row + rank, :] = acc[i].astype(BF)
+    stores = [pltpu.make_async_copy(kept.at[g], out.at[g], sems.at[6 + g]) for g in range(groups)]
+    for g, copy in enumerate(stores):
+        for i in range(each):
+            kept[g, i * rank : (i + 1) * rank, :] = acc[g * each + i].astype(BF)
+        copy.start()
+    for copy in stores:
+        copy.wait()
 
 
 def project(columns, *refs):
@@ -176,53 +180,43 @@
 
 def second_pass(place, sketches, held_far, *refs):
     groups = held_far.shape[0]
-    shared_far, out, left, refs = refs[:5], refs[5], refs[6 : 6 + groups], refs[6 + groups :]
-    basis, rounded, turned, held, shared, sems = refs
+    shared_far, (out, held, shared, sems) = refs[:5], refs[5:]
     half = shared.shape[1] // 2
-    targets_of = (
+    sources = [lax.rem(place[0] + groups - s, groups) for s in range(groups)]
+    loads = [pltpu.make_async_copy(held_far.at[source], held.at[s], sems.at[s]) for s, source in enumerate(sources)]
+    ends = (
         shared.at[0],
         shared.at[1],
         shared.at[2, 0:half, :],
         shared.at[2, half : 2 * half, :],
         shared.at[3],
     )
-    loads = [pltpu.make_async_copy(held_far, held, sems.at[5])]
-    loads += [
-        pltpu.make_async_copy(source, to, sems.at[i])
-        for i, (source, to) in enumerate(zip(shared_far, targets_of, strict=True))
-    ]
-    for copy in loads:
-        copy.start()
+    panels = [
+        pltpu.make_async_copy(source, to, sems.at[groups + i])
+        for i, (source, to) in enumerate(zip(shared_far, ends, strict=True))
+    ]
+    arrivals = ((0,), (1,), (2, 3), (4,))
+    for s in range(groups):
+        loads[s].start()
+        for i in arrivals[s]:
+            panels[i].start()
     cuts, rows, _ = sketches.shape
-    width = basis.shape[1]
+    width = held.shape[2]
     targets = held.shape[1] // LANES
     rank = rows // targets
-    own = left[0].shape[0]
     whole = [
         jnp.concatenate([sketches[z, t * rank : (t + 1) * rank, :] for z in range(cuts)], axis=1)
         for t in range(targets)
     ]
-    grams = [lax.dot_general(s, s, NT, preferred_element_type=F32) for s in whole]
-    inverses = inverse_factors(grams)
-    for t in range(targets):
-        found = jnp.dot(
-            jnp.concatenate(split_bf(inverses[t], 3), axis=0), whole[t], preferred_element_type=F32
-        )
-        found = (found[0:rank] + found[rank : 2 * rank]) + found[2 * rank : 3 * rank]
-        basis[t * rank : (t + 1) * rank, :] = found
-        rounded[t * rank : (t + 1) * rank, :] = found.astype(BF)
-    for copy in loads:
-        copy.wait()
     total = jnp.zeros((rows, width), F32)
     for s in range(groups):
-        source = lax.rem(place[0] + groups - s, groups)
+        loads[s].wait()
+        for i in arrivals[s]:
+            panels[i].wait()
         summed = jnp.concatenate(
             [
                 lax.dot_general(
-                    held[source, t * LANES : (t + 1) * LANES, :],
-                    rounded[t * rank : (t + 1) * rank, :],
-                    NT,
-                    preferred_element_type=F32,
+                    held[s, t * LANES : (t + 1) * LANES, :], whole[t], NT, preferred_element_type=F32
                 )
                 for t in range(targets)
             ],
@@ -248,33 +242,53 @@
             total = total + jnp.dot(part, shared[s, 0:LANES, :], preferred_element_type=F32)
     for c in range(width // LANES):
         out[c * LANES : (c + 1) * LANES, :] = total[:, c * LANES : (c + 1) * LANES].T.astype(out.dtype)
-    for s in range(groups):
-        owner = lax.rem(place[0] + s, groups)
-        start = owner * (width // groups) + place[1] * own
-        aligned = (start // LANES) * LANES
-        turned[...] = basis[:, pl.ds(pl.multiple_of(aligned, LANES), LANES)].T
-        left[s][...] = turned[pl.ds(pl.multiple_of(start - aligned, 32), own), :]
+
+
+def factor(place, sketches, *refs):
+    sent, (turned,) = refs[:-1], refs[-1:]
+    cuts, rows, cut = sketches.shape
+    targets = 2
+    rank = rows // targets
+    whole = [
+        jnp.concatenate([sketches[z, t * rank : (t + 1) * rank, :] for z in range(cuts)], axis=1)
+        for t in range(targets)
+    ]
+    grams = [lax.dot_general(s, s, NT, preferred_element_type=F32) for s in whole]
+    inverses = jnp.concatenate(inverse_factors(grams), axis=1)
+    owners = len(sent)
+    own = sent[0].shape[0] - rank
+    for s in range(owners):
+        owner = lax.rem(place[0] + s, owners)
+        start = owner * (cuts * cut // owners) + place[1] * own
+        piece = start // cut
+        turned[...] = sketches[piece].astype(F32).T
+        sent[s][0:rank, :] = inverses
+        sent[s][rank : rank + own, :] = turned[pl.ds(pl.multiple_of(start - piece * cut, 32), own), :]
 
 
 def finish(place, parts, *refs):
-    left_parts, (left, right) = refs[:-2], refs[-2:]
-    owners = len(left_parts)
+    received, (left, right) = refs[:-2], refs[-2:]
+    owners = len(received)
     groups = parts.shape[0] // owners
     targets = left.shape[0] // owners
-    rank = left.shape[2]
+    own, rank = left.shape[1], left.shape[2]
     root = math.sqrt(1024)
-    for y in range(owners):
-        total = parts[y * groups].astype(F32)
-        for z in range(1, groups):
-            total = total + parts[y * groups + z].astype(F32)
-        total = total / root
-        for t in range(targets):
-            right[y * targets + t] = total[:, t * rank : (t + 1) * rank]
     for s in range(owners):
         owner = lax.rem(place[0] + owners - s, owners)
-        rows = left_parts[s][...] * root
+        total = parts[owner * groups].astype(F32)
+        for z in range(1, groups):
+            total = total + parts[owner * groups + z].astype(F32)
+        both = jnp.concatenate([received[s][rank : rank + own, :] * root, total / root], axis=0)
         for t in range(targets):
-            left[owner * targets + t] = rows[:, t * rank : (t + 1) * rank]
+            found = lax.dot_general(
+                both[:, t * rank : (t + 1) * rank],
+                received[s][0:rank, t * rank : (t + 1) * rank],
+                NT,
+                precision=HIGHEST,
+                preferred_element_type=F32,
+            )
+            left[owner * targets + t] = found[0:own]
+            right[owner * targets + t] = found[own : 2 * own]
 
 
 def shards(sizes, entry_factor, entry_panel, entry_target, entry_count, panel_shared, coupling, probes):
@@ -301,14 +315,15 @@
         sum_factors,
         out_shape=jax.ShapeDtypeStruct((ny, held_rows, width), BF),
         in_specs=[in_any] * 4,
-        out_specs=in_vmem,
+        out_specs=in_any,
         scratch_shapes=[
             VMEM((slots, rank, width), BF),
             VMEM((targets * panels, rank, width), F32),
+            VMEM((ny, held_rows, width), BF),
             SMEM((slots,), jnp.int32),
             SMEM((slots,), jnp.int32),
             SMEM((1,), jnp.int32),
-            pltpu.SemaphoreType.DMA((6,)),
+            pltpu.SemaphoreType.DMA((6 + ny,)),
             pltpu.SemaphoreType.DMA((3,)),
         ],
         compiler_params=params(56),
@@ -362,25 +377,32 @@
     sketches = lax.all_to_all(copies, "z", 0, 0, tiled=True)
 
     keep = width // (ny * nz)
-    rows_part, *left = pl.pallas_call(
+    rows_part = pl.pallas_call(
         second_pass,
-        out_shape=(jax.ShapeDtypeStruct((width, own_rows), BF),)
-        + (jax.ShapeDtypeStruct((keep, own_rows), F32),) * ny,
+        out_shape=jax.ShapeDtypeStruct((width, own_rows), BF),
         in_specs=[in_smem, in_vmem] + [in_any] * 6,
-        out_specs=(in_vmem,) * (ny + 1),
+        out_specs=in_vmem,
         scratch_shapes=[
-            VMEM((own_rows, width), F32),
-            VMEM((own_rows, width), BF),
-            VMEM((LANES, own_rows), F32),
             VMEM((ny, held_rows, width), BF),
             VMEM((ny, rows + 2 * TAIL, width), BF),
-            pltpu.SemaphoreType.DMA((6,)),
+            pltpu.SemaphoreType.DMA((ny + 5,)),
         ],
         compiler_params=params(52),
         name="second_pass",
     )(place, sketches, held, *all_shared)
-    left_parts = [left[0]] + [turn(left[s], "y", ny, s) for s in range(1, ny)]
     row_parts = lax.all_to_all(rows_part.reshape(ny * nz, keep, own_rows), ("y", "z"), 0, 0, tiled=True)
+    sketches, _ = lax.optimization_barrier((sketches, rows_part))
+    sent = pl.pallas_call(
+        factor,
+        out_shape=(jax.ShapeDtypeStruct((rank + keep, own_rows), F32),) * ny,
+        in_specs=[in_smem, in_vmem],
+        out_specs=(in_vmem,) * ny,
+        scratch_shapes=[VMEM((cut, own_rows), F32)],
+        compiler_params=params(8),
+        cost_estimate=pl.CostEstimate(flops=10**7, bytes_accessed=5 * 10**5, transcendentals=0),
+        name="factor",
+    )(place, sketches)
+    received = [sent[0]] + [turn(sent[s], "y", ny, s) for s in range(1, ny)]
     out = jax.ShapeDtypeStruct((targets, keep, rank), F32)
     left_out, right_out = pl.pallas_call(
         finish,
@@ -389,7 +411,7 @@
         out_specs=(in_vmem, in_vmem),
         compiler_params=params(8),
         name="finish",
-    )(place, row_parts, *left_parts)
+    )(place, row_parts, *received)
     return left_out.transpose(0, 2, 1), right_out.transpose(0, 2, 1)
 
 

time: 104 us -> 102 us (0.981)
  waiting for transfers between devices: 35.6 us -> 33.3 us
    all_to_all x1, waiting for transfers between devices: 2.61 us -> 0.01 us  [shards(): lax.all_to_all(rows_part.reshape(ny * nz, keep, own_rows), ('y', 'z'), 0,...]
    pallas_call x1 -> x2, Pallas kernels: 8.94 us -> 8.69 us  [the longest x1 5.65 us: shards(): pl.pallas_call(second_pass, out_shape=jax.ShapeDtypeStruct((width, own_ro...]
  transfers between devices with their start and end apart: 18 -> 18, of which waited for: 13 -> 12; matrix products, arithmetic and copies ran while one was open for 1% -> 1% of each run, Pallas kernels for 3% -> 6%
where the time goes in v5:
time: 102 us; the launch traced here: 101 us
  starting transfers between devices  44.4 us (44%)
  waiting for transfers between devices  33.3 us (33%)
  Pallas kernels  20 us (20%)
  local copies, waits for them, and re-layouts  2.03 us (2%)
  between operations  1.39 us (1%)
    ppermute x14, waiting for transfers between devices, turn(): lax.ppermute(value, axis, [(i, (i + by) % size) for i in range(size)])  29.8 us
    ppermute x14, starting transfers between devices, turn(): lax.ppermute(value, axis, [(i, (i + by) % size) for i in range(size)])  20.3 us
    all_to_all x1, starting transfers between devices, shards(): parts = lax.all_to_all(sketch, 'z', 0, 0, tiled=True)  8.54 us
    all_to_all x1, starting transfers between devices, shards(): sketches = lax.all_to_all(copies, 'z', 0, 0, tiled=True)  6.85 us
    pallas_call x1, Pallas kernels, shards(): pl.pallas_call(second_pass, out_shape=jax.ShapeDtypeStruct((width, own_ro...  5.65 us
    all_to_all x1, starting transfers between devices, shards(): held = lax.all_to_all(sums, 'y', 0, 0, tiled=True)  4.48 us
    all_to_all x1, starting transfers between devices, shards(): lax.all_to_all(rows_part.reshape(ny * nz, keep, own_rows), ('y', 'z'), 0,...  4.26 us
    pallas_call x1, Pallas kernels, shards(): pl.pallas_call(sum_factors, out_shape=jax.ShapeDtypeStruct((ny, held_rows...  3.85 us
  transfers between devices with their start and end apart: 18, of which 12 were waited for; matrix products, arithmetic and copies ran while one was open for 1% of the time, Pallas kernels for 6%

profile of v5, /device:TPU:6, one launch (start us, length us, event | category | flops | bytes accessed | tf_op | source)
XLA Modules:
  0.0 101.3 jit_solution(17842374476175415557)
XLA Ops:
  1.3 3.8 %sum_factors.1 = bf16[4,256,1024]{2,1,0:T(8,128)(2,1)} custom-call(s32[36]{0:T(128)} %bitcast.27, s32[36]{0:T(128)} %bitcast.28, s32[1]{0:T(128)} %bitcast.21.count, bf16[36,64,1024]{2,1,0:T(8,128)(2,1)} %bitcast.22), custom_call_target="tpu_custom_call" | custom-call | flops 10000000 | bytes 7000000 | tf_op jit(solution)/shard_map/sum_factors/pallas_call | solution.py:314
  5.1 0.0 copy-start.7
  5.1 4.5 %all-to-all-start = ((bf16[4,256,1024]{2,1,0:T(8,128)(2,1)}), bf16[4,256,1024]{2,1,0:T(8,128)(2,1)S(1)}, u32[]{:S(2)}, u32[]{:S(2)}) async-start(bf16[4,256,1024]{2,1,0:T(8,128)(2,1)} %sum_factors.1), calls=%async_computation | async-start | bytes 4194304 | tf_op jit(solution)/shard_map/all_to_all | solution.py:333
  9.6 0.0 collective-permute-start
  9.6 1.2 %collective-permute-done = bf16[128,128]{1,0:T(8,128)(2,1)S(1)} collective-permute-done((bf16[128,128]{1,0:T(8,128)(2,1)S(1)}, bf16[128,128]{1,0:T(8,128)(2,1)S(1)}, u32[]{:S(2)}, u32[]{:S(2)}) %collective-permute-start) | collective-permute-done | bytes 32800 | tf_op jit(solution)/shard_map/ppermute | solution.py:312
  10.8 0.0 copy-start.3
  10.9 0.9 collective-permute-start.3
  11.8 2.1 %collective-permute-start.2 = (bf16[2,128,128]{2,1,0:T(8,128)(2,1)S(1)}, bf16[2,128,128]{2,1,0:T(8,128)(2,1)S(1)}, u32[]{:S(2)}, u32[]{:S(2)}) collective-permute-start(bf16[2,128,128]{2,1,0:T(8,128)(2,1)S(1)} %pad_maximum_fusion.refs_0_), channel_id=1, source_target_pairs={{0,4},{2,6},{4,0},{6,2},{1,5},{3,7},{5,1},{7,3},{8,12},{10,14},{12... | collective-permute-start | bytes 196616 | tf_op jit(solution)/shard_map/ppermute | solution.py:312
  13.8 1.1 %collective-permute-start.1 = (bf16[2,128,128]{2,1,0:T(8,128)(2,1)S(1)}, bf16[2,128,128]{2,1,0:T(8,128)(2,1)S(1)}, u32[]{:S(2)}, u32[]{:S(2)}) collective-permute-start(bf16[2,128,128]{2,1,0:T(8,128)(2,1)S(1)} %pad_maximum_fusion.refs_0_), channel_id=1, source_target_pairs={{0,2},{2,4},{4,6},{6,0},{1,3},{3,5},{5,7},{7,1},{8,10},{10,12},{12... | collective-permute-start | bytes 196616 | tf_op jit(solution)/shard_map/ppermute | solution.py:312
  15.0 0.6 stack.57.columns
  15.6 2.2 %collective-permute-done.3.refs_3_ = bf16[2,128,128]{2,1,0:T(8,128)(2,1)S(1)} collective-permute-done((bf16[2,128,128]{2,1,0:T(8,128)(2,1)S(1)}, bf16[2,128,128]{2,1,0:T(8,128)(2,1)S(1)}, u32[]{:S(2)}, u32[]{:S(2)}) %collective-permute-start.3) | collective-permute-done | bytes 65568 | tf_op jit(solution)/shard_map/ppermute | solution.py:312
  17.8 0.0 collective-permute-done.2.refs_2_
  17.8 0.5 collective-permute-done.1.refs_1_
  18.3 0.2 copy-done.4
  18.4 0.0 copy-done.5
  18.5 0.4 copy-done.6
  18.9 3.2 %project.1 = (bf16[160,1024]{1,0:T(8,128)(2,1)}, bf16[128,128]{1,0:T(8,128)(2,1)}, bf16[128,128]{1,0:T(8,128)(2,1)}, bf16[128,128]{1,0:T(8,128)(2,1)}, bf16[128,128]{1,0:T(8,128)(2,1)}) custom-call(s32[9]{0:T(128)} %stack.57.columns, bf16[2,128,128]{2,1,0:T(8,128)(2,1)} %copy-done.3, bf16[2,128,128]{2,1,0:T(8,128)(2,1)} %copy-done.6, ...), custom_call_target="tpu_custom_call" | custom-call | tf_op jit(solution)/shard_map/project/pallas_call | solution.py:341
  22.1 2.0 %collective-permute-start.4 = (bf16[128,128]{1,0:T(8,128)(2,1)}, bf16[128,128]{1,0:T(8,128)(2,1)S(1)}, u32[]{:S(2)}, u32[]{:S(2)}) collective-permute-start(bf16[128,128]{1,0:T(8,128)(2,1)} %get-tuple-element.24), channel_id=1, source_target_pairs={{0,64},{64,128},{128,192},{192,0},{1,65},{65,129},{129,193},{193,1... | collective-permute-start | bytes 98312 | tf_op jit(solution)/shard_map/ppermute | solution.py:312
  24.1 2.7 %collective-permute-start.5 = (bf16[128,128]{1,0:T(8,128)(2,1)}, bf16[128,128]{1,0:T(8,128)(2,1)S(1)}, u32[]{:S(2)}, u32[]{:S(2)}) collective-permute-start(bf16[128,128]{1,0:T(8,128)(2,1)} %get-tuple-element.25), channel_id=1, source_target_pairs={{0,128},{64,192},{128,0},{192,64},{1,129},{65,193},{129,1},{193,65... | collective-permute-start | bytes 98312 | tf_op jit(solution)/shard_map/ppermute | solution.py:312
  26.8 1.5 %collective-permute-start.6 = (bf16[128,128]{1,0:T(8,128)(2,1)}, bf16[128,128]{1,0:T(8,128)(2,1)S(1)}, u32[]{:S(2)}, u32[]{:S(2)}) collective-permute-start(bf16[128,128]{1,0:T(8,128)(2,1)} %get-tuple-element.26), channel_id=1, source_target_pairs={{0,192},{64,0},{128,64},{192,128},{1,193},{65,1},{129,65},{193,129... | collective-permute-start | bytes 98312 | tf_op jit(solution)/shard_map/ppermute | solution.py:312
  28.3 0.1 pad_add_fusion.place
  28.4 7.0 %collective-permute-done.4.refs_1_ = bf16[128,128]{1,0:T(8,128)(2,1)S(1)} collective-permute-done((bf16[128,128]{1,0:T(8,128)(2,1)}, bf16[128,128]{1,0:T(8,128)(2,1)S(1)}, u32[]{:S(2)}, u32[]{:S(2)}) %collective-permute-start.4) | collective-permute-done | bytes 32800 | tf_op jit(solution)/shard_map/ppermute | solution.py:312
  35.3 2.1 %collective-permute-done.5.refs_2_ = bf16[128,128]{1,0:T(8,128)(2,1)S(1)} collective-permute-done((bf16[128,128]{1,0:T(8,128)(2,1)}, bf16[128,128]{1,0:T(8,128)(2,1)S(1)}, u32[]{:S(2)}, u32[]{:S(2)}) %collective-permute-start.5) | collective-permute-done | bytes 32800 | tf_op jit(solution)/shard_map/ppermute | solution.py:312
  37.4 0.0 collective-permute-done.6.refs_3_
  37.4 0.0 all-to-all-done.held.held_far
  37.4 0.7 copy-done.2
  38.2 1.7 %first_pass.1 = bf16[8,128,128]{2,1,0:T(8,128)(2,1)} custom-call(s32[2]{0:T(128)S(1)} %pad_add_fusion.place, bf16[4,256,1024]{2,1,0:T(8,128)(2,1)S(1)} %all-to-all-done.held.held_far, bf16[128,128]{1,0:T(8,128)(2,1)S(1)} %copy-done.2, bf16[128,128]{1,0:T(8,128)(2,1)S(1)} %collective-permute-done.4.refs_1_, ...), custom_call_target="tpu_custom_call" | custom-call | tf_op jit(solution)/shard_map/first_pass/pallas_call | solution.py:354
  39.9 8.5 %all-to-all-start.1 = ((bf16[8,128,128]{2,1,0:T(8,128)(2,1)}), bf16[8,128,128]{2,1,0:T(8,128)(2,1)S(1)}, u32[]{:S(2)}, u32[]{:S(2)}) async-start(bf16[8,128,128]{2,1,0:T(8,128)(2,1)} %first_pass.1), calls=%async_computation.1 | async-start | bytes 524288 | tf_op jit(solution)/shard_map/all_to_all | solution.py:364
  48.4 1.2 %collective-permute-start.8 = (bf16[160,1024]{1,0:T(8,128)(2,1)S(1)}, bf16[160,1024]{1,0:T(8,128)(2,1)S(1)}, u32[]{:S(2)}, u32[]{:S(2)}) collective-permute-start(bf16[160,1024]{1,0:T(8,128)(2,1)S(1)} %copy-done.1), channel_id=1, source_target_pairs={{0,192},{64,0},{128,64},{192,128},{1,193},{65,1},{129,65},{193,129... | collective-permute-start | bytes 983048 | tf_op jit(solution)/shard_map/ppermute | solution.py:312
  49.6 0.9 collective-permute-start.7
  50.5 6.1 %collective-permute-done.8.refs_4_ = bf16[160,1024]{1,0:T(8,128)(2,1)S(1)} collective-permute-done((bf16[160,1024]{1,0:T(8,128)(2,1)S(1)}, bf16[160,1024]{1,0:T(8,128)(2,1)S(1)}, u32[]{:S(2)}, u32[]{:S(2)}) %collective-permute-start.8) | collective-permute-done | bytes 327712 | tf_op jit(solution)/shard_map/ppermute | solution.py:312
  56.6 3.3 %collective-permute-done.7.refs_1_ = bf16[160,1024]{1,0:T(8,128)(2,1)S(1)} collective-permute-done((bf16[160,1024]{1,0:T(8,128)(2,1)S(1)}, bf16[160,1024]{1,0:T(8,128)(2,1)S(1)}, u32[]{:S(2)}, u32[]{:S(2)}) %collective-permute-start.7) | collective-permute-done | bytes 327712 | tf_op jit(solution)/shard_map/ppermute | solution.py:312
  59.9 0.8 add_up.1
  60.7 6.8 %all-to-all-start.2 = ((bf16[8,128,128]{2,1,0:T(8,128)(2,1)}), bf16[8,128,128]{2,1,0:T(8,128)(2,1)S(1)}, u32[]{:S(2)}, u32[]{:S(2)}) async-start(bf16[8,128,128]{2,1,0:T(8,128)(2,1)} %add_up.1), calls=%async_computation.2 | async-start | bytes 524288 | tf_op jit(solution)/shard_map/all_to_all | solution.py:377
  67.6 0.4 collective-permute-start.10
  67.9 1.7 %collective-permute-start.9 = (bf16[80,1024]{1,0:T(8,128)(2,1)S(1)}, bf16[80,1024]{1,0:T(8,128)(2,1)S(1)}, u32[]{:S(2)}, u32[]{:S(2)}) collective-permute-start(bf16[80,1024]{1,0:T(8,128)(2,1)S(1)} %slice.6), channel_id=1, source_target_pairs={{0,64},{64,128},{128,192},{192,0},{1,65},{65,129},{129,193},{193,1... | collective-permute-start | bytes 491528 | tf_op jit(solution)/shard_map/ppermute | solution.py:312
  69.7 3.3 %collective-permute-done.10.refs_3_ = bf16[80,1024]{1,0:T(8,128)(2,1)S(1)} collective-permute-done((bf16[80,1024]{1,0:T(8,128)(2,1)S(1)}, bf16[80,1024]{1,0:T(8,128)(2,1)S(1)}, u32[]{:S(2)}, u32[]{:S(2)}) %collective-permute-start.10) | collective-permute-done | bytes 163872 | tf_op jit(solution)/shard_map/ppermute | solution.py:312
  72.9 1.5 %collective-permute-done.9.refs_2_ = bf16[80,1024]{1,0:T(8,128)(2,1)S(1)} collective-permute-done((bf16[80,1024]{1,0:T(8,128)(2,1)S(1)}, bf16[80,1024]{1,0:T(8,128)(2,1)S(1)}, u32[]{:S(2)}, u32[]{:S(2)}) %collective-permute-start.9) | collective-permute-done | bytes 163872 | tf_op jit(solution)/shard_map/ppermute | solution.py:312
  74.4 3.5 %all-to-all-done.2.sketches = bf16[8,128,128]{2,1,0:T(8,128)(2,1)S(1)} async-done(((bf16[8,128,128]{2,1,0:T(8,128)(2,1)}), bf16[8,128,128]{2,1,0:T(8,128)(2,1)S(1)}, u32[]{:S(2)}, u32[]{:S(2)}) %all-to-all-start.2) | async-done | bytes 262176 | tf_op jit(solution)/shard_map/all_to_all | solution.py:377
  78.0 5.6 %second_pass.1 = bf16[1024,128]{1,0:T(8,128)(2,1)} custom-call(s32[2]{0:T(128)S(1)} %pad_add_fusion.place, bf16[8,128,128]{2,1,0:T(8,128)(2,1)S(1)} %all-to-all-done.2.sketches, bf16[4,256,1024]{2,1,0:T(8,128)(2,1)} %copy-done, bf16[160,1024]{1,0:T(8,128)(2,1)S(1)} %copy-done.1, bf16[160,1024]{1,0:T(8,128)(2,1)S(1)} %collective-permute-done.7.refs_1_, ...), custom_call_target="tpu_custom_call" | custom-call | tf_op jit(solution)/shard_map/second_pass/pallas_call | solution.py:380
  83.6 4.3 %all-to-all-start.3 = ((bf16[32,32,128]{2,1,0:T(8,128)(2,1)}), bf16[32,32,128]{2,1,0:T(8,128)(2,1)S(1)}, u32[]{:S(2)}, u32[]{:S(2)}) async-start(bf16[32,32,128]{2,1,0:T(8,128)(2,1)} %bitcast.18), calls=%async_computation.3 | async-start | bytes 524288 | tf_op jit(solution)/shard_map/all_to_all | solution.py:393
  87.9 3.0 %factor.1 = (f32[96,128]{1,0:T(8,128)S(1)}, f32[96,128]{1,0:T(8,128)S(1)}, f32[96,128]{1,0:T(8,128)S(1)}, f32[96,128]{1,0:T(8,128)S(1)}) custom-call(s32[2]{0:T(128)S(1)} %pad_add_fusion.place, bf16[8,128,128]{2,1,0:T(8,128)(2,1)S(1)} %all-to-all-done.2.sketches), custom_call_target="tpu_custom_call" | custom-call | flops 10000000 | bytes 500000 | tf_op jit(solution)/shard_map/factor/pallas_call | solution.py:395
  91.0 1.7 %collective-permute-start.11 = (f32[96,128]{1,0:T(8,128)S(1)}, f32[96,128]{1,0:T(8,128)S(1)}, u32[]{:S(2)}, u32[]{:S(2)}) collective-permute-start(f32[96,128]{1,0:T(8,128)S(1)} %get-tuple-element.35), channel_id=1, source_target_pairs={{0,64},{64,128},{128,192},{192,0},{1,65},{65,129},{129,193},{193,1... | collective-permute-start | bytes 147464 | tf_op jit(solution)/shard_map/ppermute | solution.py:312
  92.7 2.7 %collective-permute-start.12 = (f32[96,128]{1,0:T(8,128)S(1)}, f32[96,128]{1,0:T(8,128)S(1)}, u32[]{:S(2)}, u32[]{:S(2)}) collective-permute-start(f32[96,128]{1,0:T(8,128)S(1)} %get-tuple-element.36), channel_id=1, source_target_pairs={{0,128},{64,192},{128,0},{192,64},{1,129},{65,193},{129,1},{193,65... | collective-permute-start | bytes 147464 | tf_op jit(solution)/shard_map/ppermute | solution.py:312
  95.4 1.4 %collective-permute-start.13 = (f32[96,128]{1,0:T(8,128)S(1)}, f32[96,128]{1,0:T(8,128)S(1)}, u32[]{:S(2)}, u32[]{:S(2)}) collective-permute-start(f32[96,128]{1,0:T(8,128)S(1)} %get-tuple-element.37), channel_id=1, source_target_pairs={{0,192},{64,0},{128,64},{192,128},{1,193},{65,1},{129,65},{193,129... | collective-permute-start | bytes 147464 | tf_op jit(solution)/shard_map/ppermute | solution.py:312
  96.8 1.6 %collective-permute-done.12.refs_2_ = f32[96,128]{1,0:T(8,128)S(1)} collective-permute-done((f32[96,128]{1,0:T(8,128)S(1)}, f32[96,128]{1,0:T(8,128)S(1)}, u32[]{:S(2)}, u32[]{:S(2)}) %collective-permute-start.12) | collective-permute-done | bytes 49184 | tf_op jit(solution)/shard_map/ppermute | solution.py:312
  98.4 1.1 %collective-permute-done.13.refs_3_ = f32[96,128]{1,0:T(8,128)S(1)} collective-permute-done((f32[96,128]{1,0:T(8,128)S(1)}, f32[96,128]{1,0:T(8,128)S(1)}, u32[]{:S(2)}, u32[]{:S(2)}) %collective-permute-start.13) | collective-permute-done | bytes 49184 | tf_op jit(solution)/shard_map/ppermute | solution.py:312
  99.5 1.8 %finish.1 = (f32[8,32,64]{2,1,0:T(8,128)}, f32[8,32,64]{2,1,0:T(8,128)}) custom-call(s32[2]{0:T(128)S(1)} %pad_add_fusion.place, bf16[32,32,128]{2,1,0:T(8,128)(2,1)S(1)} %all-to-all-done.3.parts, f32[96,128]{1,0:T(8,128)S(1)} %get-tuple-element.34.refs_0_, f32[96,128]{1,0:T(8,128)S(1)} %collective-permute-done.11.refs_1_, ...), custom_call_target="tpu_custom_call" | custom-call | tf_op jit(solution)/shard_map/finish/pallas_call | solution.py:407
  (16 shorter events, 0.1 us)
Async XLA Ops:
  5.1 4.5 %copy-start.7 = (bf16[2,64,128]{2,1,0:T(8,128)(2,1)S(1)}, bf16[2,64,128]{2,1,0:T(8,128)(2,1)}, u32[]{:S(2)}) copy-start(bf16[2,64,128]{2,1,0:T(8,128)(2,1)} %param.11) | copy-start | bytes 98308
  5.1 32.3 %all-to-all-start = ((bf16[4,256,1024]{2,1,0:T(8,128)(2,1)}), bf16[4,256,1024]{2,1,0:T(8,128)(2,1)S(1)}, u32[]{:S(2)}, u32[]{:S(2)}) async-start(bf16[4,256,1024]{2,1,0:T(8,128)(2,1)} %sum_factors.1), calls=%async_computation | async-start | bytes 4194304 | tf_op jit(solution)/shard_map/all_to_all | solution.py:333
  9.6 1.2 %collective-permute-start = (bf16[128,128]{1,0:T(8,128)(2,1)S(1)}, bf16[128,128]{1,0:T(8,128)(2,1)S(1)}, u32[]{:S(2)}, u32[]{:S(2)}) collective-permute-start(bf16[128,128]{1,0:T(8,128)(2,1)S(1)} %bitcast.24), channel_id=1, source_target_pairs={{0,1},{1,0},{2,3},{3,2},{4,5},{5,4},{6,7},{7,6},{8,9},{9,8},{10,11... | collective-permute-start | bytes 98312 | tf_op jit(solution)/shard_map/ppermute | solution.py:312
  10.8 7.4 %copy-start.3 = (bf16[2,128,128]{2,1,0:T(8,128)(2,1)}, bf16[2,128,128]{2,1,0:T(8,128)(2,1)S(1)}, u32[]{:S(2)}) copy-start(bf16[2,128,128]{2,1,0:T(8,128)(2,1)S(1)} %pad_maximum_fusion.refs_0_) | copy-start | bytes 196612
  10.9 7.0 %collective-permute-start.3 = (bf16[2,128,128]{2,1,0:T(8,128)(2,1)S(1)}, bf16[2,128,128]{2,1,0:T(8,128)(2,1)S(1)}, u32[]{:S(2)}, u32[]{:S(2)}) collective-permute-start(bf16[2,128,128]{2,1,0:T(8,128)(2,1)S(1)} %pad_maximum_fusion.refs_0_), channel_id=1, source_target_pairs={{0,6},{2,0},{4,2},{6,4},{1,7},{3,1},{5,3},{7,5},{8,14},{10,8},{12,... | collective-permute-start | bytes 196616 | tf_op jit(solution)/shard_map/ppermute | solution.py:312
  11.8 6.1 %collective-permute-start.2 = (bf16[2,128,128]{2,1,0:T(8,128)(2,1)S(1)}, bf16[2,128,128]{2,1,0:T(8,128)(2,1)S(1)}, u32[]{:S(2)}, u32[]{:S(2)}) collective-permute-start(bf16[2,128,128]{2,1,0:T(8,128)(2,1)S(1)} %pad_maximum_fusion.refs_0_), channel_id=1, source_target_pairs={{0,4},{2,6},{4,0},{6,2},{1,5},{3,7},{5,1},{7,3},{8,12},{10,14},{12... | collective-permute-start | bytes 196616 | tf_op jit(solution)/shard_map/ppermute | solution.py:312
  13.8 4.4 %collective-permute-start.1 = (bf16[2,128,128]{2,1,0:T(8,128)(2,1)S(1)}, bf16[2,128,128]{2,1,0:T(8,128)(2,1)S(1)}, u32[]{:S(2)}, u32[]{:S(2)}) collective-permute-start(bf16[2,128,128]{2,1,0:T(8,128)(2,1)S(1)} %pad_maximum_fusion.refs_0_), channel_id=1, source_target_pairs={{0,2},{2,4},{4,6},{6,0},{1,3},{3,5},{5,7},{7,1},{8,10},{10,12},{12... | collective-permute-start | bytes 196616 | tf_op jit(solution)/shard_map/ppermute | solution.py:312
  17.8 0.6 copy-start.4
  17.8 0.6 copy-start.5
  18.3 0.6 copy-start.6
  22.1 26.3 %copy-start.1 = (bf16[160,1024]{1,0:T(8,128)(2,1)S(1)}, bf16[160,1024]{1,0:T(8,128)(2,1)}, u32[]{:S(2)}) copy-start(bf16[160,1024]{1,0:T(8,128)(2,1)} %get-tuple-element.30.refs_0_) | copy-start | bytes 983044
  22.1 13.2 %collective-permute-start.4 = (bf16[128,128]{1,0:T(8,128)(2,1)}, bf16[128,128]{1,0:T(8,128)(2,1)S(1)}, u32[]{:S(2)}, u32[]{:S(2)}) collective-permute-start(bf16[128,128]{1,0:T(8,128)(2,1)} %get-tuple-element.24), channel_id=1, source_target_pairs={{0,64},{64,128},{128,192},{192,0},{1,65},{65,129},{129,193},{193,1... | collective-permute-start | bytes 98312 | tf_op jit(solution)/shard_map/ppermute | solution.py:312
  24.1 13.2 %collective-permute-start.5 = (bf16[128,128]{1,0:T(8,128)(2,1)}, bf16[128,128]{1,0:T(8,128)(2,1)S(1)}, u32[]{:S(2)}, u32[]{:S(2)}) collective-permute-start(bf16[128,128]{1,0:T(8,128)(2,1)} %get-tuple-element.25), channel_id=1, source_target_pairs={{0,128},{64,192},{128,0},{192,64},{1,129},{65,193},{129,1},{193,65... | collective-permute-start | bytes 98312 | tf_op jit(solution)/shard_map/ppermute | solution.py:312
  26.8 10.6 %collective-permute-start.6 = (bf16[128,128]{1,0:T(8,128)(2,1)}, bf16[128,128]{1,0:T(8,128)(2,1)S(1)}, u32[]{:S(2)}, u32[]{:S(2)}) collective-permute-start(bf16[128,128]{1,0:T(8,128)(2,1)} %get-tuple-element.26), channel_id=1, source_target_pairs={{0,192},{64,0},{128,64},{192,128},{1,193},{65,1},{129,65},{193,129... | collective-permute-start | bytes 98312 | tf_op jit(solution)/shard_map/ppermute | solution.py:312
  37.4 30.1 %copy-start = (bf16[4,256,1024]{2,1,0:T(8,128)(2,1)}, bf16[4,256,1024]{2,1,0:T(8,128)(2,1)S(1)}, u32[]{:S(2)}) copy-start(bf16[4,256,1024]{2,1,0:T(8,128)(2,1)S(1)} %all-to-all-done.held.held_far) | copy-start | bytes 6291460
  37.4 0.8 copy-start.2
  39.9 20.0 %all-to-all-start.1 = ((bf16[8,128,128]{2,1,0:T(8,128)(2,1)}), bf16[8,128,128]{2,1,0:T(8,128)(2,1)S(1)}, u32[]{:S(2)}, u32[]{:S(2)}) async-start(bf16[8,128,128]{2,1,0:T(8,128)(2,1)} %first_pass.1), calls=%async_computation.1 | async-start | bytes 524288 | tf_op jit(solution)/shard_map/all_to_all | solution.py:364
  48.4 8.2 %collective-permute-start.8 = (bf16[160,1024]{1,0:T(8,128)(2,1)S(1)}, bf16[160,1024]{1,0:T(8,128)(2,1)S(1)}, u32[]{:S(2)}, u32[]{:S(2)}) collective-permute-start(bf16[160,1024]{1,0:T(8,128)(2,1)S(1)} %copy-done.1), channel_id=1, source_target_pairs={{0,192},{64,0},{128,64},{192,128},{1,193},{65,1},{129,65},{193,129... | collective-permute-start | bytes 983048 | tf_op jit(solution)/shard_map/ppermute | solution.py:312
  49.6 10.3 %collective-permute-start.7 = (bf16[160,1024]{1,0:T(8,128)(2,1)S(1)}, bf16[160,1024]{1,0:T(8,128)(2,1)S(1)}, u32[]{:S(2)}, u32[]{:S(2)}) collective-permute-start(bf16[160,1024]{1,0:T(8,128)(2,1)S(1)} %copy-done.1), channel_id=1, source_target_pairs={{0,64},{64,128},{128,192},{192,0},{1,65},{65,129},{129,193},{193,1... | collective-permute-start | bytes 983048 | tf_op jit(solution)/shard_map/ppermute | solution.py:312
  60.7 17.3 %all-to-all-start.2 = ((bf16[8,128,128]{2,1,0:T(8,128)(2,1)}), bf16[8,128,128]{2,1,0:T(8,128)(2,1)S(1)}, u32[]{:S(2)}, u32[]{:S(2)}) async-start(bf16[8,128,128]{2,1,0:T(8,128)(2,1)} %add_up.1), calls=%async_computation.2 | async-start | bytes 524288 | tf_op jit(solution)/shard_map/all_to_all | solution.py:377
  67.6 5.4 %collective-permute-start.10 = (bf16[80,1024]{1,0:T(8,128)(2,1)S(1)}, bf16[80,1024]{1,0:T(8,128)(2,1)S(1)}, u32[]{:S(2)}, u32[]{:S(2)}) collective-permute-start(bf16[80,1024]{1,0:T(8,128)(2,1)S(1)} %slice.7), channel_id=1, source_target_pairs={{0,192},{64,0},{128,64},{192,128},{1,193},{65,1},{129,65},{193,129... | collective-permute-start | bytes 491528 | tf_op jit(solution)/shard_map/ppermute | solution.py:312
  67.9 6.5 %collective-permute-start.9 = (bf16[80,1024]{1,0:T(8,128)(2,1)S(1)}, bf16[80,1024]{1,0:T(8,128)(2,1)S(1)}, u32[]{:S(2)}, u32[]{:S(2)}) collective-permute-start(bf16[80,1024]{1,0:T(8,128)(2,1)S(1)} %slice.6), channel_id=1, source_target_pairs={{0,64},{64,128},{128,192},{192,0},{1,65},{65,129},{129,193},{193,1... | collective-permute-start | bytes 491528 | tf_op jit(solution)/shard_map/ppermute | solution.py:312
  83.6 15.8 %all-to-all-start.3 = ((bf16[32,32,128]{2,1,0:T(8,128)(2,1)}), bf16[32,32,128]{2,1,0:T(8,128)(2,1)S(1)}, u32[]{:S(2)}, u32[]{:S(2)}) async-start(bf16[32,32,128]{2,1,0:T(8,128)(2,1)} %bitcast.18), calls=%async_computation.3 | async-start | bytes 524288 | tf_op jit(solution)/shard_map/all_to_all | solution.py:393
  91.0 5.8 %collective-permute-start.11 = (f32[96,128]{1,0:T(8,128)S(1)}, f32[96,128]{1,0:T(8,128)S(1)}, u32[]{:S(2)}, u32[]{:S(2)}) collective-permute-start(f32[96,128]{1,0:T(8,128)S(1)} %get-tuple-element.35), channel_id=1, source_target_pairs={{0,64},{64,128},{128,192},{192,0},{1,65},{65,129},{129,193},{193,1... | collective-permute-start | bytes 147464 | tf_op jit(solution)/shard_map/ppermute | solution.py:312
  92.7 5.7 %collective-permute-start.12 = (f32[96,128]{1,0:T(8,128)S(1)}, f32[96,128]{1,0:T(8,128)S(1)}, u32[]{:S(2)}, u32[]{:S(2)}) collective-permute-start(f32[96,128]{1,0:T(8,128)S(1)} %get-tuple-element.36), channel_id=1, source_target_pairs={{0,128},{64,192},{128,0},{192,64},{1,129},{65,193},{129,1},{193,65... | collective-permute-start | bytes 147464 | tf_op jit(solution)/shard_map/ppermute | solution.py:312
  95.4 4.1 %collective-permute-start.13 = (f32[96,128]{1,0:T(8,128)S(1)}, f32[96,128]{1,0:T(8,128)S(1)}, u32[]{:S(2)}, u32[]{:S(2)}) collective-permute-start(f32[96,128]{1,0:T(8,128)S(1)} %get-tuple-element.37), channel_id=1, source_target_pairs={{0,192},{64,0},{128,64},{192,128},{1,193},{65,1},{129,65},{193,129... | collective-permute-start | bytes 147464 | tf_op jit(solution)/shard_map/ppermute | solution.py:312

commit v6 on v5

--- a/solution.py
+++ b/solution.py
@@ -17,8 +17,9 @@
 SMEM = pltpu.SMEM
 VMEM = pltpu.VMEM
 LANES = 128
+BLOCK = 8
 TAIL = 16
-BLOCK = 8
+RELAY = 80
 
 
 def params(mib):
@@ -38,10 +39,8 @@
     return jnp.concatenate([block[q * TAIL : (q + 1) * TAIL] for q in range(block.shape[0] // TAIL)], axis=1)
 
 
-def unpack_rows(ref, lead, row, first, count):
-    return jnp.concatenate(
-        [ref[lead, row : row + TAIL, q * LANES : (q + 1) * LANES] for q in range(first, first + count)], axis=0
-    )
+def unpack_rows(block):
+    return jnp.concatenate([block[:, q * LANES : (q + 1) * LANES] for q in range(block.shape[1] // LANES)], axis=0)
 
 
 def sum_factors(panel, target, count, factors, out, loaded, acc, kept, panel_at, target_at, count_at, sems, small):
@@ -92,8 +91,8 @@
 
 def project(columns, *refs):
     pieces, refs = refs[:4], refs[4:]
-    probes, coupling, shared, table = refs[0], refs[1], refs[2], refs[-1]
-    sent = refs[3:-1]
+    probes, coupling, mine, other = refs[:4]
+    sent, (shared, table) = refs[4:-2], refs[-2:]
     rows = pieces[0].shape[1]
     at = 0
     for piece in pieces:
@@ -108,17 +107,17 @@
         [jnp.concatenate([first, zero], axis=1), jnp.concatenate([zero, second], axis=1)], axis=0
     )
     projected = lax.dot_general(probes[...], shared[0:rows, :], NT, preferred_element_type=F32)
-    table[...] = lax.dot_general(
-        projected, diagonal, NT, precision=HIGHEST, preferred_element_type=F32
-    ).astype(BF)
+    table[...] = lax.dot_general(projected, diagonal, NT, precision=HIGHEST, preferred_element_type=F32)
     each = sent[0].shape[0]
     for s in range(len(sent)):
         owner = lax.rem(columns[at] + s, len(sent))
-        sent[s][...] = table[pl.ds(pl.multiple_of(owner * each, each), each), :]
-    high, mid, low = split_bf(jnp.concatenate([first, second], axis=1), 3)
-    shared[rows : rows + TAIL, :] = jnp.concatenate([pack_rows(high), pack_rows(mid)], axis=1)
-    tail = pack_rows(low)
-    shared[rows + TAIL : rows + 2 * TAIL, :] = jnp.concatenate([tail, jnp.zeros_like(tail)], axis=1)
+        sent[s][...] = table[pl.ds(pl.multiple_of(owner * each, each), each), :].astype(sent[s].dtype)
+    high, low = split_bf(jnp.concatenate([first, second], axis=1), 2)
+    shared[rows : rows + TAIL, :] = jnp.concatenate([pack_rows(high), pack_rows(low)], axis=1)
+    half = mine.shape[1]
+    core = columns[at + 1]
+    mine[...] = shared[:, pl.ds(pl.multiple_of(core * half, half), half)]
+    other[...] = shared[:, pl.ds(pl.multiple_of((1 - core) * half, half), half)]
 
 
 def first_pass(place, held, *refs):
@@ -127,17 +126,18 @@
     targets = rows // LANES
     rank = out.shape[1] // targets
     cut = out.shape[2]
-    for t in range(targets):
-        total = jnp.zeros((rank, width), F32)
-        for s in range(groups):
-            source = lax.rem(place[0] + groups - s, groups)
-            total = total + jnp.dot(
+    totals = [jnp.zeros((rank, width), F32) for _ in range(targets)]
+    for s in range(groups):
+        source = lax.rem(place[0] + groups - s, groups)
+        for t in range(targets):
+            totals[t] = totals[t] + jnp.dot(
                 coefficients[s][t * rank : (t + 1) * rank, :],
                 held[source, t * LANES : (t + 1) * LANES, :],
                 preferred_element_type=F32,
             )
+    for t in range(targets):
         for z in range(out.shape[0]):
-            out[z, t * rank : (t + 1) * rank, :] = total[:, z * cut : (z + 1) * cut].astype(BF)
+            out[z, t * rank : (t + 1) * rank, :] = totals[t][:, z * cut : (z + 1) * cut].astype(BF)
 
 
 def add_up(parts, out):
@@ -178,29 +178,10 @@
     ]
 
 
-def second_pass(place, sketches, held_far, *refs):
-    groups = held_far.shape[0]
-    shared_far, (out, held, shared, sems) = refs[:5], refs[5:]
-    half = shared.shape[1] // 2
-    sources = [lax.rem(place[0] + groups - s, groups) for s in range(groups)]
-    loads = [pltpu.make_async_copy(held_far.at[source], held.at[s], sems.at[s]) for s, source in enumerate(sources)]
-    ends = (
-        shared.at[0],
-        shared.at[1],
-        shared.at[2, 0:half, :],
-        shared.at[2, half : 2 * half, :],
-        shared.at[3],
-    )
-    panels = [
-        pltpu.make_async_copy(source, to, sems.at[groups + i])
-        for i, (source, to) in enumerate(zip(shared_far, ends, strict=True))
-    ]
-    arrivals = ((0,), (1,), (2, 3), (4,))
-    for s in range(groups):
-        loads[s].start()
-        for i in arrivals[s]:
-            panels[i].start()
-    cuts, rows, _ = sketches.shape
+def second_pass(place, sketches, held, *refs):
+    groups = held.shape[0]
+    out, sent, turned = refs[10], refs[11:-1], refs[-1]
+    cuts, rows, cut = sketches.shape
     width = held.shape[2]
     targets = held.shape[1] // LANES
     rank = rows // targets
@@ -208,23 +189,31 @@
         jnp.concatenate([sketches[z, t * rank : (t + 1) * rank, :] for z in range(cuts)], axis=1)
         for t in range(targets)
     ]
-    total = jnp.zeros((rows, width), F32)
+    grams = [lax.dot_general(s, s, NT, preferred_element_type=F32) for s in whole]
+    inverses = jnp.concatenate(inverse_factors(grams), axis=1)
+    halves = [
+        [
+            refs[at][...],
+            refs[at + 1][...],
+            jnp.concatenate([refs[at + 2][...], refs[at + 3][...]], axis=0),
+            refs[at + 4][...],
+        ]
+        for at in (0, 5)
+    ]
+    half = width // 2
+    totals = [jnp.zeros((rows, half), F32) for _ in halves]
     for s in range(groups):
-        loads[s].wait()
-        for i in arrivals[s]:
-            panels[i].wait()
+        source = lax.rem(place[0] + groups - s, groups)
         summed = jnp.concatenate(
             [
                 lax.dot_general(
-                    held[s, t * LANES : (t + 1) * LANES, :], whole[t], NT, preferred_element_type=F32
+                    held[source, t * LANES : (t + 1) * LANES, :], whole[t], NT, preferred_element_type=F32
                 )
                 for t in range(targets)
             ],
             axis=1,
         )
-        coupling = (
-            unpack_rows(shared, s, LANES, 0, 4).astype(F32) + unpack_rows(shared, s, LANES, 4, 4).astype(F32)
-        ) + unpack_rows(shared, s, LANES + TAIL, 0, 4).astype(F32)
+        coupling = unpack_rows(halves[0][s][LANES:]).astype(F32) + unpack_rows(halves[1][s][LANES:]).astype(F32)
         middle = jnp.concatenate(
             [
                 lax.dot_general(
@@ -239,27 +228,17 @@
             axis=0,
         ).T
         for part in split_bf(middle, 2):
-            total = total + jnp.dot(part, shared[s, 0:LANES, :], preferred_element_type=F32)
-    for c in range(width // LANES):
-        out[c * LANES : (c + 1) * LANES, :] = total[:, c * LANES : (c + 1) * LANES].T.astype(out.dtype)
-
-
-def factor(place, sketches, *refs):
-    sent, (turned,) = refs[:-1], refs[-1:]
-    cuts, rows, cut = sketches.shape
-    targets = 2
-    rank = rows // targets
-    whole = [
-        jnp.concatenate([sketches[z, t * rank : (t + 1) * rank, :] for z in range(cuts)], axis=1)
-        for t in range(targets)
-    ]
-    grams = [lax.dot_general(s, s, NT, preferred_element_type=F32) for s in whole]
-    inverses = jnp.concatenate(inverse_factors(grams), axis=1)
-    owners = len(sent)
+            for h, panels in enumerate(halves):
+                totals[h] = totals[h] + jnp.dot(part, panels[s][0:LANES], preferred_element_type=F32)
+    for h, total in enumerate(totals):
+        side = place[2] if h == 0 else 1 - place[2]
+        for c in range(half // LANES):
+            start = pl.multiple_of(side * half + c * LANES, LANES)
+            out[pl.ds(start, LANES), :] = total[:, c * LANES : (c + 1) * LANES].T.astype(out.dtype)
     own = sent[0].shape[0] - rank
-    for s in range(owners):
-        owner = lax.rem(place[0] + s, owners)
-        start = owner * (cuts * cut // owners) + place[1] * own
+    for s in range(groups):
+        owner = lax.rem(place[0] + s, groups)
+        start = owner * (width // groups) + place[1] * own
         piece = start // cut
         turned[...] = sketches[piece].astype(F32).T
         sent[s][0:rank, :] = inverses
@@ -295,7 +274,7 @@
     ny, nz, nx, nc = sizes
     y, z = lax.axis_index("y"), lax.axis_index("z")
     x, c = lax.axis_index("x"), lax.axis_index("core")
-    place = jnp.stack([y, z]).astype(jnp.int32)
+    place = jnp.stack([y, z, c]).astype(jnp.int32)
     factors = entry_factor[:, 0]
     slots, rank, width = factors.shape
     panels = panel_shared.shape[0]
@@ -336,19 +315,20 @@
     pair = jnp.stack([own, turn(own, "core", nc, 1)])
     pieces = [pair] + [turn(pair, "x", nx, s) for s in range(1, nx)]
     columns = jnp.stack(
-        [((x + nx - s) % nx) * nc + k for s in range(nx) for k in (c, (c + 1) % nc)] + [y]
+        [((x + nx - s) % nx) * nc + k for s in range(nx) for k in (c, (c + 1) % nc)] + [y, c]
     ).astype(jnp.int32)
-    shared, *sent = pl.pallas_call(
+    mine_half, other_half, *sent = pl.pallas_call(
         project,
-        out_shape=(jax.ShapeDtypeStruct((rows + 2 * TAIL, width), BF),)
-        + (jax.ShapeDtypeStruct((own_rows, rows), BF),) * ny,
+        out_shape=(jax.ShapeDtypeStruct((rows + TAIL, width // 2), BF),) * 2
+        + (jax.ShapeDtypeStruct((own_rows, rows), F32),)
+        + (jax.ShapeDtypeStruct((own_rows, rows), BF),) * (ny - 1),
         in_specs=[in_smem] + [in_vmem] * (nx + 2),
-        out_specs=(in_vmem,) * (ny + 1),
-        scratch_shapes=[VMEM((targets * rank, rows), BF)],
+        out_specs=(in_vmem,) * (ny + 2),
+        scratch_shapes=[VMEM((rows + TAIL, width), BF), VMEM((targets * rank, rows), F32)],
         compiler_params=params(60),
         name="project",
     )(columns, *pieces, probes.reshape(targets * rank, width), coupling)
-    coefficients = [sent[0]] + [turn(sent[s], "y", ny, s) for s in range(1, ny)]
+    coefficients = [sent[0].astype(BF)] + [turn(sent[s], "y", ny, s) for s in range(1, ny)]
 
     cut = width // nz
     sketch = pl.pallas_call(
@@ -359,13 +339,13 @@
         compiler_params=params(20),
         name="first_pass",
     )(place, held, *coefficients)
-    shared, sketch = lax.optimization_barrier((shared, sketch))
-    near = [turn(shared, "y", ny, s) for s in (1, ny - 1)]
+    mine_half, sketch = lax.optimization_barrier((mine_half, sketch))
+    near = [turn(mine_half, "y", ny, s) for s in (1, ny - 1)]
     parts = lax.all_to_all(sketch, "z", 0, 0, tiled=True)
-    parts, shared, *near = lax.optimization_barrier((parts, shared, *near))
-    middle_row = shared.shape[0] // 2
-    far = [turn(near[0][:middle_row], "y", ny, 1), turn(near[1][middle_row:], "y", ny, ny - 1)]
-    all_shared = [shared, near[0], *far, near[1]]
+    parts, *near = lax.optimization_barrier((parts, *near))
+    far = [turn(near[0][:RELAY], "y", ny, 1), turn(near[1][RELAY:], "y", ny, ny - 1)]
+    halves = [near[0], *far, near[1]]
+    all_shared = [mine_half, *halves, other_half] + [turn(h, "core", nc, 1) for h in halves]
     copies = pl.pallas_call(
         add_up,
         out_shape=jax.ShapeDtypeStruct((nz, own_rows, cut), BF),
@@ -377,31 +357,17 @@
     sketches = lax.all_to_all(copies, "z", 0, 0, tiled=True)
 
     keep = width // (ny * nz)
-    rows_part = pl.pallas_call(
+    rows_part, *sent = pl.pallas_call(
         second_pass,
-        out_shape=jax.ShapeDtypeStruct((width, own_rows), BF),
-        in_specs=[in_smem, in_vmem] + [in_any] * 6,
-        out_specs=in_vmem,
-        scratch_shapes=[
-            VMEM((ny, held_rows, width), BF),
-            VMEM((ny, rows + 2 * TAIL, width), BF),
-            pltpu.SemaphoreType.DMA((ny + 5,)),
-        ],
+        out_shape=(jax.ShapeDtypeStruct((width, own_rows), BF),)
+        + (jax.ShapeDtypeStruct((rank + keep, own_rows), F32),) * ny,
+        in_specs=[in_smem] + [in_vmem] * 12,
+        out_specs=(in_vmem,) * (ny + 1),
+        scratch_shapes=[VMEM((cut, own_rows), F32)],
         compiler_params=params(52),
         name="second_pass",
     )(place, sketches, held, *all_shared)
     row_parts = lax.all_to_all(rows_part.reshape(ny * nz, keep, own_rows), ("y", "z"), 0, 0, tiled=True)
-    sketches, _ = lax.optimization_barrier((sketches, rows_part))
-    sent = pl.pallas_call(
-        factor,
-        out_shape=(jax.ShapeDtypeStruct((rank + keep, own_rows), F32),) * ny,
-        in_specs=[in_smem, in_vmem],
-        out_specs=(in_vmem,) * ny,
-        scratch_shapes=[VMEM((cut, own_rows), F32)],
-        compiler_params=params(8),
-        cost_estimate=pl.CostEstimate(flops=10**7, bytes_accessed=5 * 10**5, transcendentals=0),
-        name="factor",
-    )(place, sketches)
     received = [sent[0]] + [turn(sent[s], "y", ny, s) for s in range(1, ny)]
     out = jax.ShapeDtypeStruct((targets, keep, rank), F32)
     left_out, right_out = pl.pallas_call(

time: 102 us -> 102 us (level)
  Pallas kernels: 20 us -> 17.4 us
  starting transfers between devices: 44.4 us -> 46.5 us
    ppermute x14 -> x18, waiting for transfers between devices: 29.8 us -> 24 us  [turn(): lax.ppermute(value, axis, [(i, (i + by) % size) for i in range(size)])]
    all_to_all x1, waiting for transfers between devices: 0.01 us -> 3.77 us  [shards(): lax.all_to_all(rows_part.reshape(ny * nz, keep, own_rows), ('y', 'z'), 0,...]
    all_to_all x1, waiting for transfers between devices: 0.01 us -> 3.07 us  [shards(): parts = lax.all_to_all(sketch, 'z', 0, 0, tiled=True)]
    all_to_all x1, starting transfers between devices: 4.26 us -> 7.18 us  [shards(): lax.all_to_all(rows_part.reshape(ny * nz, keep, own_rows), ('y', 'z'), 0,...]
    all_to_all x1, starting transfers between devices: 6.85 us -> 3.99 us  [shards(): sketches = lax.all_to_all(copies, 'z', 0, 0, tiled=True)]
    pallas_call x3 -> x2, Pallas kernels: 11.9 us -> 9.36 us  [the longest x1 6.13 us: shards(): pl.pallas_call(second_pass, out_shape=(jax.ShapeDtypeStruct((width, own_r...]
    ppermute x14 -> x18, starting transfers between devices: 20.3 us -> 22.3 us  [turn(): lax.ppermute(value, axis, [(i, (i + by) % size) for i in range(size)])]
  transfers between devices with their start and end apart: 18 -> 22, of which waited for: 12 -> 16; matrix products, arithmetic and copies ran while one was open for 1% -> 2% of each run, Pallas kernels for 6% -> 3%
where the time goes in v6:
time: 102 us; the launch traced here: 101 us
  starting transfers between devices  46.5 us (46%)
  waiting for transfers between devices  33.8 us (33%)
  Pallas kernels  17.4 us (17%)
  between operations  1.37 us (1%)
  local copies, waits for them, and re-layouts  1.33 us (1%)
    ppermute x18, waiting for transfers between devices, turn(): lax.ppermute(value, axis, [(i, (i + by) % size) for i in range(size)])  24 us
    ppermute x18, starting transfers between devices, turn(): lax.ppermute(value, axis, [(i, (i + by) % size) for i in range(size)])  22.3 us
    all_to_all x1, starting transfers between devices, shards(): parts = lax.all_to_all(sketch, 'z', 0, 0, tiled=True)  8.47 us
    all_to_all x1, starting transfers between devices, shards(): lax.all_to_all(rows_part.reshape(ny * nz, keep, own_rows), ('y', 'z'), 0,...  7.18 us
    pallas_call x1, Pallas kernels, shards(): pl.pallas_call(second_pass, out_shape=(jax.ShapeDtypeStruct((width, own_r...  6.13 us
    all_to_all x1, starting transfers between devices, shards(): held = lax.all_to_all(sums, 'y', 0, 0, tiled=True)  4.48 us
    all_to_all x1, starting transfers between devices, shards(): sketches = lax.all_to_all(copies, 'z', 0, 0, tiled=True)  3.99 us
    pallas_call x1, Pallas kernels, shards(): pl.pallas_call(sum_factors, out_shape=jax.ShapeDtypeStruct((ny, held_rows...  3.83 us
  transfers between devices with their start and end apart: 22, of which 16 were waited for; matrix products, arithmetic and copies ran while one was open for 2% of the time, Pallas kernels for 3%

profile of v6, /device:TPU:6, one launch (start us, length us, event | category | flops | bytes accessed | tf_op | source)
XLA Modules:
  0.0 101.3 jit_solution(13682032034454360725)
XLA Ops:
  1.3 3.8 %sum_factors.1 = bf16[4,256,1024]{2,1,0:T(8,128)(2,1)} custom-call(s32[36]{0:T(128)} %bitcast.28, s32[36]{0:T(128)} %bitcast.29, s32[1]{0:T(128)} %bitcast.22.count, bf16[36,64,1024]{2,1,0:T(8,128)(2,1)} %bitcast.23), custom_call_target="tpu_custom_call" | custom-call | flops 10000000 | bytes 7000000 | tf_op jit(solution)/shard_map/sum_factors/pallas_call | solution.py:293
  5.1 0.0 copy-start.7
  5.1 4.5 %all-to-all-start = ((bf16[4,256,1024]{2,1,0:T(8,128)(2,1)}), bf16[4,256,1024]{2,1,0:T(8,128)(2,1)S(1)}, u32[]{:S(2)}, u32[]{:S(2)}) async-start(bf16[4,256,1024]{2,1,0:T(8,128)(2,1)} %sum_factors.1), calls=%async_computation | async-start | bytes 4194304 | tf_op jit(solution)/shard_map/all_to_all | solution.py:312
  9.6 1.2 %collective-permute-done = bf16[128,128]{1,0:T(8,128)(2,1)S(1)} collective-permute-done((bf16[128,128]{1,0:T(8,128)(2,1)S(1)}, bf16[128,128]{1,0:T(8,128)(2,1)S(1)}, u32[]{:S(2)}, u32[]{:S(2)}) %collective-permute-start) | collective-permute-done | bytes 32800 | tf_op jit(solution)/shard_map/ppermute | solution.py:291
  10.8 0.9 collective-permute-start.3
  11.7 2.1 %collective-permute-start.2 = (bf16[2,128,128]{2,1,0:T(8,128)(2,1)S(1)}, bf16[2,128,128]{2,1,0:T(8,128)(2,1)S(1)}, u32[]{:S(2)}, u32[]{:S(2)}) collective-permute-start(bf16[2,128,128]{2,1,0:T(8,128)(2,1)S(1)} %pad_maximum_fusion.refs_0_), channel_id=1, source_target_pairs={{0,4},{2,6},{4,0},{6,2},{1,5},{3,7},{5,1},{7,3},{8,12},{10,14},{12... | collective-permute-start | bytes 196616 | tf_op jit(solution)/shard_map/ppermute | solution.py:291
  13.8 1.1 %collective-permute-start.1 = (bf16[2,128,128]{2,1,0:T(8,128)(2,1)S(1)}, bf16[2,128,128]{2,1,0:T(8,128)(2,1)S(1)}, u32[]{:S(2)}, u32[]{:S(2)}) collective-permute-start(bf16[2,128,128]{2,1,0:T(8,128)(2,1)S(1)} %pad_maximum_fusion.refs_0_), channel_id=1, source_target_pairs={{0,2},{2,4},{4,6},{6,0},{1,3},{3,5},{5,7},{7,1},{8,10},{10,12},{12... | collective-permute-start | bytes 196616 | tf_op jit(solution)/shard_map/ppermute | solution.py:291
  14.9 0.7 stack.62.columns
  15.6 2.2 %collective-permute-done.3.refs_3_ = bf16[2,128,128]{2,1,0:T(8,128)(2,1)S(1)} collective-permute-done((bf16[2,128,128]{2,1,0:T(8,128)(2,1)S(1)}, bf16[2,128,128]{2,1,0:T(8,128)(2,1)S(1)}, u32[]{:S(2)}, u32[]{:S(2)}) %collective-permute-start.3) | collective-permute-done | bytes 65568 | tf_op jit(solution)/shard_map/ppermute | solution.py:291
  17.8 0.5 collective-permute-done.1.refs_1_
  18.3 0.2 copy-done.4
  18.4 0.0 copy-done.5
  18.4 0.4 copy-done.6
  18.9 3.2 %project.1 = (bf16[144,512]{1,0:T(8,128)(2,1)}, bf16[144,512]{1,0:T(8,128)(2,1)}, f32[128,128]{1,0:T(8,128)}, bf16[128,128]{1,0:T(8,128)(2,1)}, bf16[128,128]{1,0:T(8,128)(2,1)}, /*index=5*/bf16[128,128]{1,0:T(8,128)(2,1)}) custom-call(s32[10]{0:T(128)} %stack.62.columns, bf16[2,128,128]{2,1,0:T(8,128)(2,1)} %copy-done.3, bf16[2,128,128]{2,1,0:T(8,128)(2,1)} %copy-done.6, ...), custom_call_target="tpu_custom_call" | custom-call | tf_op jit(solution)/shard_map/project/pallas_call | solution.py:320
  22.1 2.1 %collective-permute-start.4 = (bf16[128,128]{1,0:T(8,128)(2,1)}, bf16[128,128]{1,0:T(8,128)(2,1)S(1)}, u32[]{:S(2)}, u32[]{:S(2)}) collective-permute-start(bf16[128,128]{1,0:T(8,128)(2,1)} %get-tuple-element.24), channel_id=1, source_target_pairs={{0,64},{64,128},{128,192},{192,0},{1,65},{65,129},{129,193},{193,1... | collective-permute-start | bytes 98312 | tf_op jit(solution)/shard_map/ppermute | solution.py:291
  24.2 2.7 %collective-permute-start.5 = (bf16[128,128]{1,0:T(8,128)(2,1)}, bf16[128,128]{1,0:T(8,128)(2,1)S(1)}, u32[]{:S(2)}, u32[]{:S(2)}) collective-permute-start(bf16[128,128]{1,0:T(8,128)(2,1)} %get-tuple-element.25), channel_id=1, source_target_pairs={{0,128},{64,192},{128,0},{192,64},{1,129},{65,193},{129,1},{193,65... | collective-permute-start | bytes 98312 | tf_op jit(solution)/shard_map/ppermute | solution.py:291
  26.9 1.5 %collective-permute-start.6 = (bf16[128,128]{1,0:T(8,128)(2,1)}, bf16[128,128]{1,0:T(8,128)(2,1)S(1)}, u32[]{:S(2)}, u32[]{:S(2)}) collective-permute-start(bf16[128,128]{1,0:T(8,128)(2,1)} %get-tuple-element.26), channel_id=1, source_target_pairs={{0,192},{64,0},{128,64},{192,128},{1,193},{65,1},{129,65},{193,129... | collective-permute-start | bytes 98312 | tf_op jit(solution)/shard_map/ppermute | solution.py:291
  28.3 0.1 pad_add_fusion.place
  28.4 0.8 convert_element_type.3.refs_0_
  29.3 6.1 %collective-permute-done.4.refs_1_ = bf16[128,128]{1,0:T(8,128)(2,1)S(1)} collective-permute-done((bf16[128,128]{1,0:T(8,128)(2,1)}, bf16[128,128]{1,0:T(8,128)(2,1)S(1)}, u32[]{:S(2)}, u32[]{:S(2)}) %collective-permute-start.4) | collective-permute-done | bytes 32800 | tf_op jit(solution)/shard_map/ppermute | solution.py:291
  35.3 2.1 %collective-permute-done.5.refs_2_ = bf16[128,128]{1,0:T(8,128)(2,1)S(1)} collective-permute-done((bf16[128,128]{1,0:T(8,128)(2,1)}, bf16[128,128]{1,0:T(8,128)(2,1)S(1)}, u32[]{:S(2)}, u32[]{:S(2)}) %collective-permute-start.5) | collective-permute-done | bytes 32800 | tf_op jit(solution)/shard_map/ppermute | solution.py:291
  37.4 1.7 %first_pass.1 = bf16[8,128,128]{2,1,0:T(8,128)(2,1)} custom-call(s32[3]{0:T(128)S(1)} %pad_add_fusion.place, bf16[4,256,1024]{2,1,0:T(8,128)(2,1)S(1)} %all-to-all-done.held, bf16[128,128]{1,0:T(8,128)(2,1)S(1)} %convert_element_type.3.refs_0_, bf16[128,128]{1,0:T(8,128)(2,1)S(1)} %collective-permute-done.4.refs_1_, ...), custom_call_target="tpu_custom_call" | custom-call | tf_op jit(solution)/shard_map/first_pass/pallas_call | solution.py:334
  39.1 8.5 %all-to-all-start.1 = ((bf16[8,128,128]{2,1,0:T(8,128)(2,1)}), bf16[8,128,128]{2,1,0:T(8,128)(2,1)S(1)}, u32[]{:S(2)}, u32[]{:S(2)}) async-start(bf16[8,128,128]{2,1,0:T(8,128)(2,1)} %first_pass.1), calls=%async_computation.1 | async-start | bytes 524288 | tf_op jit(solution)/shard_map/all_to_all | solution.py:344
  47.5 1.2 %collective-permute-start.8 = (bf16[144,512]{1,0:T(8,128)(2,1)S(1)}, bf16[144,512]{1,0:T(8,128)(2,1)S(1)}, u32[]{:S(2)}, u32[]{:S(2)}) collective-permute-start(bf16[144,512]{1,0:T(8,128)(2,1)S(1)} %copy-done.1), channel_id=1, source_target_pairs={{0,192},{64,0},{128,64},{192,128},{1,193},{65,1},{129,65},{193,129... | collective-permute-start | bytes 442376 | tf_op jit(solution)/shard_map/ppermute | solution.py:291
  48.7 0.9 collective-permute-start.7
  49.6 3.1 %collective-permute-done.8.refs_4_ = bf16[144,512]{1,0:T(8,128)(2,1)S(1)} collective-permute-done((bf16[144,512]{1,0:T(8,128)(2,1)S(1)}, bf16[144,512]{1,0:T(8,128)(2,1)S(1)}, u32[]{:S(2)}, u32[]{:S(2)}) %collective-permute-start.8) | collective-permute-done | bytes 147488 | tf_op jit(solution)/shard_map/ppermute | solution.py:291
  52.8 2.4 %collective-permute-done.7.refs_1_ = bf16[144,512]{1,0:T(8,128)(2,1)S(1)} collective-permute-done((bf16[144,512]{1,0:T(8,128)(2,1)S(1)}, bf16[144,512]{1,0:T(8,128)(2,1)S(1)}, u32[]{:S(2)}, u32[]{:S(2)}) %collective-permute-start.7) | collective-permute-done | bytes 147488 | tf_op jit(solution)/shard_map/ppermute | solution.py:291
  55.2 3.1 %all-to-all-done.1.parts = bf16[8,128,128]{2,1,0:T(8,128)(2,1)S(1)} async-done(((bf16[8,128,128]{2,1,0:T(8,128)(2,1)}), bf16[8,128,128]{2,1,0:T(8,128)(2,1)S(1)}, u32[]{:S(2)}, u32[]{:S(2)}) %all-to-all-start.1) | async-done | bytes 262176 | tf_op jit(solution)/shard_map/all_to_all | solution.py:344
  58.2 0.7 add_up.1
  59.0 4.0 %all-to-all-start.2 = ((bf16[8,128,128]{2,1,0:T(8,128)(2,1)}), bf16[8,128,128]{2,1,0:T(8,128)(2,1)S(1)}, u32[]{:S(2)}, u32[]{:S(2)}) async-start(bf16[8,128,128]{2,1,0:T(8,128)(2,1)} %add_up.1), calls=%async_computation.2 | async-start | bytes 524288 | tf_op jit(solution)/shard_map/all_to_all | solution.py:357
  63.0 1.4 %collective-permute-start.9 = (bf16[80,512]{1,0:T(8,128)(2,1)S(1)}, bf16[80,512]{1,0:T(8,128)(2,1)S(1)}, u32[]{:S(2)}, u32[]{:S(2)}) collective-permute-start(bf16[80,512]{1,0:T(8,128)(2,1)S(1)} %slice.6), channel_id=1, source_target_pairs={{0,64},{64,128},{128,192},{192,0},{1,65},{65,129},{129,193},{193,1... | collective-permute-start | bytes 245768 | tf_op jit(solution)/shard_map/ppermute | solution.py:291
  64.4 0.5 collective-permute-start.14
  64.9 1.9 %collective-permute-start.10 = (bf16[64,512]{1,0:T(8,128)(2,1)S(1)}, bf16[64,512]{1,0:T(8,128)(2,1)S(1)}, u32[]{:S(2)}, u32[]{:S(2)}) collective-permute-start(bf16[64,512]{1,0:T(8,128)(2,1)S(1)} %slice.7), channel_id=1, source_target_pairs={{0,192},{64,0},{128,64},{192,128},{1,193},{65,1},{129,65},{193,129... | collective-permute-start | bytes 196616 | tf_op jit(solution)/shard_map/ppermute | solution.py:291
  66.8 1.9 %collective-permute-done.9.refs_2_ = bf16[80,512]{1,0:T(8,128)(2,1)S(1)} collective-permute-done((bf16[80,512]{1,0:T(8,128)(2,1)S(1)}, bf16[80,512]{1,0:T(8,128)(2,1)S(1)}, u32[]{:S(2)}, u32[]{:S(2)}) %collective-permute-start.9) | collective-permute-done | bytes 81952 | tf_op jit(solution)/shard_map/ppermute | solution.py:291
  68.7 0.4 collective-permute-done.10.refs_3_
  69.1 0.1 collective-permute-start.13
  69.2 1.2 %collective-permute-done.13.refs_8_ = bf16[64,512]{1,0:T(8,128)(2,1)S(1)} collective-permute-done((bf16[64,512]{1,0:T(8,128)(2,1)S(1)}, bf16[64,512]{1,0:T(8,128)(2,1)S(1)}, u32[]{:S(2)}, u32[]{:S(2)}) %collective-permute-start.13) | collective-permute-done | bytes 65568 | tf_op jit(solution)/shard_map/ppermute | solution.py:291
  70.4 3.0 %all-to-all-done.2.sketches = bf16[8,128,128]{2,1,0:T(8,128)(2,1)S(1)} async-done(((bf16[8,128,128]{2,1,0:T(8,128)(2,1)}), bf16[8,128,128]{2,1,0:T(8,128)(2,1)S(1)}, u32[]{:S(2)}, u32[]{:S(2)}) %all-to-all-start.2) | async-done | bytes 262176 | tf_op jit(solution)/shard_map/all_to_all | solution.py:357
  73.4 6.1 %second_pass.1 = (bf16[1024,128]{1,0:T(8,128)(2,1)}, f32[96,128]{1,0:T(8,128)S(1)}, f32[96,128]{1,0:T(8,128)S(1)}, f32[96,128]{1,0:T(8,128)S(1)}, f32[96,128]{1,0:T(8,128)S(1)}) custom-call(s32[3]{0:T(128)S(1)} %pad_add_fusion.place, bf16[8,128,128]{2,1,0:T(8,128)(2,1)S(1)} %all-to-all-done.2.sketches, bf16[4,256,1024]{2,1,0:T(8,128)(2,1)} %copy-done, ...), custom_call_target="tpu_custom_call" | custom-call | tf_op jit(solution)/shard_map/second_pass/pallas_call | solution.py:360
  79.6 7.2 %all-to-all-start.3 = ((bf16[32,32,128]{2,1,0:T(8,128)(2,1)}), bf16[32,32,128]{2,1,0:T(8,128)(2,1)S(1)}, u32[]{:S(2)}, u32[]{:S(2)}) async-start(bf16[32,32,128]{2,1,0:T(8,128)(2,1)} %bitcast.19), calls=%async_computation.3 | async-start | bytes 524288 | tf_op jit(solution)/shard_map/all_to_all | solution.py:370
  86.8 1.9 %collective-permute-start.15 = (f32[96,128]{1,0:T(8,128)S(1)}, f32[96,128]{1,0:T(8,128)S(1)}, u32[]{:S(2)}, u32[]{:S(2)}) collective-permute-start(f32[96,128]{1,0:T(8,128)S(1)} %get-tuple-element.35), channel_id=1, source_target_pairs={{0,64},{64,128},{128,192},{192,0},{1,65},{65,129},{129,193},{193,1... | collective-permute-start | bytes 147464 | tf_op jit(solution)/shard_map/ppermute | solution.py:291
  88.6 2.7 %collective-permute-start.16 = (f32[96,128]{1,0:T(8,128)S(1)}, f32[96,128]{1,0:T(8,128)S(1)}, u32[]{:S(2)}, u32[]{:S(2)}) collective-permute-start(f32[96,128]{1,0:T(8,128)S(1)} %get-tuple-element.36), channel_id=1, source_target_pairs={{0,128},{64,192},{128,0},{192,64},{1,129},{65,193},{129,1},{193,65... | collective-permute-start | bytes 147464 | tf_op jit(solution)/shard_map/ppermute | solution.py:291
  91.3 1.4 %collective-permute-start.17 = (f32[96,128]{1,0:T(8,128)S(1)}, f32[96,128]{1,0:T(8,128)S(1)}, u32[]{:S(2)}, u32[]{:S(2)}) collective-permute-start(f32[96,128]{1,0:T(8,128)S(1)} %get-tuple-element.37), channel_id=1, source_target_pairs={{0,192},{64,0},{128,64},{192,128},{1,193},{65,1},{129,65},{193,129... | collective-permute-start | bytes 147464 | tf_op jit(solution)/shard_map/ppermute | solution.py:291
  92.8 0.3 collective-permute-done.15.refs_1_
  93.1 1.4 %collective-permute-done.16.refs_2_ = f32[96,128]{1,0:T(8,128)S(1)} collective-permute-done((f32[96,128]{1,0:T(8,128)S(1)}, f32[96,128]{1,0:T(8,128)S(1)}, u32[]{:S(2)}, u32[]{:S(2)}) %collective-permute-start.16) | collective-permute-done | bytes 49184 | tf_op jit(solution)/shard_map/ppermute | solution.py:291
  94.5 1.2 %collective-permute-done.17.refs_3_ = f32[96,128]{1,0:T(8,128)S(1)} collective-permute-done((f32[96,128]{1,0:T(8,128)S(1)}, f32[96,128]{1,0:T(8,128)S(1)}, u32[]{:S(2)}, u32[]{:S(2)}) %collective-permute-start.17) | collective-permute-done | bytes 49184 | tf_op jit(solution)/shard_map/ppermute | solution.py:291
  95.7 3.8 %all-to-all-done.3.parts = bf16[32,32,128]{2,1,0:T(8,128)(2,1)S(1)} async-done(((bf16[32,32,128]{2,1,0:T(8,128)(2,1)}), bf16[32,32,128]{2,1,0:T(8,128)(2,1)S(1)}, u32[]{:S(2)}, u32[]{:S(2)}) %all-to-all-start.3) | async-done | bytes 262176 | tf_op jit(solution)/shard_map/all_to_all | solution.py:370
  99.5 1.8 %finish.1 = (f32[8,32,64]{2,1,0:T(8,128)}, f32[8,32,64]{2,1,0:T(8,128)}) custom-call(s32[3]{0:T(128)S(1)} %pad_add_fusion.place, bf16[32,32,128]{2,1,0:T(8,128)(2,1)S(1)} %all-to-all-done.3.parts, f32[96,128]{1,0:T(8,128)S(1)} %get-tuple-element.34.refs_0_, f32[96,128]{1,0:T(8,128)S(1)} %collective-permute-done.15.refs_1_, ...), custom_call_target="tpu_custom_call" | custom-call | tf_op jit(solution)/shard_map/finish/pallas_call | solution.py:373
  (24 shorter events, 0.1 us)
Async XLA Ops:
  5.1 4.5 %copy-start.7 = (bf16[2,64,128]{2,1,0:T(8,128)(2,1)S(1)}, bf16[2,64,128]{2,1,0:T(8,128)(2,1)}, u32[]{:S(2)}) copy-start(bf16[2,64,128]{2,1,0:T(8,128)(2,1)} %param.11) | copy-start | bytes 98308
  5.1 32.3 %all-to-all-start = ((bf16[4,256,1024]{2,1,0:T(8,128)(2,1)}), bf16[4,256,1024]{2,1,0:T(8,128)(2,1)S(1)}, u32[]{:S(2)}, u32[]{:S(2)}) async-start(bf16[4,256,1024]{2,1,0:T(8,128)(2,1)} %sum_factors.1), calls=%async_computation | async-start | bytes 4194304 | tf_op jit(solution)/shard_map/all_to_all | solution.py:312
  9.6 1.2 %collective-permute-start = (bf16[128,128]{1,0:T(8,128)(2,1)S(1)}, bf16[128,128]{1,0:T(8,128)(2,1)S(1)}, u32[]{:S(2)}, u32[]{:S(2)}) collective-permute-start(bf16[128,128]{1,0:T(8,128)(2,1)S(1)} %bitcast.25), channel_id=1, source_target_pairs={{0,1},{1,0},{2,3},{3,2},{4,5},{5,4},{6,7},{7,6},{8,9},{9,8},{10,11... | collective-permute-start | bytes 98312 | tf_op jit(solution)/shard_map/ppermute | solution.py:291
  10.8 7.4 %copy-start.3 = (bf16[2,128,128]{2,1,0:T(8,128)(2,1)}, bf16[2,128,128]{2,1,0:T(8,128)(2,1)S(1)}, u32[]{:S(2)}) copy-start(bf16[2,128,128]{2,1,0:T(8,128)(2,1)S(1)} %pad_maximum_fusion.refs_0_) | copy-start | bytes 196612
  10.8 7.0 %collective-permute-start.3 = (bf16[2,128,128]{2,1,0:T(8,128)(2,1)S(1)}, bf16[2,128,128]{2,1,0:T(8,128)(2,1)S(1)}, u32[]{:S(2)}, u32[]{:S(2)}) collective-permute-start(bf16[2,128,128]{2,1,0:T(8,128)(2,1)S(1)} %pad_maximum_fusion.refs_0_), channel_id=1, source_target_pairs={{0,6},{2,0},{4,2},{6,4},{1,7},{3,1},{5,3},{7,5},{8,14},{10,8},{12,... | collective-permute-start | bytes 196616 | tf_op jit(solution)/shard_map/ppermute | solution.py:291
  11.7 6.1 %collective-permute-start.2 = (bf16[2,128,128]{2,1,0:T(8,128)(2,1)S(1)}, bf16[2,128,128]{2,1,0:T(8,128)(2,1)S(1)}, u32[]{:S(2)}, u32[]{:S(2)}) collective-permute-start(bf16[2,128,128]{2,1,0:T(8,128)(2,1)S(1)} %pad_maximum_fusion.refs_0_), channel_id=1, source_target_pairs={{0,4},{2,6},{4,0},{6,2},{1,5},{3,7},{5,1},{7,3},{8,12},{10,14},{12... | collective-permute-start | bytes 196616 | tf_op jit(solution)/shard_map/ppermute | solution.py:291
  13.8 4.4 %collective-permute-start.1 = (bf16[2,128,128]{2,1,0:T(8,128)(2,1)S(1)}, bf16[2,128,128]{2,1,0:T(8,128)(2,1)S(1)}, u32[]{:S(2)}, u32[]{:S(2)}) collective-permute-start(bf16[2,128,128]{2,1,0:T(8,128)(2,1)S(1)} %pad_maximum_fusion.refs_0_), channel_id=1, source_target_pairs={{0,2},{2,4},{4,6},{6,0},{1,3},{3,5},{5,7},{7,1},{8,10},{10,12},{12... | collective-permute-start | bytes 196616 | tf_op jit(solution)/shard_map/ppermute | solution.py:291
  17.8 0.6 copy-start.4
  17.8 0.6 copy-start.5
  18.3 0.6 copy-start.6
  22.1 25.4 %copy-start.1 = (bf16[144,512]{1,0:T(8,128)(2,1)S(1)}, bf16[144,512]{1,0:T(8,128)(2,1)}, u32[]{:S(2)}) copy-start(bf16[144,512]{1,0:T(8,128)(2,1)} %get-tuple-element.28.refs_0_) | copy-start | bytes 442372
  22.1 13.2 %collective-permute-start.4 = (bf16[128,128]{1,0:T(8,128)(2,1)}, bf16[128,128]{1,0:T(8,128)(2,1)S(1)}, u32[]{:S(2)}, u32[]{:S(2)}) collective-permute-start(bf16[128,128]{1,0:T(8,128)(2,1)} %get-tuple-element.24), channel_id=1, source_target_pairs={{0,64},{64,128},{128,192},{192,0},{1,65},{65,129},{129,193},{193,1... | collective-permute-start | bytes 98312 | tf_op jit(solution)/shard_map/ppermute | solution.py:291
  24.2 13.2 %collective-permute-start.5 = (bf16[128,128]{1,0:T(8,128)(2,1)}, bf16[128,128]{1,0:T(8,128)(2,1)S(1)}, u32[]{:S(2)}, u32[]{:S(2)}) collective-permute-start(bf16[128,128]{1,0:T(8,128)(2,1)} %get-tuple-element.25), channel_id=1, source_target_pairs={{0,128},{64,192},{128,0},{192,64},{1,129},{65,193},{129,1},{193,65... | collective-permute-start | bytes 98312 | tf_op jit(solution)/shard_map/ppermute | solution.py:291
  26.9 10.5 %collective-permute-start.6 = (bf16[128,128]{1,0:T(8,128)(2,1)}, bf16[128,128]{1,0:T(8,128)(2,1)S(1)}, u32[]{:S(2)}, u32[]{:S(2)}) collective-permute-start(bf16[128,128]{1,0:T(8,128)(2,1)} %get-tuple-element.26), channel_id=1, source_target_pairs={{0,192},{64,0},{128,64},{192,128},{1,193},{65,1},{129,65},{193,129... | collective-permute-start | bytes 98312 | tf_op jit(solution)/shard_map/ppermute | solution.py:291
  29.3 44.2 %copy-start.2 = (bf16[144,512]{1,0:T(8,128)(2,1)S(1)}, bf16[144,512]{1,0:T(8,128)(2,1)}, u32[]{:S(2)}) copy-start(bf16[144,512]{1,0:T(8,128)(2,1)} %get-tuple-element.32.refs_5_) | copy-start | bytes 442372
  37.4 25.6 %copy-start = (bf16[4,256,1024]{2,1,0:T(8,128)(2,1)}, bf16[4,256,1024]{2,1,0:T(8,128)(2,1)S(1)}, u32[]{:S(2)}) copy-start(bf16[4,256,1024]{2,1,0:T(8,128)(2,1)S(1)} %all-to-all-done.held) | copy-start | bytes 6291460
  39.1 19.2 %all-to-all-start.1 = ((bf16[8,128,128]{2,1,0:T(8,128)(2,1)}), bf16[8,128,128]{2,1,0:T(8,128)(2,1)S(1)}, u32[]{:S(2)}, u32[]{:S(2)}) async-start(bf16[8,128,128]{2,1,0:T(8,128)(2,1)} %first_pass.1), calls=%async_computation.1 | async-start | bytes 524288 | tf_op jit(solution)/shard_map/all_to_all | solution.py:344
  47.5 5.2 %collective-permute-start.8 = (bf16[144,512]{1,0:T(8,128)(2,1)S(1)}, bf16[144,512]{1,0:T(8,128)(2,1)S(1)}, u32[]{:S(2)}, u32[]{:S(2)}) collective-permute-start(bf16[144,512]{1,0:T(8,128)(2,1)S(1)} %copy-done.1), channel_id=1, source_target_pairs={{0,192},{64,0},{128,64},{192,128},{1,193},{65,1},{129,65},{193,129... | collective-permute-start | bytes 442376 | tf_op jit(solution)/shard_map/ppermute | solution.py:291
  48.7 6.4 %collective-permute-start.7 = (bf16[144,512]{1,0:T(8,128)(2,1)S(1)}, bf16[144,512]{1,0:T(8,128)(2,1)S(1)}, u32[]{:S(2)}, u32[]{:S(2)}) collective-permute-start(bf16[144,512]{1,0:T(8,128)(2,1)S(1)} %copy-done.1), channel_id=1, source_target_pairs={{0,64},{64,128},{128,192},{192,0},{1,65},{65,129},{129,193},{193,1... | collective-permute-start | bytes 442376 | tf_op jit(solution)/shard_map/ppermute | solution.py:291
  59.0 14.5 %all-to-all-start.2 = ((bf16[8,128,128]{2,1,0:T(8,128)(2,1)}), bf16[8,128,128]{2,1,0:T(8,128)(2,1)S(1)}, u32[]{:S(2)}, u32[]{:S(2)}) async-start(bf16[8,128,128]{2,1,0:T(8,128)(2,1)} %add_up.1), calls=%async_computation.2 | async-start | bytes 524288 | tf_op jit(solution)/shard_map/all_to_all | solution.py:357
  63.0 5.7 %collective-permute-start.9 = (bf16[80,512]{1,0:T(8,128)(2,1)S(1)}, bf16[80,512]{1,0:T(8,128)(2,1)S(1)}, u32[]{:S(2)}, u32[]{:S(2)}) collective-permute-start(bf16[80,512]{1,0:T(8,128)(2,1)S(1)} %slice.6), channel_id=1, source_target_pairs={{0,64},{64,128},{128,192},{192,0},{1,65},{65,129},{129,193},{193,1... | collective-permute-start | bytes 245768 | tf_op jit(solution)/shard_map/ppermute | solution.py:291
  64.4 6.0 %collective-permute-start.11 = (bf16[144,512]{1,0:T(8,128)(2,1)S(1)}, bf16[144,512]{1,0:T(8,128)(2,1)S(1)}, u32[]{:S(2)}, u32[]{:S(2)}) collective-permute-start(bf16[144,512]{1,0:T(8,128)(2,1)S(1)} %collective-permute-done.7.refs_1_), channel_id=1, source_target_pairs={{0,1},{1,0},{2,3},{3,2},{4,5},{5,4},{6,7},{7,6},{8,9},{9,8},{10,11... | collective-permute-start | bytes 442376 | tf_op jit(solution)/shard_map/ppermute | solution.py:291
  64.4 6.0 %collective-permute-start.14 = (bf16[144,512]{1,0:T(8,128)(2,1)S(1)}, bf16[144,512]{1,0:T(8,128)(2,1)S(1)}, u32[]{:S(2)}, u32[]{:S(2)}) collective-permute-start(bf16[144,512]{1,0:T(8,128)(2,1)S(1)} %collective-permute-done.8.refs_4_), channel_id=1, source_target_pairs={{0,1},{1,0},{2,3},{3,2},{4,5},{5,4},{6,7},{7,6},{8,9},{9,8},{10,11... | collective-permute-start | bytes 442376 | tf_op jit(solution)/shard_map/ppermute | solution.py:291
  64.9 4.3 %collective-permute-start.10 = (bf16[64,512]{1,0:T(8,128)(2,1)S(1)}, bf16[64,512]{1,0:T(8,128)(2,1)S(1)}, u32[]{:S(2)}, u32[]{:S(2)}) collective-permute-start(bf16[64,512]{1,0:T(8,128)(2,1)S(1)} %slice.7), channel_id=1, source_target_pairs={{0,192},{64,0},{128,64},{192,128},{1,193},{65,1},{129,65},{193,129... | collective-permute-start | bytes 196616 | tf_op jit(solution)/shard_map/ppermute | solution.py:291
  68.7 1.7 %collective-permute-start.12 = (bf16[80,512]{1,0:T(8,128)(2,1)S(1)}, bf16[80,512]{1,0:T(8,128)(2,1)S(1)}, u32[]{:S(2)}, u32[]{:S(2)}) collective-permute-start(bf16[80,512]{1,0:T(8,128)(2,1)S(1)} %collective-permute-done.9.refs_2_), channel_id=1, source_target_pairs={{0,1},{1,0},{2,3},{3,2},{4,5},{5,4},{6,7},{7,6},{8,9},{9,8},{10,11... | collective-permute-start | bytes 245768 | tf_op jit(solution)/shard_map/ppermute | solution.py:291
  69.1 1.3 %collective-permute-start.13 = (bf16[64,512]{1,0:T(8,128)(2,1)S(1)}, bf16[64,512]{1,0:T(8,128)(2,1)S(1)}, u32[]{:S(2)}, u32[]{:S(2)}) collective-permute-start(bf16[64,512]{1,0:T(8,128)(2,1)S(1)} %collective-permute-done.10.refs_3_), channel_id=1, source_target_pairs={{0,1},{1,0},{2,3},{3,2},{4,5},{5,4},{6,7},{7,6},{8,9},{9,8},{10,11... | collective-permute-start | bytes 196616 | tf_op jit(solution)/shard_map/ppermute | solution.py:291
  79.6 19.9 %all-to-all-start.3 = ((bf16[32,32,128]{2,1,0:T(8,128)(2,1)}), bf16[32,32,128]{2,1,0:T(8,128)(2,1)S(1)}, u32[]{:S(2)}, u32[]{:S(2)}) async-start(bf16[32,32,128]{2,1,0:T(8,128)(2,1)} %bitcast.19), calls=%async_computation.3 | async-start | bytes 524288 | tf_op jit(solution)/shard_map/all_to_all | solution.py:370
  86.8 6.3 %collective-permute-start.15 = (f32[96,128]{1,0:T(8,128)S(1)}, f32[96,128]{1,0:T(8,128)S(1)}, u32[]{:S(2)}, u32[]{:S(2)}) collective-permute-start(f32[96,128]{1,0:T(8,128)S(1)} %get-tuple-element.35), channel_id=1, source_target_pairs={{0,64},{64,128},{128,192},{192,0},{1,65},{65,129},{129,193},{193,1... | collective-permute-start | bytes 147464 | tf_op jit(solution)/shard_map/ppermute | solution.py:291
  88.6 5.9 %collective-permute-start.16 = (f32[96,128]{1,0:T(8,128)S(1)}, f32[96,128]{1,0:T(8,128)S(1)}, u32[]{:S(2)}, u32[]{:S(2)}) collective-permute-start(f32[96,128]{1,0:T(8,128)S(1)} %get-tuple-element.36), channel_id=1, source_target_pairs={{0,128},{64,192},{128,0},{192,64},{1,129},{65,193},{129,1},{193,65... | collective-permute-start | bytes 147464 | tf_op jit(solution)/shard_map/ppermute | solution.py:291
  91.3 4.4 %collective-permute-start.17 = (f32[96,128]{1,0:T(8,128)S(1)}, f32[96,128]{1,0:T(8,128)S(1)}, u32[]{:S(2)}, u32[]{:S(2)}) collective-permute-start(f32[96,128]{1,0:T(8,128)S(1)} %get-tuple-element.37), channel_id=1, source_target_pairs={{0,192},{64,0},{128,64},{192,128},{1,193},{65,1},{129,65},{193,129... | collective-permute-start | bytes 147464 | tf_op jit(solution)/shard_map/ppermute | solution.py:291

commit v7 on v6

--- a/solution.py
+++ b/solution.py
@@ -43,7 +43,8 @@
     return jnp.concatenate([block[:, q * LANES : (q + 1) * LANES] for q in range(block.shape[1] // LANES)], axis=0)
 
 
-def sum_factors(panel, target, count, factors, out, loaded, acc, kept, panel_at, target_at, count_at, sems, small):
+def sum_factors(panel, target, count, factors, *refs):
+    out, (loaded, acc, kept, panel_at, target_at, count_at, sems, small) = refs[:-8], refs[-8:]
     slots, rank, _ = loaded.shape
     pairs = acc.shape[0]
     panels = pairs // 8
@@ -78,13 +79,15 @@
     for i, copy in enumerate(loads):
         copy.wait()
         lax.fori_loop(i * chunk, jnp.minimum(live, (i + 1) * chunk), add, 0)
-    groups = out.shape[0]
+    groups = len(out)
     each = pairs // groups
-    stores = [pltpu.make_async_copy(kept.at[g], out.at[g], sems.at[6 + g]) for g in range(groups)]
-    for g, copy in enumerate(stores):
+    here = lax.axis_index("y")
+    stores = [pltpu.make_async_copy(kept.at[s], out[s], sems.at[6 + s]) for s in range(groups)]
+    for s in [*range(1, groups), 0]:
+        owner = lax.rem(here + s, groups)
         for i in range(each):
-            kept[g, i * rank : (i + 1) * rank, :] = acc[g * each + i].astype(BF)
-        copy.start()
+            kept[s, i * rank : (i + 1) * rank, :] = acc[owner * each + i].astype(BF)
+        stores[s].start()
     for copy in stores:
         copy.wait()
 
@@ -120,19 +123,19 @@
     other[...] = shared[:, pl.ds(pl.multiple_of((1 - core) * half, half), half)]
 
 
-def first_pass(place, held, *refs):
-    coefficients, out = refs[:-1], refs[-1]
-    groups, rows, width = held.shape
+def first_pass(*refs):
+    groups = len(refs) // 2
+    held, coefficients, out = refs[:groups], refs[groups:-1], refs[-1]
+    rows, width = held[0].shape
     targets = rows // LANES
     rank = out.shape[1] // targets
     cut = out.shape[2]
     totals = [jnp.zeros((rank, width), F32) for _ in range(targets)]
     for s in range(groups):
-        source = lax.rem(place[0] + groups - s, groups)
         for t in range(targets):
             totals[t] = totals[t] + jnp.dot(
                 coefficients[s][t * rank : (t + 1) * rank, :],
-                held[source, t * LANES : (t + 1) * LANES, :],
+                held[s][t * LANES : (t + 1) * LANES, :],
                 preferred_element_type=F32,
             )
     for t in range(targets):
@@ -178,12 +181,13 @@
     ]
 
 
-def second_pass(place, sketches, held, *refs):
-    groups = held.shape[0]
+def second_pass(place, sketches, *refs):
+    held, refs = refs[:4], refs[4:]
+    groups = len(held)
     out, sent, turned = refs[10], refs[11:-1], refs[-1]
     cuts, rows, cut = sketches.shape
-    width = held.shape[2]
-    targets = held.shape[1] // LANES
+    width = held[0].shape[1]
+    targets = held[0].shape[0] // LANES
     rank = rows // targets
     whole = [
         jnp.concatenate([sketches[z, t * rank : (t + 1) * rank, :] for z in range(cuts)], axis=1)
@@ -203,11 +207,10 @@
     half = width // 2
     totals = [jnp.zeros((rows, half), F32) for _ in halves]
     for s in range(groups):
-        source = lax.rem(place[0] + groups - s, groups)
         summed = jnp.concatenate(
             [
                 lax.dot_general(
-                    held[source, t * LANES : (t + 1) * LANES, :], whole[t], NT, preferred_element_type=F32
+                    held[s][t * LANES : (t + 1) * LANES, :], whole[t], NT, preferred_element_type=F32
                 )
                 for t in range(targets)
             ],
@@ -292,9 +295,9 @@
 
     sums = pl.pallas_call(
         sum_factors,
-        out_shape=jax.ShapeDtypeStruct((ny, held_rows, width), BF),
+        out_shape=(jax.ShapeDtypeStruct((held_rows, width), BF),) * ny,
         in_specs=[in_any] * 4,
-        out_specs=in_any,
+        out_specs=(in_any,) * ny,
         scratch_shapes=[
             VMEM((slots, rank, width), BF),
             VMEM((targets * panels, rank, width), F32),
@@ -309,7 +312,7 @@
         cost_estimate=pl.CostEstimate(flops=10**7, bytes_accessed=7 * 10**6, transcendentals=0),
         name="sum_factors",
     )(entry_panel[:, 0], entry_target[:, 0], entry_count[0], factors)
-    held = lax.all_to_all(sums, "y", 0, 0, tiled=True)
+    held = [sums[0]] + [turn(sums[s], "y", ny, s) for s in range(1, ny)]
 
     own, _ = lax.optimization_barrier((panel_shared.reshape(rows, LANES), sums))
     pair = jnp.stack([own, turn(own, "core", nc, 1)])
@@ -334,18 +337,19 @@
     sketch = pl.pallas_call(
         first_pass,
         out_shape=jax.ShapeDtypeStruct((nz, own_rows, cut), BF),
-        in_specs=[in_smem] + [in_vmem] * (ny + 1),
+        in_specs=[in_vmem] * (2 * ny),
         out_specs=in_vmem,
         compiler_params=params(20),
         name="first_pass",
-    )(place, held, *coefficients)
+    )(*held, *coefficients)
     mine_half, sketch = lax.optimization_barrier((mine_half, sketch))
     near = [turn(mine_half, "y", ny, s) for s in (1, ny - 1)]
     parts = lax.all_to_all(sketch, "z", 0, 0, tiled=True)
-    parts, *near = lax.optimization_barrier((parts, *near))
+    crossed = [turn(h, "core", nc, 1) for h in near]
+    parts, near, crossed = lax.optimization_barrier((parts, near, crossed))
     far = [turn(near[0][:RELAY], "y", ny, 1), turn(near[1][RELAY:], "y", ny, ny - 1)]
-    halves = [near[0], *far, near[1]]
-    all_shared = [mine_half, *halves, other_half] + [turn(h, "core", nc, 1) for h in halves]
+    far_crossed = [turn(h, "core", nc, 1) for h in far]
+    all_shared = [mine_half, near[0], *far, near[1], other_half, crossed[0], *far_crossed, crossed[1]]
     copies = pl.pallas_call(
         add_up,
         out_shape=jax.ShapeDtypeStruct((nz, own_rows, cut), BF),
@@ -361,12 +365,12 @@
         second_pass,
         out_shape=(jax.ShapeDtypeStruct((width, own_rows), BF),)
         + (jax.ShapeDtypeStruct((rank + keep, own_rows), F32),) * ny,
-        in_specs=[in_smem] + [in_vmem] * 12,
+        in_specs=[in_smem] + [in_vmem] * 15,
         out_specs=(in_vmem,) * (ny + 1),
         scratch_shapes=[VMEM((cut, own_rows), F32)],
-        compiler_params=params(52),
+        compiler_params=params(20),
         name="second_pass",
-    )(place, sketches, held, *all_shared)
+    )(place, sketches, *held, *all_shared)
     row_parts = lax.all_to_all(rows_part.reshape(ny * nz, keep, own_rows), ("y", "z"), 0, 0, tiled=True)
     received = [sent[0]] + [turn(sent[s], "y", ny, s) for s in range(1, ny)]
     out = jax.ShapeDtypeStruct((targets, keep, rank), F32)

time: 102 us -> 106 us (1.039)
  waiting for transfers between devices: 33.8 us -> 41.2 us
  starting transfers between devices: 46.5 us -> 41.7 us
  local copies, waits for them, and re-layouts: 1.33 us -> 4.13 us
  Pallas kernels: 17.4 us -> 15.8 us
    ppermute x18 -> x21, waiting for transfers between devices: 24 us -> 31.9 us  [turn(): lax.ppermute(value, axis, [(i, (i + by) % size) for i in range(size)])]
    all_to_all x1 -> x0, starting transfers between devices: 4.48 us -> none  [shards(): held = lax.all_to_all(sums, 'y', 0, 0, tiled=True)]
    unnamed x16 -> x18, local copies, waits for them, and re-layouts: 0.65 us -> 3.49 us
    all_to_all x1, starting transfers between devices: 3.99 us -> 6.45 us  [shards(): sketches = lax.all_to_all(copies, 'z', 0, 0, tiled=True)]
    all_to_all x1, waiting for transfers between devices: 3.07 us -> 0.76 us  [shards(): parts = lax.all_to_all(sketch, 'z', 0, 0, tiled=True)]
    all_to_all x1, waiting for transfers between devices: 3.02 us -> 4.99 us  [shards(): sketches = lax.all_to_all(copies, 'z', 0, 0, tiled=True)]
    all_to_all x1, starting transfers between devices: 7.18 us -> 5.28 us  [shards(): lax.all_to_all(rows_part.reshape(ny * nz, keep, own_rows), ('y', 'z'), 0,...]
    pallas_call x1, Pallas kernels: 6.13 us -> 5.03 us  [shards(): pl.pallas_call(second_pass, out_shape=(jax.ShapeDtypeStruct((width, own_r...]
  transfers between devices with their start and end apart: 22 -> 24, of which waited for: 16 -> 17; matrix products, arithmetic and copies ran while one was open for 2% -> 1% of each run, Pallas kernels for 3% -> 3%
where the time goes in v7:
time: 106 us; the launch traced here: 105 us
  starting transfers between devices  41.7 us (39%)
  waiting for transfers between devices  41.2 us (39%)
  Pallas kernels  15.8 us (15%)
  local copies, waits for them, and re-layouts  4.13 us (4%)
  between operations  1.39 us (1%)
    ppermute x21, waiting for transfers between devices, turn(): lax.ppermute(value, axis, [(i, (i + by) % size) for i in range(size)])  31.9 us
    ppermute x21, starting transfers between devices, turn(): lax.ppermute(value, axis, [(i, (i + by) % size) for i in range(size)])  21.5 us
    all_to_all x1, starting transfers between devices, shards(): parts = lax.all_to_all(sketch, 'z', 0, 0, tiled=True)  8.46 us
    all_to_all x1, starting transfers between devices, shards(): sketches = lax.all_to_all(copies, 'z', 0, 0, tiled=True)  6.45 us
    all_to_all x1, starting transfers between devices, shards(): lax.all_to_all(rows_part.reshape(ny * nz, keep, own_rows), ('y', 'z'), 0,...  5.28 us
    pallas_call x1, Pallas kernels, shards(): pl.pallas_call(second_pass, out_shape=(jax.ShapeDtypeStruct((width, own_r...  5.03 us
    all_to_all x1, waiting for transfers between devices, shards(): sketches = lax.all_to_all(copies, 'z', 0, 0, tiled=True)  4.99 us
    pallas_call x1, Pallas kernels, shards(): pl.pallas_call(sum_factors, out_shape=(jax.ShapeDtypeStruct((held_rows, w...  3.83 us
  transfers between devices with their start and end apart: 24, of which 17 were waited for; matrix products, arithmetic and copies ran while one was open for 1% of the time, Pallas kernels for 3%

profile of v7, /device:TPU:6, one launch (start us, length us, event | category | flops | bytes accessed | tf_op | source)
XLA Modules:
  0.0 105.2 jit_solution(1510231114274334270)
XLA Ops:
  1.3 3.8 %sum_factors.1 = (bf16[256,1024]{1,0:T(8,128)(2,1)}, bf16[256,1024]{1,0:T(8,128)(2,1)}, bf16[256,1024]{1,0:T(8,128)(2,1)}, bf16[256,1024]{1,0:T(8,128)(2,1)}) custom-call(s32[36]{0:T(128)} %bitcast.28, s32[36]{0:T(128)} %bitcast.29, s32[1]{0:T(128)} %bitcast.22.count, bf16[36,64,1024]{2,1,0:T(8,128)(2,1)} %bitcast.23), custom_call_target="tpu_custom_call" | custom-call | flops 10000000 | bytes 7000000 | tf_op jit(solution)/shard_map/sum_factors/pallas_call | solution.py:296
  5.1 1.7 %collective-permute-start.4 = (bf16[256,1024]{1,0:T(8,128)(2,1)}, bf16[256,1024]{1,0:T(8,128)(2,1)S(1)}, u32[]{:S(2)}, u32[]{:S(2)}) collective-permute-start(bf16[256,1024]{1,0:T(8,128)(2,1)} %get-tuple-element.28), channel_id=1, source_target_pairs={{0,64},{64,128},{128,192},{192,0},{1,65},{65,129},{129,193},{193,1... | collective-permute-start | bytes 1572872 | tf_op jit(solution)/shard_map/ppermute | solution.py:294
  6.8 3.1 %collective-permute-start.5 = (bf16[256,1024]{1,0:T(8,128)(2,1)}, bf16[256,1024]{1,0:T(8,128)(2,1)S(1)}, u32[]{:S(2)}, u32[]{:S(2)}) collective-permute-start(bf16[256,1024]{1,0:T(8,128)(2,1)} %get-tuple-element.29), channel_id=1, source_target_pairs={{0,128},{64,192},{128,0},{192,64},{1,129},{65,193},{129,1},{193,65... | collective-permute-start | bytes 1572872 | tf_op jit(solution)/shard_map/ppermute | solution.py:294
  9.9 1.2 %collective-permute-start.6 = (bf16[256,1024]{1,0:T(8,128)(2,1)}, bf16[256,1024]{1,0:T(8,128)(2,1)S(1)}, u32[]{:S(2)}, u32[]{:S(2)}) collective-permute-start(bf16[256,1024]{1,0:T(8,128)(2,1)} %get-tuple-element.30), channel_id=1, source_target_pairs={{0,192},{64,0},{128,64},{192,128},{1,193},{65,1},{129,65},{193,129... | collective-permute-start | bytes 1572872 | tf_op jit(solution)/shard_map/ppermute | solution.py:294
  11.0 1.2 %collective-permute-done = bf16[128,128]{1,0:T(8,128)(2,1)S(1)} collective-permute-done((bf16[128,128]{1,0:T(8,128)(2,1)S(1)}, bf16[128,128]{1,0:T(8,128)(2,1)S(1)}, u32[]{:S(2)}, u32[]{:S(2)}) %collective-permute-start) | collective-permute-done | bytes 32800 | tf_op jit(solution)/shard_map/ppermute | solution.py:294
  12.3 0.9 collective-permute-start.3
  13.2 1.1 %collective-permute-start.2 = (bf16[2,128,128]{2,1,0:T(8,128)(2,1)S(1)}, bf16[2,128,128]{2,1,0:T(8,128)(2,1)S(1)}, u32[]{:S(2)}, u32[]{:S(2)}) collective-permute-start(bf16[2,128,128]{2,1,0:T(8,128)(2,1)S(1)} %pad_maximum_fusion.refs_0_), channel_id=1, source_target_pairs={{0,4},{2,6},{4,0},{6,2},{1,5},{3,7},{5,1},{7,3},{8,12},{10,14},{12... | collective-permute-start | bytes 196616 | tf_op jit(solution)/shard_map/ppermute | solution.py:294
  14.3 4.9 %collective-permute-done.3.refs_3_ = bf16[2,128,128]{2,1,0:T(8,128)(2,1)S(1)} collective-permute-done((bf16[2,128,128]{2,1,0:T(8,128)(2,1)S(1)}, bf16[2,128,128]{2,1,0:T(8,128)(2,1)S(1)}, u32[]{:S(2)}, u32[]{:S(2)}) %collective-permute-start.3) | collective-permute-done | bytes 65568 | tf_op jit(solution)/shard_map/ppermute | solution.py:294
  19.2 0.6 stack.62.columns
  19.9 3.6 %collective-permute-done.1.refs_1_ = bf16[2,128,128]{2,1,0:T(8,128)(2,1)S(1)} collective-permute-done((bf16[2,128,128]{2,1,0:T(8,128)(2,1)S(1)}, bf16[2,128,128]{2,1,0:T(8,128)(2,1)S(1)}, u32[]{:S(2)}, u32[]{:S(2)}) %collective-permute-start.1) | collective-permute-done | bytes 65568 | tf_op jit(solution)/shard_map/ppermute | solution.py:294
  23.5 0.6 copy-done.7
  24.1 3.2 %project.1 = (bf16[144,512]{1,0:T(8,128)(2,1)}, bf16[144,512]{1,0:T(8,128)(2,1)}, f32[128,128]{1,0:T(8,128)}, bf16[128,128]{1,0:T(8,128)(2,1)}, bf16[128,128]{1,0:T(8,128)(2,1)}, /*index=5*/bf16[128,128]{1,0:T(8,128)(2,1)}) custom-call(s32[10]{0:T(128)} %stack.62.columns, bf16[2,128,128]{2,1,0:T(8,128)(2,1)} %copy-done.4, bf16[2,128,128]{2,1,0:T(8,128)(2,1)} %copy-done.7, ...), custom_call_target="tpu_custom_call" | custom-call | tf_op jit(solution)/shard_map/project/pallas_call | solution.py:323
  27.4 0.7 collective-permute-start.7
  28.1 0.7 collective-permute-start.8
  28.8 5.0 %collective-permute-done.7.refs_5_ = bf16[128,128]{1,0:T(8,128)(2,1)S(1)} collective-permute-done((bf16[128,128]{1,0:T(8,128)(2,1)}, bf16[128,128]{1,0:T(8,128)(2,1)S(1)}, u32[]{:S(2)}, u32[]{:S(2)}) %collective-permute-start.7) | collective-permute-done | bytes 32800 | tf_op jit(solution)/shard_map/ppermute | solution.py:294
  33.9 0.6 collective-permute-start.9
  34.4 0.8 convert_element_type.3.refs_4_
  35.3 2.7 %collective-permute-done.9.refs_7_ = bf16[128,128]{1,0:T(8,128)(2,1)S(1)} collective-permute-done((bf16[128,128]{1,0:T(8,128)(2,1)}, bf16[128,128]{1,0:T(8,128)(2,1)S(1)}, u32[]{:S(2)}, u32[]{:S(2)}) %collective-permute-start.9) | collective-permute-done | bytes 32800 | tf_op jit(solution)/shard_map/ppermute | solution.py:294
  38.0 1.0 copy-done
  39.1 1.1 %first_pass.1 = bf16[8,128,128]{2,1,0:T(8,128)(2,1)} custom-call(bf16[256,1024]{1,0:T(8,128)(2,1)S(1)} %copy-done, bf16[256,1024]{1,0:T(8,128)(2,1)S(1)} %collective-permute-done.4.refs_1_, bf16[256,1024]{1,0:T(8,128)(2,1)S(1)} %collective-permute-done.5.refs_2_, bf16[256,1024]{1,0:T(8,128)(2,1)S(1)} %collective-permute-done.6.refs_3_, ...), custom_call_target="tpu_custom_call" | custom-call | tf_op jit(solution)/shard_map/first_pass/pallas_call | solution.py:337
  40.2 8.5 %all-to-all-start = ((bf16[8,128,128]{2,1,0:T(8,128)(2,1)}), bf16[8,128,128]{2,1,0:T(8,128)(2,1)S(1)}, u32[]{:S(2)}, u32[]{:S(2)}) async-start(bf16[8,128,128]{2,1,0:T(8,128)(2,1)} %first_pass.1), calls=%async_computation | async-start | bytes 524288 | tf_op jit(solution)/shard_map/all_to_all | solution.py:347
  48.6 1.8 %collective-permute-start.11 = (bf16[144,512]{1,0:T(8,128)(2,1)}, bf16[144,512]{1,0:T(8,128)(2,1)S(1)}, u32[]{:S(2)}, u32[]{:S(2)}) collective-permute-start(bf16[144,512]{1,0:T(8,128)(2,1)} %get-tuple-element.38.refs_4_), channel_id=1, source_target_pairs={{0,192},{64,0},{128,64},{192,128},{1,193},{65,1},{129,65},{193,129... | collective-permute-start | bytes 442376 | tf_op jit(solution)/shard_map/ppermute | solution.py:294
  50.4 0.2 collective-permute-start.10
  50.7 3.3 %collective-permute-done.11.refs_8_ = bf16[144,512]{1,0:T(8,128)(2,1)S(1)} collective-permute-done((bf16[144,512]{1,0:T(8,128)(2,1)}, bf16[144,512]{1,0:T(8,128)(2,1)S(1)}, u32[]{:S(2)}, u32[]{:S(2)}) %collective-permute-start.11) | collective-permute-done | bytes 147488 | tf_op jit(solution)/shard_map/ppermute | solution.py:294
  54.0 3.0 %collective-permute-done.10.refs_5_ = bf16[144,512]{1,0:T(8,128)(2,1)S(1)} collective-permute-done((bf16[144,512]{1,0:T(8,128)(2,1)}, bf16[144,512]{1,0:T(8,128)(2,1)S(1)}, u32[]{:S(2)}, u32[]{:S(2)}) %collective-permute-start.10) | collective-permute-done | bytes 147488 | tf_op jit(solution)/shard_map/ppermute | solution.py:294
  57.0 1.4 %collective-permute-done.12.refs_10_ = bf16[144,512]{1,0:T(8,128)(2,1)S(1)} collective-permute-done((bf16[144,512]{1,0:T(8,128)(2,1)S(1)}, bf16[144,512]{1,0:T(8,128)(2,1)S(1)}, u32[]{:S(2)}, u32[]{:S(2)}) %collective-permute-start.12) | collective-permute-done | bytes 147488 | tf_op jit(solution)/shard_map/ppermute | solution.py:294
  58.4 0.8 all-to-all-done.parts
  59.1 0.7 add_up.1
  59.9 6.4 %all-to-all-start.1 = ((bf16[8,128,128]{2,1,0:T(8,128)(2,1)}), bf16[8,128,128]{2,1,0:T(8,128)(2,1)S(1)}, u32[]{:S(2)}, u32[]{:S(2)}) async-start(bf16[8,128,128]{2,1,0:T(8,128)(2,1)} %add_up.1), calls=%async_computation.1 | async-start | bytes 524288 | tf_op jit(solution)/shard_map/all_to_all | solution.py:361
  66.3 0.3 collective-permute-start.14
  66.6 3.2 %collective-permute-start.15 = (bf16[64,512]{1,0:T(8,128)(2,1)S(1)}, bf16[64,512]{1,0:T(8,128)(2,1)S(1)}, u32[]{:S(2)}, u32[]{:S(2)}) collective-permute-start(bf16[64,512]{1,0:T(8,128)(2,1)S(1)} %slice.7), channel_id=1, source_target_pairs={{0,192},{64,0},{128,64},{192,128},{1,193},{65,1},{129,65},{193,129... | collective-permute-start | bytes 196616 | tf_op jit(solution)/shard_map/ppermute | solution.py:294
  69.8 1.9 %collective-permute-done.15.refs_7_ = bf16[64,512]{1,0:T(8,128)(2,1)S(1)} collective-permute-done((bf16[64,512]{1,0:T(8,128)(2,1)S(1)}, bf16[64,512]{1,0:T(8,128)(2,1)S(1)}, u32[]{:S(2)}, u32[]{:S(2)}) %collective-permute-start.15) | collective-permute-done | bytes 65568 | tf_op jit(solution)/shard_map/ppermute | solution.py:294
  71.7 0.5 collective-permute-done.14.refs_6_
  72.2 0.1 pad_add_fusion.place
  72.3 0.7 collective-permute-done.17.refs_12_
  73.0 0.5 collective-permute-done.16.refs_11_
  73.5 5.0 %all-to-all-done.1.sketches = bf16[8,128,128]{2,1,0:T(8,128)(2,1)S(1)} async-done(((bf16[8,128,128]{2,1,0:T(8,128)(2,1)}), bf16[8,128,128]{2,1,0:T(8,128)(2,1)S(1)}, u32[]{:S(2)}, u32[]{:S(2)}) %all-to-all-start.1) | async-done | bytes 262176 | tf_op jit(solution)/shard_map/all_to_all | solution.py:361
  78.5 0.9 copy-done.2
  79.4 0.9 copy-done.3
  80.3 5.0 %second_pass.1 = (bf16[1024,128]{1,0:T(8,128)(2,1)}, f32[96,128]{1,0:T(8,128)S(1)}, f32[96,128]{1,0:T(8,128)S(1)}, f32[96,128]{1,0:T(8,128)S(1)}, f32[96,128]{1,0:T(8,128)S(1)}) custom-call(s32[3]{0:T(128)S(1)} %pad_add_fusion.place, bf16[8,128,128]{2,1,0:T(8,128)(2,1)S(1)} %all-to-all-done.1.sketches, bf16[256,1024]{1,0:T(8,128)(2,1)S(1)} %copy-done.1, ...), custom_call_target="tpu_custom_call" | custom-call | tf_op jit(solution)/shard_map/second_pass/pallas_call | solution.py:364
  85.4 5.3 %all-to-all-start.2 = ((bf16[32,32,128]{2,1,0:T(8,128)(2,1)}), bf16[32,32,128]{2,1,0:T(8,128)(2,1)S(1)}, u32[]{:S(2)}, u32[]{:S(2)}) async-start(bf16[32,32,128]{2,1,0:T(8,128)(2,1)} %bitcast.19), calls=%async_computation.2 | async-start | bytes 524288 | tf_op jit(solution)/shard_map/all_to_all | solution.py:374
  90.7 1.9 %collective-permute-start.18 = (f32[96,128]{1,0:T(8,128)S(1)}, f32[96,128]{1,0:T(8,128)S(1)}, u32[]{:S(2)}, u32[]{:S(2)}) collective-permute-start(f32[96,128]{1,0:T(8,128)S(1)} %get-tuple-element.47), channel_id=1, source_target_pairs={{0,64},{64,128},{128,192},{192,0},{1,65},{65,129},{129,193},{193,1... | collective-permute-start | bytes 147464 | tf_op jit(solution)/shard_map/ppermute | solution.py:294
  92.5 2.7 %collective-permute-start.19 = (f32[96,128]{1,0:T(8,128)S(1)}, f32[96,128]{1,0:T(8,128)S(1)}, u32[]{:S(2)}, u32[]{:S(2)}) collective-permute-start(f32[96,128]{1,0:T(8,128)S(1)} %get-tuple-element.48), channel_id=1, source_target_pairs={{0,128},{64,192},{128,0},{192,64},{1,129},{65,193},{129,1},{193,65... | collective-permute-start | bytes 147464 | tf_op jit(solution)/shard_map/ppermute | solution.py:294
  95.2 1.4 %collective-permute-start.20 = (f32[96,128]{1,0:T(8,128)S(1)}, f32[96,128]{1,0:T(8,128)S(1)}, u32[]{:S(2)}, u32[]{:S(2)}) collective-permute-start(f32[96,128]{1,0:T(8,128)S(1)} %get-tuple-element.49), channel_id=1, source_target_pairs={{0,192},{64,0},{128,64},{192,128},{1,193},{65,1},{129,65},{193,129... | collective-permute-start | bytes 147464 | tf_op jit(solution)/shard_map/ppermute | solution.py:294
  96.7 1.8 %collective-permute-done.19.refs_2_ = f32[96,128]{1,0:T(8,128)S(1)} collective-permute-done((f32[96,128]{1,0:T(8,128)S(1)}, f32[96,128]{1,0:T(8,128)S(1)}, u32[]{:S(2)}, u32[]{:S(2)}) %collective-permute-start.19) | collective-permute-done | bytes 49184 | tf_op jit(solution)/shard_map/ppermute | solution.py:294
  98.5 1.3 %collective-permute-done.20.refs_3_ = f32[96,128]{1,0:T(8,128)S(1)} collective-permute-done((f32[96,128]{1,0:T(8,128)S(1)}, f32[96,128]{1,0:T(8,128)S(1)}, u32[]{:S(2)}, u32[]{:S(2)}) %collective-permute-start.20) | collective-permute-done | bytes 49184 | tf_op jit(solution)/shard_map/ppermute | solution.py:294
  99.8 3.5 %all-to-all-done.2.parts = bf16[32,32,128]{2,1,0:T(8,128)(2,1)S(1)} async-done(((bf16[32,32,128]{2,1,0:T(8,128)(2,1)}), bf16[32,32,128]{2,1,0:T(8,128)(2,1)S(1)}, u32[]{:S(2)}, u32[]{:S(2)}) %all-to-all-start.2) | async-done | bytes 262176 | tf_op jit(solution)/shard_map/all_to_all | solution.py:374
  103.3 1.8 %finish.1 = (f32[8,32,64]{2,1,0:T(8,128)}, f32[8,32,64]{2,1,0:T(8,128)}) custom-call(s32[3]{0:T(128)S(1)} %pad_add_fusion.place, bf16[32,32,128]{2,1,0:T(8,128)(2,1)S(1)} %all-to-all-done.2.parts, f32[96,128]{1,0:T(8,128)S(1)} %get-tuple-element.46.refs_0_, f32[96,128]{1,0:T(8,128)S(1)} %collective-permute-done.18.refs_1_, ...), custom_call_target="tpu_custom_call" | custom-call | tf_op jit(solution)/shard_map/finish/pallas_call | solution.py:377
  (30 shorter events, 0.1 us)
Async XLA Ops:
  0.6 10.4 %copy-start.8 = (bf16[2,64,128]{2,1,0:T(8,128)(2,1)S(1)}, bf16[2,64,128]{2,1,0:T(8,128)(2,1)}, u32[]{:S(2)}) copy-start(bf16[2,64,128]{2,1,0:T(8,128)(2,1)} %param.11) | copy-start | bytes 98308
  5.1 73.4 %copy-start.1 = (bf16[256,1024]{1,0:T(8,128)(2,1)S(1)}, bf16[256,1024]{1,0:T(8,128)(2,1)}, u32[]{:S(2)}) copy-start(bf16[256,1024]{1,0:T(8,128)(2,1)} %get-tuple-element.27.refs_0_) | copy-start | bytes 1572868
  5.1 32.9 %collective-permute-start.4 = (bf16[256,1024]{1,0:T(8,128)(2,1)}, bf16[256,1024]{1,0:T(8,128)(2,1)S(1)}, u32[]{:S(2)}, u32[]{:S(2)}) collective-permute-start(bf16[256,1024]{1,0:T(8,128)(2,1)} %get-tuple-element.28), channel_id=1, source_target_pairs={{0,64},{64,128},{128,192},{192,0},{1,65},{65,129},{129,193},{193,1... | collective-permute-start | bytes 1572872 | tf_op jit(solution)/shard_map/ppermute | solution.py:294
  6.8 31.2 %collective-permute-start.5 = (bf16[256,1024]{1,0:T(8,128)(2,1)}, bf16[256,1024]{1,0:T(8,128)(2,1)S(1)}, u32[]{:S(2)}, u32[]{:S(2)}) collective-permute-start(bf16[256,1024]{1,0:T(8,128)(2,1)} %get-tuple-element.29), channel_id=1, source_target_pairs={{0,128},{64,192},{128,0},{192,64},{1,129},{65,193},{129,1},{193,65... | collective-permute-start | bytes 1572872 | tf_op jit(solution)/shard_map/ppermute | solution.py:294
  9.9 28.2 %collective-permute-start.6 = (bf16[256,1024]{1,0:T(8,128)(2,1)}, bf16[256,1024]{1,0:T(8,128)(2,1)S(1)}, u32[]{:S(2)}, u32[]{:S(2)}) collective-permute-start(bf16[256,1024]{1,0:T(8,128)(2,1)} %get-tuple-element.30), channel_id=1, source_target_pairs={{0,192},{64,0},{128,64},{192,128},{1,193},{65,1},{129,65},{193,129... | collective-permute-start | bytes 1572872 | tf_op jit(solution)/shard_map/ppermute | solution.py:294
  11.0 1.2 %collective-permute-start = (bf16[128,128]{1,0:T(8,128)(2,1)S(1)}, bf16[128,128]{1,0:T(8,128)(2,1)S(1)}, u32[]{:S(2)}, u32[]{:S(2)}) collective-permute-start(bf16[128,128]{1,0:T(8,128)(2,1)S(1)} %bitcast.25), channel_id=1, source_target_pairs={{0,1},{1,0},{2,3},{3,2},{4,5},{5,4},{6,7},{7,6},{8,9},{9,8},{10,11... | collective-permute-start | bytes 98312 | tf_op jit(solution)/shard_map/ppermute | solution.py:294
  12.3 11.2 %copy-start.4 = (bf16[2,128,128]{2,1,0:T(8,128)(2,1)}, bf16[2,128,128]{2,1,0:T(8,128)(2,1)S(1)}, u32[]{:S(2)}) copy-start(bf16[2,128,128]{2,1,0:T(8,128)(2,1)S(1)} %pad_maximum_fusion.refs_0_) | copy-start | bytes 196612
  12.3 7.0 %collective-permute-start.3 = (bf16[2,128,128]{2,1,0:T(8,128)(2,1)S(1)}, bf16[2,128,128]{2,1,0:T(8,128)(2,1)S(1)}, u32[]{:S(2)}, u32[]{:S(2)}) collective-permute-start(bf16[2,128,128]{2,1,0:T(8,128)(2,1)S(1)} %pad_maximum_fusion.refs_0_), channel_id=1, source_target_pairs={{0,6},{2,0},{4,2},{6,4},{1,7},{3,1},{5,3},{7,5},{8,14},{10,8},{12,... | collective-permute-start | bytes 196616 | tf_op jit(solution)/shard_map/ppermute | solution.py:294
  13.2 6.7 %collective-permute-start.2 = (bf16[2,128,128]{2,1,0:T(8,128)(2,1)S(1)}, bf16[2,128,128]{2,1,0:T(8,128)(2,1)S(1)}, u32[]{:S(2)}, u32[]{:S(2)}) collective-permute-start(bf16[2,128,128]{2,1,0:T(8,128)(2,1)S(1)} %pad_maximum_fusion.refs_0_), channel_id=1, source_target_pairs={{0,4},{2,6},{4,0},{6,2},{1,5},{3,7},{5,1},{7,3},{8,12},{10,14},{12... | collective-permute-start | bytes 196616 | tf_op jit(solution)/shard_map/ppermute | solution.py:294
  19.2 4.3 %copy-start.5 = (bf16[2,128,128]{2,1,0:T(8,128)(2,1)}, bf16[2,128,128]{2,1,0:T(8,128)(2,1)S(1)}, u32[]{:S(2)}) copy-start(bf16[2,128,128]{2,1,0:T(8,128)(2,1)S(1)} %collective-permute-done.3.refs_3_) | copy-start | bytes 196612
  19.2 4.3 %collective-permute-start.1 = (bf16[2,128,128]{2,1,0:T(8,128)(2,1)S(1)}, bf16[2,128,128]{2,1,0:T(8,128)(2,1)S(1)}, u32[]{:S(2)}, u32[]{:S(2)}) collective-permute-start(bf16[2,128,128]{2,1,0:T(8,128)(2,1)S(1)} %pad_maximum_fusion.refs_0_), channel_id=1, source_target_pairs={{0,2},{2,4},{4,6},{6,0},{1,3},{3,5},{5,7},{7,1},{8,10},{10,12},{12... | collective-permute-start | bytes 196616 | tf_op jit(solution)/shard_map/ppermute | solution.py:294
  19.9 3.6 %copy-start.6 = (bf16[2,128,128]{2,1,0:T(8,128)(2,1)}, bf16[2,128,128]{2,1,0:T(8,128)(2,1)S(1)}, u32[]{:S(2)}) copy-start(bf16[2,128,128]{2,1,0:T(8,128)(2,1)S(1)} %collective-permute-done.2.refs_2_) | copy-start | bytes 196612
  23.5 0.6 copy-start.7
  27.4 6.5 %collective-permute-start.7 = (bf16[128,128]{1,0:T(8,128)(2,1)}, bf16[128,128]{1,0:T(8,128)(2,1)S(1)}, u32[]{:S(2)}, u32[]{:S(2)}) collective-permute-start(bf16[128,128]{1,0:T(8,128)(2,1)} %get-tuple-element.34), channel_id=1, source_target_pairs={{0,64},{64,128},{128,192},{192,0},{1,65},{65,129},{129,193},{193,1... | collective-permute-start | bytes 98312 | tf_op jit(solution)/shard_map/ppermute | solution.py:294
  28.1 7.2 %collective-permute-start.8 = (bf16[128,128]{1,0:T(8,128)(2,1)}, bf16[128,128]{1,0:T(8,128)(2,1)S(1)}, u32[]{:S(2)}, u32[]{:S(2)}) collective-permute-start(bf16[128,128]{1,0:T(8,128)(2,1)} %get-tuple-element.35), channel_id=1, source_target_pairs={{0,128},{64,192},{128,0},{192,64},{1,129},{65,193},{129,1},{193,65... | collective-permute-start | bytes 98312 | tf_op jit(solution)/shard_map/ppermute | solution.py:294
  33.9 4.1 %collective-permute-start.9 = (bf16[128,128]{1,0:T(8,128)(2,1)}, bf16[128,128]{1,0:T(8,128)(2,1)S(1)}, u32[]{:S(2)}, u32[]{:S(2)}) collective-permute-start(bf16[128,128]{1,0:T(8,128)(2,1)} %get-tuple-element.36), channel_id=1, source_target_pairs={{0,192},{64,0},{128,64},{192,128},{1,193},{65,1},{129,65},{193,129... | collective-permute-start | bytes 98312 | tf_op jit(solution)/shard_map/ppermute | solution.py:294
  38.0 1.0 copy-start
  40.2 18.9 %all-to-all-start = ((bf16[8,128,128]{2,1,0:T(8,128)(2,1)}), bf16[8,128,128]{2,1,0:T(8,128)(2,1)S(1)}, u32[]{:S(2)}, u32[]{:S(2)}) async-start(bf16[8,128,128]{2,1,0:T(8,128)(2,1)} %first_pass.1), calls=%async_computation | async-start | bytes 524288 | tf_op jit(solution)/shard_map/all_to_all | solution.py:347
  48.6 5.4 %collective-permute-start.11 = (bf16[144,512]{1,0:T(8,128)(2,1)}, bf16[144,512]{1,0:T(8,128)(2,1)S(1)}, u32[]{:S(2)}, u32[]{:S(2)}) collective-permute-start(bf16[144,512]{1,0:T(8,128)(2,1)} %get-tuple-element.38.refs_4_), channel_id=1, source_target_pairs={{0,192},{64,0},{128,64},{192,128},{1,193},{65,1},{129,65},{193,129... | collective-permute-start | bytes 442376 | tf_op jit(solution)/shard_map/ppermute | solution.py:294
  50.4 6.6 %collective-permute-start.10 = (bf16[144,512]{1,0:T(8,128)(2,1)}, bf16[144,512]{1,0:T(8,128)(2,1)S(1)}, u32[]{:S(2)}, u32[]{:S(2)}) collective-permute-start(bf16[144,512]{1,0:T(8,128)(2,1)} %get-tuple-element.38.refs_4_), channel_id=1, source_target_pairs={{0,64},{64,128},{128,192},{192,0},{1,65},{65,129},{129,193},{193,1... | collective-permute-start | bytes 442376 | tf_op jit(solution)/shard_map/ppermute | solution.py:294
  54.0 3.0 %collective-permute-start.13 = (bf16[144,512]{1,0:T(8,128)(2,1)S(1)}, bf16[144,512]{1,0:T(8,128)(2,1)S(1)}, u32[]{:S(2)}, u32[]{:S(2)}) collective-permute-start(bf16[144,512]{1,0:T(8,128)(2,1)S(1)} %collective-permute-done.11.refs_8_), channel_id=1, source_target_pairs={{0,1},{1,0},{2,3},{3,2},{4,5},{5,4},{6,7},{7,6},{8,9},{9,8},{10,11... | collective-permute-start | bytes 442376 | tf_op jit(solution)/shard_map/ppermute | solution.py:294
  57.0 1.4 %collective-permute-start.12 = (bf16[144,512]{1,0:T(8,128)(2,1)S(1)}, bf16[144,512]{1,0:T(8,128)(2,1)S(1)}, u32[]{:S(2)}, u32[]{:S(2)}) collective-permute-start(bf16[144,512]{1,0:T(8,128)(2,1)S(1)} %collective-permute-done.10.refs_5_), channel_id=1, source_target_pairs={{0,1},{1,0},{2,3},{3,2},{4,5},{5,4},{6,7},{7,6},{8,9},{9,8},{10,11... | collective-permute-start | bytes 442376 | tf_op jit(solution)/shard_map/ppermute | solution.py:294
  59.9 18.6 %all-to-all-start.1 = ((bf16[8,128,128]{2,1,0:T(8,128)(2,1)}), bf16[8,128,128]{2,1,0:T(8,128)(2,1)S(1)}, u32[]{:S(2)}, u32[]{:S(2)}) async-start(bf16[8,128,128]{2,1,0:T(8,128)(2,1)} %add_up.1), calls=%async_computation.1 | async-start | bytes 524288 | tf_op jit(solution)/shard_map/all_to_all | solution.py:361
  66.3 5.9 %collective-permute-start.14 = (bf16[80,512]{1,0:T(8,128)(2,1)S(1)}, bf16[80,512]{1,0:T(8,128)(2,1)S(1)}, u32[]{:S(2)}, u32[]{:S(2)}) collective-permute-start(bf16[80,512]{1,0:T(8,128)(2,1)S(1)} %slice.6), channel_id=1, source_target_pairs={{0,64},{64,128},{128,192},{192,0},{1,65},{65,129},{129,193},{193,1... | collective-permute-start | bytes 245768 | tf_op jit(solution)/shard_map/ppermute | solution.py:294
  66.6 5.1 %collective-permute-start.15 = (bf16[64,512]{1,0:T(8,128)(2,1)S(1)}, bf16[64,512]{1,0:T(8,128)(2,1)S(1)}, u32[]{:S(2)}, u32[]{:S(2)}) collective-permute-start(bf16[64,512]{1,0:T(8,128)(2,1)S(1)} %slice.7), channel_id=1, source_target_pairs={{0,192},{64,0},{128,64},{192,128},{1,193},{65,1},{129,65},{193,129... | collective-permute-start | bytes 196616 | tf_op jit(solution)/shard_map/ppermute | solution.py:294
  71.7 1.3 %collective-permute-start.17 = (bf16[64,512]{1,0:T(8,128)(2,1)S(1)}, bf16[64,512]{1,0:T(8,128)(2,1)S(1)}, u32[]{:S(2)}, u32[]{:S(2)}) collective-permute-start(bf16[64,512]{1,0:T(8,128)(2,1)S(1)} %collective-permute-done.15.refs_7_), channel_id=1, source_target_pairs={{0,1},{1,0},{2,3},{3,2},{4,5},{5,4},{6,7},{7,6},{8,9},{9,8},{10,11... | collective-permute-start | bytes 196616 | tf_op jit(solution)/shard_map/ppermute | solution.py:294
  72.2 1.3 %collective-permute-start.16 = (bf16[80,512]{1,0:T(8,128)(2,1)S(1)}, bf16[80,512]{1,0:T(8,128)(2,1)S(1)}, u32[]{:S(2)}, u32[]{:S(2)}) collective-permute-start(bf16[80,512]{1,0:T(8,128)(2,1)S(1)} %collective-permute-done.14.refs_6_), channel_id=1, source_target_pairs={{0,1},{1,0},{2,3},{3,2},{4,5},{5,4},{6,7},{7,6},{8,9},{9,8},{10,11... | collective-permute-start | bytes 245768 | tf_op jit(solution)/shard_map/ppermute | solution.py:294
  78.5 0.9 copy-start.2
  79.4 0.9 copy-start.3
  85.4 18.0 %all-to-all-start.2 = ((bf16[32,32,128]{2,1,0:T(8,128)(2,1)}), bf16[32,32,128]{2,1,0:T(8,128)(2,1)S(1)}, u32[]{:S(2)}, u32[]{:S(2)}) async-start(bf16[32,32,128]{2,1,0:T(8,128)(2,1)} %bitcast.19), calls=%async_computation.2 | async-start | bytes 524288 | tf_op jit(solution)/shard_map/all_to_all | solution.py:374
  90.7 6.0 %collective-permute-start.18 = (f32[96,128]{1,0:T(8,128)S(1)}, f32[96,128]{1,0:T(8,128)S(1)}, u32[]{:S(2)}, u32[]{:S(2)}) collective-permute-start(f32[96,128]{1,0:T(8,128)S(1)} %get-tuple-element.47), channel_id=1, source_target_pairs={{0,64},{64,128},{128,192},{192,0},{1,65},{65,129},{129,193},{193,1... | collective-permute-start | bytes 147464 | tf_op jit(solution)/shard_map/ppermute | solution.py:294
  92.5 6.0 %collective-permute-start.19 = (f32[96,128]{1,0:T(8,128)S(1)}, f32[96,128]{1,0:T(8,128)S(1)}, u32[]{:S(2)}, u32[]{:S(2)}) collective-permute-start(f32[96,128]{1,0:T(8,128)S(1)} %get-tuple-element.48), channel_id=1, source_target_pairs={{0,128},{64,192},{128,0},{192,64},{1,129},{65,193},{129,1},{193,65... | collective-permute-start | bytes 147464 | tf_op jit(solution)/shard_map/ppermute | solution.py:294
  95.2 4.5 %collective-permute-start.20 = (f32[96,128]{1,0:T(8,128)S(1)}, f32[96,128]{1,0:T(8,128)S(1)}, u32[]{:S(2)}, u32[]{:S(2)}) collective-permute-start(f32[96,128]{1,0:T(8,128)S(1)} %get-tuple-element.49), channel_id=1, source_target_pairs={{0,192},{64,0},{128,64},{192,128},{1,193},{65,1},{129,65},{193,129... | collective-permute-start | bytes 147464 | tf_op jit(solution)/shard_map/ppermute | solution.py:294

commit v8 on v7

--- a/solution.py
+++ b/solution.py
@@ -82,20 +82,25 @@
     groups = len(out)
     each = pairs // groups
     here = lax.axis_index("y")
-    stores = [pltpu.make_async_copy(kept.at[s], out[s], sems.at[6 + s]) for s in range(groups)]
-    for s in [*range(1, groups), 0]:
+    stores = [pltpu.make_async_copy(kept.at[s - 1], out[s], sems.at[5 + s]) for s in range(1, groups)]
+    direct = [
+        pltpu.make_async_copy(acc.at[here * each + i], out[0].at[pl.ds(i * rank, rank)], sems.at[5 + groups + i])
+        for i in range(each)
+    ]
+    for i in range(each):
+        direct[i].start()
+    for s in range(1, groups):
         owner = lax.rem(here + s, groups)
         for i in range(each):
-            kept[s, i * rank : (i + 1) * rank, :] = acc[owner * each + i].astype(BF)
-        stores[s].start()
-    for copy in stores:
+            kept[s - 1, i * rank : (i + 1) * rank, :] = acc[owner * each + i].astype(BF)
+        stores[s - 1].start()
+    for copy in direct + stores:
         copy.wait()
 
 
 def project(columns, *refs):
     pieces, refs = refs[:4], refs[4:]
-    probes, coupling, mine, other = refs[:4]
-    sent, (shared, table) = refs[4:-2], refs[-2:]
+    probes, coupling, mine, coefficients, shared = refs
     rows = pieces[0].shape[1]
     at = 0
     for piece in pieces:
@@ -110,31 +115,30 @@
         [jnp.concatenate([first, zero], axis=1), jnp.concatenate([zero, second], axis=1)], axis=0
     )
     projected = lax.dot_general(probes[...], shared[0:rows, :], NT, preferred_element_type=F32)
-    table[...] = lax.dot_general(projected, diagonal, NT, precision=HIGHEST, preferred_element_type=F32)
-    each = sent[0].shape[0]
-    for s in range(len(sent)):
-        owner = lax.rem(columns[at] + s, len(sent))
-        sent[s][...] = table[pl.ds(pl.multiple_of(owner * each, each), each), :].astype(sent[s].dtype)
+    found = lax.dot_general(projected, diagonal, NT, precision=HIGHEST, preferred_element_type=F32).astype(BF)
+    each = coefficients.shape[1]
+    for g in range(coefficients.shape[0]):
+        coefficients[g] = found[g * each : (g + 1) * each]
     high, low = split_bf(jnp.concatenate([first, second], axis=1), 2)
     shared[rows : rows + TAIL, :] = jnp.concatenate([pack_rows(high), pack_rows(low)], axis=1)
     half = mine.shape[1]
-    core = columns[at + 1]
-    mine[...] = shared[:, pl.ds(pl.multiple_of(core * half, half), half)]
-    other[...] = shared[:, pl.ds(pl.multiple_of((1 - core) * half, half), half)]
+    mine[...] = shared[:, pl.ds(pl.multiple_of(columns[at] * half, half), half)].astype(F32)
 
 
 def first_pass(*refs):
-    groups = len(refs) // 2
-    held, coefficients, out = refs[:groups], refs[groups:-1], refs[-1]
+    held, (coefficients, out) = refs[:-2], refs[-2:]
+    groups = len(held)
+    here = lax.axis_index("y")
     rows, width = held[0].shape
     targets = rows // LANES
     rank = out.shape[1] // targets
     cut = out.shape[2]
     totals = [jnp.zeros((rank, width), F32) for _ in range(targets)]
     for s in range(groups):
+        source = lax.rem(here + groups - s, groups)
         for t in range(targets):
             totals[t] = totals[t] + jnp.dot(
-                coefficients[s][t * rank : (t + 1) * rank, :],
+                coefficients[source, t * rank : (t + 1) * rank, :],
                 held[s][t * LANES : (t + 1) * LANES, :],
                 preferred_element_type=F32,
             )
@@ -184,7 +188,7 @@
 def second_pass(place, sketches, *refs):
     held, refs = refs[:4], refs[4:]
     groups = len(held)
-    out, sent, turned = refs[10], refs[11:-1], refs[-1]
+    out, sent, (turned, kept, sems) = refs[10], refs[11:-3], refs[-3:]
     cuts, rows, cut = sketches.shape
     width = held[0].shape[1]
     targets = held[0].shape[0] // LANES
@@ -244,8 +248,13 @@
         start = owner * (width // groups) + place[1] * own
         piece = start // cut
         turned[...] = sketches[piece].astype(F32).T
-        sent[s][0:rank, :] = inverses
-        sent[s][rank : rank + own, :] = turned[pl.ds(pl.multiple_of(start - piece * cut, 32), own), :]
+        kept[s, 0:rank, :] = inverses
+        kept[s, rank : rank + own, :] = turned[pl.ds(pl.multiple_of(start - piece * cut, 32), own), :]
+    copies = [pltpu.make_async_copy(kept.at[s], sent[s], sems.at[s]) for s in range(groups)]
+    for copy in copies:
+        copy.start()
+    for copy in copies:
+        copy.wait()
 
 
 def finish(place, parts, *refs):
@@ -295,61 +304,65 @@
 
     sums = pl.pallas_call(
         sum_factors,
-        out_shape=(jax.ShapeDtypeStruct((held_rows, width), BF),) * ny,
+        out_shape=(jax.ShapeDtypeStruct((held_rows, width), F32),)
+        + (jax.ShapeDtypeStruct((held_rows, width), BF),) * (ny - 1),
         in_specs=[in_any] * 4,
         out_specs=(in_any,) * ny,
         scratch_shapes=[
             VMEM((slots, rank, width), BF),
             VMEM((targets * panels, rank, width), F32),
-            VMEM((ny, held_rows, width), BF),
+            VMEM((ny - 1, held_rows, width), BF),
             SMEM((slots,), jnp.int32),
             SMEM((slots,), jnp.int32),
             SMEM((1,), jnp.int32),
-            pltpu.SemaphoreType.DMA((6 + ny,)),
+            pltpu.SemaphoreType.DMA((5 + ny + mine * panels,)),
             pltpu.SemaphoreType.DMA((3,)),
         ],
         compiler_params=params(56),
         cost_estimate=pl.CostEstimate(flops=10**7, bytes_accessed=7 * 10**6, transcendentals=0),
         name="sum_factors",
     )(entry_panel[:, 0], entry_target[:, 0], entry_count[0], factors)
-    held = [sums[0]] + [turn(sums[s], "y", ny, s) for s in range(1, ny)]
+    held = [sums[0].astype(BF)] + [turn(sums[s], "y", ny, s) for s in range(1, ny)]
 
     own, _ = lax.optimization_barrier((panel_shared.reshape(rows, LANES), sums))
     pair = jnp.stack([own, turn(own, "core", nc, 1)])
     pieces = [pair] + [turn(pair, "x", nx, s) for s in range(1, nx)]
     columns = jnp.stack(
-        [((x + nx - s) % nx) * nc + k for s in range(nx) for k in (c, (c + 1) % nc)] + [y, c]
+        [((x + nx - s) % nx) * nc + k for s in range(nx) for k in (c, (c + 1) % nc)] + [c]
     ).astype(jnp.int32)
-    mine_half, other_half, *sent = pl.pallas_call(
+    mine_half, found = pl.pallas_call(
         project,
-        out_shape=(jax.ShapeDtypeStruct((rows + TAIL, width // 2), BF),) * 2
-        + (jax.ShapeDtypeStruct((own_rows, rows), F32),)
-        + (jax.ShapeDtypeStruct((own_rows, rows), BF),) * (ny - 1),
+        out_shape=(
+            jax.ShapeDtypeStruct((rows + TAIL, width // 2), F32),
+            jax.ShapeDtypeStruct((ny, own_rows, rows), BF),
+        ),
         in_specs=[in_smem] + [in_vmem] * (nx + 2),
-        out_specs=(in_vmem,) * (ny + 2),
-        scratch_shapes=[VMEM((rows + TAIL, width), BF), VMEM((targets * rank, rows), F32)],
+        out_specs=(in_vmem,) * 2,
+        scratch_shapes=[VMEM((rows + TAIL, width), BF)],
         compiler_params=params(60),
         name="project",
     )(columns, *pieces, probes.reshape(targets * rank, width), coupling)
-    coefficients = [sent[0].astype(BF)] + [turn(sent[s], "y", ny, s) for s in range(1, ny)]
+    coefficients = lax.all_to_all(found, "y", 0, 0, tiled=True)
+    mine_half = mine_half.astype(BF)
 
     cut = width // nz
     sketch = pl.pallas_call(
         first_pass,
         out_shape=jax.ShapeDtypeStruct((nz, own_rows, cut), BF),
-        in_specs=[in_vmem] * (2 * ny),
+        in_specs=[in_vmem] * (ny + 1),
         out_specs=in_vmem,
         compiler_params=params(20),
         name="first_pass",
-    )(*held, *coefficients)
+    )(*held, coefficients)
     mine_half, sketch = lax.optimization_barrier((mine_half, sketch))
     near = [turn(mine_half, "y", ny, s) for s in (1, ny - 1)]
     parts = lax.all_to_all(sketch, "z", 0, 0, tiled=True)
-    crossed = [turn(h, "core", nc, 1) for h in near]
-    parts, near, crossed = lax.optimization_barrier((parts, near, crossed))
+    other_half = turn(mine_half, "core", nc, 1)
+    parts, near, other_half = lax.optimization_barrier((parts, near, other_half))
     far = [turn(near[0][:RELAY], "y", ny, 1), turn(near[1][RELAY:], "y", ny, ny - 1)]
-    far_crossed = [turn(h, "core", nc, 1) for h in far]
-    all_shared = [mine_half, near[0], *far, near[1], other_half, crossed[0], *far_crossed, crossed[1]]
+    near, far = lax.optimization_barrier((near, far))
+    halves = [near[0], *far, near[1]]
+    all_shared = [mine_half, *halves, other_half] + [turn(h, "core", nc, 1) for h in halves]
     copies = pl.pallas_call(
         add_up,
         out_shape=jax.ShapeDtypeStruct((nz, own_rows, cut), BF),
@@ -364,10 +377,14 @@
     rows_part, *sent = pl.pallas_call(
         second_pass,
         out_shape=(jax.ShapeDtypeStruct((width, own_rows), BF),)
-        + (jax.ShapeDtypeStruct((rank + keep, own_rows), F32),) * ny,
+        + (pltpu.HBM((rank + keep, own_rows), F32),) * ny,
         in_specs=[in_smem] + [in_vmem] * 15,
-        out_specs=(in_vmem,) * (ny + 1),
-        scratch_shapes=[VMEM((cut, own_rows), F32)],
+        out_specs=(in_vmem,) + (pl.BlockSpec(memory_space=pltpu.HBM),) * ny,
+        scratch_shapes=[
+            VMEM((cut, own_rows), F32),
+            VMEM((ny, rank + keep, own_rows), F32),
+            pltpu.SemaphoreType.DMA((ny,)),
+        ],
         compiler_params=params(20),
         name="second_pass",
     )(place, sketches, *held, *all_shared)

time: 106 us -> 103 us (0.972)
  waiting for transfers between devices: 41.2 us -> 35.4 us
  local copies, waits for them, and re-layouts: 4.13 us -> 2.1 us
  starting transfers between devices: 41.7 us -> 43.6 us
  other arithmetic: 0.93 us -> 2.36 us
    ppermute x21 -> x19, waiting for transfers between devices: 31.9 us -> 22.4 us  [turn(): lax.ppermute(value, axis, [(i, (i + by) % size) for i in range(size)])]
    all_to_all x0 -> x1, waiting for transfers between devices: none -> 3.65 us  [shards(): coefficients = lax.all_to_all(found, 'y', 0, 0, tiled=True)]
    all_to_all x0 -> x1, starting transfers between devices: none -> 3.33 us  [shards(): coefficients = lax.all_to_all(found, 'y', 0, 0, tiled=True)]
    unnamed x18 -> x12, local copies, waits for them, and re-layouts: 3.49 us -> 1.42 us
    convert_element_type x1 -> x2, other arithmetic: 0.84 us -> 2.28 us  [the longest x1 1.29 us: shards(): sums[0].astype(BF)]
    all_to_all x1, starting transfers between devices: 6.45 us -> 5.09 us  [shards(): sketches = lax.all_to_all(copies, 'z', 0, 0, tiled=True)]
    all_to_all x1, waiting for transfers between devices: 0.76 us -> 2.1 us  [shards(): parts = lax.all_to_all(sketch, 'z', 0, 0, tiled=True)]
    all_to_all x1, waiting for transfers between devices: 4.99 us -> 3.76 us  [shards(): sketches = lax.all_to_all(copies, 'z', 0, 0, tiled=True)]
  transfers between devices with their start and end apart: 24 -> 23, of which waited for: 17 -> 15; matrix products, arithmetic and copies ran while one was open for 1% -> 3% of each run, Pallas kernels for 3% -> 3%
where the time goes in v8:
time: 103 us; the launch traced here: 102 us
  starting transfers between devices  43.6 us (42%)
  waiting for transfers between devices  35.4 us (34%)
  Pallas kernels  16.7 us (16%)
  other arithmetic  2.36 us (2%)
  local copies, waits for them, and re-layouts  2.1 us (2%)
  between operations  1.41 us (1%)
    ppermute x19, waiting for transfers between devices, turn(): lax.ppermute(value, axis, [(i, (i + by) % size) for i in range(size)])  22.4 us
    ppermute x19, starting transfers between devices, turn(): lax.ppermute(value, axis, [(i, (i + by) % size) for i in range(size)])  20.4 us
    all_to_all x1, starting transfers between devices, shards(): parts = lax.all_to_all(sketch, 'z', 0, 0, tiled=True)  8.46 us
    all_to_all x1, starting transfers between devices, shards(): lax.all_to_all(rows_part.reshape(ny * nz, keep, own_rows), ('y', 'z'), 0,...  6.4 us
    pallas_call x1, Pallas kernels, shards(): pl.pallas_call(second_pass, out_shape=(jax.ShapeDtypeStruct((width, own_r...  5.86 us
    all_to_all x1, starting transfers between devices, shards(): sketches = lax.all_to_all(copies, 'z', 0, 0, tiled=True)  5.09 us
    pallas_call x1, Pallas kernels, shards(): pl.pallas_call(sum_factors, out_shape=(jax.ShapeDtypeStruct((held_rows, w...  3.94 us
    all_to_all x1, waiting for transfers between devices, shards(): sketches = lax.all_to_all(copies, 'z', 0, 0, tiled=True)  3.76 us
  transfers between devices with their start and end apart: 23, of which 15 were waited for; matrix products, arithmetic and copies ran while one was open for 3% of the time, Pallas kernels for 3%

profile of v8, /device:TPU:6, one launch (start us, length us, event | category | flops | bytes accessed | tf_op | source)
XLA Modules:
  0.0 101.6 jit_solution(12628504547638833061)
XLA Ops:
  1.3 3.9 %sum_factors.1 = (f32[256,1024]{1,0:T(8,128)}, bf16[256,1024]{1,0:T(8,128)(2,1)}, bf16[256,1024]{1,0:T(8,128)(2,1)}, bf16[256,1024]{1,0:T(8,128)(2,1)}) custom-call(s32[36]{0:T(128)} %bitcast.28, s32[36]{0:T(128)} %bitcast.29, s32[1]{0:T(128)} %bitcast.22.count, bf16[36,64,1024]{2,1,0:T(8,128)(2,1)} %bitcast.23), custom_call_target="tpu_custom_call" | custom-call | flops 10000000 | bytes 7000000 | tf_op jit(solution)/shard_map/sum_factors/pallas_call | solution.py:305
  5.2 1.7 %collective-permute-start.4 = (bf16[256,1024]{1,0:T(8,128)(2,1)}, bf16[256,1024]{1,0:T(8,128)(2,1)S(1)}, u32[]{:S(2)}, u32[]{:S(2)}) collective-permute-start(bf16[256,1024]{1,0:T(8,128)(2,1)} %get-tuple-element.27), channel_id=1, source_target_pairs={{0,64},{64,128},{128,192},{192,0},{1,65},{65,129},{129,193},{193,1... | collective-permute-start | bytes 1572872 | tf_op jit(solution)/shard_map/ppermute | solution.py:303
  6.9 2.9 %collective-permute-start.5 = (bf16[256,1024]{1,0:T(8,128)(2,1)}, bf16[256,1024]{1,0:T(8,128)(2,1)S(1)}, u32[]{:S(2)}, u32[]{:S(2)}) collective-permute-start(bf16[256,1024]{1,0:T(8,128)(2,1)} %get-tuple-element.28), channel_id=1, source_target_pairs={{0,128},{64,192},{128,0},{192,64},{1,129},{65,193},{129,1},{193,65... | collective-permute-start | bytes 1572872 | tf_op jit(solution)/shard_map/ppermute | solution.py:303
  9.8 1.3 %collective-permute-start.6 = (bf16[256,1024]{1,0:T(8,128)(2,1)}, bf16[256,1024]{1,0:T(8,128)(2,1)S(1)}, u32[]{:S(2)}, u32[]{:S(2)}) collective-permute-start(bf16[256,1024]{1,0:T(8,128)(2,1)} %get-tuple-element.29), channel_id=1, source_target_pairs={{0,192},{64,0},{128,64},{192,128},{1,193},{65,1},{129,65},{193,129... | collective-permute-start | bytes 1572872 | tf_op jit(solution)/shard_map/ppermute | solution.py:303
  11.2 1.2 %collective-permute-done = bf16[128,128]{1,0:T(8,128)(2,1)S(1)} collective-permute-done((bf16[128,128]{1,0:T(8,128)(2,1)S(1)}, bf16[128,128]{1,0:T(8,128)(2,1)S(1)}, u32[]{:S(2)}, u32[]{:S(2)}) %collective-permute-start) | collective-permute-done | bytes 32800 | tf_op jit(solution)/shard_map/ppermute | solution.py:303
  12.4 0.0 copy-start.1
  12.4 0.9 collective-permute-start.3
  13.3 1.1 %collective-permute-start.2 = (bf16[2,128,128]{2,1,0:T(8,128)(2,1)S(1)}, bf16[2,128,128]{2,1,0:T(8,128)(2,1)S(1)}, u32[]{:S(2)}, u32[]{:S(2)}) collective-permute-start(bf16[2,128,128]{2,1,0:T(8,128)(2,1)S(1)} %pad_maximum_fusion.refs_0_), channel_id=1, source_target_pairs={{0,4},{2,6},{4,0},{6,2},{1,5},{3,7},{5,1},{7,3},{8,12},{10,14},{12... | collective-permute-start | bytes 196616 | tf_op jit(solution)/shard_map/ppermute | solution.py:303
  14.4 4.9 %collective-permute-done.3.refs_3_ = bf16[2,128,128]{2,1,0:T(8,128)(2,1)S(1)} collective-permute-done((bf16[2,128,128]{2,1,0:T(8,128)(2,1)S(1)}, bf16[2,128,128]{2,1,0:T(8,128)(2,1)S(1)}, u32[]{:S(2)}, u32[]{:S(2)}) %collective-permute-start.3) | collective-permute-done | bytes 65568 | tf_op jit(solution)/shard_map/ppermute | solution.py:303
  19.3 0.7 stack.61.columns
  20.0 0.0 collective-permute-done.2.refs_2_
  20.0 3.6 %collective-permute-done.1.refs_1_ = bf16[2,128,128]{2,1,0:T(8,128)(2,1)S(1)} collective-permute-done((bf16[2,128,128]{2,1,0:T(8,128)(2,1)S(1)}, bf16[2,128,128]{2,1,0:T(8,128)(2,1)S(1)}, u32[]{:S(2)}, u32[]{:S(2)}) %collective-permute-start.1) | collective-permute-done | bytes 65568 | tf_op jit(solution)/shard_map/ppermute | solution.py:303
  23.6 0.6 copy-done.4
  24.2 3.2 %project.1 = (f32[144,512]{1,0:T(8,128)}, bf16[4,128,128]{2,1,0:T(8,128)(2,1)}) custom-call(s32[9]{0:T(128)} %stack.61.columns, bf16[2,128,128]{2,1,0:T(8,128)(2,1)} %copy-done.1, bf16[2,128,128]{2,1,0:T(8,128)(2,1)} %copy-done.4, bf16[2,128,128]{2,1,0:T(8,128)(2,1)} %copy-done.3, bf16[2,128,128]{2,1,0:T(8,128)(2,1)} %copy-done.2, ...), custom_call_target="tpu_custom_call" | custom-call | tf_op jit(solution)/shard_map/project/pallas_call | solution.py:333
  27.4 3.3 %all-to-all-start = ((bf16[4,128,128]{2,1,0:T(8,128)(2,1)}), bf16[4,128,128]{2,1,0:T(8,128)(2,1)S(1)}, u32[]{:S(2)}, u32[]{:S(2)}) async-start(bf16[4,128,128]{2,1,0:T(8,128)(2,1)} %get-tuple-element.32), calls=%async_computation | async-start | bytes 262144 | tf_op jit(solution)/shard_map/all_to_all | solution.py:345
  30.8 1.3 %convert_element_type.7.refs_0_ = bf16[256,1024]{1,0:T(8,128)(2,1)S(1)} convert(f32[256,1024]{1,0:T(8,128)} %get-tuple-element.26) | non-fusion elementwise | flops 262144 | bytes 1572864 | tf_op jit(solution)/shard_map/convert_element_type | solution.py:325
  32.1 1.0 convert_element_type.6.refs_4_
  33.0 3.7 %all-to-all-done.refs_4_ = bf16[4,128,128]{2,1,0:T(8,128)(2,1)S(1)} async-done(((bf16[4,128,128]{2,1,0:T(8,128)(2,1)}), bf16[4,128,128]{2,1,0:T(8,128)(2,1)S(1)}, u32[]{:S(2)}, u32[]{:S(2)}) %all-to-all-start) | async-done | bytes 131104 | tf_op jit(solution)/shard_map/all_to_all | solution.py:345
  36.7 1.1 %first_pass.1 = bf16[8,128,128]{2,1,0:T(8,128)(2,1)} custom-call(bf16[256,1024]{1,0:T(8,128)(2,1)S(1)} %convert_element_type.7.refs_0_, bf16[256,1024]{1,0:T(8,128)(2,1)S(1)} %collective-permute-done.4.refs_1_, bf16[256,1024]{1,0:T(8,128)(2,1)S(1)} %collective-permute-done.5.refs_2_, bf16[256,1024]{1,0:T(8,128)(2,1)S(1)} %collective-permute-done.6.refs_3_, ...), custom_call_target="tpu_custom_call" | custom-call | tf_op jit(solution)/shard_map/first_pass/pallas_call | solution.py:349
  37.8 8.5 %all-to-all-start.1 = ((bf16[8,128,128]{2,1,0:T(8,128)(2,1)}), bf16[8,128,128]{2,1,0:T(8,128)(2,1)S(1)}, u32[]{:S(2)}, u32[]{:S(2)}) async-start(bf16[8,128,128]{2,1,0:T(8,128)(2,1)} %first_pass.1), calls=%async_computation.1 | async-start | bytes 524288 | tf_op jit(solution)/shard_map/all_to_all | solution.py:359
  46.3 1.2 %collective-permute-start.8 = (bf16[144,512]{1,0:T(8,128)(2,1)S(1)}, bf16[144,512]{1,0:T(8,128)(2,1)S(1)}, u32[]{:S(2)}, u32[]{:S(2)}) collective-permute-start(bf16[144,512]{1,0:T(8,128)(2,1)S(1)} %convert_element_type.6.refs_4_), channel_id=1, source_target_pairs={{0,192},{64,0},{128,64},{192,128},{1,193},{65,1},{129,65},{193,129... | collective-permute-start | bytes 442376 | tf_op jit(solution)/shard_map/ppermute | solution.py:303
  47.6 0.9 collective-permute-start.7
  48.4 4.2 %collective-permute-done.8.refs_8_ = bf16[144,512]{1,0:T(8,128)(2,1)S(1)} collective-permute-done((bf16[144,512]{1,0:T(8,128)(2,1)S(1)}, bf16[144,512]{1,0:T(8,128)(2,1)S(1)}, u32[]{:S(2)}, u32[]{:S(2)}) %collective-permute-start.8) | collective-permute-done | bytes 147488 | tf_op jit(solution)/shard_map/ppermute | solution.py:303
  52.6 2.1 %collective-permute-done.7.refs_5_ = bf16[144,512]{1,0:T(8,128)(2,1)S(1)} collective-permute-done((bf16[144,512]{1,0:T(8,128)(2,1)S(1)}, bf16[144,512]{1,0:T(8,128)(2,1)S(1)}, u32[]{:S(2)}, u32[]{:S(2)}) %collective-permute-start.7) | collective-permute-done | bytes 147488 | tf_op jit(solution)/shard_map/ppermute | solution.py:303
  54.7 2.1 %all-to-all-done.1.parts = bf16[8,128,128]{2,1,0:T(8,128)(2,1)S(1)} async-done(((bf16[8,128,128]{2,1,0:T(8,128)(2,1)}), bf16[8,128,128]{2,1,0:T(8,128)(2,1)S(1)}, u32[]{:S(2)}, u32[]{:S(2)}) %all-to-all-start.1) | async-done | bytes 262176 | tf_op jit(solution)/shard_map/all_to_all | solution.py:359
  56.8 0.7 add_up.1
  57.5 5.1 %all-to-all-start.2 = ((bf16[8,128,128]{2,1,0:T(8,128)(2,1)}), bf16[8,128,128]{2,1,0:T(8,128)(2,1)S(1)}, u32[]{:S(2)}, u32[]{:S(2)}) async-start(bf16[8,128,128]{2,1,0:T(8,128)(2,1)} %add_up.1), calls=%async_computation.2 | async-start | bytes 524288 | tf_op jit(solution)/shard_map/all_to_all | solution.py:374
  62.6 0.1 collective-permute-start.10
  62.7 3.2 %collective-permute-start.11 = (bf16[64,512]{1,0:T(8,128)(2,1)S(1)}, bf16[64,512]{1,0:T(8,128)(2,1)S(1)}, u32[]{:S(2)}, u32[]{:S(2)}) collective-permute-start(bf16[64,512]{1,0:T(8,128)(2,1)S(1)} %slice.7), channel_id=1, source_target_pairs={{0,192},{64,0},{128,64},{192,128},{1,193},{65,1},{129,65},{193,129... | collective-permute-start | bytes 196616 | tf_op jit(solution)/shard_map/ppermute | solution.py:303
  65.9 1.9 %collective-permute-done.11.refs_7_ = bf16[64,512]{1,0:T(8,128)(2,1)S(1)} collective-permute-done((bf16[64,512]{1,0:T(8,128)(2,1)S(1)}, bf16[64,512]{1,0:T(8,128)(2,1)S(1)}, u32[]{:S(2)}, u32[]{:S(2)}) %collective-permute-start.11) | collective-permute-done | bytes 65568 | tf_op jit(solution)/shard_map/ppermute | solution.py:303
  67.8 0.5 collective-permute-done.10.refs_6_
  68.4 0.5 collective-permute-start.15
  68.9 0.0 collective-permute-start.14
  68.9 0.5 collective-permute-start.13
  69.4 0.1 pad_add_fusion.place
  69.4 0.7 collective-permute-done.14.refs_12_
  70.1 0.2 collective-permute-done.13.refs_11_
  70.3 3.8 %all-to-all-done.2.sketches = bf16[8,128,128]{2,1,0:T(8,128)(2,1)S(1)} async-done(((bf16[8,128,128]{2,1,0:T(8,128)(2,1)}), bf16[8,128,128]{2,1,0:T(8,128)(2,1)S(1)}, u32[]{:S(2)}, u32[]{:S(2)}) %all-to-all-start.2) | async-done | bytes 262176 | tf_op jit(solution)/shard_map/all_to_all | solution.py:374
  74.1 5.9 %second_pass.1 = (bf16[1024,128]{1,0:T(8,128)(2,1)}, f32[96,128]{1,0:T(8,128)}, f32[96,128]{1,0:T(8,128)}, f32[96,128]{1,0:T(8,128)}, f32[96,128]{1,0:T(8,128)}) custom-call(s32[3]{0:T(128)S(1)} %pad_add_fusion.place, bf16[8,128,128]{2,1,0:T(8,128)(2,1)S(1)} %all-to-all-done.2.sketches, bf16[256,1024]{1,0:T(8,128)(2,1)S(1)} %convert_element_type.7.refs_0_, ...), custom_call_target="tpu_custom_call" | custom-call | tf_op jit(solution)/shard_map/second_pass/pallas_call | solution.py:377
  79.9 6.4 %all-to-all-start.3 = ((bf16[32,32,128]{2,1,0:T(8,128)(2,1)}), bf16[32,32,128]{2,1,0:T(8,128)(2,1)S(1)}, u32[]{:S(2)}, u32[]{:S(2)}) async-start(bf16[32,32,128]{2,1,0:T(8,128)(2,1)} %bitcast.19), calls=%async_computation.3 | async-start | bytes 524288 | tf_op jit(solution)/shard_map/all_to_all | solution.py:391
  86.3 1.9 %collective-permute-start.16 = (f32[96,128]{1,0:T(8,128)}, f32[96,128]{1,0:T(8,128)S(1)}, u32[]{:S(2)}, u32[]{:S(2)}) collective-permute-start(f32[96,128]{1,0:T(8,128)} %get-tuple-element.45), channel_id=1, source_target_pairs={{0,64},{64,128},{128,192},{192,0},{1,65},{65,129},{129,193},{193,1... | collective-permute-start | bytes 147464 | tf_op jit(solution)/shard_map/ppermute | solution.py:303
  88.2 2.7 %collective-permute-start.17 = (f32[96,128]{1,0:T(8,128)}, f32[96,128]{1,0:T(8,128)S(1)}, u32[]{:S(2)}, u32[]{:S(2)}) collective-permute-start(f32[96,128]{1,0:T(8,128)} %get-tuple-element.46), channel_id=1, source_target_pairs={{0,128},{64,192},{128,0},{192,64},{1,129},{65,193},{129,1},{193,65... | collective-permute-start | bytes 147464 | tf_op jit(solution)/shard_map/ppermute | solution.py:303
  90.9 1.4 %collective-permute-start.18 = (f32[96,128]{1,0:T(8,128)}, f32[96,128]{1,0:T(8,128)S(1)}, u32[]{:S(2)}, u32[]{:S(2)}) collective-permute-start(f32[96,128]{1,0:T(8,128)} %get-tuple-element.47), channel_id=1, source_target_pairs={{0,192},{64,0},{128,64},{192,128},{1,193},{65,1},{129,65},{193,129... | collective-permute-start | bytes 147464 | tf_op jit(solution)/shard_map/ppermute | solution.py:303
  92.4 2.0 %collective-permute-done.17.refs_2_ = f32[96,128]{1,0:T(8,128)S(1)} collective-permute-done((f32[96,128]{1,0:T(8,128)}, f32[96,128]{1,0:T(8,128)S(1)}, u32[]{:S(2)}, u32[]{:S(2)}) %collective-permute-start.17) | collective-permute-done | bytes 49184 | tf_op jit(solution)/shard_map/ppermute | solution.py:303
  94.4 1.1 %collective-permute-done.18.refs_3_ = f32[96,128]{1,0:T(8,128)S(1)} collective-permute-done((f32[96,128]{1,0:T(8,128)}, f32[96,128]{1,0:T(8,128)S(1)}, u32[]{:S(2)}, u32[]{:S(2)}) %collective-permute-start.18) | collective-permute-done | bytes 49184 | tf_op jit(solution)/shard_map/ppermute | solution.py:303
  95.5 3.5 %all-to-all-done.3.parts = bf16[32,32,128]{2,1,0:T(8,128)(2,1)S(1)} async-done(((bf16[32,32,128]{2,1,0:T(8,128)(2,1)}), bf16[32,32,128]{2,1,0:T(8,128)(2,1)S(1)}, u32[]{:S(2)}, u32[]{:S(2)}) %all-to-all-start.3) | async-done | bytes 262176 | tf_op jit(solution)/shard_map/all_to_all | solution.py:391
  99.0 0.8 copy-done
  99.8 1.8 %finish.1 = (f32[8,32,64]{2,1,0:T(8,128)}, f32[8,32,64]{2,1,0:T(8,128)}) custom-call(s32[3]{0:T(128)S(1)} %pad_add_fusion.place, bf16[32,32,128]{2,1,0:T(8,128)(2,1)S(1)} %all-to-all-done.3.parts, f32[96,128]{1,0:T(8,128)S(1)} %copy-done, f32[96,128]{1,0:T(8,128)S(1)} %collective-permute-done.16.refs_1_, f32[96,128]{1,0:T(8,128)S(1)} %collective-permute-done.17.refs_2_, ...), custom_call_target="tpu_custom_call" | custom-call | tf_op jit(solution)/shard_map/finish/pallas_call | solution.py:394
  (23 shorter events, 0.1 us)
Async XLA Ops:
  0.6 10.5 %copy-start.5 = (bf16[2,64,128]{2,1,0:T(8,128)(2,1)S(1)}, bf16[2,64,128]{2,1,0:T(8,128)(2,1)}, u32[]{:S(2)}) copy-start(bf16[2,64,128]{2,1,0:T(8,128)(2,1)} %param.11) | copy-start | bytes 98308
  5.2 31.5 %collective-permute-start.4 = (bf16[256,1024]{1,0:T(8,128)(2,1)}, bf16[256,1024]{1,0:T(8,128)(2,1)S(1)}, u32[]{:S(2)}, u32[]{:S(2)}) collective-permute-start(bf16[256,1024]{1,0:T(8,128)(2,1)} %get-tuple-element.27), channel_id=1, source_target_pairs={{0,64},{64,128},{128,192},{192,0},{1,65},{65,129},{129,193},{193,1... | collective-permute-start | bytes 1572872 | tf_op jit(solution)/shard_map/ppermute | solution.py:303
  6.9 29.8 %collective-permute-start.5 = (bf16[256,1024]{1,0:T(8,128)(2,1)}, bf16[256,1024]{1,0:T(8,128)(2,1)S(1)}, u32[]{:S(2)}, u32[]{:S(2)}) collective-permute-start(bf16[256,1024]{1,0:T(8,128)(2,1)} %get-tuple-element.28), channel_id=1, source_target_pairs={{0,128},{64,192},{128,0},{192,64},{1,129},{65,193},{129,1},{193,65... | collective-permute-start | bytes 1572872 | tf_op jit(solution)/shard_map/ppermute | solution.py:303
  9.8 26.9 %collective-permute-start.6 = (bf16[256,1024]{1,0:T(8,128)(2,1)}, bf16[256,1024]{1,0:T(8,128)(2,1)S(1)}, u32[]{:S(2)}, u32[]{:S(2)}) collective-permute-start(bf16[256,1024]{1,0:T(8,128)(2,1)} %get-tuple-element.29), channel_id=1, source_target_pairs={{0,192},{64,0},{128,64},{192,128},{1,193},{65,1},{129,65},{193,129... | collective-permute-start | bytes 1572872 | tf_op jit(solution)/shard_map/ppermute | solution.py:303
  11.2 1.2 %collective-permute-start = (bf16[128,128]{1,0:T(8,128)(2,1)S(1)}, bf16[128,128]{1,0:T(8,128)(2,1)S(1)}, u32[]{:S(2)}, u32[]{:S(2)}) collective-permute-start(bf16[128,128]{1,0:T(8,128)(2,1)S(1)} %bitcast.25), channel_id=1, source_target_pairs={{0,1},{1,0},{2,3},{3,2},{4,5},{5,4},{6,7},{7,6},{8,9},{9,8},{10,11... | collective-permute-start | bytes 98312 | tf_op jit(solution)/shard_map/ppermute | solution.py:303
  12.4 11.2 %copy-start.1 = (bf16[2,128,128]{2,1,0:T(8,128)(2,1)}, bf16[2,128,128]{2,1,0:T(8,128)(2,1)S(1)}, u32[]{:S(2)}) copy-start(bf16[2,128,128]{2,1,0:T(8,128)(2,1)S(1)} %pad_maximum_fusion.refs_0_) | copy-start | bytes 196612
  12.4 7.0 %collective-permute-start.3 = (bf16[2,128,128]{2,1,0:T(8,128)(2,1)S(1)}, bf16[2,128,128]{2,1,0:T(8,128)(2,1)S(1)}, u32[]{:S(2)}, u32[]{:S(2)}) collective-permute-start(bf16[2,128,128]{2,1,0:T(8,128)(2,1)S(1)} %pad_maximum_fusion.refs_0_), channel_id=1, source_target_pairs={{0,6},{2,0},{4,2},{6,4},{1,7},{3,1},{5,3},{7,5},{8,14},{10,8},{12,... | collective-permute-start | bytes 196616 | tf_op jit(solution)/shard_map/ppermute | solution.py:303
  13.3 6.7 %collective-permute-start.2 = (bf16[2,128,128]{2,1,0:T(8,128)(2,1)S(1)}, bf16[2,128,128]{2,1,0:T(8,128)(2,1)S(1)}, u32[]{:S(2)}, u32[]{:S(2)}) collective-permute-start(bf16[2,128,128]{2,1,0:T(8,128)(2,1)S(1)} %pad_maximum_fusion.refs_0_), channel_id=1, source_target_pairs={{0,4},{2,6},{4,0},{6,2},{1,5},{3,7},{5,1},{7,3},{8,12},{10,14},{12... | collective-permute-start | bytes 196616 | tf_op jit(solution)/shard_map/ppermute | solution.py:303
  19.3 4.3 %copy-start.2 = (bf16[2,128,128]{2,1,0:T(8,128)(2,1)}, bf16[2,128,128]{2,1,0:T(8,128)(2,1)S(1)}, u32[]{:S(2)}) copy-start(bf16[2,128,128]{2,1,0:T(8,128)(2,1)S(1)} %collective-permute-done.3.refs_3_) | copy-start | bytes 196612
  19.3 4.3 %collective-permute-start.1 = (bf16[2,128,128]{2,1,0:T(8,128)(2,1)S(1)}, bf16[2,128,128]{2,1,0:T(8,128)(2,1)S(1)}, u32[]{:S(2)}, u32[]{:S(2)}) collective-permute-start(bf16[2,128,128]{2,1,0:T(8,128)(2,1)S(1)} %pad_maximum_fusion.refs_0_), channel_id=1, source_target_pairs={{0,2},{2,4},{4,6},{6,0},{1,3},{3,5},{5,7},{7,1},{8,10},{10,12},{12... | collective-permute-start | bytes 196616 | tf_op jit(solution)/shard_map/ppermute | solution.py:303
  20.0 3.6 %copy-start.3 = (bf16[2,128,128]{2,1,0:T(8,128)(2,1)}, bf16[2,128,128]{2,1,0:T(8,128)(2,1)S(1)}, u32[]{:S(2)}) copy-start(bf16[2,128,128]{2,1,0:T(8,128)(2,1)S(1)} %collective-permute-done.2.refs_2_) | copy-start | bytes 196612
  23.6 0.6 copy-start.4
  27.4 9.3 %all-to-all-start = ((bf16[4,128,128]{2,1,0:T(8,128)(2,1)}), bf16[4,128,128]{2,1,0:T(8,128)(2,1)S(1)}, u32[]{:S(2)}, u32[]{:S(2)}) async-start(bf16[4,128,128]{2,1,0:T(8,128)(2,1)} %get-tuple-element.32), calls=%async_computation | async-start | bytes 262144 | tf_op jit(solution)/shard_map/all_to_all | solution.py:345
  37.8 18.9 %all-to-all-start.1 = ((bf16[8,128,128]{2,1,0:T(8,128)(2,1)}), bf16[8,128,128]{2,1,0:T(8,128)(2,1)S(1)}, u32[]{:S(2)}, u32[]{:S(2)}) async-start(bf16[8,128,128]{2,1,0:T(8,128)(2,1)} %first_pass.1), calls=%async_computation.1 | async-start | bytes 524288 | tf_op jit(solution)/shard_map/all_to_all | solution.py:359
  46.3 2.1 %collective-permute-start.9 = (bf16[144,512]{1,0:T(8,128)(2,1)S(1)}, bf16[144,512]{1,0:T(8,128)(2,1)S(1)}, u32[]{:S(2)}, u32[]{:S(2)}) collective-permute-start(bf16[144,512]{1,0:T(8,128)(2,1)S(1)} %convert_element_type.6.refs_4_), channel_id=1, source_target_pairs={{0,1},{1,0},{2,3},{3,2},{4,5},{5,4},{6,7},{7,6},{8,9},{9,8},{10,11... | collective-permute-start | bytes 442376 | tf_op jit(solution)/shard_map/ppermute | solution.py:303
  46.3 6.3 %collective-permute-start.8 = (bf16[144,512]{1,0:T(8,128)(2,1)S(1)}, bf16[144,512]{1,0:T(8,128)(2,1)S(1)}, u32[]{:S(2)}, u32[]{:S(2)}) collective-permute-start(bf16[144,512]{1,0:T(8,128)(2,1)S(1)} %convert_element_type.6.refs_4_), channel_id=1, source_target_pairs={{0,192},{64,0},{128,64},{192,128},{1,193},{65,1},{129,65},{193,129... | collective-permute-start | bytes 442376 | tf_op jit(solution)/shard_map/ppermute | solution.py:303
  47.6 7.1 %collective-permute-start.7 = (bf16[144,512]{1,0:T(8,128)(2,1)S(1)}, bf16[144,512]{1,0:T(8,128)(2,1)S(1)}, u32[]{:S(2)}, u32[]{:S(2)}) collective-permute-start(bf16[144,512]{1,0:T(8,128)(2,1)S(1)} %convert_element_type.6.refs_4_), channel_id=1, source_target_pairs={{0,64},{64,128},{128,192},{192,0},{1,65},{65,129},{129,193},{193,1... | collective-permute-start | bytes 442376 | tf_op jit(solution)/shard_map/ppermute | solution.py:303
  57.5 16.5 %all-to-all-start.2 = ((bf16[8,128,128]{2,1,0:T(8,128)(2,1)}), bf16[8,128,128]{2,1,0:T(8,128)(2,1)S(1)}, u32[]{:S(2)}, u32[]{:S(2)}) async-start(bf16[8,128,128]{2,1,0:T(8,128)(2,1)} %add_up.1), calls=%async_computation.2 | async-start | bytes 524288 | tf_op jit(solution)/shard_map/all_to_all | solution.py:374
  62.6 5.7 %collective-permute-start.10 = (bf16[80,512]{1,0:T(8,128)(2,1)S(1)}, bf16[80,512]{1,0:T(8,128)(2,1)S(1)}, u32[]{:S(2)}, u32[]{:S(2)}) collective-permute-start(bf16[80,512]{1,0:T(8,128)(2,1)S(1)} %slice.6), channel_id=1, source_target_pairs={{0,64},{64,128},{128,192},{192,0},{1,65},{65,129},{129,193},{193,1... | collective-permute-start | bytes 245768 | tf_op jit(solution)/shard_map/ppermute | solution.py:303
  62.7 5.1 %collective-permute-start.11 = (bf16[64,512]{1,0:T(8,128)(2,1)S(1)}, bf16[64,512]{1,0:T(8,128)(2,1)S(1)}, u32[]{:S(2)}, u32[]{:S(2)}) collective-permute-start(bf16[64,512]{1,0:T(8,128)(2,1)S(1)} %slice.7), channel_id=1, source_target_pairs={{0,192},{64,0},{128,64},{192,128},{1,193},{65,1},{129,65},{193,129... | collective-permute-start | bytes 196616 | tf_op jit(solution)/shard_map/ppermute | solution.py:303
  68.3 1.9 %collective-permute-start.12 = (bf16[144,512]{1,0:T(8,128)(2,1)S(1)}, bf16[144,512]{1,0:T(8,128)(2,1)S(1)}, u32[]{:S(2)}, u32[]{:S(2)}) collective-permute-start(bf16[144,512]{1,0:T(8,128)(2,1)S(1)} %collective-permute-done.7.refs_5_), channel_id=1, source_target_pairs={{0,1},{1,0},{2,3},{3,2},{4,5},{5,4},{6,7},{7,6},{8,9},{9,8},{10,11... | collective-permute-start | bytes 442376 | tf_op jit(solution)/shard_map/ppermute | solution.py:303
  68.4 1.9 %collective-permute-start.15 = (bf16[144,512]{1,0:T(8,128)(2,1)S(1)}, bf16[144,512]{1,0:T(8,128)(2,1)S(1)}, u32[]{:S(2)}, u32[]{:S(2)}) collective-permute-start(bf16[144,512]{1,0:T(8,128)(2,1)S(1)} %collective-permute-done.8.refs_8_), channel_id=1, source_target_pairs={{0,1},{1,0},{2,3},{3,2},{4,5},{5,4},{6,7},{7,6},{8,9},{9,8},{10,11... | collective-permute-start | bytes 442376 | tf_op jit(solution)/shard_map/ppermute | solution.py:303
  68.9 1.3 %collective-permute-start.14 = (bf16[64,512]{1,0:T(8,128)(2,1)S(1)}, bf16[64,512]{1,0:T(8,128)(2,1)S(1)}, u32[]{:S(2)}, u32[]{:S(2)}) collective-permute-start(bf16[64,512]{1,0:T(8,128)(2,1)S(1)} %collective-permute-done.11.refs_7_), channel_id=1, source_target_pairs={{0,1},{1,0},{2,3},{3,2},{4,5},{5,4},{6,7},{7,6},{8,9},{9,8},{10,11... | collective-permute-start | bytes 196616 | tf_op jit(solution)/shard_map/ppermute | solution.py:303
  68.9 1.4 %collective-permute-start.13 = (bf16[80,512]{1,0:T(8,128)(2,1)S(1)}, bf16[80,512]{1,0:T(8,128)(2,1)S(1)}, u32[]{:S(2)}, u32[]{:S(2)}) collective-permute-start(bf16[80,512]{1,0:T(8,128)(2,1)S(1)} %collective-permute-done.10.refs_6_), channel_id=1, source_target_pairs={{0,1},{1,0},{2,3},{3,2},{4,5},{5,4},{6,7},{7,6},{8,9},{9,8},{10,11... | collective-permute-start | bytes 245768 | tf_op jit(solution)/shard_map/ppermute | solution.py:303
  79.9 19.1 %all-to-all-start.3 = ((bf16[32,32,128]{2,1,0:T(8,128)(2,1)}), bf16[32,32,128]{2,1,0:T(8,128)(2,1)S(1)}, u32[]{:S(2)}, u32[]{:S(2)}) async-start(bf16[32,32,128]{2,1,0:T(8,128)(2,1)} %bitcast.19), calls=%async_computation.3 | async-start | bytes 524288 | tf_op jit(solution)/shard_map/all_to_all | solution.py:391
  86.3 6.0 %collective-permute-start.16 = (f32[96,128]{1,0:T(8,128)}, f32[96,128]{1,0:T(8,128)S(1)}, u32[]{:S(2)}, u32[]{:S(2)}) collective-permute-start(f32[96,128]{1,0:T(8,128)} %get-tuple-element.45), channel_id=1, source_target_pairs={{0,64},{64,128},{128,192},{192,0},{1,65},{65,129},{129,193},{193,1... | collective-permute-start | bytes 147464 | tf_op jit(solution)/shard_map/ppermute | solution.py:303
  88.2 6.1 %collective-permute-start.17 = (f32[96,128]{1,0:T(8,128)}, f32[96,128]{1,0:T(8,128)S(1)}, u32[]{:S(2)}, u32[]{:S(2)}) collective-permute-start(f32[96,128]{1,0:T(8,128)} %get-tuple-element.46), channel_id=1, source_target_pairs={{0,128},{64,192},{128,0},{192,64},{1,129},{65,193},{129,1},{193,65... | collective-permute-start | bytes 147464 | tf_op jit(solution)/shard_map/ppermute | solution.py:303
  90.9 4.6 %collective-permute-start.18 = (f32[96,128]{1,0:T(8,128)}, f32[96,128]{1,0:T(8,128)S(1)}, u32[]{:S(2)}, u32[]{:S(2)}) collective-permute-start(f32[96,128]{1,0:T(8,128)} %get-tuple-element.47), channel_id=1, source_target_pairs={{0,192},{64,0},{128,64},{192,128},{1,193},{65,1},{129,65},{193,129... | collective-permute-start | bytes 147464 | tf_op jit(solution)/shard_map/ppermute | solution.py:303
  99.0 0.8 copy-start

commit v9 on v8

--- a/solution.py
+++ b/solution.py
@@ -209,6 +209,7 @@
         for at in (0, 5)
     ]
     half = width // 2
+    own = sent[0].shape[0] - rank
     totals = [jnp.zeros((rows, half), F32) for _ in halves]
     for s in range(groups):
         summed = jnp.concatenate(
@@ -240,9 +241,11 @@
     for h, total in enumerate(totals):
         side = place[2] if h == 0 else 1 - place[2]
         for c in range(half // LANES):
-            start = pl.multiple_of(side * half + c * LANES, LANES)
-            out[pl.ds(start, LANES), :] = total[:, c * LANES : (c + 1) * LANES].T.astype(out.dtype)
-    own = sent[0].shape[0] - rank
+            block = total[:, c * LANES : (c + 1) * LANES].T.astype(out.dtype)
+            first = side * (half // own) + c * (LANES // own)
+            for k in range(LANES // own):
+                to = lax.rem(first + k, cuts) * groups + (first + k) // cuts
+                out[pl.ds(pl.multiple_of(to * own, own), own), :] = block[k * own : (k + 1) * own]
     for s in range(groups):
         owner = lax.rem(place[0] + s, groups)
         start = owner * (width // groups) + place[1] * own
@@ -257,18 +260,23 @@
         copy.wait()
 
 
-def finish(place, parts, *refs):
-    received, (left, right) = refs[:-2], refs[-2:]
+def finish(place, parts, own_far, *refs):
+    received, (left, right, own_near, sem) = refs[:-4], refs[-4:]
+    copy = pltpu.make_async_copy(own_far, own_near, sem)
+    copy.start()
+    received = [own_near, *received]
     owners = len(received)
     groups = parts.shape[0] // owners
     targets = left.shape[0] // owners
     own, rank = left.shape[1], left.shape[2]
     root = math.sqrt(1024)
-    for s in range(owners):
+    for s in [*range(1, owners), 0]:
+        if s == 0:
+            copy.wait()
         owner = lax.rem(place[0] + owners - s, owners)
-        total = parts[owner * groups].astype(F32)
+        total = parts[owner].astype(F32)
         for z in range(1, groups):
-            total = total + parts[owner * groups + z].astype(F32)
+            total = total + parts[z * owners + owner].astype(F32)
         both = jnp.concatenate([received[s][rank : rank + own, :] * root, total / root], axis=0)
         for t in range(targets):
             found = lax.dot_general(
@@ -388,14 +396,15 @@
         compiler_params=params(20),
         name="second_pass",
     )(place, sketches, *held, *all_shared)
-    row_parts = lax.all_to_all(rows_part.reshape(ny * nz, keep, own_rows), ("y", "z"), 0, 0, tiled=True)
-    received = [sent[0]] + [turn(sent[s], "y", ny, s) for s in range(1, ny)]
+    row_parts = lax.all_to_all(rows_part.reshape(ny * nz, keep, own_rows), ("z", "y"), 0, 0, tiled=True)
+    received = [pltpu.with_memory_space_constraint(sent[0], pltpu.HBM)] + [turn(sent[s], "y", ny, s) for s in range(1, ny)]
     out = jax.ShapeDtypeStruct((targets, keep, rank), F32)
     left_out, right_out = pl.pallas_call(
         finish,
         out_shape=(out, out),
-        in_specs=[in_smem] + [in_vmem] * (ny + 1),
+        in_specs=[in_smem, in_vmem, pl.BlockSpec(memory_space=pltpu.HBM)] + [in_vmem] * (ny - 1),
         out_specs=(in_vmem, in_vmem),
+        scratch_shapes=[VMEM((rank + keep, own_rows), F32), pltpu.SemaphoreType.DMA],
         compiler_params=params(8),
         name="finish",
     )(place, row_parts, *received)

time: 103 us -> 103 us (level)
  no operation moved by 1% of the time
where the time goes in v9:
time: 103 us; the launch traced here: 102 us
  starting transfers between devices  43.6 us (42%)
  waiting for transfers between devices  36.4 us (35%)
  Pallas kernels  17.3 us (17%)
  other arithmetic  2.36 us (2%)
  between operations  1.57 us (2%)
  local copies, waits for them, and re-layouts  1.25 us (1%)
    ppermute x19, waiting for transfers between devices, turn(): lax.ppermute(value, axis, [(i, (i + by) % size) for i in range(size)])  22.4 us
    ppermute x19, starting transfers between devices, turn(): lax.ppermute(value, axis, [(i, (i + by) % size) for i in range(size)])  20.4 us
    all_to_all x1, starting transfers between devices, shards(): parts = lax.all_to_all(sketch, 'z', 0, 0, tiled=True)  8.47 us
    all_to_all x1, starting transfers between devices, shards(): lax.all_to_all(rows_part.reshape(ny * nz, keep, own_rows), ('z', 'y'), 0,...  6.4 us
    pallas_call x1, Pallas kernels, shards(): pl.pallas_call(second_pass, out_shape=(jax.ShapeDtypeStruct((width, own_r...  5.99 us
    all_to_all x1, starting transfers between devices, shards(): sketches = lax.all_to_all(copies, 'z', 0, 0, tiled=True)  5.09 us
    all_to_all x1, waiting for transfers between devices, shards(): lax.all_to_all(rows_part.reshape(ny * nz, keep, own_rows), ('z', 'y'), 0,...  4.46 us
    pallas_call x1, Pallas kernels, shards(): pl.pallas_call(sum_factors, out_shape=(jax.ShapeDtypeStruct((held_rows, w...  3.95 us
  transfers between devices with their start and end apart: 23, of which 15 were waited for; matrix products, arithmetic and copies ran while one was open for 3% of the time, Pallas kernels for 3%

profile of v9, /device:TPU:6, one launch (start us, length us, event | category | flops | bytes accessed | tf_op | source)
XLA Modules:
  0.0 102.5 jit_solution(17374643354314360702)
XLA Ops:
  1.3 4.0 %sum_factors.1 = (f32[256,1024]{1,0:T(8,128)}, bf16[256,1024]{1,0:T(8,128)(2,1)}, bf16[256,1024]{1,0:T(8,128)(2,1)}, bf16[256,1024]{1,0:T(8,128)(2,1)}) custom-call(s32[36]{0:T(128)} %bitcast.28, s32[36]{0:T(128)} %bitcast.29, s32[1]{0:T(128)} %bitcast.22.count, bf16[36,64,1024]{2,1,0:T(8,128)(2,1)} %bitcast.23), custom_call_target="tpu_custom_call" | custom-call | flops 10000000 | bytes 7000000 | tf_op jit(solution)/shard_map/sum_factors/pallas_call | solution.py:313
  5.3 1.7 %collective-permute-start.4 = (bf16[256,1024]{1,0:T(8,128)(2,1)}, bf16[256,1024]{1,0:T(8,128)(2,1)S(1)}, u32[]{:S(2)}, u32[]{:S(2)}) collective-permute-start(bf16[256,1024]{1,0:T(8,128)(2,1)} %get-tuple-element.27), channel_id=1, source_target_pairs={{0,64},{64,128},{128,192},{192,0},{1,65},{65,129},{129,193},{193,1... | collective-permute-start | bytes 1572872 | tf_op jit(solution)/shard_map/ppermute | solution.py:311
  6.9 2.9 %collective-permute-start.5 = (bf16[256,1024]{1,0:T(8,128)(2,1)}, bf16[256,1024]{1,0:T(8,128)(2,1)S(1)}, u32[]{:S(2)}, u32[]{:S(2)}) collective-permute-start(bf16[256,1024]{1,0:T(8,128)(2,1)} %get-tuple-element.28), channel_id=1, source_target_pairs={{0,128},{64,192},{128,0},{192,64},{1,129},{65,193},{129,1},{193,65... | collective-permute-start | bytes 1572872 | tf_op jit(solution)/shard_map/ppermute | solution.py:311
  9.8 1.3 %collective-permute-start.6 = (bf16[256,1024]{1,0:T(8,128)(2,1)}, bf16[256,1024]{1,0:T(8,128)(2,1)S(1)}, u32[]{:S(2)}, u32[]{:S(2)}) collective-permute-start(bf16[256,1024]{1,0:T(8,128)(2,1)} %get-tuple-element.29), channel_id=1, source_target_pairs={{0,192},{64,0},{128,64},{192,128},{1,193},{65,1},{129,65},{193,129... | collective-permute-start | bytes 1572872 | tf_op jit(solution)/shard_map/ppermute | solution.py:311
  11.2 0.0 collective-permute-start
  11.2 1.2 %collective-permute-done = bf16[128,128]{1,0:T(8,128)(2,1)S(1)} collective-permute-done((bf16[128,128]{1,0:T(8,128)(2,1)S(1)}, bf16[128,128]{1,0:T(8,128)(2,1)S(1)}, u32[]{:S(2)}, u32[]{:S(2)}) %collective-permute-start) | collective-permute-done | bytes 32800 | tf_op jit(solution)/shard_map/ppermute | solution.py:311
  12.4 0.0 copy-start
  12.4 0.9 collective-permute-start.3
  13.3 1.1 %collective-permute-start.2 = (bf16[2,128,128]{2,1,0:T(8,128)(2,1)S(1)}, bf16[2,128,128]{2,1,0:T(8,128)(2,1)S(1)}, u32[]{:S(2)}, u32[]{:S(2)}) collective-permute-start(bf16[2,128,128]{2,1,0:T(8,128)(2,1)S(1)} %pad_maximum_fusion.refs_0_), channel_id=1, source_target_pairs={{0,4},{2,6},{4,0},{6,2},{1,5},{3,7},{5,1},{7,3},{8,12},{10,14},{12... | collective-permute-start | bytes 196616 | tf_op jit(solution)/shard_map/ppermute | solution.py:311
  14.4 4.9 %collective-permute-done.3.refs_3_ = bf16[2,128,128]{2,1,0:T(8,128)(2,1)S(1)} collective-permute-done((bf16[2,128,128]{2,1,0:T(8,128)(2,1)S(1)}, bf16[2,128,128]{2,1,0:T(8,128)(2,1)S(1)}, u32[]{:S(2)}, u32[]{:S(2)}) %collective-permute-start.3) | collective-permute-done | bytes 65568 | tf_op jit(solution)/shard_map/ppermute | solution.py:311
  19.3 0.0 collective-permute-start.1
  19.4 0.6 stack.61.columns
  20.0 3.6 %collective-permute-done.1.refs_1_ = bf16[2,128,128]{2,1,0:T(8,128)(2,1)S(1)} collective-permute-done((bf16[2,128,128]{2,1,0:T(8,128)(2,1)S(1)}, bf16[2,128,128]{2,1,0:T(8,128)(2,1)S(1)}, u32[]{:S(2)}, u32[]{:S(2)}) %collective-permute-start.1) | collective-permute-done | bytes 65568 | tf_op jit(solution)/shard_map/ppermute | solution.py:311
  23.6 0.6 copy-done.3
  24.2 3.2 %project.1 = (f32[144,512]{1,0:T(8,128)}, bf16[4,128,128]{2,1,0:T(8,128)(2,1)}) custom-call(s32[9]{0:T(128)} %stack.61.columns, bf16[2,128,128]{2,1,0:T(8,128)(2,1)} %copy-done, bf16[2,128,128]{2,1,0:T(8,128)(2,1)} %copy-done.3, bf16[2,128,128]{2,1,0:T(8,128)(2,1)} %copy-done.2, bf16[2,128,128]{2,1,0:T(8,128)(2,1)} %copy-done.1, bf16[512,1024]{1,0:T(8,128)(2,1)} %bitcast.24, ...), custom_call_target="tpu_custom_call" | custom-call | tf_op jit(solution)/shard_map/project/pallas_call | solution.py:341
  27.4 3.3 %all-to-all-start = ((bf16[4,128,128]{2,1,0:T(8,128)(2,1)}), bf16[4,128,128]{2,1,0:T(8,128)(2,1)S(1)}, u32[]{:S(2)}, u32[]{:S(2)}) async-start(bf16[4,128,128]{2,1,0:T(8,128)(2,1)} %get-tuple-element.32), calls=%async_computation | async-start | bytes 262144 | tf_op jit(solution)/shard_map/all_to_all | solution.py:353
  30.8 1.3 %convert_element_type.7.refs_0_ = bf16[256,1024]{1,0:T(8,128)(2,1)S(1)} convert(f32[256,1024]{1,0:T(8,128)} %get-tuple-element.26) | non-fusion elementwise | flops 262144 | bytes 1572864 | tf_op jit(solution)/shard_map/convert_element_type | solution.py:333
  32.1 1.0 convert_element_type.6.refs_4_
  33.0 3.7 %all-to-all-done.refs_4_ = bf16[4,128,128]{2,1,0:T(8,128)(2,1)S(1)} async-done(((bf16[4,128,128]{2,1,0:T(8,128)(2,1)}), bf16[4,128,128]{2,1,0:T(8,128)(2,1)S(1)}, u32[]{:S(2)}, u32[]{:S(2)}) %all-to-all-start) | async-done | bytes 131104 | tf_op jit(solution)/shard_map/all_to_all | solution.py:353
  36.7 1.1 %first_pass.1 = bf16[8,128,128]{2,1,0:T(8,128)(2,1)} custom-call(bf16[256,1024]{1,0:T(8,128)(2,1)S(1)} %convert_element_type.7.refs_0_, bf16[256,1024]{1,0:T(8,128)(2,1)S(1)} %collective-permute-done.4.refs_1_, bf16[256,1024]{1,0:T(8,128)(2,1)S(1)} %collective-permute-done.5.refs_2_, bf16[256,1024]{1,0:T(8,128)(2,1)S(1)} %collective-permute-done.6.refs_3_, ...), custom_call_target="tpu_custom_call" | custom-call | tf_op jit(solution)/shard_map/first_pass/pallas_call | solution.py:357
  37.8 8.5 %all-to-all-start.1 = ((bf16[8,128,128]{2,1,0:T(8,128)(2,1)}), bf16[8,128,128]{2,1,0:T(8,128)(2,1)S(1)}, u32[]{:S(2)}, u32[]{:S(2)}) async-start(bf16[8,128,128]{2,1,0:T(8,128)(2,1)} %first_pass.1), calls=%async_computation.1 | async-start | bytes 524288 | tf_op jit(solution)/shard_map/all_to_all | solution.py:367
  46.3 1.2 %collective-permute-start.8 = (bf16[144,512]{1,0:T(8,128)(2,1)S(1)}, bf16[144,512]{1,0:T(8,128)(2,1)S(1)}, u32[]{:S(2)}, u32[]{:S(2)}) collective-permute-start(bf16[144,512]{1,0:T(8,128)(2,1)S(1)} %convert_element_type.6.refs_4_), channel_id=1, source_target_pairs={{0,192},{64,0},{128,64},{192,128},{1,193},{65,1},{129,65},{193,129... | collective-permute-start | bytes 442376 | tf_op jit(solution)/shard_map/ppermute | solution.py:311
  47.6 0.9 collective-permute-start.7
  48.4 4.2 %collective-permute-done.8.refs_8_ = bf16[144,512]{1,0:T(8,128)(2,1)S(1)} collective-permute-done((bf16[144,512]{1,0:T(8,128)(2,1)S(1)}, bf16[144,512]{1,0:T(8,128)(2,1)S(1)}, u32[]{:S(2)}, u32[]{:S(2)}) %collective-permute-start.8) | collective-permute-done | bytes 147488 | tf_op jit(solution)/shard_map/ppermute | solution.py:311
  52.6 2.1 %collective-permute-done.7.refs_5_ = bf16[144,512]{1,0:T(8,128)(2,1)S(1)} collective-permute-done((bf16[144,512]{1,0:T(8,128)(2,1)S(1)}, bf16[144,512]{1,0:T(8,128)(2,1)S(1)}, u32[]{:S(2)}, u32[]{:S(2)}) %collective-permute-start.7) | collective-permute-done | bytes 147488 | tf_op jit(solution)/shard_map/ppermute | solution.py:311
  54.7 2.1 %all-to-all-done.1.parts = bf16[8,128,128]{2,1,0:T(8,128)(2,1)S(1)} async-done(((bf16[8,128,128]{2,1,0:T(8,128)(2,1)}), bf16[8,128,128]{2,1,0:T(8,128)(2,1)S(1)}, u32[]{:S(2)}, u32[]{:S(2)}) %all-to-all-start.1) | async-done | bytes 262176 | tf_op jit(solution)/shard_map/all_to_all | solution.py:367
  56.8 0.7 add_up.1
  57.5 5.1 %all-to-all-start.2 = ((bf16[8,128,128]{2,1,0:T(8,128)(2,1)}), bf16[8,128,128]{2,1,0:T(8,128)(2,1)S(1)}, u32[]{:S(2)}, u32[]{:S(2)}) async-start(bf16[8,128,128]{2,1,0:T(8,128)(2,1)} %add_up.1), calls=%async_computation.2 | async-start | bytes 524288 | tf_op jit(solution)/shard_map/all_to_all | solution.py:382
  62.6 0.1 collective-permute-start.10
  62.7 3.2 %collective-permute-start.11 = (bf16[64,512]{1,0:T(8,128)(2,1)S(1)}, bf16[64,512]{1,0:T(8,128)(2,1)S(1)}, u32[]{:S(2)}, u32[]{:S(2)}) collective-permute-start(bf16[64,512]{1,0:T(8,128)(2,1)S(1)} %slice.7), channel_id=1, source_target_pairs={{0,192},{64,0},{128,64},{192,128},{1,193},{65,1},{129,65},{193,129... | collective-permute-start | bytes 196616 | tf_op jit(solution)/shard_map/ppermute | solution.py:311
  65.9 1.9 %collective-permute-done.11.refs_7_ = bf16[64,512]{1,0:T(8,128)(2,1)S(1)} collective-permute-done((bf16[64,512]{1,0:T(8,128)(2,1)S(1)}, bf16[64,512]{1,0:T(8,128)(2,1)S(1)}, u32[]{:S(2)}, u32[]{:S(2)}) %collective-permute-start.11) | collective-permute-done | bytes 65568 | tf_op jit(solution)/shard_map/ppermute | solution.py:311
  67.8 0.5 collective-permute-done.10.refs_6_
  68.4 0.5 collective-permute-start.15
  68.9 0.0 collective-permute-start.14
  68.9 0.5 collective-permute-start.13
  69.4 0.1 pad_add_fusion.place
  69.5 0.7 collective-permute-done.14.refs_12_
  70.1 0.2 collective-permute-done.13.refs_11_
  70.3 3.8 %all-to-all-done.2.sketches = bf16[8,128,128]{2,1,0:T(8,128)(2,1)S(1)} async-done(((bf16[8,128,128]{2,1,0:T(8,128)(2,1)}), bf16[8,128,128]{2,1,0:T(8,128)(2,1)S(1)}, u32[]{:S(2)}, u32[]{:S(2)}) %all-to-all-start.2) | async-done | bytes 262176 | tf_op jit(solution)/shard_map/all_to_all | solution.py:382
  74.1 6.0 %second_pass.1 = (bf16[1024,128]{1,0:T(8,128)(2,1)}, f32[96,128]{1,0:T(8,128)}, f32[96,128]{1,0:T(8,128)}, f32[96,128]{1,0:T(8,128)}, f32[96,128]{1,0:T(8,128)}) custom-call(s32[3]{0:T(128)S(1)} %pad_add_fusion.place, bf16[8,128,128]{2,1,0:T(8,128)(2,1)S(1)} %all-to-all-done.2.sketches, bf16[256,1024]{1,0:T(8,128)(2,1)S(1)} %convert_element_type.7.refs_0_, ...), custom_call_target="tpu_custom_call" | custom-call | tf_op jit(solution)/shard_map/second_pass/pallas_call | solution.py:385
  80.1 6.4 %all-to-all-start.3 = ((bf16[32,32,128]{2,1,0:T(8,128)(2,1)}), bf16[32,32,128]{2,1,0:T(8,128)(2,1)S(1)}, u32[]{:S(2)}, u32[]{:S(2)}) async-start(bf16[32,32,128]{2,1,0:T(8,128)(2,1)} %bitcast.19), calls=%async_computation.3 | async-start | bytes 524288 | tf_op jit(solution)/shard_map/all_to_all | solution.py:399
  86.5 1.9 %collective-permute-start.16 = (f32[96,128]{1,0:T(8,128)}, f32[96,128]{1,0:T(8,128)S(1)}, u32[]{:S(2)}, u32[]{:S(2)}) collective-permute-start(f32[96,128]{1,0:T(8,128)} %get-tuple-element.45), channel_id=1, source_target_pairs={{0,64},{64,128},{128,192},{192,0},{1,65},{65,129},{129,193},{193,1... | collective-permute-start | bytes 147464 | tf_op jit(solution)/shard_map/ppermute | solution.py:311
  88.3 2.7 %collective-permute-start.17 = (f32[96,128]{1,0:T(8,128)}, f32[96,128]{1,0:T(8,128)S(1)}, u32[]{:S(2)}, u32[]{:S(2)}) collective-permute-start(f32[96,128]{1,0:T(8,128)} %get-tuple-element.46), channel_id=1, source_target_pairs={{0,128},{64,192},{128,0},{192,64},{1,129},{65,193},{129,1},{193,65... | collective-permute-start | bytes 147464 | tf_op jit(solution)/shard_map/ppermute | solution.py:311
  91.0 1.5 %collective-permute-start.18 = (f32[96,128]{1,0:T(8,128)}, f32[96,128]{1,0:T(8,128)S(1)}, u32[]{:S(2)}, u32[]{:S(2)}) collective-permute-start(f32[96,128]{1,0:T(8,128)} %get-tuple-element.47), channel_id=1, source_target_pairs={{0,192},{64,0},{128,64},{192,128},{1,193},{65,1},{129,65},{193,129... | collective-permute-start | bytes 147464 | tf_op jit(solution)/shard_map/ppermute | solution.py:311
  92.5 2.1 %collective-permute-done.17.refs_1_ = f32[96,128]{1,0:T(8,128)S(1)} collective-permute-done((f32[96,128]{1,0:T(8,128)}, f32[96,128]{1,0:T(8,128)S(1)}, u32[]{:S(2)}, u32[]{:S(2)}) %collective-permute-start.17) | collective-permute-done | bytes 49184 | tf_op jit(solution)/shard_map/ppermute | solution.py:311
  94.6 0.9 collective-permute-done.18.refs_2_
  95.5 4.5 %all-to-all-done.3.parts = bf16[32,32,128]{2,1,0:T(8,128)(2,1)S(1)} async-done(((bf16[32,32,128]{2,1,0:T(8,128)(2,1)}), bf16[32,32,128]{2,1,0:T(8,128)(2,1)S(1)}, u32[]{:S(2)}, u32[]{:S(2)}) %all-to-all-start.3) | async-done | bytes 262176 | tf_op jit(solution)/shard_map/all_to_all | solution.py:399
  100.0 2.3 %finish.1 = (f32[8,32,64]{2,1,0:T(8,128)}, f32[8,32,64]{2,1,0:T(8,128)}) custom-call(s32[3]{0:T(128)S(1)} %pad_add_fusion.place, bf16[32,32,128]{2,1,0:T(8,128)(2,1)S(1)} %all-to-all-done.3.parts, f32[96,128]{1,0:T(8,128)} %get-tuple-element.44.own_far, f32[96,128]{1,0:T(8,128)S(1)} %collective-permute-done.16.refs_0_, ...), custom_call_target="tpu_custom_call" | custom-call | tf_op jit(solution)/shard_map/finish/pallas_call | solution.py:402
  (21 shorter events, 0.1 us)
Async XLA Ops:
  0.6 10.5 %copy-start.4 = (bf16[2,64,128]{2,1,0:T(8,128)(2,1)S(1)}, bf16[2,64,128]{2,1,0:T(8,128)(2,1)}, u32[]{:S(2)}) copy-start(bf16[2,64,128]{2,1,0:T(8,128)(2,1)} %param.11) | copy-start | bytes 98308
  5.3 31.5 %collective-permute-start.4 = (bf16[256,1024]{1,0:T(8,128)(2,1)}, bf16[256,1024]{1,0:T(8,128)(2,1)S(1)}, u32[]{:S(2)}, u32[]{:S(2)}) collective-permute-start(bf16[256,1024]{1,0:T(8,128)(2,1)} %get-tuple-element.27), channel_id=1, source_target_pairs={{0,64},{64,128},{128,192},{192,0},{1,65},{65,129},{129,193},{193,1... | collective-permute-start | bytes 1572872 | tf_op jit(solution)/shard_map/ppermute | solution.py:311
  6.9 29.8 %collective-permute-start.5 = (bf16[256,1024]{1,0:T(8,128)(2,1)}, bf16[256,1024]{1,0:T(8,128)(2,1)S(1)}, u32[]{:S(2)}, u32[]{:S(2)}) collective-permute-start(bf16[256,1024]{1,0:T(8,128)(2,1)} %get-tuple-element.28), channel_id=1, source_target_pairs={{0,128},{64,192},{128,0},{192,64},{1,129},{65,193},{129,1},{193,65... | collective-permute-start | bytes 1572872 | tf_op jit(solution)/shard_map/ppermute | solution.py:311
  9.8 26.9 %collective-permute-start.6 = (bf16[256,1024]{1,0:T(8,128)(2,1)}, bf16[256,1024]{1,0:T(8,128)(2,1)S(1)}, u32[]{:S(2)}, u32[]{:S(2)}) collective-permute-start(bf16[256,1024]{1,0:T(8,128)(2,1)} %get-tuple-element.29), channel_id=1, source_target_pairs={{0,192},{64,0},{128,64},{192,128},{1,193},{65,1},{129,65},{193,129... | collective-permute-start | bytes 1572872 | tf_op jit(solution)/shard_map/ppermute | solution.py:311
  11.2 1.2 %collective-permute-start = (bf16[128,128]{1,0:T(8,128)(2,1)S(1)}, bf16[128,128]{1,0:T(8,128)(2,1)S(1)}, u32[]{:S(2)}, u32[]{:S(2)}) collective-permute-start(bf16[128,128]{1,0:T(8,128)(2,1)S(1)} %bitcast.25), channel_id=1, source_target_pairs={{0,1},{1,0},{2,3},{3,2},{4,5},{5,4},{6,7},{7,6},{8,9},{9,8},{10,11... | collective-permute-start | bytes 98312 | tf_op jit(solution)/shard_map/ppermute | solution.py:311
  12.4 11.2 %copy-start = (bf16[2,128,128]{2,1,0:T(8,128)(2,1)}, bf16[2,128,128]{2,1,0:T(8,128)(2,1)S(1)}, u32[]{:S(2)}) copy-start(bf16[2,128,128]{2,1,0:T(8,128)(2,1)S(1)} %pad_maximum_fusion.refs_0_) | copy-start | bytes 196612
  12.4 7.0 %collective-permute-start.3 = (bf16[2,128,128]{2,1,0:T(8,128)(2,1)S(1)}, bf16[2,128,128]{2,1,0:T(8,128)(2,1)S(1)}, u32[]{:S(2)}, u32[]{:S(2)}) collective-permute-start(bf16[2,128,128]{2,1,0:T(8,128)(2,1)S(1)} %pad_maximum_fusion.refs_0_), channel_id=1, source_target_pairs={{0,6},{2,0},{4,2},{6,4},{1,7},{3,1},{5,3},{7,5},{8,14},{10,8},{12,... | collective-permute-start | bytes 196616 | tf_op jit(solution)/shard_map/ppermute | solution.py:311
  13.3 6.7 %collective-permute-start.2 = (bf16[2,128,128]{2,1,0:T(8,128)(2,1)S(1)}, bf16[2,128,128]{2,1,0:T(8,128)(2,1)S(1)}, u32[]{:S(2)}, u32[]{:S(2)}) collective-permute-start(bf16[2,128,128]{2,1,0:T(8,128)(2,1)S(1)} %pad_maximum_fusion.refs_0_), channel_id=1, source_target_pairs={{0,4},{2,6},{4,0},{6,2},{1,5},{3,7},{5,1},{7,3},{8,12},{10,14},{12... | collective-permute-start | bytes 196616 | tf_op jit(solution)/shard_map/ppermute | solution.py:311
  19.3 4.3 %copy-start.1 = (bf16[2,128,128]{2,1,0:T(8,128)(2,1)}, bf16[2,128,128]{2,1,0:T(8,128)(2,1)S(1)}, u32[]{:S(2)}) copy-start(bf16[2,128,128]{2,1,0:T(8,128)(2,1)S(1)} %collective-permute-done.3.refs_3_) | copy-start | bytes 196612
  19.3 4.3 %collective-permute-start.1 = (bf16[2,128,128]{2,1,0:T(8,128)(2,1)S(1)}, bf16[2,128,128]{2,1,0:T(8,128)(2,1)S(1)}, u32[]{:S(2)}, u32[]{:S(2)}) collective-permute-start(bf16[2,128,128]{2,1,0:T(8,128)(2,1)S(1)} %pad_maximum_fusion.refs_0_), channel_id=1, source_target_pairs={{0,2},{2,4},{4,6},{6,0},{1,3},{3,5},{5,7},{7,1},{8,10},{10,12},{12... | collective-permute-start | bytes 196616 | tf_op jit(solution)/shard_map/ppermute | solution.py:311
  20.0 3.7 %copy-start.2 = (bf16[2,128,128]{2,1,0:T(8,128)(2,1)}, bf16[2,128,128]{2,1,0:T(8,128)(2,1)S(1)}, u32[]{:S(2)}) copy-start(bf16[2,128,128]{2,1,0:T(8,128)(2,1)S(1)} %collective-permute-done.2.refs_2_) | copy-start | bytes 196612
  23.6 0.6 copy-start.3
  27.4 9.3 %all-to-all-start = ((bf16[4,128,128]{2,1,0:T(8,128)(2,1)}), bf16[4,128,128]{2,1,0:T(8,128)(2,1)S(1)}, u32[]{:S(2)}, u32[]{:S(2)}) async-start(bf16[4,128,128]{2,1,0:T(8,128)(2,1)} %get-tuple-element.32), calls=%async_computation | async-start | bytes 262144 | tf_op jit(solution)/shard_map/all_to_all | solution.py:353
  37.8 18.9 %all-to-all-start.1 = ((bf16[8,128,128]{2,1,0:T(8,128)(2,1)}), bf16[8,128,128]{2,1,0:T(8,128)(2,1)S(1)}, u32[]{:S(2)}, u32[]{:S(2)}) async-start(bf16[8,128,128]{2,1,0:T(8,128)(2,1)} %first_pass.1), calls=%async_computation.1 | async-start | bytes 524288 | tf_op jit(solution)/shard_map/all_to_all | solution.py:367
  46.3 2.1 %collective-permute-start.9 = (bf16[144,512]{1,0:T(8,128)(2,1)S(1)}, bf16[144,512]{1,0:T(8,128)(2,1)S(1)}, u32[]{:S(2)}, u32[]{:S(2)}) collective-permute-start(bf16[144,512]{1,0:T(8,128)(2,1)S(1)} %convert_element_type.6.refs_4_), channel_id=1, source_target_pairs={{0,1},{1,0},{2,3},{3,2},{4,5},{5,4},{6,7},{7,6},{8,9},{9,8},{10,11... | collective-permute-start | bytes 442376 | tf_op jit(solution)/shard_map/ppermute | solution.py:311
  46.3 6.3 %collective-permute-start.8 = (bf16[144,512]{1,0:T(8,128)(2,1)S(1)}, bf16[144,512]{1,0:T(8,128)(2,1)S(1)}, u32[]{:S(2)}, u32[]{:S(2)}) collective-permute-start(bf16[144,512]{1,0:T(8,128)(2,1)S(1)} %convert_element_type.6.refs_4_), channel_id=1, source_target_pairs={{0,192},{64,0},{128,64},{192,128},{1,193},{65,1},{129,65},{193,129... | collective-permute-start | bytes 442376 | tf_op jit(solution)/shard_map/ppermute | solution.py:311
  47.6 7.1 %collective-permute-start.7 = (bf16[144,512]{1,0:T(8,128)(2,1)S(1)}, bf16[144,512]{1,0:T(8,128)(2,1)S(1)}, u32[]{:S(2)}, u32[]{:S(2)}) collective-permute-start(bf16[144,512]{1,0:T(8,128)(2,1)S(1)} %convert_element_type.6.refs_4_), channel_id=1, source_target_pairs={{0,64},{64,128},{128,192},{192,0},{1,65},{65,129},{129,193},{193,1... | collective-permute-start | bytes 442376 | tf_op jit(solution)/shard_map/ppermute | solution.py:311
  57.5 16.5 %all-to-all-start.2 = ((bf16[8,128,128]{2,1,0:T(8,128)(2,1)}), bf16[8,128,128]{2,1,0:T(8,128)(2,1)S(1)}, u32[]{:S(2)}, u32[]{:S(2)}) async-start(bf16[8,128,128]{2,1,0:T(8,128)(2,1)} %add_up.1), calls=%async_computation.2 | async-start | bytes 524288 | tf_op jit(solution)/shard_map/all_to_all | solution.py:382
  62.6 5.7 %collective-permute-start.10 = (bf16[80,512]{1,0:T(8,128)(2,1)S(1)}, bf16[80,512]{1,0:T(8,128)(2,1)S(1)}, u32[]{:S(2)}, u32[]{:S(2)}) collective-permute-start(bf16[80,512]{1,0:T(8,128)(2,1)S(1)} %slice.6), channel_id=1, source_target_pairs={{0,64},{64,128},{128,192},{192,0},{1,65},{65,129},{129,193},{193,1... | collective-permute-start | bytes 245768 | tf_op jit(solution)/shard_map/ppermute | solution.py:311
  62.7 5.1 %collective-permute-start.11 = (bf16[64,512]{1,0:T(8,128)(2,1)S(1)}, bf16[64,512]{1,0:T(8,128)(2,1)S(1)}, u32[]{:S(2)}, u32[]{:S(2)}) collective-permute-start(bf16[64,512]{1,0:T(8,128)(2,1)S(1)} %slice.7), channel_id=1, source_target_pairs={{0,192},{64,0},{128,64},{192,128},{1,193},{65,1},{129,65},{193,129... | collective-permute-start | bytes 196616 | tf_op jit(solution)/shard_map/ppermute | solution.py:311
  68.4 1.9 %collective-permute-start.12 = (bf16[144,512]{1,0:T(8,128)(2,1)S(1)}, bf16[144,512]{1,0:T(8,128)(2,1)S(1)}, u32[]{:S(2)}, u32[]{:S(2)}) collective-permute-start(bf16[144,512]{1,0:T(8,128)(2,1)S(1)} %collective-permute-done.7.refs_5_), channel_id=1, source_target_pairs={{0,1},{1,0},{2,3},{3,2},{4,5},{5,4},{6,7},{7,6},{8,9},{9,8},{10,11... | collective-permute-start | bytes 442376 | tf_op jit(solution)/shard_map/ppermute | solution.py:311
  68.4 1.9 %collective-permute-start.15 = (bf16[144,512]{1,0:T(8,128)(2,1)S(1)}, bf16[144,512]{1,0:T(8,128)(2,1)S(1)}, u32[]{:S(2)}, u32[]{:S(2)}) collective-permute-start(bf16[144,512]{1,0:T(8,128)(2,1)S(1)} %collective-permute-done.8.refs_8_), channel_id=1, source_target_pairs={{0,1},{1,0},{2,3},{3,2},{4,5},{5,4},{6,7},{7,6},{8,9},{9,8},{10,11... | collective-permute-start | bytes 442376 | tf_op jit(solution)/shard_map/ppermute | solution.py:311
  68.9 1.3 %collective-permute-start.14 = (bf16[64,512]{1,0:T(8,128)(2,1)S(1)}, bf16[64,512]{1,0:T(8,128)(2,1)S(1)}, u32[]{:S(2)}, u32[]{:S(2)}) collective-permute-start(bf16[64,512]{1,0:T(8,128)(2,1)S(1)} %collective-permute-done.11.refs_7_), channel_id=1, source_target_pairs={{0,1},{1,0},{2,3},{3,2},{4,5},{5,4},{6,7},{7,6},{8,9},{9,8},{10,11... | collective-permute-start | bytes 196616 | tf_op jit(solution)/shard_map/ppermute | solution.py:311
  68.9 1.4 %collective-permute-start.13 = (bf16[80,512]{1,0:T(8,128)(2,1)S(1)}, bf16[80,512]{1,0:T(8,128)(2,1)S(1)}, u32[]{:S(2)}, u32[]{:S(2)}) collective-permute-start(bf16[80,512]{1,0:T(8,128)(2,1)S(1)} %collective-permute-done.10.refs_6_), channel_id=1, source_target_pairs={{0,1},{1,0},{2,3},{3,2},{4,5},{5,4},{6,7},{7,6},{8,9},{9,8},{10,11... | collective-permute-start | bytes 245768 | tf_op jit(solution)/shard_map/ppermute | solution.py:311
  80.1 19.9 %all-to-all-start.3 = ((bf16[32,32,128]{2,1,0:T(8,128)(2,1)}), bf16[32,32,128]{2,1,0:T(8,128)(2,1)S(1)}, u32[]{:S(2)}, u32[]{:S(2)}) async-start(bf16[32,32,128]{2,1,0:T(8,128)(2,1)} %bitcast.19), calls=%async_computation.3 | async-start | bytes 524288 | tf_op jit(solution)/shard_map/all_to_all | solution.py:399
  86.5 6.0 %collective-permute-start.16 = (f32[96,128]{1,0:T(8,128)}, f32[96,128]{1,0:T(8,128)S(1)}, u32[]{:S(2)}, u32[]{:S(2)}) collective-permute-start(f32[96,128]{1,0:T(8,128)} %get-tuple-element.45), channel_id=1, source_target_pairs={{0,64},{64,128},{128,192},{192,0},{1,65},{65,129},{129,193},{193,1... | collective-permute-start | bytes 147464 | tf_op jit(solution)/shard_map/ppermute | solution.py:311
  88.3 6.3 %collective-permute-start.17 = (f32[96,128]{1,0:T(8,128)}, f32[96,128]{1,0:T(8,128)S(1)}, u32[]{:S(2)}, u32[]{:S(2)}) collective-permute-start(f32[96,128]{1,0:T(8,128)} %get-tuple-element.46), channel_id=1, source_target_pairs={{0,128},{64,192},{128,0},{192,64},{1,129},{65,193},{129,1},{193,65... | collective-permute-start | bytes 147464 | tf_op jit(solution)/shard_map/ppermute | solution.py:311
  91.0 4.5 %collective-permute-start.18 = (f32[96,128]{1,0:T(8,128)}, f32[96,128]{1,0:T(8,128)S(1)}, u32[]{:S(2)}, u32[]{:S(2)}) collective-permute-start(f32[96,128]{1,0:T(8,128)} %get-tuple-element.47), channel_id=1, source_target_pairs={{0,192},{64,0},{128,64},{192,128},{1,193},{65,1},{129,65},{193,129... | collective-permute-start | bytes 147464 | tf_op jit(solution)/shard_map/ppermute | solution.py:311

commit v10 on v9

--- a/solution.py
+++ b/solution.py
@@ -121,8 +121,7 @@
         coefficients[g] = found[g * each : (g + 1) * each]
     high, low = split_bf(jnp.concatenate([first, second], axis=1), 2)
     shared[rows : rows + TAIL, :] = jnp.concatenate([pack_rows(high), pack_rows(low)], axis=1)
-    half = mine.shape[1]
-    mine[...] = shared[:, pl.ds(pl.multiple_of(columns[at] * half, half), half)].astype(F32)
+    mine[...] = shared[...].astype(F32)
 
 
 def first_pass(*refs):
@@ -188,7 +187,7 @@
 def second_pass(place, sketches, *refs):
     held, refs = refs[:4], refs[4:]
     groups = len(held)
-    out, sent, (turned, kept, sems) = refs[10], refs[11:-3], refs[-3:]
+    out, sent, (turned, kept, sems) = refs[5], refs[6:-3], refs[-3:]
     cuts, rows, cut = sketches.shape
     width = held[0].shape[1]
     targets = held[0].shape[0] // LANES
@@ -199,18 +198,10 @@
     ]
     grams = [lax.dot_general(s, s, NT, preferred_element_type=F32) for s in whole]
     inverses = jnp.concatenate(inverse_factors(grams), axis=1)
-    halves = [
-        [
-            refs[at][...],
-            refs[at + 1][...],
-            jnp.concatenate([refs[at + 2][...], refs[at + 3][...]], axis=0),
-            refs[at + 4][...],
-        ]
-        for at in (0, 5)
-    ]
+    panels = [refs[0][...], refs[1][...], jnp.concatenate([refs[2][...], refs[3][...]], axis=0), refs[4][...]]
     half = width // 2
     own = sent[0].shape[0] - rank
-    totals = [jnp.zeros((rows, half), F32) for _ in halves]
+    total = jnp.zeros((rows, width), F32)
     for s in range(groups):
         summed = jnp.concatenate(
             [
@@ -221,7 +212,7 @@
             ],
             axis=1,
         )
-        coupling = unpack_rows(halves[0][s][LANES:]).astype(F32) + unpack_rows(halves[1][s][LANES:]).astype(F32)
+        coupling = unpack_rows(panels[s][LANES:, :half]).astype(F32) + unpack_rows(panels[s][LANES:, half:]).astype(F32)
         middle = jnp.concatenate(
             [
                 lax.dot_general(
@@ -236,16 +227,13 @@
             axis=0,
         ).T
         for part in split_bf(middle, 2):
-            for h, panels in enumerate(halves):
-                totals[h] = totals[h] + jnp.dot(part, panels[s][0:LANES], preferred_element_type=F32)
-    for h, total in enumerate(totals):
-        side = place[2] if h == 0 else 1 - place[2]
-        for c in range(half // LANES):
-            block = total[:, c * LANES : (c + 1) * LANES].T.astype(out.dtype)
-            first = side * (half // own) + c * (LANES // own)
-            for k in range(LANES // own):
-                to = lax.rem(first + k, cuts) * groups + (first + k) // cuts
-                out[pl.ds(pl.multiple_of(to * own, own), own), :] = block[k * own : (k + 1) * own]
+            total = total + jnp.dot(part, panels[s][0:LANES], preferred_element_type=F32)
+    for c in range(width // LANES):
+        block = total[:, c * LANES : (c + 1) * LANES].T.astype(out.dtype)
+        for k in range(LANES // own):
+            first = c * (LANES // own) + k
+            to = (first % cuts) * groups + first // cuts
+            out[to * own : (to + 1) * own, :] = block[k * own : (k + 1) * own]
     for s in range(groups):
         owner = lax.rem(place[0] + s, groups)
         start = owner * (width // groups) + place[1] * own
@@ -336,12 +324,12 @@
     pair = jnp.stack([own, turn(own, "core", nc, 1)])
     pieces = [pair] + [turn(pair, "x", nx, s) for s in range(1, nx)]
     columns = jnp.stack(
-        [((x + nx - s) % nx) * nc + k for s in range(nx) for k in (c, (c + 1) % nc)] + [c]
+        [((x + nx - s) % nx) * nc + k for s in range(nx) for k in (c, (c + 1) % nc)]
     ).astype(jnp.int32)
-    mine_half, found = pl.pallas_call(
+    mine_all, found = pl.pallas_call(
         project,
         out_shape=(
-            jax.ShapeDtypeStruct((rows + TAIL, width // 2), F32),
+            jax.ShapeDtypeStruct((rows + TAIL, width), F32),
             jax.ShapeDtypeStruct((ny, own_rows, rows), BF),
         ),
         in_specs=[in_smem] + [in_vmem] * (nx + 2),
@@ -351,7 +339,7 @@
         name="project",
     )(columns, *pieces, probes.reshape(targets * rank, width), coupling)
     coefficients = lax.all_to_all(found, "y", 0, 0, tiled=True)
-    mine_half = mine_half.astype(BF)
+    mine_all = mine_all.astype(BF)
 
     cut = width // nz
     sketch = pl.pallas_call(
@@ -362,15 +350,12 @@
         compiler_params=params(20),
         name="first_pass",
     )(*held, coefficients)
-    mine_half, sketch = lax.optimization_barrier((mine_half, sketch))
-    near = [turn(mine_half, "y", ny, s) for s in (1, ny - 1)]
+    mine_all, sketch = lax.optimization_barrier((mine_all, sketch))
+    near = [turn(mine_all, "y", ny, s) for s in (1, ny - 1)]
     parts = lax.all_to_all(sketch, "z", 0, 0, tiled=True)
-    other_half = turn(mine_half, "core", nc, 1)
-    parts, near, other_half = lax.optimization_barrier((parts, near, other_half))
+    parts, near = lax.optimization_barrier((parts, near))
     far = [turn(near[0][:RELAY], "y", ny, 1), turn(near[1][RELAY:], "y", ny, ny - 1)]
-    near, far = lax.optimization_barrier((near, far))
-    halves = [near[0], *far, near[1]]
-    all_shared = [mine_half, *halves, other_half] + [turn(h, "core", nc, 1) for h in halves]
+    all_shared = [mine_all, near[0], *far, near[1]]
     copies = pl.pallas_call(
         add_up,
         out_shape=jax.ShapeDtypeStruct((nz, own_rows, cut), BF),
@@ -386,7 +371,7 @@
         second_pass,
         out_shape=(jax.ShapeDtypeStruct((width, own_rows), BF),)
         + (pltpu.HBM((rank + keep, own_rows), F32),) * ny,
-        in_specs=[in_smem] + [in_vmem] * 15,
+        in_specs=[in_smem] + [in_vmem] * 10,
         out_specs=(in_vmem,) + (pl.BlockSpec(memory_space=pltpu.HBM),) * ny,
         scratch_shapes=[
             VMEM((cut, own_rows), F32),

time: 103 us -> 102 us (level)
  waiting for transfers between devices: 36.4 us -> 33.1 us
  local copies, waits for them, and re-layouts: 1.25 us -> 2.61 us
    all_to_all x1, waiting for transfers between devices: 4.46 us -> 2.71 us  [shards(): lax.all_to_all(rows_part.reshape(ny * nz, keep, own_rows), ('z', 'y'), 0,...]
    ppermute x19 -> x14, starting transfers between devices: 20.4 us -> 19.2 us  [turn(): lax.ppermute(value, axis, [(i, (i + by) % size) for i in range(size)])]
    all_to_all x1, starting transfers between devices: 6.4 us -> 7.54 us  [shards(): lax.all_to_all(rows_part.reshape(ny * nz, keep, own_rows), ('z', 'y'), 0,...]
    ppermute x19 -> x14, waiting for transfers between devices: 22.4 us -> 22.5 us  [turn(): lax.ppermute(value, axis, [(i, (i + by) % size) for i in range(size)])]
  transfers between devices with their start and end apart: 23 -> 18, of which waited for: 15 -> 12; matrix products, arithmetic and copies ran while one was open for 3% -> 4% of each run, Pallas kernels for 3% -> 3%
where the time goes in v10:
time: 102 us
  starting transfers between devices  44.4 us (44%)
  waiting for transfers between devices  33.1 us (32%)
  Pallas kernels  17.5 us (17%)
  local copies, waits for them, and re-layouts  2.61 us (3%)
  other arithmetic  2.47 us (2%)
  between operations  1.54 us (2%)
    ppermute x14, waiting for transfers between devices, turn(): lax.ppermute(value, axis, [(i, (i + by) % size) for i in range(size)])  22.5 us
    ppermute x14, starting transfers between devices, turn(): lax.ppermute(value, axis, [(i, (i + by) % size) for i in range(size)])  19.2 us
    all_to_all x1, starting transfers between devices, shards(): parts = lax.all_to_all(sketch, 'z', 0, 0, tiled=True)  8.47 us
    all_to_all x1, starting transfers between devices, shards(): lax.all_to_all(rows_part.reshape(ny * nz, keep, own_rows), ('z', 'y'), 0,...  7.54 us
    pallas_call x1, Pallas kernels, shards(): pl.pallas_call(second_pass, out_shape=(jax.ShapeDtypeStruct((width, own_r...  6 us
    all_to_all x1, starting transfers between devices, shards(): sketches = lax.all_to_all(copies, 'z', 0, 0, tiled=True)  5.83 us
    pallas_call x1, Pallas kernels, shards(): pl.pallas_call(sum_factors, out_shape=(jax.ShapeDtypeStruct((held_rows, w...  3.95 us
    all_to_all x1, waiting for transfers between devices, shards(): coefficients = lax.all_to_all(found, 'y', 0, 0, tiled=True)  3.53 us
  transfers between devices with their start and end apart: 18, of which 12 were waited for; matrix products, arithmetic and copies ran while one was open for 4% of the time, Pallas kernels for 3%

profile of v10, /device:TPU:6, one launch (start us, length us, event | category | flops | bytes accessed | tf_op | source)
XLA Modules:
  0.0 101.6 jit_solution(4170951776475828549)
XLA Ops:
  1.3 3.9 %sum_factors.1 = (f32[256,1024]{1,0:T(8,128)}, bf16[256,1024]{1,0:T(8,128)(2,1)}, bf16[256,1024]{1,0:T(8,128)(2,1)}, bf16[256,1024]{1,0:T(8,128)(2,1)}) custom-call(s32[36]{0:T(128)} %bitcast.28, s32[36]{0:T(128)} %bitcast.29, s32[1]{0:T(128)} %bitcast.22.count, bf16[36,64,1024]{2,1,0:T(8,128)(2,1)} %bitcast.23), custom_call_target="tpu_custom_call" | custom-call | flops 10000000 | bytes 7000000 | tf_op jit(solution)/shard_map/sum_factors/pallas_call | solution.py:301
  5.2 1.7 %collective-permute-start.4 = (bf16[256,1024]{1,0:T(8,128)(2,1)}, bf16[256,1024]{1,0:T(8,128)(2,1)S(1)}, u32[]{:S(2)}, u32[]{:S(2)}) collective-permute-start(bf16[256,1024]{1,0:T(8,128)(2,1)} %get-tuple-element.22), channel_id=1, source_target_pairs={{0,64},{64,128},{128,192},{192,0},{1,65},{65,129},{129,193},{193,1... | collective-permute-start | bytes 1572872 | tf_op jit(solution)/shard_map/ppermute | solution.py:299
  6.9 2.9 %collective-permute-start.5 = (bf16[256,1024]{1,0:T(8,128)(2,1)}, bf16[256,1024]{1,0:T(8,128)(2,1)S(1)}, u32[]{:S(2)}, u32[]{:S(2)}) collective-permute-start(bf16[256,1024]{1,0:T(8,128)(2,1)} %get-tuple-element.23), channel_id=1, source_target_pairs={{0,128},{64,192},{128,0},{192,64},{1,129},{65,193},{129,1},{193,65... | collective-permute-start | bytes 1572872 | tf_op jit(solution)/shard_map/ppermute | solution.py:299
  9.8 1.3 %collective-permute-start.6 = (bf16[256,1024]{1,0:T(8,128)(2,1)}, bf16[256,1024]{1,0:T(8,128)(2,1)S(1)}, u32[]{:S(2)}, u32[]{:S(2)}) collective-permute-start(bf16[256,1024]{1,0:T(8,128)(2,1)} %get-tuple-element.24), channel_id=1, source_target_pairs={{0,192},{64,0},{128,64},{192,128},{1,193},{65,1},{129,65},{193,129... | collective-permute-start | bytes 1572872 | tf_op jit(solution)/shard_map/ppermute | solution.py:299
  11.2 0.0 collective-permute-start
  11.2 1.2 %collective-permute-done = bf16[128,128]{1,0:T(8,128)(2,1)S(1)} collective-permute-done((bf16[128,128]{1,0:T(8,128)(2,1)S(1)}, bf16[128,128]{1,0:T(8,128)(2,1)S(1)}, u32[]{:S(2)}, u32[]{:S(2)}) %collective-permute-start) | collective-permute-done | bytes 32800 | tf_op jit(solution)/shard_map/ppermute | solution.py:299
  12.4 0.0 copy-start
  12.4 0.9 collective-permute-start.3
  13.3 1.1 %collective-permute-start.2 = (bf16[2,128,128]{2,1,0:T(8,128)(2,1)S(1)}, bf16[2,128,128]{2,1,0:T(8,128)(2,1)S(1)}, u32[]{:S(2)}, u32[]{:S(2)}) collective-permute-start(bf16[2,128,128]{2,1,0:T(8,128)(2,1)S(1)} %pad_maximum_fusion.refs_0_), channel_id=1, source_target_pairs={{0,4},{2,6},{4,0},{6,2},{1,5},{3,7},{5,1},{7,3},{8,12},{10,14},{12... | collective-permute-start | bytes 196616 | tf_op jit(solution)/shard_map/ppermute | solution.py:299
  14.4 4.9 %collective-permute-done.3.refs_3_ = bf16[2,128,128]{2,1,0:T(8,128)(2,1)S(1)} collective-permute-done((bf16[2,128,128]{2,1,0:T(8,128)(2,1)S(1)}, bf16[2,128,128]{2,1,0:T(8,128)(2,1)S(1)}, u32[]{:S(2)}, u32[]{:S(2)}) %collective-permute-start.3) | collective-permute-done | bytes 65568 | tf_op jit(solution)/shard_map/ppermute | solution.py:299
  19.3 0.0 collective-permute-start.1
  19.4 0.6 stack.60.columns
  20.0 0.0 collective-permute-done.2.refs_2_
  20.0 3.6 %collective-permute-done.1.refs_1_ = bf16[2,128,128]{2,1,0:T(8,128)(2,1)S(1)} collective-permute-done((bf16[2,128,128]{2,1,0:T(8,128)(2,1)S(1)}, bf16[2,128,128]{2,1,0:T(8,128)(2,1)S(1)}, u32[]{:S(2)}, u32[]{:S(2)}) %collective-permute-start.1) | collective-permute-done | bytes 65568 | tf_op jit(solution)/shard_map/ppermute | solution.py:299
  23.6 0.6 copy-done.3
  24.2 3.3 %project.1 = (f32[144,1024]{1,0:T(8,128)}, bf16[4,128,128]{2,1,0:T(8,128)(2,1)}) custom-call(s32[8]{0:T(128)} %stack.60.columns, bf16[2,128,128]{2,1,0:T(8,128)(2,1)} %copy-done, bf16[2,128,128]{2,1,0:T(8,128)(2,1)} %copy-done.3, bf16[2,128,128]{2,1,0:T(8,128)(2,1)} %copy-done.2, bf16[2,128,128]{2,1,0:T(8,128)(2,1)} %copy-done.1, ...), custom_call_target="tpu_custom_call" | custom-call | tf_op jit(solution)/shard_map/project/pallas_call | solution.py:329
  27.6 3.3 %all-to-all-start = ((bf16[4,128,128]{2,1,0:T(8,128)(2,1)}), bf16[4,128,128]{2,1,0:T(8,128)(2,1)S(1)}, u32[]{:S(2)}, u32[]{:S(2)}) async-start(bf16[4,128,128]{2,1,0:T(8,128)(2,1)} %get-tuple-element.27), calls=%async_computation | async-start | bytes 262144 | tf_op jit(solution)/shard_map/all_to_all | solution.py:341
  30.9 1.3 %convert_element_type.7.refs_0_ = bf16[256,1024]{1,0:T(8,128)(2,1)S(1)} convert(f32[256,1024]{1,0:T(8,128)} %get-tuple-element.21) | non-fusion elementwise | flops 262144 | bytes 1572864 | tf_op jit(solution)/shard_map/convert_element_type | solution.py:321
  32.2 1.1 %convert_element_type.6.refs_4_ = bf16[144,1024]{1,0:T(8,128)(2,1)S(1)} convert(f32[144,1024]{1,0:T(8,128)} %get-tuple-element.26) | non-fusion elementwise | flops 147456 | bytes 884736 | tf_op jit(solution)/shard_map/convert_element_type | solution.py:342
  33.3 3.5 %all-to-all-done.refs_4_ = bf16[4,128,128]{2,1,0:T(8,128)(2,1)S(1)} async-done(((bf16[4,128,128]{2,1,0:T(8,128)(2,1)}), bf16[4,128,128]{2,1,0:T(8,128)(2,1)S(1)}, u32[]{:S(2)}, u32[]{:S(2)}) %all-to-all-start) | async-done | bytes 131104 | tf_op jit(solution)/shard_map/all_to_all | solution.py:341
  36.9 0.0 collective-permute-done.4.refs_1_
  36.9 0.0 collective-permute-done.5.refs_2_
  36.9 0.0 collective-permute-done.6.refs_3_
  36.9 1.1 %first_pass.1 = bf16[8,128,128]{2,1,0:T(8,128)(2,1)} custom-call(bf16[256,1024]{1,0:T(8,128)(2,1)S(1)} %convert_element_type.7.refs_0_, bf16[256,1024]{1,0:T(8,128)(2,1)S(1)} %collective-permute-done.4.refs_1_, bf16[256,1024]{1,0:T(8,128)(2,1)S(1)} %collective-permute-done.5.refs_2_, bf16[256,1024]{1,0:T(8,128)(2,1)S(1)} %collective-permute-done.6.refs_3_, ...), custom_call_target="tpu_custom_call" | custom-call | tf_op jit(solution)/shard_map/first_pass/pallas_call | solution.py:345
  38.0 8.5 %all-to-all-start.1 = ((bf16[8,128,128]{2,1,0:T(8,128)(2,1)}), bf16[8,128,128]{2,1,0:T(8,128)(2,1)S(1)}, u32[]{:S(2)}, u32[]{:S(2)}) async-start(bf16[8,128,128]{2,1,0:T(8,128)(2,1)} %first_pass.1), calls=%async_computation.1 | async-start | bytes 524288 | tf_op jit(solution)/shard_map/all_to_all | solution.py:355
  46.5 1.2 %collective-permute-start.8 = (bf16[144,1024]{1,0:T(8,128)(2,1)S(1)}, bf16[144,1024]{1,0:T(8,128)(2,1)S(1)}, u32[]{:S(2)}, u32[]{:S(2)}) collective-permute-start(bf16[144,1024]{1,0:T(8,128)(2,1)S(1)} %convert_element_type.6.refs_4_), channel_id=1, source_target_pairs={{0,192},{64,0},{128,64},{192,128},{1,193},{65,1},{129,65},{193,129... | collective-permute-start | bytes 884744 | tf_op jit(solution)/shard_map/ppermute | solution.py:299
  47.6 0.9 collective-permute-start.7
  48.5 4.7 %collective-permute-done.8.refs_8_ = bf16[144,1024]{1,0:T(8,128)(2,1)S(1)} collective-permute-done((bf16[144,1024]{1,0:T(8,128)(2,1)S(1)}, bf16[144,1024]{1,0:T(8,128)(2,1)S(1)}, u32[]{:S(2)}, u32[]{:S(2)}) %collective-permute-start.8) | collective-permute-done | bytes 294944 | tf_op jit(solution)/shard_map/ppermute | solution.py:299
  53.2 2.4 %collective-permute-done.7.refs_5_ = bf16[144,1024]{1,0:T(8,128)(2,1)S(1)} collective-permute-done((bf16[144,1024]{1,0:T(8,128)(2,1)S(1)}, bf16[144,1024]{1,0:T(8,128)(2,1)S(1)}, u32[]{:S(2)}, u32[]{:S(2)}) %collective-permute-start.7) | collective-permute-done | bytes 294944 | tf_op jit(solution)/shard_map/ppermute | solution.py:299
  55.6 1.4 %all-to-all-done.1.parts = bf16[8,128,128]{2,1,0:T(8,128)(2,1)S(1)} async-done(((bf16[8,128,128]{2,1,0:T(8,128)(2,1)}), bf16[8,128,128]{2,1,0:T(8,128)(2,1)S(1)}, u32[]{:S(2)}, u32[]{:S(2)}) %all-to-all-start.1) | async-done | bytes 262176 | tf_op jit(solution)/shard_map/all_to_all | solution.py:355
  57.0 0.7 add_up.1
  57.7 5.8 %all-to-all-start.2 = ((bf16[8,128,128]{2,1,0:T(8,128)(2,1)}), bf16[8,128,128]{2,1,0:T(8,128)(2,1)S(1)}, u32[]{:S(2)}, u32[]{:S(2)}) async-start(bf16[8,128,128]{2,1,0:T(8,128)(2,1)} %add_up.1), calls=%async_computation.2 | async-start | bytes 524288 | tf_op jit(solution)/shard_map/all_to_all | solution.py:367
  63.5 0.7 slice.6
  64.2 0.0 collective-permute-start.9
  64.2 0.7 slice.7
  64.9 3.2 %collective-permute-start.10 = (bf16[64,1024]{1,0:T(8,128)(2,1)}, bf16[64,1024]{1,0:T(8,128)(2,1)S(1)}, u32[]{:S(2)}, u32[]{:S(2)}) collective-permute-start(bf16[64,1024]{1,0:T(8,128)(2,1)} %slice.7), channel_id=1, source_target_pairs={{0,192},{64,0},{128,64},{192,128},{1,193},{65,1},{129,65},{193,129... | collective-permute-start | bytes 393224 | tf_op jit(solution)/shard_map/ppermute | solution.py:299
  68.1 0.1 pad_add_fusion.place
  68.2 2.8 %collective-permute-done.10.refs_7_ = bf16[64,1024]{1,0:T(8,128)(2,1)S(1)} collective-permute-done((bf16[64,1024]{1,0:T(8,128)(2,1)}, bf16[64,1024]{1,0:T(8,128)(2,1)S(1)}, u32[]{:S(2)}, u32[]{:S(2)}) %collective-permute-start.10) | collective-permute-done | bytes 131104 | tf_op jit(solution)/shard_map/ppermute | solution.py:299
  71.0 3.1 %all-to-all-done.2.sketches = bf16[8,128,128]{2,1,0:T(8,128)(2,1)S(1)} async-done(((bf16[8,128,128]{2,1,0:T(8,128)(2,1)}), bf16[8,128,128]{2,1,0:T(8,128)(2,1)S(1)}, u32[]{:S(2)}, u32[]{:S(2)}) %all-to-all-start.2) | async-done | bytes 262176 | tf_op jit(solution)/shard_map/all_to_all | solution.py:367
  74.0 6.0 %second_pass.1 = (bf16[1024,128]{1,0:T(8,128)(2,1)}, f32[96,128]{1,0:T(8,128)}, f32[96,128]{1,0:T(8,128)}, f32[96,128]{1,0:T(8,128)}, f32[96,128]{1,0:T(8,128)}) custom-call(s32[3]{0:T(128)S(1)} %pad_add_fusion.place, bf16[8,128,128]{2,1,0:T(8,128)(2,1)S(1)} %all-to-all-done.2.sketches, bf16[256,1024]{1,0:T(8,128)(2,1)S(1)} %convert_element_type.7.refs_0_, ...), custom_call_target="tpu_custom_call" | custom-call | tf_op jit(solution)/shard_map/second_pass/pallas_call | solution.py:370
  80.0 7.5 %all-to-all-start.3 = ((bf16[32,32,128]{2,1,0:T(8,128)(2,1)}), bf16[32,32,128]{2,1,0:T(8,128)(2,1)S(1)}, u32[]{:S(2)}, u32[]{:S(2)}) async-start(bf16[32,32,128]{2,1,0:T(8,128)(2,1)} %bitcast.19), calls=%async_computation.3 | async-start | bytes 524288 | tf_op jit(solution)/shard_map/all_to_all | solution.py:384
  87.6 1.9 %collective-permute-start.11 = (f32[96,128]{1,0:T(8,128)}, f32[96,128]{1,0:T(8,128)S(1)}, u32[]{:S(2)}, u32[]{:S(2)}) collective-permute-start(f32[96,128]{1,0:T(8,128)} %get-tuple-element.35), channel_id=1, source_target_pairs={{0,64},{64,128},{128,192},{192,0},{1,65},{65,129},{129,193},{193,1... | collective-permute-start | bytes 147464 | tf_op jit(solution)/shard_map/ppermute | solution.py:299
  89.4 2.7 %collective-permute-start.12 = (f32[96,128]{1,0:T(8,128)}, f32[96,128]{1,0:T(8,128)S(1)}, u32[]{:S(2)}, u32[]{:S(2)}) collective-permute-start(f32[96,128]{1,0:T(8,128)} %get-tuple-element.36), channel_id=1, source_target_pairs={{0,128},{64,192},{128,0},{192,64},{1,129},{65,193},{129,1},{193,65... | collective-permute-start | bytes 147464 | tf_op jit(solution)/shard_map/ppermute | solution.py:299
  92.1 1.5 %collective-permute-start.13 = (f32[96,128]{1,0:T(8,128)}, f32[96,128]{1,0:T(8,128)S(1)}, u32[]{:S(2)}, u32[]{:S(2)}) collective-permute-start(f32[96,128]{1,0:T(8,128)} %get-tuple-element.37), channel_id=1, source_target_pairs={{0,192},{64,0},{128,64},{192,128},{1,193},{65,1},{129,65},{193,129... | collective-permute-start | bytes 147464 | tf_op jit(solution)/shard_map/ppermute | solution.py:299
  93.6 2.1 %collective-permute-done.12.refs_1_ = f32[96,128]{1,0:T(8,128)S(1)} collective-permute-done((f32[96,128]{1,0:T(8,128)}, f32[96,128]{1,0:T(8,128)S(1)}, u32[]{:S(2)}, u32[]{:S(2)}) %collective-permute-start.12) | collective-permute-done | bytes 49184 | tf_op jit(solution)/shard_map/ppermute | solution.py:299
  95.7 0.7 collective-permute-done.13.refs_2_
  96.4 2.7 %all-to-all-done.3.parts = bf16[32,32,128]{2,1,0:T(8,128)(2,1)S(1)} async-done(((bf16[32,32,128]{2,1,0:T(8,128)(2,1)}), bf16[32,32,128]{2,1,0:T(8,128)(2,1)S(1)}, u32[]{:S(2)}, u32[]{:S(2)}) %all-to-all-start.3) | async-done | bytes 262176 | tf_op jit(solution)/shard_map/all_to_all | solution.py:384
  99.1 2.3 %finish.1 = (f32[8,32,64]{2,1,0:T(8,128)}, f32[8,32,64]{2,1,0:T(8,128)}) custom-call(s32[3]{0:T(128)S(1)} %pad_add_fusion.place, bf16[32,32,128]{2,1,0:T(8,128)(2,1)S(1)} %all-to-all-done.3.parts, f32[96,128]{1,0:T(8,128)} %get-tuple-element.34.own_far, f32[96,128]{1,0:T(8,128)S(1)} %collective-permute-done.11.refs_0_, ...), custom_call_target="tpu_custom_call" | custom-call | tf_op jit(solution)/shard_map/finish/pallas_call | solution.py:387
  (11 shorter events, 0.0 us)
Async XLA Ops:
  0.6 10.5 %copy-start.4 = (bf16[2,64,128]{2,1,0:T(8,128)(2,1)S(1)}, bf16[2,64,128]{2,1,0:T(8,128)(2,1)}, u32[]{:S(2)}) copy-start(bf16[2,64,128]{2,1,0:T(8,128)(2,1)} %param.11) | copy-start | bytes 98308
  5.2 31.6 %collective-permute-start.4 = (bf16[256,1024]{1,0:T(8,128)(2,1)}, bf16[256,1024]{1,0:T(8,128)(2,1)S(1)}, u32[]{:S(2)}, u32[]{:S(2)}) collective-permute-start(bf16[256,1024]{1,0:T(8,128)(2,1)} %get-tuple-element.22), channel_id=1, source_target_pairs={{0,64},{64,128},{128,192},{192,0},{1,65},{65,129},{129,193},{193,1... | collective-permute-start | bytes 1572872 | tf_op jit(solution)/shard_map/ppermute | solution.py:299
  6.9 30.0 %collective-permute-start.5 = (bf16[256,1024]{1,0:T(8,128)(2,1)}, bf16[256,1024]{1,0:T(8,128)(2,1)S(1)}, u32[]{:S(2)}, u32[]{:S(2)}) collective-permute-start(bf16[256,1024]{1,0:T(8,128)(2,1)} %get-tuple-element.23), channel_id=1, source_target_pairs={{0,128},{64,192},{128,0},{192,64},{1,129},{65,193},{129,1},{193,65... | collective-permute-start | bytes 1572872 | tf_op jit(solution)/shard_map/ppermute | solution.py:299
  9.8 27.1 %collective-permute-start.6 = (bf16[256,1024]{1,0:T(8,128)(2,1)}, bf16[256,1024]{1,0:T(8,128)(2,1)S(1)}, u32[]{:S(2)}, u32[]{:S(2)}) collective-permute-start(bf16[256,1024]{1,0:T(8,128)(2,1)} %get-tuple-element.24), channel_id=1, source_target_pairs={{0,192},{64,0},{128,64},{192,128},{1,193},{65,1},{129,65},{193,129... | collective-permute-start | bytes 1572872 | tf_op jit(solution)/shard_map/ppermute | solution.py:299
  11.2 1.2 %collective-permute-start = (bf16[128,128]{1,0:T(8,128)(2,1)S(1)}, bf16[128,128]{1,0:T(8,128)(2,1)S(1)}, u32[]{:S(2)}, u32[]{:S(2)}) collective-permute-start(bf16[128,128]{1,0:T(8,128)(2,1)S(1)} %bitcast.25), channel_id=1, source_target_pairs={{0,1},{1,0},{2,3},{3,2},{4,5},{5,4},{6,7},{7,6},{8,9},{9,8},{10,11... | collective-permute-start | bytes 98312 | tf_op jit(solution)/shard_map/ppermute | solution.py:299
  12.4 11.2 %copy-start = (bf16[2,128,128]{2,1,0:T(8,128)(2,1)}, bf16[2,128,128]{2,1,0:T(8,128)(2,1)S(1)}, u32[]{:S(2)}) copy-start(bf16[2,128,128]{2,1,0:T(8,128)(2,1)S(1)} %pad_maximum_fusion.refs_0_) | copy-start | bytes 196612
  12.4 7.0 %collective-permute-start.3 = (bf16[2,128,128]{2,1,0:T(8,128)(2,1)S(1)}, bf16[2,128,128]{2,1,0:T(8,128)(2,1)S(1)}, u32[]{:S(2)}, u32[]{:S(2)}) collective-permute-start(bf16[2,128,128]{2,1,0:T(8,128)(2,1)S(1)} %pad_maximum_fusion.refs_0_), channel_id=1, source_target_pairs={{0,6},{2,0},{4,2},{6,4},{1,7},{3,1},{5,3},{7,5},{8,14},{10,8},{12,... | collective-permute-start | bytes 196616 | tf_op jit(solution)/shard_map/ppermute | solution.py:299
  13.3 6.7 %collective-permute-start.2 = (bf16[2,128,128]{2,1,0:T(8,128)(2,1)S(1)}, bf16[2,128,128]{2,1,0:T(8,128)(2,1)S(1)}, u32[]{:S(2)}, u32[]{:S(2)}) collective-permute-start(bf16[2,128,128]{2,1,0:T(8,128)(2,1)S(1)} %pad_maximum_fusion.refs_0_), channel_id=1, source_target_pairs={{0,4},{2,6},{4,0},{6,2},{1,5},{3,7},{5,1},{7,3},{8,12},{10,14},{12... | collective-permute-start | bytes 196616 | tf_op jit(solution)/shard_map/ppermute | solution.py:299
  19.3 4.3 %copy-start.1 = (bf16[2,128,128]{2,1,0:T(8,128)(2,1)}, bf16[2,128,128]{2,1,0:T(8,128)(2,1)S(1)}, u32[]{:S(2)}) copy-start(bf16[2,128,128]{2,1,0:T(8,128)(2,1)S(1)} %collective-permute-done.3.refs_3_) | copy-start | bytes 196612
  19.3 4.3 %collective-permute-start.1 = (bf16[2,128,128]{2,1,0:T(8,128)(2,1)S(1)}, bf16[2,128,128]{2,1,0:T(8,128)(2,1)S(1)}, u32[]{:S(2)}, u32[]{:S(2)}) collective-permute-start(bf16[2,128,128]{2,1,0:T(8,128)(2,1)S(1)} %pad_maximum_fusion.refs_0_), channel_id=1, source_target_pairs={{0,2},{2,4},{4,6},{6,0},{1,3},{3,5},{5,7},{7,1},{8,10},{10,12},{12... | collective-permute-start | bytes 196616 | tf_op jit(solution)/shard_map/ppermute | solution.py:299
  20.0 3.6 %copy-start.2 = (bf16[2,128,128]{2,1,0:T(8,128)(2,1)}, bf16[2,128,128]{2,1,0:T(8,128)(2,1)S(1)}, u32[]{:S(2)}) copy-start(bf16[2,128,128]{2,1,0:T(8,128)(2,1)S(1)} %collective-permute-done.2.refs_2_) | copy-start | bytes 196612
  23.6 0.6 copy-start.3
  27.6 9.3 %all-to-all-start = ((bf16[4,128,128]{2,1,0:T(8,128)(2,1)}), bf16[4,128,128]{2,1,0:T(8,128)(2,1)S(1)}, u32[]{:S(2)}, u32[]{:S(2)}) async-start(bf16[4,128,128]{2,1,0:T(8,128)(2,1)} %get-tuple-element.27), calls=%async_computation | async-start | bytes 262144 | tf_op jit(solution)/shard_map/all_to_all | solution.py:341
  38.0 18.9 %all-to-all-start.1 = ((bf16[8,128,128]{2,1,0:T(8,128)(2,1)}), bf16[8,128,128]{2,1,0:T(8,128)(2,1)S(1)}, u32[]{:S(2)}, u32[]{:S(2)}) async-start(bf16[8,128,128]{2,1,0:T(8,128)(2,1)} %first_pass.1), calls=%async_computation.1 | async-start | bytes 524288 | tf_op jit(solution)/shard_map/all_to_all | solution.py:355
  46.5 6.7 %collective-permute-start.8 = (bf16[144,1024]{1,0:T(8,128)(2,1)S(1)}, bf16[144,1024]{1,0:T(8,128)(2,1)S(1)}, u32[]{:S(2)}, u32[]{:S(2)}) collective-permute-start(bf16[144,1024]{1,0:T(8,128)(2,1)S(1)} %convert_element_type.6.refs_4_), channel_id=1, source_target_pairs={{0,192},{64,0},{128,64},{192,128},{1,193},{65,1},{129,65},{193,129... | collective-permute-start | bytes 884744 | tf_op jit(solution)/shard_map/ppermute | solution.py:299
  47.6 7.9 %collective-permute-start.7 = (bf16[144,1024]{1,0:T(8,128)(2,1)S(1)}, bf16[144,1024]{1,0:T(8,128)(2,1)S(1)}, u32[]{:S(2)}, u32[]{:S(2)}) collective-permute-start(bf16[144,1024]{1,0:T(8,128)(2,1)S(1)} %convert_element_type.6.refs_4_), channel_id=1, source_target_pairs={{0,64},{64,128},{128,192},{192,0},{1,65},{65,129},{129,193},{193,1... | collective-permute-start | bytes 884744 | tf_op jit(solution)/shard_map/ppermute | solution.py:299
  57.7 16.3 %all-to-all-start.2 = ((bf16[8,128,128]{2,1,0:T(8,128)(2,1)}), bf16[8,128,128]{2,1,0:T(8,128)(2,1)S(1)}, u32[]{:S(2)}, u32[]{:S(2)}) async-start(bf16[8,128,128]{2,1,0:T(8,128)(2,1)} %add_up.1), calls=%async_computation.2 | async-start | bytes 524288 | tf_op jit(solution)/shard_map/all_to_all | solution.py:367
  64.2 6.7 %collective-permute-start.9 = (bf16[80,1024]{1,0:T(8,128)(2,1)}, bf16[80,1024]{1,0:T(8,128)(2,1)S(1)}, u32[]{:S(2)}, u32[]{:S(2)}) collective-permute-start(bf16[80,1024]{1,0:T(8,128)(2,1)} %slice.6), channel_id=1, source_target_pairs={{0,64},{64,128},{128,192},{192,0},{1,65},{65,129},{129,193},{193,1... | collective-permute-start | bytes 491528 | tf_op jit(solution)/shard_map/ppermute | solution.py:299
  64.9 6.1 %collective-permute-start.10 = (bf16[64,1024]{1,0:T(8,128)(2,1)}, bf16[64,1024]{1,0:T(8,128)(2,1)S(1)}, u32[]{:S(2)}, u32[]{:S(2)}) collective-permute-start(bf16[64,1024]{1,0:T(8,128)(2,1)} %slice.7), channel_id=1, source_target_pairs={{0,192},{64,0},{128,64},{192,128},{1,193},{65,1},{129,65},{193,129... | collective-permute-start | bytes 393224 | tf_op jit(solution)/shard_map/ppermute | solution.py:299
  80.0 19.1 %all-to-all-start.3 = ((bf16[32,32,128]{2,1,0:T(8,128)(2,1)}), bf16[32,32,128]{2,1,0:T(8,128)(2,1)S(1)}, u32[]{:S(2)}, u32[]{:S(2)}) async-start(bf16[32,32,128]{2,1,0:T(8,128)(2,1)} %bitcast.19), calls=%async_computation.3 | async-start | bytes 524288 | tf_op jit(solution)/shard_map/all_to_all | solution.py:384
  87.6 6.0 %collective-permute-start.11 = (f32[96,128]{1,0:T(8,128)}, f32[96,128]{1,0:T(8,128)S(1)}, u32[]{:S(2)}, u32[]{:S(2)}) collective-permute-start(f32[96,128]{1,0:T(8,128)} %get-tuple-element.35), channel_id=1, source_target_pairs={{0,64},{64,128},{128,192},{192,0},{1,65},{65,129},{129,193},{193,1... | collective-permute-start | bytes 147464 | tf_op jit(solution)/shard_map/ppermute | solution.py:299
  89.4 6.3 %collective-permute-start.12 = (f32[96,128]{1,0:T(8,128)}, f32[96,128]{1,0:T(8,128)S(1)}, u32[]{:S(2)}, u32[]{:S(2)}) collective-permute-start(f32[96,128]{1,0:T(8,128)} %get-tuple-element.36), channel_id=1, source_target_pairs={{0,128},{64,192},{128,0},{192,64},{1,129},{65,193},{129,1},{193,65... | collective-permute-start | bytes 147464 | tf_op jit(solution)/shard_map/ppermute | solution.py:299
  92.1 4.3 %collective-permute-start.13 = (f32[96,128]{1,0:T(8,128)}, f32[96,128]{1,0:T(8,128)S(1)}, u32[]{:S(2)}, u32[]{:S(2)}) collective-permute-start(f32[96,128]{1,0:T(8,128)} %get-tuple-element.37), channel_id=1, source_target_pairs={{0,192},{64,0},{128,64},{192,128},{1,193},{65,1},{129,65},{193,129... | collective-permute-start | bytes 147464 | tf_op jit(solution)/shard_map/ppermute | solution.py:299

commit v11 on v10

--- a/solution.py
+++ b/solution.py
@@ -146,12 +146,20 @@
             out[z, t * rank : (t + 1) * rank, :] = totals[t][:, z * cut : (z + 1) * cut].astype(BF)
 
 
-def add_up(parts, out):
+def add_up(parts, above, below, out, first, second, sems):
+    moves = [
+        pltpu.make_async_copy(above.at[0:RELAY, :], first, sems.at[0]),
+        pltpu.make_async_copy(below.at[RELAY:, :], second, sems.at[1]),
+    ]
+    for copy in moves:
+        copy.start()
     total = parts[0].astype(F32)
     for z in range(1, parts.shape[0]):
         total = total + parts[z].astype(F32)
     for z in range(out.shape[0]):
         out[z] = total.astype(out.dtype)
+    for copy in moves:
+        copy.wait()
 
 
 def inverse_factors(grams):
@@ -354,16 +362,21 @@
     near = [turn(mine_all, "y", ny, s) for s in (1, ny - 1)]
     parts = lax.all_to_all(sketch, "z", 0, 0, tiled=True)
     parts, near = lax.optimization_barrier((parts, near))
-    far = [turn(near[0][:RELAY], "y", ny, 1), turn(near[1][RELAY:], "y", ny, ny - 1)]
-    all_shared = [mine_all, near[0], *far, near[1]]
-    copies = pl.pallas_call(
+    copies, above, below = pl.pallas_call(
         add_up,
-        out_shape=jax.ShapeDtypeStruct((nz, own_rows, cut), BF),
-        in_specs=[in_vmem],
-        out_specs=in_vmem,
+        out_shape=(
+            jax.ShapeDtypeStruct((nz, own_rows, cut), BF),
+            pltpu.HBM((RELAY, width), BF),
+            pltpu.HBM((rows + TAIL - RELAY, width), BF),
+        ),
+        in_specs=[in_vmem] * 3,
+        out_specs=(in_vmem,) + (pl.BlockSpec(memory_space=pltpu.HBM),) * 2,
+        scratch_shapes=[pltpu.SemaphoreType.DMA((2,))],
         compiler_params=params(8),
         name="add_up",
-    )(parts)
+    )(parts, *near)
+    far = [turn(above, "y", ny, 1), turn(below, "y", ny, ny - 1)]
+    all_shared = [mine_all, near[0], *far, near[1]]
     sketches = lax.all_to_all(copies, "z", 0, 0, tiled=True)
 
     keep = width // (ny * nz)

time: 102 us -> 102 us (level)
  starting transfers between devices: 44.4 us -> 43 us
  waiting for transfers between devices: 33.1 us -> 34.5 us
  local copies, waits for them, and re-layouts: 2.61 us -> 1.27 us
    slice x2 -> x0, local copies, waits for them, and re-layouts: 1.35 us -> none  [the longest x1 0.68 us: shards(): near[0][:RELAY]]
    all_to_all x1, starting transfers between devices: 7.54 us -> 6.2 us  [shards(): lax.all_to_all(rows_part.reshape(ny * nz, keep, own_rows), ('z', 'y'), 0,...]
  transfers between devices with their start and end apart: 18 -> 18, of which waited for: 12 -> 13; matrix products, arithmetic and copies ran while one was open for 4% -> 3% of each run, Pallas kernels for 3% -> 3%
where the time goes in v11:
time: 102 us; the launch traced here: 101 us
  starting transfers between devices  43 us (42%)
  waiting for transfers between devices  34.5 us (34%)
  Pallas kernels  18.2 us (18%)
  other arithmetic  2.47 us (2%)
  between operations  1.55 us (2%)
  local copies, waits for them, and re-layouts  1.27 us (1%)
    ppermute x14, waiting for transfers between devices, turn(): lax.ppermute(value, axis, [(i, (i + by) % size) for i in range(size)])  23.1 us
    ppermute x14, starting transfers between devices, turn(): lax.ppermute(value, axis, [(i, (i + by) % size) for i in range(size)])  19.2 us
    all_to_all x1, starting transfers between devices, shards(): parts = lax.all_to_all(sketch, 'z', 0, 0, tiled=True)  8.47 us
    all_to_all x1, starting transfers between devices, shards(): lax.all_to_all(rows_part.reshape(ny * nz, keep, own_rows), ('z', 'y'), 0,...  6.2 us
    pallas_call x1, Pallas kernels, shards(): pl.pallas_call(second_pass, out_shape=(jax.ShapeDtypeStruct((width, own_r...  6 us
    all_to_all x1, starting transfers between devices, shards(): sketches = lax.all_to_all(copies, 'z', 0, 0, tiled=True)  5.84 us
    pallas_call x1, Pallas kernels, shards(): pl.pallas_call(sum_factors, out_shape=(jax.ShapeDtypeStruct((held_rows, w...  3.95 us
    all_to_all x1, waiting for transfers between devices, shards(): sketches = lax.all_to_all(copies, 'z', 0, 0, tiled=True)  3.74 us
  transfers between devices with their start and end apart: 18, of which 13 were waited for; matrix products, arithmetic and copies ran while one was open for 3% of the time, Pallas kernels for 3%

profile of v11, /device:TPU:6, one launch (start us, length us, event | category | flops | bytes accessed | tf_op | source)
XLA Modules:
  0.0 101.0 jit_solution(9021741917668543658)
XLA Ops:
  1.3 4.0 %sum_factors.1 = (f32[256,1024]{1,0:T(8,128)}, bf16[256,1024]{1,0:T(8,128)(2,1)}, bf16[256,1024]{1,0:T(8,128)(2,1)}, bf16[256,1024]{1,0:T(8,128)(2,1)}) custom-call(s32[36]{0:T(128)} %bitcast.28, s32[36]{0:T(128)} %bitcast.29, s32[1]{0:T(128)} %bitcast.22.count, bf16[36,64,1024]{2,1,0:T(8,128)(2,1)} %bitcast.23), custom_call_target="tpu_custom_call" | custom-call | flops 10000000 | bytes 7000000 | tf_op jit(solution)/shard_map/sum_factors/pallas_call | solution.py:309
  5.3 1.7 %collective-permute-start.4 = (bf16[256,1024]{1,0:T(8,128)(2,1)}, bf16[256,1024]{1,0:T(8,128)(2,1)S(1)}, u32[]{:S(2)}, u32[]{:S(2)}) collective-permute-start(bf16[256,1024]{1,0:T(8,128)(2,1)} %get-tuple-element.25), channel_id=1, source_target_pairs={{0,64},{64,128},{128,192},{192,0},{1,65},{65,129},{129,193},{193,1... | collective-permute-start | bytes 1572872 | tf_op jit(solution)/shard_map/ppermute | solution.py:307
  6.9 2.9 %collective-permute-start.5 = (bf16[256,1024]{1,0:T(8,128)(2,1)}, bf16[256,1024]{1,0:T(8,128)(2,1)S(1)}, u32[]{:S(2)}, u32[]{:S(2)}) collective-permute-start(bf16[256,1024]{1,0:T(8,128)(2,1)} %get-tuple-element.26), channel_id=1, source_target_pairs={{0,128},{64,192},{128,0},{192,64},{1,129},{65,193},{129,1},{193,65... | collective-permute-start | bytes 1572872 | tf_op jit(solution)/shard_map/ppermute | solution.py:307
  9.8 1.3 %collective-permute-start.6 = (bf16[256,1024]{1,0:T(8,128)(2,1)}, bf16[256,1024]{1,0:T(8,128)(2,1)S(1)}, u32[]{:S(2)}, u32[]{:S(2)}) collective-permute-start(bf16[256,1024]{1,0:T(8,128)(2,1)} %get-tuple-element.27), channel_id=1, source_target_pairs={{0,192},{64,0},{128,64},{192,128},{1,193},{65,1},{129,65},{193,129... | collective-permute-start | bytes 1572872 | tf_op jit(solution)/shard_map/ppermute | solution.py:307
  11.2 0.0 collective-permute-start
  11.2 1.2 %collective-permute-done = bf16[128,128]{1,0:T(8,128)(2,1)S(1)} collective-permute-done((bf16[128,128]{1,0:T(8,128)(2,1)S(1)}, bf16[128,128]{1,0:T(8,128)(2,1)S(1)}, u32[]{:S(2)}, u32[]{:S(2)}) %collective-permute-start) | collective-permute-done | bytes 32800 | tf_op jit(solution)/shard_map/ppermute | solution.py:307
  12.4 0.0 copy-start
  12.4 1.1 %collective-permute-start.3 = (bf16[2,128,128]{2,1,0:T(8,128)(2,1)S(1)}, bf16[2,128,128]{2,1,0:T(8,128)(2,1)S(1)}, u32[]{:S(2)}, u32[]{:S(2)}) collective-permute-start(bf16[2,128,128]{2,1,0:T(8,128)(2,1)S(1)} %pad_maximum_fusion.refs_0_), channel_id=1, source_target_pairs={{0,6},{2,0},{4,2},{6,4},{1,7},{3,1},{5,3},{7,5},{8,14},{10,8},{12,... | collective-permute-start | bytes 196616 | tf_op jit(solution)/shard_map/ppermute | solution.py:307
  13.5 1.0 collective-permute-start.2
  14.4 4.9 %collective-permute-done.3.refs_3_ = bf16[2,128,128]{2,1,0:T(8,128)(2,1)S(1)} collective-permute-done((bf16[2,128,128]{2,1,0:T(8,128)(2,1)S(1)}, bf16[2,128,128]{2,1,0:T(8,128)(2,1)S(1)}, u32[]{:S(2)}, u32[]{:S(2)}) %collective-permute-start.3) | collective-permute-done | bytes 65568 | tf_op jit(solution)/shard_map/ppermute | solution.py:307
  19.4 0.0 collective-permute-start.1
  19.4 0.6 stack.60.columns
  20.0 0.0 collective-permute-done.2.refs_2_
  20.0 3.6 %collective-permute-done.1.refs_1_ = bf16[2,128,128]{2,1,0:T(8,128)(2,1)S(1)} collective-permute-done((bf16[2,128,128]{2,1,0:T(8,128)(2,1)S(1)}, bf16[2,128,128]{2,1,0:T(8,128)(2,1)S(1)}, u32[]{:S(2)}, u32[]{:S(2)}) %collective-permute-start.1) | collective-permute-done | bytes 65568 | tf_op jit(solution)/shard_map/ppermute | solution.py:307
  23.6 0.6 copy-done.3
  24.2 3.3 %project.1 = (f32[144,1024]{1,0:T(8,128)}, bf16[4,128,128]{2,1,0:T(8,128)(2,1)}) custom-call(s32[8]{0:T(128)} %stack.60.columns, bf16[2,128,128]{2,1,0:T(8,128)(2,1)} %copy-done, bf16[2,128,128]{2,1,0:T(8,128)(2,1)} %copy-done.3, bf16[2,128,128]{2,1,0:T(8,128)(2,1)} %copy-done.2, bf16[2,128,128]{2,1,0:T(8,128)(2,1)} %copy-done.1, ...), custom_call_target="tpu_custom_call" | custom-call | tf_op jit(solution)/shard_map/project/pallas_call | solution.py:337
  27.6 3.3 %all-to-all-start = ((bf16[4,128,128]{2,1,0:T(8,128)(2,1)}), bf16[4,128,128]{2,1,0:T(8,128)(2,1)S(1)}, u32[]{:S(2)}, u32[]{:S(2)}) async-start(bf16[4,128,128]{2,1,0:T(8,128)(2,1)} %get-tuple-element.30), calls=%async_computation | async-start | bytes 262144 | tf_op jit(solution)/shard_map/all_to_all | solution.py:349
  30.9 1.3 %convert_element_type.7.refs_0_ = bf16[256,1024]{1,0:T(8,128)(2,1)S(1)} convert(f32[256,1024]{1,0:T(8,128)} %get-tuple-element.24) | non-fusion elementwise | flops 262144 | bytes 1572864 | tf_op jit(solution)/shard_map/convert_element_type | solution.py:329
  32.2 1.1 %convert_element_type.6.refs_4_ = bf16[144,1024]{1,0:T(8,128)(2,1)S(1)} convert(f32[144,1024]{1,0:T(8,128)} %get-tuple-element.29) | non-fusion elementwise | flops 147456 | bytes 884736 | tf_op jit(solution)/shard_map/convert_element_type | solution.py:350
  33.3 3.5 %all-to-all-done.refs_4_ = bf16[4,128,128]{2,1,0:T(8,128)(2,1)S(1)} async-done(((bf16[4,128,128]{2,1,0:T(8,128)(2,1)}), bf16[4,128,128]{2,1,0:T(8,128)(2,1)S(1)}, u32[]{:S(2)}, u32[]{:S(2)}) %all-to-all-start) | async-done | bytes 131104 | tf_op jit(solution)/shard_map/all_to_all | solution.py:349
  36.9 0.0 collective-permute-done.4.refs_1_
  36.9 0.0 collective-permute-done.5.refs_2_
  36.9 0.0 collective-permute-done.6.refs_3_
  36.9 1.1 %first_pass.1 = bf16[8,128,128]{2,1,0:T(8,128)(2,1)} custom-call(bf16[256,1024]{1,0:T(8,128)(2,1)S(1)} %convert_element_type.7.refs_0_, bf16[256,1024]{1,0:T(8,128)(2,1)S(1)} %collective-permute-done.4.refs_1_, bf16[256,1024]{1,0:T(8,128)(2,1)S(1)} %collective-permute-done.5.refs_2_, bf16[256,1024]{1,0:T(8,128)(2,1)S(1)} %collective-permute-done.6.refs_3_, ...), custom_call_target="tpu_custom_call" | custom-call | tf_op jit(solution)/shard_map/first_pass/pallas_call | solution.py:353
  38.0 8.5 %all-to-all-start.1 = ((bf16[8,128,128]{2,1,0:T(8,128)(2,1)}), bf16[8,128,128]{2,1,0:T(8,128)(2,1)S(1)}, u32[]{:S(2)}, u32[]{:S(2)}) async-start(bf16[8,128,128]{2,1,0:T(8,128)(2,1)} %first_pass.1), calls=%async_computation.1 | async-start | bytes 524288 | tf_op jit(solution)/shard_map/all_to_all | solution.py:363
  46.5 1.2 %collective-permute-start.8 = (bf16[144,1024]{1,0:T(8,128)(2,1)S(1)}, bf16[144,1024]{1,0:T(8,128)(2,1)S(1)}, u32[]{:S(2)}, u32[]{:S(2)}) collective-permute-start(bf16[144,1024]{1,0:T(8,128)(2,1)S(1)} %convert_element_type.6.refs_4_), channel_id=1, source_target_pairs={{0,192},{64,0},{128,64},{192,128},{1,193},{65,1},{129,65},{193,129... | collective-permute-start | bytes 884744 | tf_op jit(solution)/shard_map/ppermute | solution.py:307
  47.6 0.9 collective-permute-start.7
  48.5 4.7 %collective-permute-done.8.below.refs_8_ = bf16[144,1024]{1,0:T(8,128)(2,1)S(1)} collective-permute-done((bf16[144,1024]{1,0:T(8,128)(2,1)S(1)}, bf16[144,1024]{1,0:T(8,128)(2,1)S(1)}, u32[]{:S(2)}, u32[]{:S(2)}) %collective-permute-start.8) | collective-permute-done | bytes 294944 | tf_op jit(solution)/shard_map/ppermute | solution.py:307
  53.2 2.4 %collective-permute-done.7.above.refs_5_ = bf16[144,1024]{1,0:T(8,128)(2,1)S(1)} collective-permute-done((bf16[144,1024]{1,0:T(8,128)(2,1)S(1)}, bf16[144,1024]{1,0:T(8,128)(2,1)S(1)}, u32[]{:S(2)}, u32[]{:S(2)}) %collective-permute-start.7) | collective-permute-done | bytes 294944 | tf_op jit(solution)/shard_map/ppermute | solution.py:307
  55.6 1.4 %all-to-all-done.1.parts = bf16[8,128,128]{2,1,0:T(8,128)(2,1)S(1)} async-done(((bf16[8,128,128]{2,1,0:T(8,128)(2,1)}), bf16[8,128,128]{2,1,0:T(8,128)(2,1)S(1)}, u32[]{:S(2)}, u32[]{:S(2)}) %all-to-all-start.1) | async-done | bytes 262176 | tf_op jit(solution)/shard_map/all_to_all | solution.py:363
  57.0 1.4 %add_up.1 = (bf16[8,128,128]{2,1,0:T(8,128)(2,1)}, bf16[80,1024]{1,0:T(8,128)(2,1)}, bf16[64,1024]{1,0:T(8,128)(2,1)}) custom-call(bf16[8,128,128]{2,1,0:T(8,128)(2,1)S(1)} %all-to-all-done.1.parts, bf16[144,1024]{1,0:T(8,128)(2,1)S(1)} %collective-permute-done.7.above.refs_5_, bf16[144,1024]{1,0:T(8,128)(2,1)S(1)} %collective-permute-done.8.below.refs_8_), custom_call_target="tpu_custom_call" | custom-call | tf_op jit(solution)/shard_map/add_up/pallas_call | solution.py:365
  58.4 5.8 %all-to-all-start.2 = ((bf16[8,128,128]{2,1,0:T(8,128)(2,1)}), bf16[8,128,128]{2,1,0:T(8,128)(2,1)S(1)}, u32[]{:S(2)}, u32[]{:S(2)}) async-start(bf16[8,128,128]{2,1,0:T(8,128)(2,1)} %get-tuple-element.36), calls=%async_computation.2 | async-start | bytes 524288 | tf_op jit(solution)/shard_map/all_to_all | solution.py:380
  64.2 0.0 collective-permute-start.9
  64.2 3.2 %collective-permute-start.10 = (bf16[64,1024]{1,0:T(8,128)(2,1)}, bf16[64,1024]{1,0:T(8,128)(2,1)S(1)}, u32[]{:S(2)}, u32[]{:S(2)}) collective-permute-start(bf16[64,1024]{1,0:T(8,128)(2,1)} %get-tuple-element.38), channel_id=1, source_target_pairs={{0,192},{64,0},{128,64},{192,128},{1,193},{65,1},{129,65},{193,129... | collective-permute-start | bytes 393224 | tf_op jit(solution)/shard_map/ppermute | solution.py:307
  67.5 0.1 pad_add_fusion.place
  67.5 2.8 %collective-permute-done.10.refs_7_ = bf16[64,1024]{1,0:T(8,128)(2,1)S(1)} collective-permute-done((bf16[64,1024]{1,0:T(8,128)(2,1)}, bf16[64,1024]{1,0:T(8,128)(2,1)S(1)}, u32[]{:S(2)}, u32[]{:S(2)}) %collective-permute-start.10) | collective-permute-done | bytes 131104 | tf_op jit(solution)/shard_map/ppermute | solution.py:307
  70.3 0.7 collective-permute-done.9.refs_6_
  71.0 3.7 %all-to-all-done.2.sketches = bf16[8,128,128]{2,1,0:T(8,128)(2,1)S(1)} async-done(((bf16[8,128,128]{2,1,0:T(8,128)(2,1)}), bf16[8,128,128]{2,1,0:T(8,128)(2,1)S(1)}, u32[]{:S(2)}, u32[]{:S(2)}) %all-to-all-start.2) | async-done | bytes 262176 | tf_op jit(solution)/shard_map/all_to_all | solution.py:380
  74.7 6.0 %second_pass.1 = (bf16[1024,128]{1,0:T(8,128)(2,1)}, f32[96,128]{1,0:T(8,128)}, f32[96,128]{1,0:T(8,128)}, f32[96,128]{1,0:T(8,128)}, f32[96,128]{1,0:T(8,128)}) custom-call(s32[3]{0:T(128)S(1)} %pad_add_fusion.place, bf16[8,128,128]{2,1,0:T(8,128)(2,1)S(1)} %all-to-all-done.2.sketches, bf16[256,1024]{1,0:T(8,128)(2,1)S(1)} %convert_element_type.7.refs_0_, ...), custom_call_target="tpu_custom_call" | custom-call | tf_op jit(solution)/shard_map/second_pass/pallas_call | solution.py:383
  80.7 6.2 %all-to-all-start.3 = ((bf16[32,32,128]{2,1,0:T(8,128)(2,1)}), bf16[32,32,128]{2,1,0:T(8,128)(2,1)S(1)}, u32[]{:S(2)}, u32[]{:S(2)}) async-start(bf16[32,32,128]{2,1,0:T(8,128)(2,1)} %bitcast.19), calls=%async_computation.3 | async-start | bytes 524288 | tf_op jit(solution)/shard_map/all_to_all | solution.py:397
  86.9 1.9 %collective-permute-start.11 = (f32[96,128]{1,0:T(8,128)}, f32[96,128]{1,0:T(8,128)S(1)}, u32[]{:S(2)}, u32[]{:S(2)}) collective-permute-start(f32[96,128]{1,0:T(8,128)} %get-tuple-element.41), channel_id=1, source_target_pairs={{0,64},{64,128},{128,192},{192,0},{1,65},{65,129},{129,193},{193,1... | collective-permute-start | bytes 147464 | tf_op jit(solution)/shard_map/ppermute | solution.py:307
  88.8 2.7 %collective-permute-start.12 = (f32[96,128]{1,0:T(8,128)}, f32[96,128]{1,0:T(8,128)S(1)}, u32[]{:S(2)}, u32[]{:S(2)}) collective-permute-start(f32[96,128]{1,0:T(8,128)} %get-tuple-element.42), channel_id=1, source_target_pairs={{0,128},{64,192},{128,0},{192,64},{1,129},{65,193},{129,1},{193,65... | collective-permute-start | bytes 147464 | tf_op jit(solution)/shard_map/ppermute | solution.py:307
  91.5 1.5 %collective-permute-start.13 = (f32[96,128]{1,0:T(8,128)}, f32[96,128]{1,0:T(8,128)S(1)}, u32[]{:S(2)}, u32[]{:S(2)}) collective-permute-start(f32[96,128]{1,0:T(8,128)} %get-tuple-element.43), channel_id=1, source_target_pairs={{0,192},{64,0},{128,64},{192,128},{1,193},{65,1},{129,65},{193,129... | collective-permute-start | bytes 147464 | tf_op jit(solution)/shard_map/ppermute | solution.py:307
  92.9 0.0 collective-permute-done.11.refs_0_
  92.9 2.1 %collective-permute-done.12.refs_1_ = f32[96,128]{1,0:T(8,128)S(1)} collective-permute-done((f32[96,128]{1,0:T(8,128)}, f32[96,128]{1,0:T(8,128)S(1)}, u32[]{:S(2)}, u32[]{:S(2)}) %collective-permute-start.12) | collective-permute-done | bytes 49184 | tf_op jit(solution)/shard_map/ppermute | solution.py:307
  95.1 0.7 collective-permute-done.13.refs_2_
  95.8 2.7 %all-to-all-done.3.parts = bf16[32,32,128]{2,1,0:T(8,128)(2,1)S(1)} async-done(((bf16[32,32,128]{2,1,0:T(8,128)(2,1)}), bf16[32,32,128]{2,1,0:T(8,128)(2,1)S(1)}, u32[]{:S(2)}, u32[]{:S(2)}) %all-to-all-start.3) | async-done | bytes 262176 | tf_op jit(solution)/shard_map/all_to_all | solution.py:397
  98.5 2.3 %finish.1 = (f32[8,32,64]{2,1,0:T(8,128)}, f32[8,32,64]{2,1,0:T(8,128)}) custom-call(s32[3]{0:T(128)S(1)} %pad_add_fusion.place, bf16[32,32,128]{2,1,0:T(8,128)(2,1)S(1)} %all-to-all-done.3.parts, f32[96,128]{1,0:T(8,128)} %get-tuple-element.40.own_far, f32[96,128]{1,0:T(8,128)S(1)} %collective-permute-done.11.refs_0_, ...), custom_call_target="tpu_custom_call" | custom-call | tf_op jit(solution)/shard_map/finish/pallas_call | solution.py:400
  (9 shorter events, 0.0 us)
Async XLA Ops:
  0.6 10.5 %copy-start.4 = (bf16[2,64,128]{2,1,0:T(8,128)(2,1)S(1)}, bf16[2,64,128]{2,1,0:T(8,128)(2,1)}, u32[]{:S(2)}) copy-start(bf16[2,64,128]{2,1,0:T(8,128)(2,1)} %param.11) | copy-start | bytes 98308
  5.3 31.6 %collective-permute-start.4 = (bf16[256,1024]{1,0:T(8,128)(2,1)}, bf16[256,1024]{1,0:T(8,128)(2,1)S(1)}, u32[]{:S(2)}, u32[]{:S(2)}) collective-permute-start(bf16[256,1024]{1,0:T(8,128)(2,1)} %get-tuple-element.25), channel_id=1, source_target_pairs={{0,64},{64,128},{128,192},{192,0},{1,65},{65,129},{129,193},{193,1... | collective-permute-start | bytes 1572872 | tf_op jit(solution)/shard_map/ppermute | solution.py:307
  6.9 30.0 %collective-permute-start.5 = (bf16[256,1024]{1,0:T(8,128)(2,1)}, bf16[256,1024]{1,0:T(8,128)(2,1)S(1)}, u32[]{:S(2)}, u32[]{:S(2)}) collective-permute-start(bf16[256,1024]{1,0:T(8,128)(2,1)} %get-tuple-element.26), channel_id=1, source_target_pairs={{0,128},{64,192},{128,0},{192,64},{1,129},{65,193},{129,1},{193,65... | collective-permute-start | bytes 1572872 | tf_op jit(solution)/shard_map/ppermute | solution.py:307
  9.8 27.1 %collective-permute-start.6 = (bf16[256,1024]{1,0:T(8,128)(2,1)}, bf16[256,1024]{1,0:T(8,128)(2,1)S(1)}, u32[]{:S(2)}, u32[]{:S(2)}) collective-permute-start(bf16[256,1024]{1,0:T(8,128)(2,1)} %get-tuple-element.27), channel_id=1, source_target_pairs={{0,192},{64,0},{128,64},{192,128},{1,193},{65,1},{129,65},{193,129... | collective-permute-start | bytes 1572872 | tf_op jit(solution)/shard_map/ppermute | solution.py:307
  11.2 1.2 %collective-permute-start = (bf16[128,128]{1,0:T(8,128)(2,1)S(1)}, bf16[128,128]{1,0:T(8,128)(2,1)S(1)}, u32[]{:S(2)}, u32[]{:S(2)}) collective-permute-start(bf16[128,128]{1,0:T(8,128)(2,1)S(1)} %bitcast.25), channel_id=1, source_target_pairs={{0,1},{1,0},{2,3},{3,2},{4,5},{5,4},{6,7},{7,6},{8,9},{9,8},{10,11... | collective-permute-start | bytes 98312 | tf_op jit(solution)/shard_map/ppermute | solution.py:307
  12.4 11.2 %copy-start = (bf16[2,128,128]{2,1,0:T(8,128)(2,1)}, bf16[2,128,128]{2,1,0:T(8,128)(2,1)S(1)}, u32[]{:S(2)}) copy-start(bf16[2,128,128]{2,1,0:T(8,128)(2,1)S(1)} %pad_maximum_fusion.refs_0_) | copy-start | bytes 196612
  12.4 7.0 %collective-permute-start.3 = (bf16[2,128,128]{2,1,0:T(8,128)(2,1)S(1)}, bf16[2,128,128]{2,1,0:T(8,128)(2,1)S(1)}, u32[]{:S(2)}, u32[]{:S(2)}) collective-permute-start(bf16[2,128,128]{2,1,0:T(8,128)(2,1)S(1)} %pad_maximum_fusion.refs_0_), channel_id=1, source_target_pairs={{0,6},{2,0},{4,2},{6,4},{1,7},{3,1},{5,3},{7,5},{8,14},{10,8},{12,... | collective-permute-start | bytes 196616 | tf_op jit(solution)/shard_map/ppermute | solution.py:307
  13.5 6.5 %collective-permute-start.2 = (bf16[2,128,128]{2,1,0:T(8,128)(2,1)S(1)}, bf16[2,128,128]{2,1,0:T(8,128)(2,1)S(1)}, u32[]{:S(2)}, u32[]{:S(2)}) collective-permute-start(bf16[2,128,128]{2,1,0:T(8,128)(2,1)S(1)} %pad_maximum_fusion.refs_0_), channel_id=1, source_target_pairs={{0,4},{2,6},{4,0},{6,2},{1,5},{3,7},{5,1},{7,3},{8,12},{10,14},{12... | collective-permute-start | bytes 196616 | tf_op jit(solution)/shard_map/ppermute | solution.py:307
  19.3 4.3 %copy-start.1 = (bf16[2,128,128]{2,1,0:T(8,128)(2,1)}, bf16[2,128,128]{2,1,0:T(8,128)(2,1)S(1)}, u32[]{:S(2)}) copy-start(bf16[2,128,128]{2,1,0:T(8,128)(2,1)S(1)} %collective-permute-done.3.refs_3_) | copy-start | bytes 196612
  19.4 4.3 %collective-permute-start.1 = (bf16[2,128,128]{2,1,0:T(8,128)(2,1)S(1)}, bf16[2,128,128]{2,1,0:T(8,128)(2,1)S(1)}, u32[]{:S(2)}, u32[]{:S(2)}) collective-permute-start(bf16[2,128,128]{2,1,0:T(8,128)(2,1)S(1)} %pad_maximum_fusion.refs_0_), channel_id=1, source_target_pairs={{0,2},{2,4},{4,6},{6,0},{1,3},{3,5},{5,7},{7,1},{8,10},{10,12},{12... | collective-permute-start | bytes 196616 | tf_op jit(solution)/shard_map/ppermute | solution.py:307
  20.0 3.6 %copy-start.2 = (bf16[2,128,128]{2,1,0:T(8,128)(2,1)}, bf16[2,128,128]{2,1,0:T(8,128)(2,1)S(1)}, u32[]{:S(2)}) copy-start(bf16[2,128,128]{2,1,0:T(8,128)(2,1)S(1)} %collective-permute-done.2.refs_2_) | copy-start | bytes 196612
  23.6 0.6 copy-start.3
  27.6 9.3 %all-to-all-start = ((bf16[4,128,128]{2,1,0:T(8,128)(2,1)}), bf16[4,128,128]{2,1,0:T(8,128)(2,1)S(1)}, u32[]{:S(2)}, u32[]{:S(2)}) async-start(bf16[4,128,128]{2,1,0:T(8,128)(2,1)} %get-tuple-element.30), calls=%async_computation | async-start | bytes 262144 | tf_op jit(solution)/shard_map/all_to_all | solution.py:349
  38.0 18.9 %all-to-all-start.1 = ((bf16[8,128,128]{2,1,0:T(8,128)(2,1)}), bf16[8,128,128]{2,1,0:T(8,128)(2,1)S(1)}, u32[]{:S(2)}, u32[]{:S(2)}) async-start(bf16[8,128,128]{2,1,0:T(8,128)(2,1)} %first_pass.1), calls=%async_computation.1 | async-start | bytes 524288 | tf_op jit(solution)/shard_map/all_to_all | solution.py:363
  46.5 6.7 %collective-permute-start.8 = (bf16[144,1024]{1,0:T(8,128)(2,1)S(1)}, bf16[144,1024]{1,0:T(8,128)(2,1)S(1)}, u32[]{:S(2)}, u32[]{:S(2)}) collective-permute-start(bf16[144,1024]{1,0:T(8,128)(2,1)S(1)} %convert_element_type.6.refs_4_), channel_id=1, source_target_pairs={{0,192},{64,0},{128,64},{192,128},{1,193},{65,1},{129,65},{193,129... | collective-permute-start | bytes 884744 | tf_op jit(solution)/shard_map/ppermute | solution.py:307
  47.6 7.9 %collective-permute-start.7 = (bf16[144,1024]{1,0:T(8,128)(2,1)S(1)}, bf16[144,1024]{1,0:T(8,128)(2,1)S(1)}, u32[]{:S(2)}, u32[]{:S(2)}) collective-permute-start(bf16[144,1024]{1,0:T(8,128)(2,1)S(1)} %convert_element_type.6.refs_4_), channel_id=1, source_target_pairs={{0,64},{64,128},{128,192},{192,0},{1,65},{65,129},{129,193},{193,1... | collective-permute-start | bytes 884744 | tf_op jit(solution)/shard_map/ppermute | solution.py:307
  58.4 16.3 %all-to-all-start.2 = ((bf16[8,128,128]{2,1,0:T(8,128)(2,1)}), bf16[8,128,128]{2,1,0:T(8,128)(2,1)S(1)}, u32[]{:S(2)}, u32[]{:S(2)}) async-start(bf16[8,128,128]{2,1,0:T(8,128)(2,1)} %get-tuple-element.36), calls=%async_computation.2 | async-start | bytes 524288 | tf_op jit(solution)/shard_map/all_to_all | solution.py:380
  64.2 6.7 %collective-permute-start.9 = (bf16[80,1024]{1,0:T(8,128)(2,1)}, bf16[80,1024]{1,0:T(8,128)(2,1)S(1)}, u32[]{:S(2)}, u32[]{:S(2)}) collective-permute-start(bf16[80,1024]{1,0:T(8,128)(2,1)} %get-tuple-element.37), channel_id=1, source_target_pairs={{0,64},{64,128},{128,192},{192,0},{1,65},{65,129},{129,193},{193,1... | collective-permute-start | bytes 491528 | tf_op jit(solution)/shard_map/ppermute | solution.py:307
  64.2 6.1 %collective-permute-start.10 = (bf16[64,1024]{1,0:T(8,128)(2,1)}, bf16[64,1024]{1,0:T(8,128)(2,1)S(1)}, u32[]{:S(2)}, u32[]{:S(2)}) collective-permute-start(bf16[64,1024]{1,0:T(8,128)(2,1)} %get-tuple-element.38), channel_id=1, source_target_pairs={{0,192},{64,0},{128,64},{192,128},{1,193},{65,1},{129,65},{193,129... | collective-permute-start | bytes 393224 | tf_op jit(solution)/shard_map/ppermute | solution.py:307
  80.7 17.8 %all-to-all-start.3 = ((bf16[32,32,128]{2,1,0:T(8,128)(2,1)}), bf16[32,32,128]{2,1,0:T(8,128)(2,1)S(1)}, u32[]{:S(2)}, u32[]{:S(2)}) async-start(bf16[32,32,128]{2,1,0:T(8,128)(2,1)} %bitcast.19), calls=%async_computation.3 | async-start | bytes 524288 | tf_op jit(solution)/shard_map/all_to_all | solution.py:397
  86.9 6.0 %collective-permute-start.11 = (f32[96,128]{1,0:T(8,128)}, f32[96,128]{1,0:T(8,128)S(1)}, u32[]{:S(2)}, u32[]{:S(2)}) collective-permute-start(f32[96,128]{1,0:T(8,128)} %get-tuple-element.41), channel_id=1, source_target_pairs={{0,64},{64,128},{128,192},{192,0},{1,65},{65,129},{129,193},{193,1... | collective-permute-start | bytes 147464 | tf_op jit(solution)/shard_map/ppermute | solution.py:307
  88.8 6.3 %collective-permute-start.12 = (f32[96,128]{1,0:T(8,128)}, f32[96,128]{1,0:T(8,128)S(1)}, u32[]{:S(2)}, u32[]{:S(2)}) collective-permute-start(f32[96,128]{1,0:T(8,128)} %get-tuple-element.42), channel_id=1, source_target_pairs={{0,128},{64,192},{128,0},{192,64},{1,129},{65,193},{129,1},{193,65... | collective-permute-start | bytes 147464 | tf_op jit(solution)/shard_map/ppermute | solution.py:307
  91.5 4.3 %collective-permute-start.13 = (f32[96,128]{1,0:T(8,128)}, f32[96,128]{1,0:T(8,128)S(1)}, u32[]{:S(2)}, u32[]{:S(2)}) collective-permute-start(f32[96,128]{1,0:T(8,128)} %get-tuple-element.43), channel_id=1, source_target_pairs={{0,192},{64,0},{128,64},{192,128},{1,193},{65,1},{129,65},{193,129... | collective-permute-start | bytes 147464 | tf_op jit(solution)/shard_map/ppermute | solution.py:307
